TPU v7x, 32 devices: a whole 2x2x4 slice. The times are simulated.
32 devices in a mesh: batch: 4 (over x, core), blk: 8 (over z, y).
Axes of the slice: x: 2, y: 2, z: 4, core: 2. Of those that a mesh axis runs over, the one named last changes fastest.
Arguments:
- tokens_in: bfloat16 [4, 1024, 1024], P('batch', 'blk'), may hold values from -6 to 6
- clip_lengths: int32 [4, 8], P('batch'), may hold values from 1 to 1017, as said below
- attn_gain: bfloat16 [1024], replicated, may hold values from 0.099609375 to 1.8984375
- attn_shift: bfloat16 [1024], replicated, may hold values from -3 to 3
- qkv_weight: bfloat16 [1024, 3072], replicated, may hold values from -0.25 to 0.25
- qkv_bias: bfloat16 [3072], replicated, may hold values from -3 to 3
- proj_weight: bfloat16 [1024, 1024], replicated, may hold values from -1.5 to 1.5
- proj_bias: bfloat16 [1024], replicated, may hold values from -3 to 3
- mlp_gain: bfloat16 [1024], replicated, may hold values from 0.099609375 to 1.8984375
- mlp_shift: bfloat16 [1024], replicated, may hold values from -3 to 3
- up_weight: bfloat16 [1024, 4096], replicated, may hold values from -0.1875 to 0.1875
- up_bias: bfloat16 [4096], replicated, may hold values from -3 to 3
- down_weight: bfloat16 [4096, 1024], replicated, may hold values from -0.09375 to 0.09375
- down_bias: bfloat16 [1024], replicated, may hold values from -3 to 3
- out_cotangent: bfloat16 [4, 1024, 1024], P('batch', 'blk'), may hold values from -6 to 6
Outputs:
- layer_out: bfloat16 [4, 1024, 1024], P('batch', 'blk')
- tokens_grad: float32 [4, 1024, 1024], P('batch', 'blk')
- attn_gain_grad: float32 [1024], P(('batch', 'blk'))
- attn_shift_grad: float32 [1024], P(('batch', 'blk'))
- qkv_weight_grad: float32 [1024, 3072], P(('batch', 'blk'))
- qkv_bias_grad: float32 [3072], P(('batch', 'blk'))
- proj_weight_grad: float32 [1024, 1024], P(('batch', 'blk'))
- proj_bias_grad: float32 [1024], P(('batch', 'blk'))
- mlp_gain_grad: float32 [1024], P(('batch', 'blk'))
- mlp_shift_grad: float32 [1024], P(('batch', 'blk'))
- up_weight_grad: float32 [1024, 4096], P(('batch', 'blk'))
- up_bias_grad: float32 [4096], P(('batch', 'blk'))
- down_weight_grad: float32 [4096, 1024], P(('batch', 'blk'))
- down_bias_grad: float32 [1024], P(('batch', 'blk'))
Inputs may be any that keep to these rules, and one draw needn't show every extreme that they name: `clip_lengths`: the 8 lengths of each row sum to 1024; in every row one clip starts among the first 128 tokens and ends among the last 128, and the other clips together hold fewer than 128 tokens.
All inputs are finite; a program needn't handle non-finite values.
Results may differ from a plain program's by a relative error of at most 0.025.
Values may be sent and summed in bfloat16 or wider, within the bound.
No kernel may reach another device: no remote copies, remote signals or barrier semaphores. Data moves between devices by JAX's collectives and lax.ppermute only.
A program may use at most 320 MiB of HBM per device.

v0:
```python
import math

import jax
import jax.numpy as jnp
from jax import lax
from jax.sharding import PartitionSpec as P

H = 16
HD = 64


NEG_FILL = -1e30


def pair_table():
    part_map = [0] * 10 + [1] * 11 + [2] * 11
    freq_list = [10000.0 ** (-rank / 10.0) for rank in range(10)] + [
        10000.0 ** (-rank / 11.0) for rank in range(11)
    ] * 2
    table_rows = [
        [freq_list[column] if part_map[column] == axis_id else 0.0 for column in range(32)]
        for axis_id in range(3)
    ]
    return jnp.array(table_rows, dtype=jnp.float32)


def clip_of(lengths_row, positions):
    clip_end = jnp.cumsum(lengths_row)
    return jnp.sum((positions[:, None] >= clip_end[None, :]).astype(jnp.int32), axis=1)


def clip_layout(lengths_row, positions):
    clip_end = jnp.cumsum(lengths_row)
    starts = clip_end - lengths_row
    clip_ids = jnp.sum((positions[:, None] >= clip_end[None, :]).astype(jnp.int32), axis=1)
    member = clip_ids[:, None] == jnp.arange(lengths_row.shape[0], dtype=jnp.int32)[None, :]
    within = positions - jnp.sum(jnp.where(member, starts[None, :], 0), axis=1)
    coords = jnp.stack([within // 196, within // 14 % 14, within % 14], axis=1).astype(jnp.float32)
    angles = jnp.dot(coords, pair_table(), precision=lax.Precision.HIGHEST)
    return (clip_ids, jnp.cos(angles), jnp.sin(angles))


def rotate(values, cos_tab, sin_tab):
    half_dim = values.shape[-1] // 2
    first_half = values[..., :half_dim]
    second_half = values[..., half_dim:]
    cos_b = cos_tab[:, None, :]
    sin_b = sin_tab[:, None, :]
    return jnp.concatenate(
        [first_half * cos_b - second_half * sin_b, first_half * sin_b + second_half * cos_b],
        axis=-1,
    )


def norm_fwd(values, gain_vec, shift_vec):
    row_mean = jnp.mean(values, -1, keepdims=True)
    centered = values - row_mean
    inv_std = lax.rsqrt(jnp.mean(centered * centered, -1, keepdims=True) + 1e-06)
    normalized = centered * inv_std
    return (normalized * gain_vec + shift_vec, normalized, inv_std)


def norm_back(upstream, normalized, inv_std, gain_vec):
    scaled = upstream * gain_vec
    inner = (
        scaled
        - jnp.mean(scaled, -1, keepdims=True)
        - normalized * jnp.mean(scaled * normalized, -1, keepdims=True)
    )
    return (inv_std * inner, jnp.sum(upstream * normalized, 0), jnp.sum(upstream, 0))


def outer_sum(left, right):
    return lax.dot_general(
        left, right, (((0,), (0,)), ((), ())), preferred_element_type=jnp.float32
    )


def times_transposed(left, right):
    return lax.dot_general(
        left, right, (((1,), (1,)), ((), ())), preferred_element_type=jnp.float32
    )


def add_rows(buffer, block, first_key):
    current = lax.dynamic_slice_in_dim(buffer, first_key, block.shape[0], 0)
    return lax.dynamic_update_slice_in_dim(buffer, current + block, first_key, 0)


def in_blocks(block_step, running, pieces):
    row_count = pieces[0].shape[0]
    block_rows = math.gcd(row_count, 2048)

    def advance(block_idx, state):
        first_row = block_idx * block_rows
        sliced = tuple(
            (lax.dynamic_slice_in_dim(piece, first_row, block_rows, 0) for piece in pieces)
        )
        return block_step(state, sliced, first_row)

    return lax.fori_loop(0, row_count // block_rows, advance, running)


def shards(
    tokens_in,
    clip_lengths,
    attn_gain,
    attn_shift,
    qkv_weight,
    qkv_bias,
    proj_weight,
    proj_bias,
    mlp_gain,
    mlp_shift,
    up_weight,
    up_bias,
    down_weight,
    down_bias,
    out_cotangent,
):
    tok_rows = tokens_in.shape[1]
    model_width = tokens_in.shape[2]
    seq_len = tok_rows * lax.axis_size("blk")
    lens_row = clip_lengths[0]
    own_pos = lax.axis_index("blk") * tok_rows + jnp.arange(tok_rows, dtype=jnp.int32)
    clip_q, cos_tab, sin_tab = clip_layout(lens_row, own_pos)
    residual = tokens_in[0].astype(jnp.float32)
    attn_gain_f = attn_gain.astype(jnp.float32)
    mlp_gain_f = mlp_gain.astype(jnp.float32)
    normed, hat_one, inv_one = norm_fwd(residual, attn_gain_f, attn_shift.astype(jnp.float32))
    normed_low = normed.astype(jnp.bfloat16)
    qkv_mixed = jnp.dot(
        normed_low, qkv_weight, preferred_element_type=jnp.float32
    ) + qkv_bias.astype(jnp.float32)
    query_h = rotate(qkv_mixed[:, :model_width].reshape(tok_rows, H, HD), cos_tab, sin_tab).astype(
        jnp.bfloat16
    )
    key_low = (
        rotate(
            qkv_mixed[:, model_width : 2 * model_width].reshape(tok_rows, H, HD), cos_tab, sin_tab
        )
        .astype(jnp.bfloat16)
        .reshape(tok_rows, model_width)
    )
    value_low = qkv_mixed[:, 2 * model_width :].astype(jnp.bfloat16)

    def block_scores(keys_blk, first_key):
        key_count = keys_blk.shape[0]
        clip_k = clip_of(lens_row, first_key + jnp.arange(key_count, dtype=jnp.int32))
        raw_scores = jnp.einsum(
            "qhd,khd->hqk",
            query_h,
            keys_blk.reshape(key_count, H, HD),
            preferred_element_type=jnp.float32,
        )
        allowed = (clip_q[:, None] == clip_k[None, :])[None]
        return (jnp.where(allowed, 0.125 * raw_scores, NEG_FILL), allowed)

    def stats_step(state, sliced, first_key):
        row_max, row_sum = state
        scores, allowed = block_scores(sliced[0], first_key)
        new_max = jnp.maximum(row_max, jnp.max(scores, -1))
        weights = jnp.where(allowed, jnp.exp(scores - new_max[:, :, None]), 0.0)
        return (new_max, row_sum * jnp.exp(row_max - new_max) + jnp.sum(weights, -1))

    stats_init = (
        jnp.full((H, tok_rows), NEG_FILL, jnp.float32),
        jnp.zeros((H, tok_rows), jnp.float32),
    )
    row_max, row_sum = in_blocks(
        stats_step, stats_init, (lax.all_gather(key_low, "blk", axis=0, tiled=True),)
    )
    log_sum = row_max + jnp.log(row_sum)

    def output_step(acc_state, sliced, first_key):
        keys_blk, values_blk = sliced
        key_count = keys_blk.shape[0]
        scores, allowed = block_scores(keys_blk, first_key)
        weights = jnp.where(allowed, jnp.exp(scores - log_sum[:, :, None]), 0.0)
        return acc_state + jnp.einsum(
            "hqk,khd->qhd",
            weights.astype(jnp.bfloat16),
            values_blk.reshape(key_count, H, HD),
            preferred_element_type=jnp.float32,
        )

    acc_init = jnp.zeros((tok_rows, H, HD), jnp.float32)
    attended_f = in_blocks(
        output_step,
        acc_init,
        (
            lax.all_gather(key_low, "blk", axis=0, tiled=True),
            lax.all_gather(value_low, "blk", axis=0, tiled=True),
        ),
    )
    attended_low = attended_f.reshape(tok_rows, model_width).astype(jnp.bfloat16)
    middle = (
        residual
        + jnp.dot(attended_low, proj_weight, preferred_element_type=jnp.float32)
        + proj_bias.astype(jnp.float32)
    )
    normed_two, hat_two, inv_two = norm_fwd(middle, mlp_gain_f, mlp_shift.astype(jnp.float32))
    normed_two_low = normed_two.astype(jnp.bfloat16)
    hidden = jnp.dot(
        normed_two_low, up_weight, preferred_element_type=jnp.float32
    ) + up_bias.astype(jnp.float32)
    active_low = jax.nn.gelu(hidden).astype(jnp.bfloat16)
    result = (
        middle
        + jnp.dot(active_low, down_weight, preferred_element_type=jnp.float32)
        + down_bias.astype(jnp.float32)
    )
    layer_out = result.astype(jnp.bfloat16)[None]
    cot_low = out_cotangent[0]
    cot_f = cot_low.astype(jnp.float32)
    grad_down_w = outer_sum(active_low, cot_low)
    grad_down_b = jnp.sum(cot_f, 0)
    d_active = times_transposed(cot_low, down_weight)
    hidden_unused, gelu_back = jax.vjp(jax.nn.gelu, hidden)
    d_hidden = gelu_back(d_active)[0].astype(jnp.bfloat16)
    grad_up_w = outer_sum(normed_two_low, d_hidden)
    grad_up_b = jnp.sum(d_hidden.astype(jnp.float32), 0)
    d_normed_two = times_transposed(d_hidden, up_weight)
    d_mid_norm, grad_mlp_gain, grad_mlp_shift = norm_back(
        d_normed_two, hat_two, inv_two, mlp_gain_f
    )
    d_middle = cot_f + d_mid_norm
    d_branch = d_middle.astype(jnp.bfloat16)
    grad_proj_w = outer_sum(attended_low, d_branch)
    grad_proj_b = jnp.sum(d_branch.astype(jnp.float32), 0)
    d_attended = (
        times_transposed(d_branch, proj_weight).astype(jnp.bfloat16).reshape(tok_rows, H, HD)
    )
    delta = jnp.einsum("qhd,qhd->hq", d_attended.astype(jnp.float32), attended_f)

    def back_step(state, sliced, first_key):
        dq_acc, buffers = state
        keys_blk, values_blk = sliced
        key_count = keys_blk.shape[0]
        scores, allowed = block_scores(keys_blk, first_key)
        weights = jnp.where(allowed, jnp.exp(scores - log_sum[:, :, None]), 0.0)
        d_weights = jnp.einsum(
            "qhd,khd->hqk",
            d_attended,
            values_blk.reshape(key_count, H, HD),
            preferred_element_type=jnp.float32,
        )
        d_scores = (weights * (d_weights - delta[:, :, None])).astype(jnp.bfloat16)
        dq_acc = dq_acc + 0.125 * jnp.einsum(
            "hqk,khd->qhd",
            d_scores,
            keys_blk.reshape(key_count, H, HD),
            preferred_element_type=jnp.float32,
        )
        d_keys = 0.125 * jnp.einsum(
            "hqk,qhd->khd", d_scores, query_h, preferred_element_type=jnp.float32
        )
        d_values = jnp.einsum(
            "hqk,qhd->khd",
            weights.astype(jnp.bfloat16),
            d_attended,
            preferred_element_type=jnp.float32,
        )
        key_buffer = add_rows(buffers[0], d_keys.reshape(key_count, model_width), first_key)
        value_buffer = add_rows(buffers[1], d_values.reshape(key_count, model_width), first_key)
        buffers = (key_buffer, value_buffer)
        return (dq_acc, buffers)

    buffer_init = (
        jnp.zeros((seq_len, model_width), jnp.float32),
        jnp.zeros((seq_len, model_width), jnp.float32),
    )
    back_init = (jnp.zeros((tok_rows, H, HD), jnp.float32), buffer_init)
    d_queries, key_grads = in_blocks(
        back_step,
        back_init,
        (
            lax.all_gather(key_low, "blk", axis=0, tiled=True),
            lax.all_gather(value_low, "blk", axis=0, tiled=True),
        ),
    )
    d_keys_own, d_values_own = (
        lax.psum_scatter(key_grads[0], "blk", scatter_dimension=0, tiled=True),
        lax.psum_scatter(key_grads[1], "blk", scatter_dimension=0, tiled=True),
    )
    d_queries_pre = rotate(d_queries, cos_tab, -sin_tab).reshape(tok_rows, model_width)
    d_keys_pre = rotate(d_keys_own.reshape(tok_rows, H, HD), cos_tab, -sin_tab).reshape(
        tok_rows, model_width
    )
    d_mixed = jnp.concatenate([d_queries_pre, d_keys_pre, d_values_own], axis=1).astype(
        jnp.bfloat16
    )
    grad_qkv_w = outer_sum(normed_low, d_mixed)
    grad_qkv_b = jnp.sum(d_mixed.astype(jnp.float32), 0)
    d_normed = times_transposed(d_mixed, qkv_weight)
    d_res_norm, grad_attn_gain, grad_attn_shift = norm_back(d_normed, hat_one, inv_one, attn_gain_f)
    tokens_grad = (d_middle + d_res_norm)[None]
    summed = (
        lax.psum_scatter(grad_qkv_w, ("batch", "blk"), scatter_dimension=0, tiled=True),
        lax.psum_scatter(grad_proj_w, ("batch", "blk"), scatter_dimension=0, tiled=True),
        lax.psum_scatter(grad_up_w, ("batch", "blk"), scatter_dimension=0, tiled=True),
        lax.psum_scatter(grad_down_w, ("batch", "blk"), scatter_dimension=0, tiled=True),
        lax.psum_scatter(grad_attn_gain, ("batch", "blk"), scatter_dimension=0, tiled=True),
        lax.psum_scatter(grad_attn_shift, ("batch", "blk"), scatter_dimension=0, tiled=True),
        lax.psum_scatter(grad_qkv_b, ("batch", "blk"), scatter_dimension=0, tiled=True),
        lax.psum_scatter(grad_proj_b, ("batch", "blk"), scatter_dimension=0, tiled=True),
        lax.psum_scatter(grad_mlp_gain, ("batch", "blk"), scatter_dimension=0, tiled=True),
        lax.psum_scatter(grad_mlp_shift, ("batch", "blk"), scatter_dimension=0, tiled=True),
        lax.psum_scatter(grad_up_b, ("batch", "blk"), scatter_dimension=0, tiled=True),
        lax.psum_scatter(grad_down_b, ("batch", "blk"), scatter_dimension=0, tiled=True),
    )
    return (
        layer_out,
        tokens_grad,
        summed[4],
        summed[5],
        summed[0],
        summed[6],
        summed[1],
        summed[7],
        summed[8],
        summed[9],
        summed[2],
        summed[10],
        summed[3],
        summed[11],
    )


def solution(mesh):
    placed = (
        P("batch", "blk", None),
        P("batch", None),
        P(),
        P(),
        P(),
        P(),
        P(),
        P(),
        P(),
        P(),
        P(),
        P(),
        P(),
        P(),
        P("batch", "blk", None),
    )
    return jax.shard_map(
        shards,
        mesh=mesh,
        in_specs=placed,
        out_specs=(
            P("batch", "blk", None),
            P("batch", "blk", None),
            P(("batch", "blk")),
            P(("batch", "blk")),
            P(("batch", "blk"), None),
            P(("batch", "blk")),
            P(("batch", "blk"), None),
            P(("batch", "blk")),
            P(("batch", "blk")),
            P(("batch", "blk")),
            P(("batch", "blk"), None),
            P(("batch", "blk")),
            P(("batch", "blk"), None),
            P(("batch", "blk")),
        ),
        check_vma=False,
    )
```

profile of v0, /device:TPU:0, one launch (start us, length us, event | category | flops | bytes accessed | tf_op | source)
XLA Modules:
  0.0 1372.9 jit_solution(10443173002430680793)
XLA Ops:
  7.2 0.8 convert_element_type.107
  8.1 0.7 convert_element_type.105
  8.8 0.7 convert_element_type.104
  9.4 1.1 convert_reduce_fusion.3
  10.5 1.2 fusion.29
  12.2 4.0 convolution_add_fusion.1
  16.2 1.1 copy-done.8
  17.4 0.9 fusion.59
  18.8 1.2 copy.48
  20.6 0.7 pad_maximum_fusion.2
  21.4 1.8 slice.73
  23.3 0.6 convert_element_type.115
  23.8 1.3 convert_element_type.119
  25.2 0.7 convert_element_type.117
  25.8 0.7 convert_element_type.116
  26.5 0.7 convert_reduce_fusion.5
  27.3 0.8 broadcast_compare_fusion
  28.1 47.2 %all-gather.5.cloned.1.call-done = bf16[1024,1024]{0,1:T(8,128)(2,1)} async-done(((bf16[128,1024]{0,1:T(8,128)(2,1)}), bf16[1024,1024]{0,1:T(8,128)(2,1)}) %all-gather.5.cloned.1.call-update) | async-done | bytes 2097168 | tf_op jit(solution)/shard_map/all_gather | solution.py:192
  75.3 3.2 fusion.1
  78.5 2.6 select_reduce_fusion
  81.1 0.6 copy-done.2
  81.7 43.7 %all-gather.3.cloned.1.call-done = bf16[1024,1024]{1,0:T(8,128)(2,1)} async-done(((bf16[128,1024]{1,0:T(8,128)(2,1)}), bf16[1024,1024]{1,0:T(8,128)(2,1)}) %all-gather.3.cloned.1.call-update) | async-done | bytes 2097168 | tf_op jit(solution)/shard_map/all_gather | solution.py:193
  125.5 3.9 copy.46
  129.5 7.2 bitcast_convert_fusion
  137.6 1.3 convolution_add_fusion
  139.2 1.4 slice-done.3
  140.5 4.5 convert_reduce_fusion
  145.0 3.5 multiply_reduce_fusion
  148.6 0.9 convert_reduce_fusion.4
  149.4 1.5 convolution_convert_fusion
  151.0 1.1 copy.49
  152.1 7.9 fusion.55
  160.1 1.3 fusion.30
  161.9 7.0 multiply_convert_fusion
  168.9 3.1 convolution_multiply_fusion
  172.2 0.9 copy-done.24
  173.1 2.6 fusion.46
  175.8 0.6 copy-done.28
  176.5 0.9 copy-done.7
  177.4 4.6 fusion.10
  182.0 65.1 %reduce-scatter.9.cloned.1.call-done = f32[128,1024]{0,1:T(8,128)} async-done(((f32[1024,1024]{0,1:T(8,128)}), f32[128,1024]{0,1:T(8,128)}) %reduce-scatter.9.cloned.1.call-update) | async-done | bytes 524304 | tf_op jit(solution)/shard_map/reduce_scatter | solution.py:284
  247.1 1.1 convert.43
  248.2 91.1 %reduce-scatter.7.cloned.1.call-done = f32[128,1024]{0,1:T(8,128)} async-done(((f32[1024,1024]{0,1:T(8,128)}), f32[128,1024]{0,1:T(8,128)}) %reduce-scatter.7.cloned.1.call-update) | async-done | bytes 524304 | tf_op jit(solution)/shard_map/reduce_scatter | solution.py:283
  339.3 1.3 subtract_convert_fusion.1
  340.7 6.4 fusion.50
  347.5 0.9 copy-done.10
  348.4 8.2 fusion.54
  356.7 1.5 copy-done.6
  358.2 9.1 fusion.31
  367.3 0.6 copy-done.46
  368.0 5.7 fusion.13
  374.1 5.4 fusion.28
  379.5 43.1 %all-reduce.8 = (f32[1024]{0:T(1024)S(1)}, f32[1024]{0:T(1024)S(1)}, f32[3072]{0:T(1024)S(1)}, f32[1024]{0:T(1024)S(1)}, f32[1024]{0:T(1024)S(1)}, /*index=5*/f3...) all-reduce(f32[1024]{0:T(1024)S(1)} %get-tuple-element.80, ...), channel_id=4, replica_groups=mesh['batch'=4,'blk'=8] {'batch','blk'}, use_global_device_ids=true, to_apply=%region_17.18.clone | all-reduce | flops 13312 | bytes 106496
  422.6 0.6 dynamic-slice
  423.1 0.6 dynamic-slice.1
  423.7 0.6 dynamic-slice.3
  424.3 0.6 dynamic-slice.4
  426.1 0.6 dynamic-slice.2
  426.6 0.6 dynamic-slice.6
  427.2 1.0 fusion.27
  428.3 57.5 %reduce-scatter.13.cloned.1.call-done = f32[32,1024]{1,0:T(8,128)} async-done(((f32[1024,1024]{1,0:T(8,128)}), f32[32,1024]{1,0:T(8,128)}) %reduce-scatter.13.cloned.1.call-update) | async-done | bytes 131088 | tf_op jit(solution)/shard_map/reduce_scatter | solution.py:300
  485.8 159.8 %reduce-scatter.11.cloned.1.call-done = f32[32,3072]{1,0:T(8,128)} async-done(((f32[1024,3072]{1,0:T(8,128)}), f32[32,3072]{1,0:T(8,128)}) %reduce-scatter.11.cloned.1.call-update) | async-done | bytes 393232 | tf_op jit(solution)/shard_map/reduce_scatter | solution.py:299
  645.6 360.2 %reduce-scatter.15.cloned.1.call-done = f32[32,4096]{1,0:T(8,128)} async-done(((f32[1024,4096]{1,0:T(8,128)}), f32[32,4096]{1,0:T(8,128)}) %reduce-scatter.15.cloned.1.call-update) | async-done | bytes 524304 | tf_op jit(solution)/shard_map/reduce_scatter | solution.py:301
  1005.8 360.3 %reduce-scatter.17.cloned.1.call-done = f32[128,1024]{1,0:T(8,128)} async-done(((f32[4096,1024]{1,0:T(8,128)}), f32[128,1024]{1,0:T(8,128)}) %reduce-scatter.17.cloned.1.call-update) | async-done | bytes 524304 | tf_op jit(solution)/shard_map/reduce_scatter | solution.py:302
  (146 shorter events, 5.5 us)
Async XLA Ops:
  7.2 129.5 %copy-start = (bf16[1024,1024]{1,0:T(8,128)(2,1)S(1)}, bf16[1024,1024]{1,0:T(8,128)(2,1)}, u32[]{:S(2)}) copy-start(bf16[1024,1024]{1,0:T(8,128)(2,1)} %param.22) | copy-start | bytes 6291460
  7.2 68.1 %all-gather.5.cloned.1.call-start = ((), (), s32[]{:S(2)}) async-start(), calls=%async_computation.7 | async-start | bytes 2359296 | tf_op jit(solution)/shard_map/all_gather | solution.py:192
  10.5 1.2 copy-start.32
  11.7 0.5 copy-start.42
  16.2 1.1 copy-start.8
  17.4 1.1 copy-start.49
  17.4 2.7 copy-start.50
  18.6 1.8 copy-start.48
  18.7 1.7 copy-start.47
  18.8 4.4 copy-start.45
  20.4 0.9 copy-start.25
  20.4 0.9 copy-start.27
  20.6 57.9 %copy-start.18 = (bf16[128,16,32]{0,2,1:T(8,128)(2,1)}, bf16[128,16,32]{0,2,1:T(8,128)(2,1)S(1)}, u32[]{:S(2)}) copy-start(bf16[128,16,32]{0,2,1:T(8,128)(2,1)S(1)} %get-tuple-element.129) | copy-start | bytes 393220
  21.3 104.1 %all-gather.3.cloned.1.call-start = ((), (), s32[]{:S(2)}) async-start(), calls=%async_computation.6 | async-start | bytes 2359296 | tf_op jit(solution)/shard_map/all_gather | solution.py:193
  23.2 223.9 %reduce-scatter.9.cloned.1.call-start = ((), (), s32[]{:S(2)}) async-start(), calls=%async_computation.9 | async-start | bytes 4718592 | tf_op jit(solution)/shard_map/reduce_scatter | solution.py:284
  28.1 101.4 %copy-start.20 = (pred[128,1024]{1,0:T(8,128)(4,1)}, pred[128,1024]{1,0:T(8,128)(4,1)S(1)}, u32[]{:S(2)}) copy-start(pred[128,1024]{1,0:T(8,128)(4,1)S(1)} %broadcast_compare_fusion) | copy-start | bytes 393220
  78.5 3.2 copy-start.2
  81.7 47.7 %copy-start.44 = (f32[16,128]{1,0:T(8,128)}, f32[16,128]{1,0:T(8,128)S(1)}, u32[]{:S(2)}) copy-start(f32[16,128]{1,0:T(8,128)S(1)} %log_add_fusion) | copy-start | bytes 24580
  129.4 8.1 slice-start
  129.4 7.3 copy-start.4
  129.4 7.2 copy-start.36
  129.5 8.0 slice-start.1
  136.7 2.2 copy-start.23
  136.7 0.8 copy-start.29
  136.7 2.3 slice-start.2
  137.3 11.3 copy-start.30
  137.5 11.0 copy-start.34
  137.5 1.6 copy-start.21
  137.6 3.0 slice-start.3
  140.5 4.5 copy-start.5
  145.0 3.5 copy-start.9
  152.1 7.9 copy-start.22
  160.0 1.8 copy-start.17
  160.1 179.3 %reduce-scatter.7.cloned.1.call-start = ((), (), s32[]{:S(2)}) async-start(), calls=%async_computation.8 | async-start | bytes 4718592 | tf_op jit(solution)/shard_map/reduce_scatter | solution.py:283
  161.9 7.1 copy-start.19
  168.9 3.2 copy-start.3
  172.2 0.9 copy-start.24
  172.2 313.6 %reduce-scatter.13.cloned.1.call-start = ((), (), s32[]{:S(2)}) async-start(), calls=%async_computation.11 | async-start | bytes 4325376 | tf_op jit(solution)/shard_map/reduce_scatter | solution.py:300
  175.7 0.7 copy-start.28
  175.7 1.6 copy-start.7
  175.8 469.8 %reduce-scatter.11.cloned.1.call-start = ((), (), s32[]{:S(2)}) async-start(), calls=%async_computation.10 | async-start | bytes 12976128 | tf_op jit(solution)/shard_map/reduce_scatter | solution.py:299
  177.4 161.9 %copy-start.26 = (f32[128,32]{0,1:T(8,128)S(1)}, f32[128,32]{0,1:T(8,128)}, u32[]{:S(2)}) copy-start(f32[128,32]{0,1:T(8,128)} %copy-done.25) | copy-start | bytes 49156
  182.0 158.7 %copy-start.33 = (f32[128]{0:T(128)S(1)}, f32[128]{0:T(128)}, u32[]{:S(2)}) copy-start(f32[128]{0:T(128)} %copy-done.32) | copy-start | bytes 1540
  182.0 158.8 %copy-start.43 = (f32[128]{0:T(128)S(1)}, f32[128]{0:T(128)}, u32[]{:S(2)}) copy-start(f32[128]{0:T(128)} %copy-done.42) | copy-start | bytes 1540
  248.2 99.0 %copy-start.11 = (bf16[128,1024]{0,1:T(8,128)(2,1)}, bf16[128,1024]{0,1:T(8,128)(2,1)S(1)}, u32[]{:S(2)}) copy-start(bf16[128,1024]{0,1:T(8,128)(2,1)S(1)} %convert.43) | copy-start | bytes 786436
  340.7 6.5 copy-start.13
  340.7 6.5 copy-start.15
  347.2 1.2 copy-start.10
  347.2 1.2 copy-start.31
  347.2 1.2 copy-start.35
  347.2 658.5 %reduce-scatter.15.cloned.1.call-start = ((), (), s32[]{:S(2)}) async-start(), calls=%async_computation.12 | async-start | bytes 17301504 | tf_op jit(solution)/shard_map/reduce_scatter | solution.py:301
  356.6 1.6 copy-start.6
  356.6 1009.4 %reduce-scatter.17.cloned.1.call-start = ((), (), s32[]{:S(2)}) async-start(), calls=%async_computation.13 | async-start | bytes 17301504 | tf_op jit(solution)/shard_map/reduce_scatter | solution.py:302
  367.3 0.7 copy-start.46
  368.0 5.7 copy-start.12
  368.0 5.7 copy-start.14
  368.0 5.7 copy-start.16
  374.0 5.4 copy-start.37
  374.0 5.4 copy-start.38
  374.0 5.4 copy-start.39
  374.0 5.4 copy-start.40
  374.0 5.4 copy-start.41
  374.0 992.0 %copy-start.1 = (bf16[1024,1024]{1,0:T(8,128)(2,1)S(1)}, bf16[1024,1024]{1,0:T(8,128)(2,1)}, u32[]{:S(2)}) copy-start(bf16[1024,1024]{1,0:T(8,128)(2,1)} %param.22) | copy-start | bytes 6291460
Sparse Core Ops, SparseCore 0:
  21.5 53.7 all-gather.4
  78.0 47.4 all-gather.2
  160.2 86.9 reduce-scatter.8
  251.1 88.2 reduce-scatter.6
  342.0 143.7 reduce-scatter.12
  492.3 153.2 reduce-scatter.10
  648.6 357.1 reduce-scatter.14
  1008.7 357.3 reduce-scatter.16
where the time goes:
time: 1370 us
  waiting for transfers between devices  1190 us (87%)
  matrix products  86.1 us (6%)
  blocking collectives  43.1 us (3%)
  local copies, waits for them, and re-layouts  24 us (2%)
  other arithmetic  19.3 us (1%)
  between operations  14.8 us (1%)
    reduce_scatter x1, waiting for transfers between devices, shards(): lax.psum_scatter(grad_down_w, ('batch', 'blk'), scatter_dimension=0, tile...  360 us
    reduce_scatter x1, waiting for transfers between devices, shards(): lax.psum_scatter(grad_up_w, ('batch', 'blk'), scatter_dimension=0, tiled=...  360 us
    reduce_scatter x1, waiting for transfers between devices, shards(): lax.psum_scatter(grad_qkv_w, ('batch', 'blk'), scatter_dimension=0, tiled...  160 us
    reduce_scatter x1, waiting for transfers between devices, shards(): lax.psum_scatter(key_grads[0], 'blk', scatter_dimension=0, tiled=True)  91.1 us
    reduce_scatter x1, waiting for transfers between devices, shards(): lax.psum_scatter(key_grads[1], 'blk', scatter_dimension=0, tiled=True)  65.1 us
    reduce_scatter x1, waiting for transfers between devices, shards(): lax.psum_scatter(grad_proj_w, ('batch', 'blk'), scatter_dimension=0, tile...  57.5 us
    all_gather x1, waiting for transfers between devices, shards(): lax.all_gather(key_low, 'blk', axis=0, tiled=True)  47.2 us
    all_gather x1, waiting for transfers between devices, shards(): lax.all_gather(value_low, 'blk', axis=0, tiled=True)  43.7 us
  transfers between devices with their start and end apart: 8, of which 8 were waited for; matrix products, arithmetic and copies ran while one was open for 5% of the time, Pallas kernels for 0%

commit v1 on v0

--- a/solution.py
+++ b/solution.py
@@ -3,6 +3,9 @@
 import jax
 import jax.numpy as jnp
 from jax import lax
+from jax.experimental import pallas as pl
+from jax.experimental.pallas import tpu as pltpu
+from jax.sharding import Mesh
 from jax.sharding import PartitionSpec as P
 
 H = 16
@@ -327,7 +330,655 @@
     )
 
 
+BF = jnp.bfloat16
+F32 = jnp.float32
+AXES = ("x", "core", "zh", "zl", "y")
+ROW = ("zh", "zl", "y")
+CLUSTER = ("core", "zl", "y")
+GELU_A = 0.7978845608028654
+GELU_B = 0.044715
+
+
+def mm(left, right):
+    return jnp.dot(left, right, preferred_element_type=F32)
+
+
+def swap_over(value, *names):
+    mask = sum(16 >> AXES.index(name) for name in names)
+    return lax.ppermute(value, AXES, [(i, i ^ mask) for i in range(32)])
+
+
+def whole(shape):
+    zeros = (0,) * len(shape)
+    return pl.BlockSpec(shape, lambda *_: zeros)
+
+
+def call(body, grid, in_specs, out_specs, out_shape, scratch, flops, nbytes, args, scalars=None):
+    params = pltpu.CompilerParams(vmem_limit_bytes=48 << 20)
+    cost = pl.CostEstimate(flops=flops, bytes_accessed=nbytes, transcendentals=0)
+    if scalars is None:
+        return pl.pallas_call(
+            body,
+            grid=grid,
+            in_specs=in_specs,
+            out_specs=out_specs,
+            out_shape=out_shape,
+            scratch_shapes=scratch,
+            compiler_params=params,
+            cost_estimate=cost,
+        )(*args)
+    return pl.pallas_call(
+        body,
+        grid_spec=pltpu.PrefetchScalarGridSpec(
+            num_scalar_prefetch=1,
+            grid=grid,
+            in_specs=in_specs,
+            out_specs=out_specs,
+            scratch_shapes=scratch,
+        ),
+        out_shape=out_shape,
+        compiler_params=params,
+        cost_estimate=cost,
+    )(scalars, *args)
+
+
+def arr(shape, dtype):
+    return jax.ShapeDtypeStruct(shape, dtype)
+
+
+def standardize(x):
+    mean = jnp.mean(x, -1, keepdims=True)
+    centered = x - mean
+    inv = lax.rsqrt(jnp.mean(centered * centered, -1, keepdims=True) + 1e-06)
+    return centered * inv, inv
+
+
+def swap_halves(x):
+    lane = lax.broadcasted_iota(jnp.int32, x.shape, 1)
+    return jnp.where(lane % 64 < 32, pltpu.roll(x, 96, 1), pltpu.roll(x, 32, 1))
+
+
+def gelu_both(h):
+    t = jnp.tanh(GELU_A * (h + GELU_B * h * h * h))
+    act = 0.5 * h * (1.0 + t)
+    slope = 0.5 * (1.0 + t) + 0.5 * h * (1.0 - t * t) * (GELU_A * (1.0 + 3.0 * GELU_B * h * h))
+    return act, slope
+
+
+def down_back_body(cot, down, d_act, bias_part):
+    @pl.when(pl.program_id(0) == 0)
+    def _():
+        bias_part[...] = jnp.sum(cot[...].astype(F32), 0, keepdims=True)
+
+    d_act[...] = times_transposed(cot[...], down[...])
+
+
+def qkv_body(
+    b0, b1, b2, b3a, b3b, gain, shift, w3, bias3, cos, sin, q_out, k_out, v_out, hat_out, normed
+):
+    g = gain[...].astype(F32)
+    s = shift[...].astype(F32)
+    first = 0
+    for block in (b0, b1, b2, b3a, b3b):
+        rows = block.shape[0]
+        hat, _ = standardize(block[...].astype(F32))
+        hat_out[first : first + rows, :] = hat.astype(BF)
+        normed[first : first + rows, :] = (hat * g + s).astype(BF)
+        first += rows
+    mixed = mm(normed[...], w3[...]) + bias3[...].astype(F32)
+    c = cos[...]
+    sn = sin[...]
+    q = mixed[:, :128]
+    k = mixed[:, 128:256]
+    q_out[...] = ((q * c + swap_halves(q) * sn) * 0.125).astype(BF)
+    k_out[...] = (k * c + swap_halves(k) * sn).astype(BF)
+    v_out[...] = mixed[:, 256:].astype(BF)
+
+
+def head_mask(shape, head):
+    return lax.broadcasted_iota(jnp.int32, shape, 1) // 64 == head
+
+
+def attend_body(place, q, k0, k1, v0, v1, id_col, id_row, att_f, att_low, probs):
+    keys = jnp.concatenate([k0[...], k1[...]], 0)
+    values = jnp.concatenate([v0[...], v1[...]], 0)
+    queries = q[...]
+    allowed = id_col[...] == id_row[...]
+    halves = []
+    for head in range(2):
+        mine = jnp.where(head_mask(queries.shape, head), queries, jnp.zeros_like(queries))
+        scores = jnp.where(allowed, times_transposed(keys, mine), NEG_FILL)
+        weights = jnp.exp(scores - jnp.max(scores, 0, keepdims=True))
+        low = (weights / jnp.sum(weights, 0, keepdims=True)).astype(BF)
+        probs[head] = low
+        halves.append(outer_sum(values, low)[64 * head : 64 * head + 64])
+    out = jnp.concatenate(halves, 0).T
+    att_f[...] = out
+    step = pl.program_id(0)
+    att_low[place[0] ^ (2 * step)] = out[:128].astype(BF)
+    att_low[place[0] ^ (2 * step + 1)] = out[128:].astype(BF)
+
+
+def proj_body(att, tok, proj_w, proj_b, gain, shift, middle, normed, att_rows):
+    rows = jnp.concatenate([att[k] for k in range(8)], 1)
+    att_rows[...] = rows
+    mid = tok[...].astype(F32) + mm(rows, proj_w[...]) + proj_b[...].astype(F32)
+    middle[...] = mid
+    hat, _ = standardize(mid)
+    normed[...] = (hat * gain[...].astype(F32) + shift[...].astype(F32)).astype(BF)
+
+
+def mlp_body(
+    normed, d_act, up_w, up_b, middle, cot, gain, proj_w,
+    active, up_bias, d_mid, d_branch, d_att, vectors, acc,
+):
+    step = pl.program_id(0)
+    hidden = mm(normed[...], up_w[...]) + up_b[...].astype(F32)
+    act, slope = gelu_both(hidden)
+    active[...] = act.astype(BF)
+    d_hidden = (d_act[...] * slope).astype(BF)
+    up_bias[...] = jnp.sum(d_hidden.astype(F32), 0, keepdims=True)
+    part = times_transposed(d_hidden, up_w[...])
+
+    @pl.when(step == 0)
+    def _():
+        acc[...] = part
+
+    @pl.when(step > 0)
+    def _():
+        acc[...] += part
+
+    @pl.when(step == pl.num_programs(0) - 1)
+    def _():
+        up = acc[...]
+        hat, inv = standardize(middle[...])
+        e = up * gain[...].astype(F32)
+        inner = e - jnp.mean(e, -1, keepdims=True) - hat * jnp.mean(e * hat, -1, keepdims=True)
+        d_m = cot[...].astype(F32) + inv * inner
+        d_mid[...] = d_m
+        d_b = d_m.astype(BF)
+        d_branch[...] = d_b
+        vectors[0:1] = jnp.sum(up * hat, 0, keepdims=True)
+        vectors[1:2] = jnp.sum(up, 0, keepdims=True)
+        vectors[2:3] = jnp.sum(d_b.astype(F32), 0, keepdims=True)
+        d_a = times_transposed(d_b, proj_w[...]).astype(BF)
+        for k in range(8):
+            d_att[k] = d_a[:, 128 * k : 128 * k + 128]
+
+
+def proj_grad_body(place, att, d_branch, out):
+    grad = outer_sum(att[...], d_branch[...])
+    for i in range(32):
+        rel = place[1] ^ i
+        x, core, zh, zl, y = ((rel >> s) & 1 for s in (4, 3, 2, 1, 0))
+        out[core * 16 + y * 8 + zl * 4 + x * 2 + zh] = grad[32 * i : 32 * i + 32]
+
+
+def mlp_grad_body(place, *refs):
+    n_refs, c_refs = refs[0:8], refs[8:16]
+    up_w, up_b, down_w = refs[16:19]
+    down_keep, down_send, up_keep, up_send, n_all, c_all, grad = refs[19:]
+    for j in range(8):
+        n_all[128 * j : 128 * j + 128, :] = n_refs[j][...]
+        c_all[128 * j : 128 * j + 128, :] = c_refs[j][...]
+    n = n_all[...]
+    c = c_all[...]
+    act, slope = gelu_both(mm(n, up_w[...]) + up_b[...].astype(F32))
+    grad_down = outer_sum(act.astype(BF), c)
+    for g in range(4):
+        rows = grad_down[128 * g : 128 * g + 128]
+        if g < 2:
+            down_keep[g] = rows
+        else:
+            down_send[g - 2] = rows.astype(BF)
+    d_hidden = (times_transposed(c, down_w[...]) * slope).astype(BF)
+    for g in range(4):
+        lanes = pl.ds(pl.multiple_of((place[2] ^ g) * 128, 128), 128)
+        grad[:, lanes] = outer_sum(n, d_hidden[:, 128 * g : 128 * g + 128])
+    for rz in range(2):
+        for core in range(2):
+            first = core * 256 + (place[4] ^ rz) * 128
+            keep = pl.multiple_of(place[3] * 512 + first, 128)
+            send = pl.multiple_of((1 - place[3]) * 512 + first, 128)
+            up_keep[rz, core] = grad[pl.ds(keep, 128), :]
+            up_send[rz, core] = grad[pl.ds(send, 128), :].astype(BF)
+
+
+def attend_back_body(
+    place, probs, d_att, att_f, q, k_all, v_all, cos, sin, d_all, bias_part, *rest
+):
+    pieces, (dq, dk, dv) = rest[:8], rest[8:]
+    step = pl.program_id(0)
+    keys = k_all[...]
+    values = v_all[...]
+    queries = q[...]
+    d_out = jnp.concatenate([d_att[place[0] ^ (2 * step)], d_att[place[0] ^ (2 * step + 1)]], 0)
+    products = (d_out.astype(F32) * att_f[...]).T
+    key_parts, value_parts, query_parts = [], [], []
+    for head in range(2):
+        weights = probs[head]
+        mine = jnp.where(head_mask(d_out.shape, head), d_out, jnp.zeros_like(d_out))
+        delta = jnp.sum(products[64 * head : 64 * head + 64], 0, keepdims=True)
+        d_weights = times_transposed(values, mine)
+        d_scores = (weights.astype(F32) * (d_weights - delta)).astype(BF)
+        key_parts.append(mm(d_scores, queries))
+        value_parts.append(mm(weights, d_out))
+        query_parts.append(outer_sum(keys, d_scores)[64 * head : 64 * head + 64])
+    first = head_mask((1024, 128), 0)
+    dk_new = jnp.where(first, key_parts[0], key_parts[1])
+    dv_new = jnp.where(first, value_parts[0], value_parts[1])
+    dq[pl.ds(pl.multiple_of(step * 256, 256), 256), :] = jnp.concatenate(query_parts, 0).T
+
+    @pl.when(step == 0)
+    def _():
+        dk[...] = dk_new
+        dv[...] = dv_new
+
+    @pl.when(step > 0)
+    def _():
+        dk[...] += dk_new
+        dv[...] += dv_new
+
+    @pl.when(step == pl.num_programs(0) - 1)
+    def _():
+        total = jnp.zeros((1, 384), F32)
+        for j in range(8):
+            rows = slice(128 * j, 128 * j + 128)
+            c = cos[rows, :]
+            sn = sin[rows, :]
+            back_q = 0.125 * dq[rows, :]
+            back_k = dk[rows, :]
+            piece = jnp.concatenate(
+                [
+                    back_q * c - swap_halves(back_q) * sn,
+                    back_k * c - swap_halves(back_k) * sn,
+                    dv[rows, :],
+                ],
+                1,
+            ).astype(BF)
+            pieces[j][...] = piece
+            d_all[rows, :] = piece
+            total = total + jnp.sum(piece.astype(F32), 0, keepdims=True)
+        bias_part[...] = total
+
+
+def rel_block(step, place):
+    rel = jnp.where(step < 2, 2, 0) + step % 2
+    return ((rel & 1) ^ place[3]) * 2 + ((rel >> 1) ^ place[5])
+
+
+def qkv_grad_body(place, h0, h1, d_all, bias_part, gain, shift, w3, send, keep, gain_part, shift_part):
+    step = pl.program_id(0)
+    d = d_all[...]
+    inner = outer_sum(h0[...], d[:512]) + outer_sum(h1[...], d[512:])
+    total = bias_part[...]
+    w = w3[...].astype(F32)
+    gain_part[...] = jnp.sum(w * inner, 1, keepdims=True)
+    shift_part[...] = jnp.sum(w * total, 1, keepdims=True)
+    grad = gain[...].astype(F32) * inner + shift[...].astype(F32) * total
+
+    @pl.when(step < 2)
+    def _():
+        send[0] = grad.astype(BF)
+
+    @pl.when(step >= 2)
+    def _():
+        keep[0] = grad
+
+
+def last_body(place, *refs):
+    pieces = refs[:8]
+    w, tok, d_mid, gain, out, d_mixed, acc = refs[8:]
+    step = pl.program_id(0)
+
+    @pl.when(step == 0)
+    def _():
+        for j in range(8):
+            lanes = pl.ds(pl.multiple_of((place[0] ^ j) * 128, 128), 128)
+            for p in range(3):
+                d_mixed[p, :, lanes] = pieces[j][:, 128 * p : 128 * p + 128]
+
+    part = times_transposed(d_mixed[step], w[...])
+
+    @pl.when(step == 0)
+    def _():
+        acc[...] = part
+
+    @pl.when(step > 0)
+    def _():
+        acc[...] += part
+
+    @pl.when(step == pl.num_programs(0) - 1)
+    def _():
+        hat, inv = standardize(tok[...].astype(F32))
+        e = acc[...] * gain[...].astype(F32)
+        inner = e - jnp.mean(e, -1, keepdims=True) - hat * jnp.mean(e * hat, -1, keepdims=True)
+        out[...] = d_mid[...] + inv * inner
+
+
+def row_tables(lens_row, k):
+    blocks = jnp.arange(8, dtype=jnp.int32) ^ k
+    pos = (blocks[:, None] * 128 + jnp.arange(128, dtype=jnp.int32)[None, :]).reshape(1024)
+    clip_end = jnp.cumsum(lens_row)
+    starts = clip_end - lens_row
+    ids = jnp.sum((pos[:, None] >= clip_end[None, :]).astype(jnp.int32), axis=1)
+    member = ids[:, None] == jnp.arange(lens_row.shape[0], dtype=jnp.int32)[None, :]
+    within = pos - jnp.sum(jnp.where(member, starts[None, :], 0), axis=1)
+    coords = jnp.stack([within // 196, within // 14 % 14, within % 14], axis=1).astype(F32)
+    pair = jnp.arange(128) % 32
+    table = pair_table()[:, pair]
+    angles = jnp.sum(coords[:, :, None] * table[None], axis=1)
+    sign = jnp.where(jnp.arange(128) % 64 < 32, -1.0, 1.0).astype(F32)
+    return ids, jnp.cos(angles), jnp.sin(angles) * sign[None, :]
+
+
+def row_gather(a):
+    half = a.shape[0] // 2
+
+    def local(v):
+        y1 = swap_over(v, "y")
+        z1 = swap_over(v, "zl")
+        return y1, z1, swap_over(z1[:half], "y"), swap_over(y1[half:], "zl")
+
+    far = swap_over(a, "zh")
+    return (a, *local(a)), (far, *local(far))
+
+
+def cluster_gather(a):
+    y1 = swap_over(a, "y")
+    z1 = swap_over(a, "zl")
+    d1 = swap_over(a, "y", "zl")
+    return [a, y1, z1, d1] + [swap_over(v, "core") for v in (a, y1, z1, d1)]
+
+
+def fast_shards(
+    tokens_in, clip_lengths, attn_gain, attn_shift, qkv_weight, qkv_bias, proj_weight, proj_bias,
+    mlp_gain, mlp_shift, up_weight, up_bias, down_weight, down_bias, out_cotangent,
+):
+    x, core, zh, zl, y = (lax.axis_index(name) for name in AXES)
+    k = zh * 4 + zl * 2 + y
+    me = x * 16 + core * 8 + k
+    place = jnp.stack([k, me, x * 2 + zh, x, zh, core]).astype(jnp.int32)
+    tok = tokens_in[0]
+    cot = out_cotangent[0]
+    row = lambda v: v.reshape(1, -1)
+
+    near, far = row_gather(tok)
+    cots = cluster_gather(lax.optimization_barrier((cot, far))[0])
+
+    ids, cos_tab, sin_tab = row_tables(clip_lengths[0], k)
+    w3 = jnp.concatenate(
+        [lax.dynamic_slice(qkv_weight, (0, p * 1024 + k * 128), (1024, 128)) for p in range(3)], 1
+    )
+    bias3 = jnp.concatenate(
+        [lax.dynamic_slice(qkv_bias, (p * 1024 + k * 128,), (128,)) for p in range(3)]
+    )
+    firsts = [
+        ((x ^ (g >> 1)) * 16 + core * 8 + (zh ^ (g & 1)) * 4 + zl * 2 + y) * 128 for g in range(4)
+    ]
+    up_part = jnp.concatenate([lax.dynamic_slice(up_weight, (0, f), (1024, 128)) for f in firsts], 1)
+    up_b_part = jnp.concatenate([lax.dynamic_slice(up_bias, (f,), (128,)) for f in firsts])
+    down_part = jnp.concatenate(
+        [lax.dynamic_slice(down_weight, (f, 0), (128, 1024)) for f in firsts], 0
+    )
+
+    d_act, down_bias_part = call(
+        down_back_body,
+        (4,),
+        [whole((128, 1024)), pl.BlockSpec((1024, 1024), lambda i: (i, 0))],
+        [pl.BlockSpec((128, 1024), lambda i: (0, i)), whole((1, 1024))],
+        [arr((128, 4096), F32), arr((1, 1024), F32)],
+        [],
+        1 << 30,
+        10 << 20,
+        (cot, down_weight),
+    )
+
+    def qkv_half(blocks, part):
+        rows = slice(512 * part, 512 * part + 512)
+        ins = (
+            *blocks, row(attn_gain), row(attn_shift), w3, row(bias3), cos_tab[rows], sin_tab[rows]
+        )
+        outs = [arr((512, 128), BF)] * 3 + [arr((512, 1024), BF)]
+        return call(
+            qkv_body,
+            (1,),
+            [whole(v.shape) for v in ins],
+            [whole(o.shape) for o in outs],
+            outs,
+            [pltpu.VMEM((512, 1024), BF)],
+            400 << 20,
+            4 << 20,
+            ins,
+        )
+
+    q0, k0, v0, hat0 = qkv_half(near, 0)
+    q1, k1, v1, hat1 = qkv_half(far, 1)
+    q_all = jnp.concatenate([q0, q1], 0)
+    k_all = jnp.concatenate([k0, k1], 0)
+    v_all = jnp.concatenate([v0, v1], 0)
+    half = whole((512, 128))
+    att_f, att_low, probs = call(
+        attend_body,
+        (4,),
+        [
+            pl.BlockSpec((256, 128), lambda i, s: (i, 0)), half, half, half, half,
+            whole((1024, 1)), pl.BlockSpec((1, 256), lambda i, s: (0, i)),
+        ],
+        [
+            pl.BlockSpec((256, 128), lambda i, s: (i, 0)),
+            whole((8, 128, 128)),
+            pl.BlockSpec((2, 1024, 256), lambda i, s: (0, 0, i)),
+        ],
+        [arr((1024, 128), F32), arr((8, 128, 128), BF), arr((2, 1024, 1024), BF)],
+        [],
+        1 << 30,
+        8 << 20,
+        (q_all, k0, k1, v0, v1, ids.reshape(1024, 1), ids.reshape(1, 1024)),
+        place,
+    )
+    att_in = lax.all_to_all(att_low, ROW, 0, 0, tiled=True)
+    ins = (
+        att_in, tok, proj_weight, row(proj_bias), row(mlp_gain), row(mlp_shift)
+    )
+    outs = [arr((128, 1024), F32), arr((128, 1024), BF), arr((128, 1024), BF)]
+    middle, normed2, att_rows = call(
+        proj_body,
+        (1,),
+        [whole(v.shape) for v in ins],
+        [whole(o.shape) for o in outs],
+        outs,
+        [],
+        256 << 20,
+        4 << 20,
+        ins,
+    )
+    normeds = cluster_gather(normed2)
+    wide = pl.BlockSpec((128, 1024), lambda i: (0, i))
+    fixed = whole((128, 1024))
+    active, up_bias_part, d_mid, d_branch, d_att, vectors = call(
+        mlp_body,
+        (4,),
+        [
+            fixed, wide, pl.BlockSpec((1024, 1024), lambda i: (0, i)),
+            pl.BlockSpec((1, 1024), lambda i: (0, i)), fixed, fixed, whole((1, 1024)),
+            whole((1024, 1024)),
+        ],
+        [
+            wide, pl.BlockSpec((1, 1024), lambda i: (0, i)), fixed, fixed, whole((8, 128, 128)),
+            whole((8, 1024)),
+        ],
+        [
+            arr((128, 4096), BF), arr((1, 4096), F32), arr((128, 1024), F32), arr((128, 1024), BF),
+            arr((8, 128, 128), BF), arr((8, 1024), F32),
+        ],
+        [pltpu.VMEM((128, 1024), F32)],
+        2 << 30,
+        16 << 20,
+        (normed2, d_act, up_weight, row(up_bias), middle, cot, row(mlp_gain), proj_weight),
+    )
+    d_att_in = lax.all_to_all(d_att, ROW, 0, 0, tiled=True)
+
+    result = middle + mm(active, down_weight) + down_bias.astype(F32)
+    layer_out = result.astype(BF)[None]
+
+    proj_parts = call(
+        proj_grad_body,
+        (1,),
+        [whole((128, 1024))] * 2,
+        whole((32, 32, 1024)),
+        arr((32, 32, 1024), F32),
+        [],
+        256 << 20,
+        5 << 20,
+        (att_rows, d_branch),
+        place,
+    )
+    total = proj_parts
+    for name in ("core", "y", "zl", "x", "zh"):
+        count = total.shape[0] // 2
+        total = total[:count] + swap_over(total[count:].astype(BF), name).astype(F32)
+    grad_proj = total[0]
+
+    ins = (*normeds, *cots, up_part, row(up_b_part), down_part)
+    outs = [
+        arr((2, 128, 1024), F32), arr((2, 128, 1024), BF), arr((2, 2, 128, 512), F32),
+        arr((2, 2, 128, 512), BF),
+    ]
+    down_keep, down_send, up_keep, up_send = call(
+        mlp_grad_body,
+        (1,),
+        [whole(v.shape) for v in ins],
+        [whole(o.shape) for o in outs],
+        outs,
+        [
+            pltpu.VMEM((1024, 1024), BF), pltpu.VMEM((1024, 1024), BF),
+            pltpu.VMEM((1024, 512), F32),
+        ],
+        4 << 30,
+        12 << 20,
+        ins,
+        place,
+    )
+
+    def two_sums(keep, send):
+        keep = keep + swap_over(send, "x").astype(F32)
+        return keep[0] + swap_over(keep[1].astype(BF), "zh").astype(F32)
+
+    grad_down = two_sums(down_keep, down_send)
+    grad_up = two_sums(up_keep, up_send).astype(BF)
+    grad_up = lax.all_to_all(grad_up.reshape(8, 32, 512), CLUSTER, 0, 0, tiled=True)
+    grad_up = grad_up.reshape(2, 4, 32, 2, 2, 128).transpose(2, 3, 0, 4, 1, 5)
+    grad_up = grad_up.reshape(32, 4096).astype(F32)
+
+    mids = jnp.concatenate(
+        [v.reshape(32, -1) for v in (vectors[0], vectors[1], vectors[2], down_bias_part, up_bias_part)],
+        1,
+    )
+    mids = jnp.sum(lax.all_to_all(mids, AXES, 0, 0, tiled=True), 0)
+
+    step_rows = pl.BlockSpec((256, 128), lambda i, s: (i, 0))
+    full = whole((1024, 128))
+    back = call(
+        attend_back_body,
+        (4,),
+        [
+            pl.BlockSpec((2, 1024, 256), lambda i, s: (0, 0, i)), whole((8, 128, 128)), step_rows,
+            step_rows, full, full, full, full,
+        ],
+        [whole((1024, 384)), whole((1, 384))] + [whole((128, 384))] * 8,
+        [arr((1024, 384), BF), arr((1, 384), F32)] + [arr((128, 384), BF)] * 8,
+        [pltpu.VMEM((1024, 128), F32)] * 3,
+        2 << 30,
+        8 << 20,
+        (probs, d_att_in, att_f, q_all, k_all, v_all, cos_tab, sin_tab),
+        place,
+    )
+    d_all, qkv_bias_part = back[:2]
+    pieces = back[2:]
+    moved = [pieces[0]] + [
+        swap_over(pieces[j], *[n for n, bit in zip(ROW, (4, 2, 1)) if j & bit]) for j in range(1, 8)
+    ]
+
+    block_of = lambda i, s: (rel_block(i, s), 0)
+    lanes_of = lambda i, s: (0, rel_block(i, s))
+    send, keep, gain_part, shift_part = call(
+        qkv_grad_body,
+        (4,),
+        [
+            pl.BlockSpec((512, 256), lanes_of), pl.BlockSpec((512, 256), lanes_of),
+            whole((1024, 384)), whole((1, 384)), pl.BlockSpec((256, 1), block_of),
+            pl.BlockSpec((256, 1), block_of), pl.BlockSpec((256, 384), block_of),
+        ],
+        [
+            pl.BlockSpec((1, 256, 384), lambda i, s: (jnp.minimum(i, 1), 0, 0)),
+            pl.BlockSpec((1, 256, 384), lambda i, s: (jnp.maximum(i - 2, 0), 0, 0)),
+            pl.BlockSpec((256, 1), block_of), pl.BlockSpec((256, 1), block_of),
+        ],
+        [
+            arr((2, 256, 384), BF), arr((2, 256, 384), F32), arr((1024, 1), F32),
+            arr((1024, 1), F32),
+        ],
+        [],
+        800 << 20,
+        4 << 20,
+        (
+            hat0, hat1, d_all, qkv_bias_part, attn_gain.reshape(1024, 1),
+            attn_shift.reshape(1024, 1), w3,
+        ),
+        place,
+    )
+    keep = keep + swap_over(send, "core").astype(F32)
+    grad_qkv = (keep[0] + swap_over(keep[1].astype(BF), "x").astype(F32)).astype(BF)
+    grad_qkv = lax.all_to_all(grad_qkv.reshape(8, 32, 384), ROW, 0, 0, tiled=True)
+    grad_qkv = grad_qkv.reshape(8, 32, 3, 128).transpose(1, 2, 0, 3).reshape(32, 3072).astype(F32)
+
+    spread = lax.dynamic_update_slice(
+        jnp.zeros((3, 1024), F32), qkv_bias_part.reshape(3, 128), (0, k * 128)
+    )
+    lates = jnp.concatenate(
+        [v.reshape(32, -1) for v in (gain_part, shift_part, spread)], 1
+    )
+    lates = jnp.sum(lax.all_to_all(lates, AXES, 0, 0, tiled=True), 0)
+
+    tokens_grad = call(
+        last_body,
+        (3,),
+        [whole((128, 384))] * 8
+        + [pl.BlockSpec((1024, 1024), lambda i, s: (0, i)), whole((128, 1024)), whole((128, 1024)),
+           whole((1, 1024))],
+        whole((128, 1024)),
+        arr((128, 1024), F32),
+        [pltpu.VMEM((3, 128, 1024), BF), pltpu.VMEM((128, 1024), F32)],
+        800 << 20,
+        8 << 20,
+        (*moved, qkv_weight, tok, d_mid, row(attn_gain)),
+        place,
+    )[None]
+
+    return (
+        layer_out, tokens_grad, lates[:32], lates[32:64], grad_qkv, lates[64:160], grad_proj,
+        mids[64:96], mids[:32], mids[32:64], grad_up, mids[128:256], grad_down, mids[96:128],
+    )
+
+
+def fast_solution(mesh):
+    wide_mesh = Mesh(mesh.devices.reshape(2, 2, 2, 2, 2), AXES)
+    batch, blk = AXES[:2], AXES[2:]
+    spread = P(batch, blk, None)
+    return jax.shard_map(
+        fast_shards,
+        mesh=wide_mesh,
+        in_specs=(spread, P(batch, None)) + (P(),) * 12 + (spread,),
+        out_specs=(spread, spread)
+        + tuple(P(AXES, None) if i in (2, 4, 8, 10) else P(AXES) for i in range(12)),
+        check_vma=False,
+    )
+
+
 def solution(mesh):
+    if tuple(mesh.devices.shape) == (4, 8):
+        return fast_solution(mesh)
     placed = (
         P("batch", "blk", None),
         P("batch", None),

time: 1370 us -> 267 us (0.19)
  waiting for transfers between devices: 1190 us -> 47.4 us
  matrix products: 86.1 us -> 5.43 us
  starting transfers between devices: 0.55 us -> 65.2 us
  Pallas kernels: 0 us -> 62.5 us
  blocking collectives: 43.1 us -> 0 us
  local copies, waits for them, and re-layouts: 24 us -> 60.4 us
    reduce_scatter x6 -> x0, waiting for transfers between devices: 1090 us -> none  [the longest x1 360 us: shards(): lax.psum_scatter(grad_down_w, ('batch', 'blk'), scatter_dimension=0, tile...]
    all_gather x2 -> x0, waiting for transfers between devices: 90.9 us -> none  [the longest x1 47.2 us: shards(): lax.all_gather(key_low, 'blk', axis=0, tiled=True)]
    dot_general x19 -> x1, matrix products: 86.1 us -> 5.43 us  [mm(): return jnp.dot(left, right, preferred_element_type=F32)]
    pallas_call x0 -> x11, Pallas kernels: none -> 62.5 us  [the longest x6 40.7 us: call(): pl.pallas_call(body, grid_spec=pltpu.PrefetchScalarGridSpec(num_scalar_pr...]
    unnamed x1 -> x0, blocking collectives: 43.1 us -> none
    ppermute x0 -> x41, starting transfers between devices: none -> 40.5 us  [swap_over(): return lax.ppermute(value, AXES, [(i, i ^ mask) for i in range(32)])]
    ppermute x0 -> x41, waiting for transfers between devices: none -> 30.7 us  [swap_over(): return lax.ppermute(value, AXES, [(i, i ^ mask) for i in range(32)])]
    all_to_all x0 -> x6, starting transfers between devices: none -> 24.6 us  [the longest x1 5.58 us: fast_shards(): mids = jnp.sum(lax.all_to_all(mids, AXES, 0, 0, tiled=True), 0)]
  transfers between devices with their start and end apart: 8 -> 47, of which waited for: 8 -> 12; matrix products, arithmetic and copies ran while one was open for 5% -> 20% of each run, Pallas kernels for 0% -> 19%
where the time goes in v1:
time: 267 us; the launch traced here: 265 us
  starting transfers between devices  65.2 us (24%)
  Pallas kernels  62.5 us (23%)
  local copies, waits for them, and re-layouts  60.4 us (23%)
  waiting for transfers between devices  47.4 us (18%)
  other arithmetic  22.9 us (9%)
  matrix products  5.43 us (2%)
    pallas_call x6, Pallas kernels, call(): pl.pallas_call(body, grid_spec=pltpu.PrefetchScalarGridSpec(num_scalar_pr...  40.7 us
    ppermute x41, starting transfers between devices, swap_over(): return lax.ppermute(value, AXES, [(i, i ^ mask) for i in range(32)])  40.5 us
    unnamed x166, local copies, waits for them, and re-layouts  34.8 us
    ppermute x41, waiting for transfers between devices, swap_over(): return lax.ppermute(value, AXES, [(i, i ^ mask) for i in range(32)])  30.7 us
    pallas_call x5, Pallas kernels, call(): pl.pallas_call(body, grid=grid, in_specs=in_specs, out_specs=out_specs, o...  21.8 us
    all_to_all x1, waiting for transfers between devices, fast_shards(): lates = jnp.sum(lax.all_to_all(lates, AXES, 0, 0, tiled=True), 0)  5.85 us
    all_to_all x1, starting transfers between devices, fast_shards(): mids = jnp.sum(lax.all_to_all(mids, AXES, 0, 0, tiled=True), 0)  5.58 us
    dot_general x1, matrix products, mm(): return jnp.dot(left, right, preferred_element_type=F32)  5.43 us
  transfers between devices with their start and end apart: 47, of which 12 were waited for; matrix products, arithmetic and copies ran while one was open for 20% of the time, Pallas kernels for 19%

profile of v1, /device:TPU:0, one launch (start us, length us, event | category | flops | bytes accessed | tf_op | source)
XLA Modules:
  0.0 265.3 jit_solution(6579994191568601795)
XLA Ops:
  0.6 3.0 %collective-permute-start = (bf16[128,1024]{1,0:T(8,128)(2,1)}, bf16[128,1024]{1,0:T(8,128)(2,1)S(1)}, u32[]{:S(2)}, u32[]{:S(2)}) collective-permute-start(bf16[128,1024]{1,0:T(8,128)(2,1)} %bitcast.68), channel_id=1, source_target_pairs={{0,1},{1,0},{2,3},{3,2},{4,5},{5,4},{6,7},{7,6},{8,9},{9,8},{10,11... | collective-permute-start | bytes 786440 | tf_op jit(solution)/shard_map/ppermute | solution.py:348
  3.7 1.6 collective-permute-start.1
  5.3 2.6 collective-permute-start.4
  7.9 1.4 gather_fusion
  11.7 1.9 sine_multiply_fusion
  16.1 2.2 constant_dynamic-slice_fusion.3
  18.3 6.0 %shard_map.267 = (f32[128,4096]{1,0:T(8,128)S(1)}, f32[1,1024]{1,0:T(1,128)S(1)}) custom-call(bf16[128,1024]{1,0:T(8,128)(2,1)S(1)} %bitcast.74, bf16[4096,1024]{1,0:T(8,128)(2,1)} %down.1), custom_call_target="tpu_custom_call" | custom-call | flops 1073741824 | bytes 10485760 | tf_op jit(solution)/shard_map/pallas_call | solution.py:360
  24.4 1.3 copy-done.4
  33.7 2.2 constant_dynamic-slice_fusion.7
  37.0 1.2 constant_dynamic-slice_fusion.10
  38.2 1.6 collective-permute-start.2
  39.8 1.6 collective-permute-start.3
  41.5 3.5 %collective-permute-done.6.b2 = bf16[128,1024]{1,0:T(8,128)(2,1)S(1)} collective-permute-done((bf16[128,1024]{1,0:T(8,128)(2,1)}, bf16[128,1024]{1,0:T(8,128)(2,1)S(1)}, u32[]{:S(2)}, u32[]{:S(2)}) %collective-permute-start.6) | collective-permute-done | bytes 262176 | tf_op jit(solution)/shard_map/ppermute | solution.py:348
  45.1 2.1 collective-permute-start.7
  47.8 1.4 shard_map.263
  50.2 2.1 collective-permute-done.8.b3b
  52.3 2.3 shard_map.264
  54.6 1.0 copy-done.14
  55.7 9.0 %shard_map.265 = (f32[1024,128]{1,0:T(8,128)S(1)}, bf16[8,128,128]{2,1,0:T(8,128)(2,1)}, bf16[2,1024,1024]{2,1,0:T(8,128)(2,1)}) custom-call(s32[6]{0:T(128)S(1)} %copy-done.43, bf16[1024,128]{1,0:T(8,128)(2,1)S(1)} %constant_dynamic-update-slice_fusion.q, bf16[512,128]{1,0:T(8,128)(2,1)S(1)} %get-tuple-element.57.k0, ...), custom_call_target="tpu_custom_call" | custom-call | flops 1073741824 | bytes 8388608 | tf_op jit(solution)/shard_map/pallas_call | solution.py:370
  65.5 4.2 %all-to-all-start = ((bf16[8,128,128]{2,1,0:T(8,128)(2,1)}), bf16[8,128,128]{2,1,0:T(8,128)(2,1)}, u32[]{:S(2)}, u32[]{:S(2)}) async-start(bf16[8,128,128]{2,1,0:T(8,128)(2,1)} %get-tuple-element.61), calls=%async_computation | async-start | bytes 524288 | tf_op jit(solution)/shard_map/all_to_all | solution.py:780
  70.4 2.4 pad_maximum_fusion.refs_16_
  72.8 2.2 pad_maximum_fusion.1.refs_18_
  75.0 1.7 collective-permute-start.30
  76.7 1.5 collective-permute-start.31
  79.6 1.8 shard_map.266
  81.4 10.3 %shard_map.268 = (bf16[128,4096]{1,0:T(8,128)(2,1)S(1)}, f32[1,4096]{1,0:T(1,128)S(1)}, f32[128,1024]{1,0:T(8,128)S(1)}, bf16[128,1024]{1,0:T(8,128)(2,1)S(1)}, ...) custom-call(bf16[128,1024]{1,0:T(8,128)(2,1)S(1)} %get-tuple-element.63.normed.refs_0_, f32[128,4096]{1,0:T(8,128)S(1)} %copy-done.5, ...), custom_call_target="tpu_custom_call" | custom-call | flops 2147483648 | bytes 16777216 | tf_op jit(solution)/shard_map/pallas_call | solution.py:360
  93.5 5.6 %all-to-all-start.4 = ((f32[32,1,256]{2,1,0:T(1,128)}), f32[32,1,256]{2,1,0:T(1,128)S(1)}, u32[]{:S(2)}, u32[]{:S(2)}) async-start(f32[32,1,256]{2,1,0:T(1,128)} %all_to_all.29), calls=%async_computation.4 | async-start | bytes 65536 | tf_op jit(solution)/shard_map/all_to_all | solution.py:878
  100.3 1.8 collective-permute-start.23
  102.1 4.2 %all-to-all-done.4 = f32[32,1,256]{2,1,0:T(1,128)S(1)} async-done(((f32[32,1,256]{2,1,0:T(1,128)}), f32[32,1,256]{2,1,0:T(1,128)S(1)}, u32[]{:S(2)}, u32[]{:S(2)}) %all-to-all-start.4) | async-done | bytes 32800 | tf_op jit(solution)/shard_map/all_to_all | solution.py:878
  106.3 3.4 %all-to-all-start.1 = ((bf16[8,128,128]{2,1,0:T(8,128)(2,1)}), bf16[8,128,128]{2,1,0:T(8,128)(2,1)S(1)}, u32[]{:S(2)}, u32[]{:S(2)}) async-start(bf16[8,128,128]{2,1,0:T(8,128)(2,1)} %get-tuple-element.67), calls=%async_computation.1 | async-start | bytes 524288 | tf_op jit(solution)/shard_map/all_to_all | solution.py:820
  109.7 5.4 %fusion.2 = bf16[1,128,1024]{2,1,0:T(8,128)(2,1)} fusion(f32[128,1024]{1,0:T(8,128)} %copy-done.6, bf16[128,4096]{1,0:T(8,128)(2,1)S(1)} %get-tuple-element.65, bf16[4096,1024]{1,0:T(8,128)(2,1)} %down.1, f32[1024]{0:T(1024)S(1)} %copy-done.70), kind=kOutput, calls=%fused_computation.7 | convolution fusion | flops 1074135040 | bytes 10227712 | tf_op jit(solution)/shard_map/dot_general | solution.py:343
  115.1 1.3 shard_map.272
  116.4 2.0 copy-done
  118.5 1.1 slice.211
  124.2 1.0 copy-done.65
  125.2 8.0 %shard_map.269 = (bf16[1024,384]{1,0:T(8,128)(2,1)S(1)}, f32[1,384]{1,0:T(1,128)S(1)}, bf16[128,384]{1,0:T(8,128)(2,1)S(1)}, bf16[128,384]{1,0:T(8,128)(2,1)S(1)...) custom-call(s32[6]{0:T(128)S(1)} %copy-done.44, ...), custom_call_target="tpu_custom_call" | custom-call | flops 2147483648 | bytes 8388608 | tf_op jit(solution)/shard_map/pallas_call | solution.py:370
  138.6 2.0 collective-permute-start.24
  140.6 1.5 collective-permute-start.25
  144.7 1.1 copy-done.18
  145.8 4.6 %shard_map.271 = (bf16[2,256,384]{2,1,0:T(8,128)(2,1)S(1)}, f32[2,256,384]{2,1,0:T(8,128)S(1)}, f32[1024,1]{1,0:T(8,128)S(1)}, f32[1024,1]{1,0:T(8,128)S(1)}) custom-call(s32[6]{0:T(128)S(1)} %copy-done.44, bf16[512,1024]{1,0:T(8,128)(2,1)S(1)} %copy-done.13, bf16[512,1024]{1,0:T(8,128)(2,1)} %copy-done.14, bf16[1024,384]{1,0:T(8,128)(2,1)S(1)} %copy-done.18, ...), custom_call_target="tpu_custom_call" | custom-call | flops 838860800 | bytes 4194304 | tf_op jit(solution)/shard_map/pallas_call | solution.py:370
  152.8 1.2 reduce.3
  154.1 1.3 reduce.2
  158.0 4.0 %all-to-all-start.2 = ((f32[32,1,160]{2,1,0:T(1,128)}), f32[32,1,160]{2,1,0:T(1,128)S(1)}, u32[]{:S(2)}, u32[]{:S(2)}) async-start(f32[32,1,160]{2,1,0:T(1,128)} %all_to_all.26), calls=%async_computation.2 | async-start | bytes 65536 | tf_op jit(solution)/shard_map/all_to_all | solution.py:942
  163.2 5.9 %all-to-all-done.2 = f32[32,1,160]{2,1,0:T(1,128)S(1)} async-done(((f32[32,1,160]{2,1,0:T(1,128)}), f32[32,1,160]{2,1,0:T(1,128)S(1)}, u32[]{:S(2)}, u32[]{:S(2)}) %all-to-all-start.2) | async-done | bytes 20512 | tf_op jit(solution)/shard_map/all_to_all | solution.py:942
  173.3 2.3 collective-permute-start.11
  178.1 2.3 collective-permute-start.13
  181.0 4.1 %collective-permute-start.15 = (bf16[128,384]{1,0:T(8,128)(2,1)}, bf16[128,384]{1,0:T(8,128)(2,1)S(1)}, u32[]{:S(2)}, u32[]{:S(2)}) collective-permute-start(bf16[128,384]{1,0:T(8,128)(2,1)} %copy-done.57), channel_id=1, source_target_pairs={{0,7},{1,6},{2,5},{3,4},{4,3},{5,2},{6,1},{7,0},{8,15},{9,14},{10,... | collective-permute-start | bytes 294920 | tf_op jit(solution)/shard_map/ppermute | solution.py:348
  185.1 5.3 %collective-permute-done.12.refs_4_ = bf16[128,384]{1,0:T(8,128)(2,1)S(1)} collective-permute-done((bf16[128,384]{1,0:T(8,128)(2,1)}, bf16[128,384]{1,0:T(8,128)(2,1)S(1)}, u32[]{:S(2)}, u32[]{:S(2)}) %collective-permute-start.12) | collective-permute-done | bytes 98336 | tf_op jit(solution)/shard_map/ppermute | solution.py:348
  190.4 1.0 copy-done.48
  195.2 10.7 %shard_map.273 = (f32[2,128,1024]{2,1,0:T(8,128)}, bf16[2,128,1024]{2,1,0:T(8,128)(2,1)S(1)}, f32[2,2,128,512]{3,2,1,0:T(8,128)}, bf16[2,2,128,512]{3,2,1,0:T(8,128)(2,1)S(1)}) custom-call(s32[6]{0:T(128)S(1)} %copy-done.44, bf16[128,1024]{1,0:T(8,128)(2,1)S(1)} %copy-done.24, bf16[128,1024]{1,0:T(8,128)(2,1)} %collective-permute-done.23.refs_1_, ...), custom_call_target="tpu_custom_call" | custom-call | flops 4294967296 | bytes 12582912 | tf_op jit(solution)/shard_map/pallas_call | solution.py:370
  206.5 1.5 collective-permute-start.39
  208.0 7.1 %shard_map.270 = f32[128,1024]{1,0:T(8,128)} custom-call(s32[6]{0:T(128)S(1)} %copy-done.44, bf16[128,384]{1,0:T(8,128)(2,1)S(1)} %get-tuple-element.69.refs_0_, bf16[128,384]{1,0:T(8,128)(2,1)S(1)} %collective-permute-done.9.refs_1_, bf16[128,384]{1,0:T(8,128)(2,1)S(1)} %collective-permute-done.10.refs_2_, ...), custom_call_target="tpu_custom_call" | custom-call | flops 838860800 | bytes 8388608 | tf_op jit(solution)/shard_map/pallas_call | solution.py:370
  217.3 3.4 %collective-permute-done.37 = bf16[2,2,128,512]{3,2,1,0:T(8,128)(2,1)S(1)} collective-permute-done((bf16[2,2,128,512]{3,2,1,0:T(8,128)(2,1)S(1)}, bf16[2,2,128,512]{3,2,1,0:T(8,128)(2,1)S(1)}, u32[]{:S(2)}, u32[]{:S(2)}) %collective-permute-start.37) | collective-permute-done | bytes 524320 | tf_op jit(solution)/shard_map/ppermute | solution.py:348
  221.6 10.3 %collective-permute-done.39 = bf16[2,128,1024]{2,1,0:T(8,128)(2,1)S(1)} collective-permute-done((bf16[2,128,1024]{2,1,0:T(8,128)(2,1)S(1)}, bf16[2,128,1024]{2,1,0:T(8,128)(2,1)S(1)}, u32[]{:S(2)}, u32[]{:S(2)}) %collective-permute-start.39) | collective-permute-done | bytes 524320 | tf_op jit(solution)/shard_map/ppermute | solution.py:348
  233.7 2.0 collective-permute-done.17
  236.4 4.0 %all-to-all-start.3 = ((bf16[8,32,384]{2,1,0:T(8,128)(2,1)}), bf16[8,32,384]{2,1,0:T(8,128)(2,1)S(1)}, u32[]{:S(2)}, u32[]{:S(2)}) async-start(bf16[8,32,384]{2,1,0:T(8,128)(2,1)} %bitcast.23), calls=%async_computation.3 | async-start | bytes 393216 | tf_op jit(solution)/shard_map/all_to_all | solution.py:933
  240.4 3.9 %collective-permute-done.20 = bf16[4,32,1024]{2,1,0:T(8,128)(2,1)} collective-permute-done((bf16[4,32,1024]{2,1,0:T(8,128)(2,1)}, bf16[4,32,1024]{2,1,0:T(8,128)(2,1)}, u32[]{:S(2)}, u32[]{:S(2)}) %collective-permute-start.20) | collective-permute-done | bytes 262176 | tf_op jit(solution)/shard_map/ppermute | solution.py:348
  244.3 1.0 slice_add_fusion.2
  246.7 1.7 fusion.5
  248.5 3.7 %all-to-all-done.3 = bf16[8,32,384]{2,1,0:T(8,128)(2,1)S(1)} async-done(((bf16[8,32,384]{2,1,0:T(8,128)(2,1)}), bf16[8,32,384]{2,1,0:T(8,128)(2,1)S(1)}, u32[]{:S(2)}, u32[]{:S(2)}) %all-to-all-start.3) | async-done | bytes 196640 | tf_op jit(solution)/shard_map/all_to_all | solution.py:933
  252.2 3.4 %all-to-all-start.5 = ((bf16[8,32,512]{2,1,0:T(8,128)(2,1)}), bf16[8,32,512]{2,1,0:T(8,128)(2,1)S(1)}, u32[]{:S(2)}, u32[]{:S(2)}) async-start(bf16[8,32,512]{2,1,0:T(8,128)(2,1)} %bitcast.29), calls=%async_computation.5 | async-start | bytes 524288 | tf_op jit(solution)/shard_map/all_to_all | solution.py:870
  257.2 1.8 fusion.3
  260.2 2.8 %all-to-all-done.5 = bf16[8,32,512]{2,1,0:T(8,128)(2,1)S(1)} async-done(((bf16[8,32,512]{2,1,0:T(8,128)(2,1)}), bf16[8,32,512]{2,1,0:T(8,128)(2,1)S(1)}, u32[]{:S(2)}, u32[]{:S(2)}) %all-to-all-start.5) | async-done | bytes 262176 | tf_op jit(solution)/shard_map/all_to_all | solution.py:870
  263.7 1.0 reshape.362
  (303 shorter events, 62.9 us)
Async XLA Ops:
  0.6 39.1 %collective-permute-start = (bf16[128,1024]{1,0:T(8,128)(2,1)}, bf16[128,1024]{1,0:T(8,128)(2,1)S(1)}, u32[]{:S(2)}, u32[]{:S(2)}) collective-permute-start(bf16[128,1024]{1,0:T(8,128)(2,1)} %bitcast.68), channel_id=1, source_target_pairs={{0,1},{1,0},{2,3},{3,2},{4,5},{5,4},{6,7},{7,6},{8,9},{9,8},{10,11... | collective-permute-start | bytes 786440 | tf_op jit(solution)/shard_map/ppermute | solution.py:348
  3.7 34.5 %collective-permute-start.1 = (bf16[128,1024]{1,0:T(8,128)(2,1)}, bf16[128,1024]{1,0:T(8,128)(2,1)S(1)}, u32[]{:S(2)}, u32[]{:S(2)}) collective-permute-start(bf16[128,1024]{1,0:T(8,128)(2,1)} %bitcast.69), channel_id=1, source_target_pairs={{0,2},{1,3},{2,0},{3,1},{4,6},{5,7},{6,4},{7,5},{8,10},{9,11},{10,... | collective-permute-start | bytes 786440 | tf_op jit(solution)/shard_map/ppermute | solution.py:348
  5.3 30.7 %collective-permute-start.4 = (bf16[128,1024]{1,0:T(8,128)(2,1)}, bf16[128,1024]{1,0:T(8,128)(2,1)}, u32[]{:S(2)}, u32[]{:S(2)}) collective-permute-start(bf16[128,1024]{1,0:T(8,128)(2,1)} %bitcast.70), channel_id=1, source_target_pairs={{0,4},{1,5},{2,6},{3,7},{4,0},{5,1},{6,2},{7,3},{8,12},{9,13},{10,... | collective-permute-start | bytes 786440 | tf_op jit(solution)/shard_map/ppermute | solution.py:348
  18.3 10.6 %copy-start.75 = (bf16[1024]{0:T(1024)(128)(2,1)S(1)}, bf16[1024]{0:T(1024)(128)(2,1)}, u32[]{:S(2)}) copy-start(bf16[1024]{0:T(1024)(128)(2,1)} %param.24) | copy-start | bytes 6148
  18.3 11.2 %copy-start.71 = (bf16[4096]{0:T(1024)(128)(2,1)S(1)}, bf16[4096]{0:T(1024)(128)(2,1)}, u32[]{:S(2)}) copy-start(bf16[4096]{0:T(1024)(128)(2,1)} %param.27) | copy-start | bytes 24580
  18.3 11.8 %copy-start.77 = (bf16[1024]{0:T(1024)(128)(2,1)S(1)}, bf16[1024]{0:T(1024)(128)(2,1)}, u32[]{:S(2)}) copy-start(bf16[1024]{0:T(1024)(128)(2,1)} %param.29) | copy-start | bytes 6148
  35.9 11.8 %copy-start.3 = (bf16[1,128,1024]{2,1,0:T(8,128)(2,1)S(1)}, bf16[1,128,1024]{2,1,0:T(8,128)(2,1)}, u32[]{:S(2)}) copy-start(bf16[1,128,1024]{2,1,0:T(8,128)(2,1)} %param.16) | copy-start | bytes 786436
  35.9 11.8 %copy-start.42 = (bf16[1,384]{1,0:T(2,128)(2,1)S(1)}, bf16[1,384]{1,0:T(2,128)(2,1)}, u32[]{:S(2)}) copy-start(bf16[1,384]{1,0:T(2,128)(2,1)} %reshape.342.bias3) | copy-start | bytes 2308
  35.9 11.3 %collective-permute-start.5 = (bf16[128,1024]{1,0:T(8,128)(2,1)}, bf16[128,1024]{1,0:T(8,128)(2,1)S(1)}, u32[]{:S(2)}, u32[]{:S(2)}) collective-permute-start(bf16[128,1024]{1,0:T(8,128)(2,1)} %collective-permute-done.4.b0), channel_id=1, source_target_pairs={{0,1},{1,0},{2,3},{3,2},{4,5},{5,4},{6,7},{7,6},{8,9},{9,8},{10,11... | collective-permute-start | bytes 786440 | tf_op jit(solution)/shard_map/ppermute | solution.py:348
  36.5 8.5 %collective-permute-start.6 = (bf16[128,1024]{1,0:T(8,128)(2,1)}, bf16[128,1024]{1,0:T(8,128)(2,1)S(1)}, u32[]{:S(2)}, u32[]{:S(2)}) collective-permute-start(bf16[128,1024]{1,0:T(8,128)(2,1)} %collective-permute-done.4.b0), channel_id=1, source_target_pairs={{0,2},{1,3},{2,0},{3,1},{4,6},{5,7},{6,4},{7,5},{8,10},{9,11},{10,... | collective-permute-start | bytes 786440 | tf_op jit(solution)/shard_map/ppermute | solution.py:348
  38.2 9.6 %collective-permute-start.2 = (bf16[64,1024]{1,0:T(8,128)(2,1)S(1)}, bf16[64,1024]{1,0:T(8,128)(2,1)S(1)}, u32[]{:S(2)}, u32[]{:S(2)}) collective-permute-start(bf16[64,1024]{1,0:T(8,128)(2,1)S(1)} %slice.150), channel_id=1, source_target_pairs={{0,1},{1,0},{2,3},{3,2},{4,5},{5,4},{6,7},{7,6},{8,9},{9,8},{10,11... | collective-permute-start | bytes 393224 | tf_op jit(solution)/shard_map/ppermute | solution.py:348
  39.8 8.0 %collective-permute-start.3 = (bf16[64,1024]{1,0:T(8,128)(2,1)S(1)}, bf16[64,1024]{1,0:T(8,128)(2,1)S(1)}, u32[]{:S(2)}, u32[]{:S(2)}) collective-permute-start(bf16[64,1024]{1,0:T(8,128)(2,1)S(1)} %slice.151), channel_id=1, source_target_pairs={{0,2},{1,3},{2,0},{3,1},{4,6},{5,7},{6,4},{7,5},{8,10},{9,11},{10,... | collective-permute-start | bytes 393224 | tf_op jit(solution)/shard_map/ppermute | solution.py:348
  45.1 5.1 %collective-permute-start.7 = (bf16[64,1024]{1,0:T(8,128)(2,1)S(1)}, bf16[64,1024]{1,0:T(8,128)(2,1)S(1)}, u32[]{:S(2)}, u32[]{:S(2)}) collective-permute-start(bf16[64,1024]{1,0:T(8,128)(2,1)S(1)} %slice.154), channel_id=1, source_target_pairs={{0,1},{1,0},{2,3},{3,2},{4,5},{5,4},{6,7},{7,6},{8,9},{9,8},{10,11... | collective-permute-start | bytes 393224 | tf_op jit(solution)/shard_map/ppermute | solution.py:348
  47.2 5.0 %collective-permute-start.8 = (bf16[64,1024]{1,0:T(8,128)(2,1)S(1)}, bf16[64,1024]{1,0:T(8,128)(2,1)S(1)}, u32[]{:S(2)}, u32[]{:S(2)}) collective-permute-start(bf16[64,1024]{1,0:T(8,128)(2,1)S(1)} %slice.155), channel_id=1, source_target_pairs={{0,2},{1,3},{2,0},{3,1},{4,6},{5,7},{6,4},{7,5},{8,10},{9,11},{10,... | collective-permute-start | bytes 393224 | tf_op jit(solution)/shard_map/ppermute | solution.py:348
  50.1 14.6 %copy-start.33 = (bf16[512,128]{1,0:T(8,128)(2,1)}, bf16[512,128]{1,0:T(8,128)(2,1)S(1)}, u32[]{:S(2)}) copy-start(bf16[512,128]{1,0:T(8,128)(2,1)S(1)} %get-tuple-element.57.k0) | copy-start | bytes 393220
  55.7 14.1 %copy-start.78 = (bf16[128]{0:T(256)(128)(2,1)S(1)}, bf16[128]{0:T(256)(128)(2,1)}, u32[]{:S(2)}) copy-start(bf16[128]{0:T(256)(128)(2,1)} %get-tuple-element.116) | copy-start | bytes 772
  55.7 14.1 %copy-start.79 = (bf16[128]{0:T(256)(128)(2,1)S(1)}, bf16[128]{0:T(256)(128)(2,1)}, u32[]{:S(2)}) copy-start(bf16[128]{0:T(256)(128)(2,1)} %get-tuple-element.117) | copy-start | bytes 772
  55.7 14.0 %copy-start.80 = (bf16[128]{0:T(256)(128)(2,1)S(1)}, bf16[128]{0:T(256)(128)(2,1)}, u32[]{:S(2)}) copy-start(bf16[128]{0:T(256)(128)(2,1)} %get-tuple-element.118) | copy-start | bytes 772
  55.7 14.0 %copy-start.81 = (bf16[128]{0:T(256)(128)(2,1)S(1)}, bf16[128]{0:T(256)(128)(2,1)}, u32[]{:S(2)}) copy-start(bf16[128]{0:T(256)(128)(2,1)} %get-tuple-element.119) | copy-start | bytes 772
  65.5 14.0 %all-to-all-start = ((bf16[8,128,128]{2,1,0:T(8,128)(2,1)}), bf16[8,128,128]{2,1,0:T(8,128)(2,1)}, u32[]{:S(2)}, u32[]{:S(2)}) async-start(bf16[8,128,128]{2,1,0:T(8,128)(2,1)} %get-tuple-element.61), calls=%async_computation | async-start | bytes 524288 | tf_op jit(solution)/shard_map/all_to_all | solution.py:780
  75.0 24.8 %collective-permute-start.30 = (bf16[128,1024]{1,0:T(8,128)(2,1)S(1)}, bf16[128,1024]{1,0:T(8,128)(2,1)}, u32[]{:S(2)}, u32[]{:S(2)}) collective-permute-start(bf16[128,1024]{1,0:T(8,128)(2,1)S(1)} %bitcast.75), channel_id=1, source_target_pairs={{0,1},{1,0},{2,3},{3,2},{4,5},{5,4},{6,7},{7,6},{8,9},{9,8},{10,11... | collective-permute-start | bytes 786440 | tf_op jit(solution)/shard_map/ppermute | solution.py:348
  76.7 23.3 %collective-permute-start.31 = (bf16[128,1024]{1,0:T(8,128)(2,1)S(1)}, bf16[128,1024]{1,0:T(8,128)(2,1)}, u32[]{:S(2)}, u32[]{:S(2)}) collective-permute-start(bf16[128,1024]{1,0:T(8,128)(2,1)S(1)} %bitcast.76), channel_id=1, source_target_pairs={{0,2},{1,3},{2,0},{3,1},{4,6},{5,7},{6,4},{7,5},{8,10},{9,11},{10,... | collective-permute-start | bytes 786440 | tf_op jit(solution)/shard_map/ppermute | solution.py:348
  78.2 60.4 %collective-permute-start.32 = (bf16[128,1024]{1,0:T(8,128)(2,1)S(1)}, bf16[128,1024]{1,0:T(8,128)(2,1)}, u32[]{:S(2)}, u32[]{:S(2)}) collective-permute-start(bf16[128,1024]{1,0:T(8,128)(2,1)S(1)} %bitcast.77), channel_id=1, source_target_pairs={{0,3},{1,2},{2,1},{3,0},{4,7},{5,6},{6,5},{7,4},{8,11},{9,10},{10,... | collective-permute-start | bytes 786440 | tf_op jit(solution)/shard_map/ppermute | solution.py:348
  78.5 62.1 %collective-permute-start.33 = (bf16[128,1024]{1,0:T(8,128)(2,1)S(1)}, bf16[128,1024]{1,0:T(8,128)(2,1)}, u32[]{:S(2)}, u32[]{:S(2)}) collective-permute-start(bf16[128,1024]{1,0:T(8,128)(2,1)S(1)} %bitcast.78), channel_id=1, source_target_pairs={{0,8},{1,9},{2,10},{3,11},{4,12},{5,13},{6,14},{7,15},{8,0},{9,1},... | collective-permute-start | bytes 786440 | tf_op jit(solution)/shard_map/ppermute | solution.py:348
  81.4 11.4 %copy-start.69 = (f32[32,32]{1,0:T(8,128)S(1)}, f32[32,32]{1,0:T(8,128)}, u32[]{:S(2)}) copy-start(f32[32,32]{1,0:T(8,128)} %reshape.357) | copy-start | bytes 12292
  81.4 17.7 %copy-start.32 = (bf16[512,128]{1,0:T(8,128)(2,1)S(1)}, bf16[512,128]{1,0:T(8,128)(2,1)}, u32[]{:S(2)}) copy-start(bf16[512,128]{1,0:T(8,128)(2,1)} %copy-done.31) | copy-start | bytes 393220
  81.4 28.3 %copy-start.70 = (f32[1024]{0:T(1024)S(1)}, f32[1024]{0:T(1024)}, u32[]{:S(2)}) copy-start(f32[1024]{0:T(1024)} %convert_element_type.98) | copy-start | bytes 12292
  93.5 12.8 %all-to-all-start.4 = ((f32[32,1,256]{2,1,0:T(1,128)}), f32[32,1,256]{2,1,0:T(1,128)S(1)}, u32[]{:S(2)}, u32[]{:S(2)}) async-start(f32[32,1,256]{2,1,0:T(1,128)} %all_to_all.29), calls=%async_computation.4 | async-start | bytes 65536 | tf_op jit(solution)/shard_map/all_to_all | solution.py:878
  99.8 55.6 %collective-permute-start.34 = (bf16[128,1024]{1,0:T(8,128)(2,1)}, bf16[128,1024]{1,0:T(8,128)(2,1)}, u32[]{:S(2)}, u32[]{:S(2)}) collective-permute-start(bf16[128,1024]{1,0:T(8,128)(2,1)} %collective-permute-done.30.refs_9_), channel_id=1, source_target_pairs={{0,8},{1,9},{2,10},{3,11},{4,12},{5,13},{6,14},{7,15},{8,0},{9,1},... | collective-permute-start | bytes 786440 | tf_op jit(solution)/shard_map/ppermute | solution.py:348
  100.1 55.4 %collective-permute-start.35 = (bf16[128,1024]{1,0:T(8,128)(2,1)}, bf16[128,1024]{1,0:T(8,128)(2,1)}, u32[]{:S(2)}, u32[]{:S(2)}) collective-permute-start(bf16[128,1024]{1,0:T(8,128)(2,1)} %collective-permute-done.31.refs_10_), channel_id=1, source_target_pairs={{0,8},{1,9},{2,10},{3,11},{4,12},{5,13},{6,14},{7,15},{8,0},{9,1},... | collective-permute-start | bytes 786440 | tf_op jit(solution)/shard_map/ppermute | solution.py:348
  100.3 55.7 %collective-permute-start.23 = (bf16[128,1024]{1,0:T(8,128)(2,1)}, bf16[128,1024]{1,0:T(8,128)(2,1)}, u32[]{:S(2)}, u32[]{:S(2)}) collective-permute-start(bf16[128,1024]{1,0:T(8,128)(2,1)} %copy-done.23), channel_id=1, source_target_pairs={{0,1},{1,0},{2,3},{3,2},{4,5},{5,4},{6,7},{7,6},{8,9},{9,8},{10,11... | collective-permute-start | bytes 786440 | tf_op jit(solution)/shard_map/ppermute | solution.py:348
  106.3 13.4 %all-to-all-start.1 = ((bf16[8,128,128]{2,1,0:T(8,128)(2,1)}), bf16[8,128,128]{2,1,0:T(8,128)(2,1)S(1)}, u32[]{:S(2)}, u32[]{:S(2)}) async-start(bf16[8,128,128]{2,1,0:T(8,128)(2,1)} %get-tuple-element.67), calls=%async_computation.1 | async-start | bytes 524288 | tf_op jit(solution)/shard_map/all_to_all | solution.py:820
  125.2 17.6 %copy-start.13 = (bf16[512,1024]{1,0:T(8,128)(2,1)S(1)}, bf16[512,1024]{1,0:T(8,128)(2,1)}, u32[]{:S(2)}) copy-start(bf16[512,1024]{1,0:T(8,128)(2,1)} %copy-done.12) | copy-start | bytes 3145732
  138.6 17.4 %collective-permute-start.24 = (bf16[128,1024]{1,0:T(8,128)(2,1)}, bf16[128,1024]{1,0:T(8,128)(2,1)}, u32[]{:S(2)}, u32[]{:S(2)}) collective-permute-start(bf16[128,1024]{1,0:T(8,128)(2,1)} %copy-done.23), channel_id=1, source_target_pairs={{0,2},{1,3},{2,0},{3,1},{4,6},{5,7},{6,4},{7,5},{8,10},{9,11},{10,... | collective-permute-start | bytes 786440 | tf_op jit(solution)/shard_map/ppermute | solution.py:348
  140.6 15.9 %collective-permute-start.25 = (bf16[128,1024]{1,0:T(8,128)(2,1)}, bf16[128,1024]{1,0:T(8,128)(2,1)}, u32[]{:S(2)}, u32[]{:S(2)}) collective-permute-start(bf16[128,1024]{1,0:T(8,128)(2,1)} %copy-done.23), channel_id=1, source_target_pairs={{0,3},{1,2},{2,1},{3,0},{4,7},{5,6},{6,5},{7,4},{8,11},{9,10},{10,... | collective-permute-start | bytes 786440 | tf_op jit(solution)/shard_map/ppermute | solution.py:348
  145.8 44.6 %copy-start.45 = (bf16[1,512]{1,0:T(2,128)(2,1)S(1)}, bf16[1,512]{1,0:T(2,128)(2,1)}, u32[]{:S(2)}) copy-start(bf16[1,512]{1,0:T(2,128)(2,1)} %reshape.359.refs_17_) | copy-start | bytes 3076
  155.4 13.6 %collective-permute-start.36 = (bf16[128,1024]{1,0:T(8,128)(2,1)}, bf16[128,1024]{1,0:T(8,128)(2,1)S(1)}, u32[]{:S(2)}, u32[]{:S(2)}) collective-permute-start(bf16[128,1024]{1,0:T(8,128)(2,1)} %collective-permute-done.32.refs_11_), channel_id=1, source_target_pairs={{0,8},{1,9},{2,10},{3,11},{4,12},{5,13},{6,14},{7,15},{8,0},{9,1},... | collective-permute-start | bytes 786440 | tf_op jit(solution)/shard_map/ppermute | solution.py:348
  155.5 14.4 %collective-permute-start.26 = (bf16[128,1024]{1,0:T(8,128)(2,1)S(1)}, bf16[128,1024]{1,0:T(8,128)(2,1)S(1)}, u32[]{:S(2)}, u32[]{:S(2)}) collective-permute-start(bf16[128,1024]{1,0:T(8,128)(2,1)S(1)} %copy-done.24), channel_id=1, source_target_pairs={{0,8},{1,9},{2,10},{3,11},{4,12},{5,13},{6,14},{7,15},{8,0},{9,1},... | collective-permute-start | bytes 786440 | tf_op jit(solution)/shard_map/ppermute | solution.py:348
  156.0 15.3 %collective-permute-start.27 = (bf16[128,1024]{1,0:T(8,128)(2,1)}, bf16[128,1024]{1,0:T(8,128)(2,1)S(1)}, u32[]{:S(2)}, u32[]{:S(2)}) collective-permute-start(bf16[128,1024]{1,0:T(8,128)(2,1)} %collective-permute-done.23.refs_1_), channel_id=1, source_target_pairs={{0,8},{1,9},{2,10},{3,11},{4,12},{5,13},{6,14},{7,15},{8,0},{9,1},... | collective-permute-start | bytes 786440 | tf_op jit(solution)/shard_map/ppermute | solution.py:348
  156.1 16.5 %collective-permute-start.28 = (bf16[128,1024]{1,0:T(8,128)(2,1)}, bf16[128,1024]{1,0:T(8,128)(2,1)S(1)}, u32[]{:S(2)}, u32[]{:S(2)}) collective-permute-start(bf16[128,1024]{1,0:T(8,128)(2,1)} %collective-permute-done.24.refs_2_), channel_id=1, source_target_pairs={{0,8},{1,9},{2,10},{3,11},{4,12},{5,13},{6,14},{7,15},{8,0},{9,1},... | collective-permute-start | bytes 786440 | tf_op jit(solution)/shard_map/ppermute | solution.py:348
  156.5 19.0 %collective-permute-start.29 = (bf16[128,1024]{1,0:T(8,128)(2,1)}, bf16[128,1024]{1,0:T(8,128)(2,1)S(1)}, u32[]{:S(2)}, u32[]{:S(2)}) collective-permute-start(bf16[128,1024]{1,0:T(8,128)(2,1)} %collective-permute-done.25.refs_3_), channel_id=1, source_target_pairs={{0,8},{1,9},{2,10},{3,11},{4,12},{5,13},{6,14},{7,15},{8,0},{9,1},... | collective-permute-start | bytes 786440 | tf_op jit(solution)/shard_map/ppermute | solution.py:348
  158.0 11.0 %all-to-all-start.2 = ((f32[32,1,160]{2,1,0:T(1,128)}), f32[32,1,160]{2,1,0:T(1,128)S(1)}, u32[]{:S(2)}, u32[]{:S(2)}) async-start(f32[32,1,160]{2,1,0:T(1,128)} %all_to_all.26), calls=%async_computation.2 | async-start | bytes 65536 | tf_op jit(solution)/shard_map/all_to_all | solution.py:942
  169.8 46.1 %collective-permute-start.18 = (bf16[16,32,1024]{2,1,0:T(8,128)(2,1)}, bf16[16,32,1024]{2,1,0:T(8,128)(2,1)S(1)}, u32[]{:S(2)}, u32[]{:S(2)}) collective-permute-start(bf16[16,32,1024]{2,1,0:T(8,128)(2,1)} %slice.211), channel_id=1, source_target_pairs={{0,8},{1,9},{2,10},{3,11},{4,12},{5,13},{6,14},{7,15},{8,0},{9,1},... | collective-permute-start | bytes 3145736 | tf_op jit(solution)/shard_map/ppermute | solution.py:348
  170.6 7.5 %collective-permute-start.9 = (bf16[128,384]{1,0:T(8,128)(2,1)}, bf16[128,384]{1,0:T(8,128)(2,1)S(1)}, u32[]{:S(2)}, u32[]{:S(2)}) collective-permute-start(bf16[128,384]{1,0:T(8,128)(2,1)} %copy-done.63), channel_id=1, source_target_pairs={{0,1},{1,0},{2,3},{3,2},{4,5},{5,4},{6,7},{7,6},{8,9},{9,8},{10,11... | collective-permute-start | bytes 294920 | tf_op jit(solution)/shard_map/ppermute | solution.py:348
  172.0 8.4 %collective-permute-start.10 = (bf16[128,384]{1,0:T(8,128)(2,1)}, bf16[128,384]{1,0:T(8,128)(2,1)S(1)}, u32[]{:S(2)}, u32[]{:S(2)}) collective-permute-start(bf16[128,384]{1,0:T(8,128)(2,1)} %copy-done.62), channel_id=1, source_target_pairs={{0,2},{1,3},{2,0},{3,1},{4,6},{5,7},{6,4},{7,5},{8,10},{9,11},{10,... | collective-permute-start | bytes 294920 | tf_op jit(solution)/shard_map/ppermute | solution.py:348
  173.3 7.7 %collective-permute-start.11 = (bf16[128,384]{1,0:T(8,128)(2,1)}, bf16[128,384]{1,0:T(8,128)(2,1)S(1)}, u32[]{:S(2)}, u32[]{:S(2)}) collective-permute-start(bf16[128,384]{1,0:T(8,128)(2,1)} %copy-done.61), channel_id=1, source_target_pairs={{0,3},{1,2},{2,1},{3,0},{4,7},{5,6},{6,5},{7,4},{8,11},{9,10},{10,... | collective-permute-start | bytes 294920 | tf_op jit(solution)/shard_map/ppermute | solution.py:348
  176.2 14.1 %collective-permute-start.12 = (bf16[128,384]{1,0:T(8,128)(2,1)}, bf16[128,384]{1,0:T(8,128)(2,1)S(1)}, u32[]{:S(2)}, u32[]{:S(2)}) collective-permute-start(bf16[128,384]{1,0:T(8,128)(2,1)} %copy-done.60), channel_id=1, source_target_pairs={{0,4},{1,5},{2,6},{3,7},{4,0},{5,1},{6,2},{7,3},{8,12},{9,13},{10,... | collective-permute-start | bytes 294920 | tf_op jit(solution)/shard_map/ppermute | solution.py:348
  178.1 27.8 %collective-permute-start.13 = (bf16[128,384]{1,0:T(8,128)(2,1)}, bf16[128,384]{1,0:T(8,128)(2,1)S(1)}, u32[]{:S(2)}, u32[]{:S(2)}) collective-permute-start(bf16[128,384]{1,0:T(8,128)(2,1)} %copy-done.59), channel_id=1, source_target_pairs={{0,5},{1,4},{2,7},{3,6},{4,1},{5,0},{6,3},{7,2},{8,13},{9,12},{10,... | collective-permute-start | bytes 294920 | tf_op jit(solution)/shard_map/ppermute | solution.py:348
  180.4 26.0 %collective-permute-start.14 = (bf16[128,384]{1,0:T(8,128)(2,1)}, bf16[128,384]{1,0:T(8,128)(2,1)S(1)}, u32[]{:S(2)}, u32[]{:S(2)}) collective-permute-start(bf16[128,384]{1,0:T(8,128)(2,1)} %copy-done.58), channel_id=1, source_target_pairs={{0,6},{1,7},{2,4},{3,5},{4,2},{5,3},{6,0},{7,1},{8,14},{9,15},{10,... | collective-permute-start | bytes 294920 | tf_op jit(solution)/shard_map/ppermute | solution.py:348
  181.0 27.0 %collective-permute-start.15 = (bf16[128,384]{1,0:T(8,128)(2,1)}, bf16[128,384]{1,0:T(8,128)(2,1)S(1)}, u32[]{:S(2)}, u32[]{:S(2)}) collective-permute-start(bf16[128,384]{1,0:T(8,128)(2,1)} %copy-done.57), channel_id=1, source_target_pairs={{0,7},{1,6},{2,5},{3,4},{4,3},{5,2},{6,1},{7,0},{8,15},{9,14},{10,... | collective-permute-start | bytes 294920 | tf_op jit(solution)/shard_map/ppermute | solution.py:348
  190.4 17.6 %copy-start.22 = (f32[128,1024]{1,0:T(8,128)S(1)}, f32[128,1024]{1,0:T(8,128)}, u32[]{:S(2)}) copy-start(f32[128,1024]{1,0:T(8,128)} %copy-done.21) | copy-start | bytes 1572868
  190.4 24.7 %collective-permute-start.16 = (bf16[2,256,384]{2,1,0:T(8,128)(2,1)}, bf16[2,256,384]{2,1,0:T(8,128)(2,1)S(1)}, u32[]{:S(2)}, u32[]{:S(2)}) collective-permute-start(bf16[2,256,384]{2,1,0:T(8,128)(2,1)} %copy-done.46), channel_id=1, source_target_pairs={{0,8},{1,9},{2,10},{3,11},{4,12},{5,13},{6,14},{7,15},{8,0},{9,1},... | collective-permute-start | bytes 1179656 | tf_op jit(solution)/shard_map/ppermute | solution.py:348
  205.9 14.7 %collective-permute-start.37 = (bf16[2,2,128,512]{3,2,1,0:T(8,128)(2,1)S(1)}, bf16[2,2,128,512]{3,2,1,0:T(8,128)(2,1)S(1)}, u32[]{:S(2)}, u32[]{:S(2)}) collective-permute-start(bf16[2,2,128,512]{3,2,1,0:T(8,128)(2,1)S(1)} %get-tuple-element.93), channel_id=1, source_target_pairs={{0,16},{1,17},{2,18},{3,19},{4,20},{5,21},{6,22},{7,23},{8,24},{9,... | collective-permute-start | bytes 1572872 | tf_op jit(solution)/shard_map/ppermute | solution.py:348
  206.5 25.4 %collective-permute-start.39 = (bf16[2,128,1024]{2,1,0:T(8,128)(2,1)S(1)}, bf16[2,128,1024]{2,1,0:T(8,128)(2,1)S(1)}, u32[]{:S(2)}, u32[]{:S(2)}) collective-permute-start(bf16[2,128,1024]{2,1,0:T(8,128)(2,1)S(1)} %get-tuple-element.95), channel_id=1, source_target_pairs={{0,16},{1,17},{2,18},{3,19},{4,20},{5,21},{6,22},{7,23},{8,24},{9,... | collective-permute-start | bytes 1572872 | tf_op jit(solution)/shard_map/ppermute | solution.py:348
  215.2 20.4 %collective-permute-start.17 = (bf16[256,384]{1,0:T(8,128)(2,1)S(1)}, bf16[256,384]{1,0:T(8,128)(2,1)S(1)}, u32[]{:S(2)}, u32[]{:S(2)}) collective-permute-start(bf16[256,384]{1,0:T(8,128)(2,1)S(1)} %fusion.10), channel_id=1, source_target_pairs={{0,16},{1,17},{2,18},{3,19},{4,20},{5,21},{6,22},{7,23},{8,24},{9,... | collective-permute-start | bytes 589832 | tf_op jit(solution)/shard_map/ppermute | solution.py:348
  216.2 15.7 %copy-start.67 = (f32[2,128,1024]{2,1,0:T(8,128)S(1)}, f32[2,128,1024]{2,1,0:T(8,128)}, u32[]{:S(2)}) copy-start(f32[2,128,1024]{2,1,0:T(8,128)} %get-tuple-element.94) | copy-start | bytes 3145732
  216.3 15.8 %collective-permute-start.19 = (bf16[8,32,1024]{2,1,0:T(8,128)(2,1)S(1)}, bf16[8,32,1024]{2,1,0:T(8,128)(2,1)S(1)}, u32[]{:S(2)}, u32[]{:S(2)}) collective-permute-start(bf16[8,32,1024]{2,1,0:T(8,128)(2,1)S(1)} %slice.212), channel_id=1, source_target_pairs={{0,1},{1,0},{2,3},{3,2},{4,5},{5,4},{6,7},{7,6},{8,9},{9,8},{10,11... | collective-permute-start | bytes 1572872 | tf_op jit(solution)/shard_map/ppermute | solution.py:348
  221.6 25.2 %collective-permute-start.38 = (bf16[2,128,512]{2,1,0:T(8,128)(2,1)}, bf16[2,128,512]{2,1,0:T(8,128)(2,1)}, u32[]{:S(2)}, u32[]{:S(2)}) collective-permute-start(bf16[2,128,512]{2,1,0:T(8,128)(2,1)} %fusion.8), channel_id=1, source_target_pairs={{0,4},{1,5},{2,6},{3,7},{4,0},{5,1},{6,2},{7,3},{8,12},{9,13},{10,... | collective-permute-start | bytes 786440 | tf_op jit(solution)/shard_map/ppermute | solution.py:348
  232.9 11.4 %collective-permute-start.20 = (bf16[4,32,1024]{2,1,0:T(8,128)(2,1)}, bf16[4,32,1024]{2,1,0:T(8,128)(2,1)}, u32[]{:S(2)}, u32[]{:S(2)}) collective-permute-start(bf16[4,32,1024]{2,1,0:T(8,128)(2,1)} %slice.213), channel_id=1, source_target_pairs={{0,2},{1,3},{2,0},{3,1},{4,6},{5,7},{6,4},{7,5},{8,10},{9,11},{10,... | collective-permute-start | bytes 786440 | tf_op jit(solution)/shard_map/ppermute | solution.py:348
  233.7 23.5 %collective-permute-start.40 = (bf16[128,1024]{1,0:T(8,128)(2,1)}, bf16[128,1024]{1,0:T(8,128)(2,1)}, u32[]{:S(2)}, u32[]{:S(2)}) collective-permute-start(bf16[128,1024]{1,0:T(8,128)(2,1)} %fusion.9), channel_id=1, source_target_pairs={{0,4},{1,5},{2,6},{3,7},{4,0},{5,1},{6,2},{7,3},{8,12},{9,13},{10,... | collective-permute-start | bytes 786440 | tf_op jit(solution)/shard_map/ppermute | solution.py:348
  236.4 15.8 %all-to-all-start.3 = ((bf16[8,32,384]{2,1,0:T(8,128)(2,1)}), bf16[8,32,384]{2,1,0:T(8,128)(2,1)S(1)}, u32[]{:S(2)}, u32[]{:S(2)}) async-start(bf16[8,32,384]{2,1,0:T(8,128)(2,1)} %bitcast.23), calls=%async_computation.3 | async-start | bytes 393216 | tf_op jit(solution)/shard_map/all_to_all | solution.py:933
  246.2 9.4 %collective-permute-start.21 = (bf16[2,32,1024]{2,1,0:T(8,128)(2,1)S(1)}, bf16[2,32,1024]{2,1,0:T(8,128)(2,1)S(1)}, u32[]{:S(2)}, u32[]{:S(2)}) collective-permute-start(bf16[2,32,1024]{2,1,0:T(8,128)(2,1)S(1)} %slice.214), channel_id=1, source_target_pairs={{0,16},{1,17},{2,18},{3,19},{4,20},{5,21},{6,22},{7,23},{8,24},{9,... | collective-permute-start | bytes 393224 | tf_op jit(solution)/shard_map/ppermute | solution.py:348
  252.2 10.8 %all-to-all-start.5 = ((bf16[8,32,512]{2,1,0:T(8,128)(2,1)}), bf16[8,32,512]{2,1,0:T(8,128)(2,1)S(1)}, u32[]{:S(2)}, u32[]{:S(2)}) async-start(bf16[8,32,512]{2,1,0:T(8,128)(2,1)} %bitcast.29), calls=%async_computation.5 | async-start | bytes 524288 | tf_op jit(solution)/shard_map/all_to_all | solution.py:870
  256.6 8.1 %collective-permute-start.22 = (bf16[1,32,1024]{2,1,0:T(8,128)(2,1)S(1)}, bf16[1,32,1024]{2,1,0:T(8,128)(2,1)S(1)}, u32[]{:S(2)}, u32[]{:S(2)}) collective-permute-start(bf16[1,32,1024]{2,1,0:T(8,128)(2,1)S(1)} %slice.215), channel_id=1, source_target_pairs={{0,4},{1,5},{2,6},{3,7},{4,0},{5,1},{6,2},{7,3},{8,12},{9,13},{10,... | collective-permute-start | bytes 196616 | tf_op jit(solution)/shard_map/ppermute | solution.py:348
  (65 other events, 226.1 us)

commit v2 on v0

--- a/solution.py
+++ b/solution.py
@@ -2,7 +2,11 @@
 
 import jax
 import jax.numpy as jnp
+import numpy as np
 from jax import lax
+from jax.experimental import pallas as pl
+from jax.experimental.pallas import tpu as pltpu
+from jax.sharding import Mesh
 from jax.sharding import PartitionSpec as P
 
 H = 16
@@ -327,7 +331,718 @@
     )
 
 
+BF = jnp.bfloat16
+F32 = jnp.float32
+AXES = ("x", "core", "zh", "zl", "y")
+ROW = ("zh", "zl", "y")
+GELU_A = 0.7978845608028654
+GELU_B = 0.044715
+VMEM_MIB = 56
+COST = 1e3
+
+
+def mm(left, right):
+    return jnp.dot(left, right, preferred_element_type=F32)
+
+
+def swap_over(value, *names):
+    mask = sum(16 >> AXES.index(name) for name in names)
+    return lax.ppermute(value, AXES, [(i, i ^ mask) for i in range(32)])
+
+
+def whole(shape):
+    zeros = (0,) * len(shape)
+    return pl.BlockSpec(shape, lambda *_: zeros)
+
+
+def arr(shape, dtype):
+    return jax.ShapeDtypeStruct(shape, dtype)
+
+
+def call(body, grid, in_specs, out_specs, out_shape, scratch, micros, scalars, args):
+    nbytes = int(micros * COST)
+    return pl.pallas_call(
+        body,
+        grid_spec=pltpu.PrefetchScalarGridSpec(
+            num_scalar_prefetch=1,
+            grid=grid,
+            in_specs=in_specs,
+            out_specs=out_specs,
+            scratch_shapes=scratch,
+        ),
+        out_shape=out_shape,
+        compiler_params=pltpu.CompilerParams(vmem_limit_bytes=VMEM_MIB << 20),
+        cost_estimate=pl.CostEstimate(flops=0, bytes_accessed=nbytes, transcendentals=0),
+    )(scalars, *args)
+
+
+def one_step(body, outs, scratch, micros, scalars, args):
+    return call(
+        body, (1,), [whole(v.shape) for v in args], [whole(o.shape) for o in outs], outs, scratch,
+        micros, scalars, args,
+    )
+
+
+def standardize(x):
+    mean = jnp.mean(x, -1, keepdims=True)
+    centered = x - mean
+    inv = lax.rsqrt(jnp.mean(centered * centered, -1, keepdims=True) + 1e-06)
+    return centered * inv, inv
+
+
+def swap_halves(x):
+    lane = lax.broadcasted_iota(jnp.int32, x.shape, 1)
+    return jnp.where(lane % 64 < 32, pltpu.roll(x, 96, 1), pltpu.roll(x, 32, 1))
+
+
+def gelu_both(h):
+    t = jnp.tanh(h * (GELU_A + (GELU_A * GELU_B) * (h * h)))
+    half = 0.5 * h
+    act = half + half * t
+    slope = (0.5 + 0.5 * t) + half * (1.0 - t * t) * (GELU_A + (3.0 * GELU_A * GELU_B) * (h * h))
+    return act, slope
+
+
+def down_back_body(place, cot, down, d_act, bias_part):
+    @pl.when(pl.program_id(0) == 0)
+    def _():
+        bias_part[...] = jnp.sum(cot[...].astype(F32), 0, keepdims=True)
+
+    d_act[...] = times_transposed(cot[...], down[...])
+
+
+def qkv_half(place, blocks, vecs, ws, cos, sin, hat_out, normed):
+    g = vecs[0:1, :]
+    s = vecs[1:2, :]
+    for j in range(4):
+        rows = slice(128 * j, 128 * j + 128)
+        hat, _ = standardize(blocks[j][...].astype(F32))
+        hat_out[rows, :] = hat.astype(BF)
+        normed[rows, :] = (hat * g + s).astype(BF)
+    lanes = pl.ds(pl.multiple_of(place[0] * 128, 128), 128)
+    bias3 = jnp.concatenate([vecs[12 + p : 13 + p, lanes] for p in range(3)], 1)
+    mixed = mm(normed[...], jnp.concatenate([w[...] for w in ws], 1)) + bias3
+    c = cos[...]
+    sn = sin[...]
+    q = mixed[:, :128]
+    k = mixed[:, 128:256]
+    return (
+        ((q * c + swap_halves(q) * sn) * 0.125).astype(BF),
+        (k * c + swap_halves(k) * sn).astype(BF),
+        mixed[:, 256:].astype(BF),
+    )
+
+
+def near_body(place, *refs):
+    blocks = refs[:4]
+    vecs, wq, wk, wv, cos, sin, hat_out, q_out, k_out, v_out, normed = refs[4:]
+    q, k, v = qkv_half(place, blocks, vecs, (wq, wk, wv), cos, sin, hat_out, normed)
+    q_out[...] = q
+    k_out[...] = k
+    v_out[...] = v
+
+
+def far_body(place, *refs):
+    blocks = refs[:4]
+    vecs, wq, wk, wv, cos, sin, q0, k0, v0, hat_out, q_out, k_out, v_out, normed = refs[4:]
+    q, k, v = qkv_half(place, blocks, vecs, (wq, wk, wv), cos, sin, hat_out, normed)
+    for out, near, far in ((q_out, q0, q), (k_out, k0, k), (v_out, v0, v)):
+        out[:512, :] = near[...]
+        out[512:, :] = far
+
+
+def head_mask(shape, head):
+    return lax.broadcasted_iota(jnp.int32, shape, 1) // 64 == head
+
+
+def attend_body(place, q, k_all, v_all, id_col, id_row, att_f, att_low, probs):
+    keys = k_all[...]
+    values = v_all[...]
+    queries = q[...]
+    own = id_col[...]
+    allowed = jnp.concatenate([own, own], 1) == id_row[0:1, :]
+    halves = []
+    for head in range(2):
+        mine = jnp.where(head_mask(queries.shape, head), queries, jnp.zeros_like(queries))
+        scores = jnp.where(allowed, times_transposed(keys, mine), NEG_FILL)
+        weights = jnp.exp(scores - jnp.max(scores, 0, keepdims=True))
+        low = (weights * (1.0 / jnp.sum(weights, 0, keepdims=True))).astype(BF)
+        probs[head] = low
+        halves.append(outer_sum(values, low)[64 * head : 64 * head + 64])
+    out = jnp.concatenate(halves, 0).T
+    att_f[...] = out
+    step = pl.program_id(0)
+    att_low[place[0] ^ (2 * step)] = out[:128].astype(BF)
+    att_low[place[0] ^ (2 * step + 1)] = out[128:].astype(BF)
+
+
+def proj_body(place, att, tok, proj_w, vecs, middle, normed, att_rows):
+    rows = jnp.concatenate([att[k] for k in range(8)], 1)
+    att_rows[...] = rows
+    mid = tok[...].astype(F32) + mm(rows, proj_w[...]) + vecs[2:3, :]
+    middle[...] = mid
+    hat, _ = standardize(mid)
+    low = (hat * vecs[3:4, :] + vecs[4:5, :]).astype(BF)
+    normed[...] = low
+
+
+def proj_grad(place, att, d_b, vectors, send, keep):
+    grad = outer_sum(att, d_b)
+    row = lax.broadcasted_iota(jnp.int32, (32, 128), 0)
+    rel_y = place[0] & 1
+    rel_zl = (place[0] >> 1) & 1
+    rel_zh = place[0] >> 2
+    for owner in range(32):
+        x, core, k = owner // 16, (owner // 8) % 2, owner % 8
+        rows = grad[32 * owner : 32 * owner + 32]
+        extra = jnp.zeros((32, 128), F32)
+        first = 128 * (owner // 4)
+        for m in range(4):
+            extra = jnp.where(row == m, vectors[m : m + 1, first : first + 128], extra)
+        group = 2 * x + core
+        last = vectors[4 + group : 5 + group, 128 * k : 128 * k + 128]
+        extra = jnp.where(row == 4, last, extra)
+        slot = ((rel_y ^ (k & 1)) * 8 + (rel_zl ^ ((k >> 1) & 1)) * 4) + (
+            (place[1] ^ x) * 2 + (rel_zh ^ (k >> 2))
+        )
+
+        @pl.when(core == place[2])
+        def _():
+            keep[slot, :, :1024] = rows
+            keep[slot, :, 1024:] = extra
+
+        @pl.when(core != place[2])
+        def _():
+            send[slot, :, :1024] = rows.astype(BF)
+            send[slot, :, 1024:] = extra.astype(BF)
+
+
+def mlp_body(
+    place, normed, d_act, up_w, vecs, middle, cot, proj_w, down_bias, att,
+    active, d_mid, d_att, proj_send, proj_keep, acc, vectors,
+):
+    step = pl.program_id(0)
+    hidden = mm(normed[...], up_w[...]) + vecs[pl.ds(8 + step, 1), :]
+    act, slope = gelu_both(hidden)
+    active[...] = act.astype(BF)
+    d_hidden = (d_act[...] * slope).astype(BF)
+    vectors[pl.ds(4 + step, 1), :] = jnp.sum(d_hidden.astype(F32), 0, keepdims=True)
+    part = times_transposed(d_hidden, up_w[...])
+
+    @pl.when(step == 0)
+    def _():
+        acc[...] = part
+
+    @pl.when(step > 0)
+    def _():
+        acc[...] += part
+
+    @pl.when(step == pl.num_programs(0) - 1)
+    def _():
+        up = acc[...]
+        hat, inv = standardize(middle[...])
+        e = up * vecs[3:4, :]
+        inner = e - jnp.mean(e, -1, keepdims=True) - hat * jnp.mean(e * hat, -1, keepdims=True)
+        d_m = cot[...].astype(F32) + inv * inner
+        d_mid[...] = d_m
+        d_b = d_m.astype(BF)
+        vectors[0:1, :] = jnp.sum(up * hat, 0, keepdims=True)
+        vectors[1:2, :] = jnp.sum(up, 0, keepdims=True)
+        vectors[2:3, :] = jnp.sum(d_b.astype(F32), 0, keepdims=True)
+        vectors[3:4, :] = down_bias[...]
+        d_a = times_transposed(d_b, proj_w[...]).astype(BF)
+        for k in range(8):
+            d_att[k] = d_a[:, 128 * k : 128 * k + 128]
+        proj_grad(place, att[...], d_b, vectors, proj_send, proj_keep)
+
+
+def mlp_grad_body(place, *refs):
+    blocks, cots, ups, downs = refs[:8], refs[8:16], refs[16:20], refs[20:24]
+    vecs, down_keep, down_send, up_keep, up_send, n_all, c_all, u_all, d_all, grad = refs[24:]
+    for j in range(8):
+        n_all[128 * j : 128 * j + 128, :] = blocks[j][...]
+        c_all[128 * j : 128 * j + 128, :] = cots[j][...]
+    lanes = pl.ds(pl.multiple_of(place[0] * 128, 128), 128)
+    up_b = []
+    rows = vecs[8:12, lanes]
+    biases = lax.broadcasted_iota(jnp.int32, (4, 128), 0)
+    for g in range(4):
+        u_all[:, 128 * g : 128 * g + 128] = ups[g][...]
+        d_all[128 * g : 128 * g + 128, :] = downs[g][...]
+        group = (place[1] ^ (g & 1)) * 2 + (place[2] ^ (g >> 1))
+        up_b.append(jnp.sum(jnp.where(biases == group, rows, 0.0), 0, keepdims=True))
+    n = n_all[...]
+    c = c_all[...]
+    act, slope = gelu_both(mm(n, u_all[...]) + jnp.concatenate(up_b, 1))
+    grad_down = outer_sum(act.astype(BF), c)
+    for g in range(4):
+        rows = grad_down[128 * g : 128 * g + 128]
+        if g < 2:
+            down_keep[g] = rows
+        else:
+            down_send[g - 2] = rows.astype(BF)
+    d_hidden = (times_transposed(c, d_all[...]) * slope).astype(BF)
+    both = outer_sum(n, d_hidden)
+    for g in range(4):
+        group = ((place[1] ^ (g & 1)) * 2) + (place[2] ^ (g >> 1))
+        lanes = pl.ds(pl.multiple_of(group * 128, 128), 128)
+        grad[:, lanes] = both[:, 128 * g : 128 * g + 128]
+    for rx in range(2):
+        first = (place[1] ^ rx) * 512
+        keep = pl.multiple_of(first + place[2] * 256, 256)
+        send = pl.multiple_of(first + (1 - place[2]) * 256, 256)
+        up_keep[rx] = grad[pl.ds(keep, 256), :]
+        up_send[rx] = grad[pl.ds(send, 256), :].astype(BF)
+
+
+def attend_back_body(
+    place, probs, d_att, att_f, q, k_all, v_all, cos, sin, d_all, bias_part, dq, dk, dv
+):
+    step = pl.program_id(0)
+    keys = k_all[...]
+    values = v_all[...]
+    queries = q[...]
+    d_out = jnp.concatenate([d_att[place[0] ^ (2 * step)], d_att[place[0] ^ (2 * step + 1)]], 0)
+    products = (d_out.astype(F32) * att_f[...]).T
+    key_parts, value_parts, query_parts = [], [], []
+    for head in range(2):
+        weights = probs[head]
+        mine = jnp.where(head_mask(d_out.shape, head), d_out, jnp.zeros_like(d_out))
+        delta = jnp.sum(products[64 * head : 64 * head + 64], 0, keepdims=True)
+        d_weights = times_transposed(values, mine)
+        d_scores = (weights.astype(F32) * (d_weights - delta)).astype(BF)
+        key_parts.append(mm(d_scores, queries))
+        value_parts.append(mm(weights, d_out))
+        query_parts.append(outer_sum(keys, d_scores)[64 * head : 64 * head + 64])
+    first = head_mask((1024, 128), 0)
+    dk_new = jnp.where(first, key_parts[0], key_parts[1])
+    dv_new = jnp.where(first, value_parts[0], value_parts[1])
+    dq[pl.ds(pl.multiple_of(step * 256, 256), 256), :] = jnp.concatenate(query_parts, 0).T
+
+    @pl.when(step == 0)
+    def _():
+        dk[...] = dk_new
+        dv[...] = dv_new
+
+    @pl.when(step > 0)
+    def _():
+        dk[...] += dk_new
+        dv[...] += dv_new
+
+    @pl.when(step == pl.num_programs(0) - 1)
+    def _():
+        total = jnp.zeros((1, 384), F32)
+        for j in range(8):
+            rows = slice(128 * j, 128 * j + 128)
+            c = cos[rows, :]
+            sn = sin[rows, :]
+            back_q = 0.125 * dq[rows, :]
+            back_k = dk[rows, :]
+            piece = jnp.concatenate(
+                [
+                    back_q * c - swap_halves(back_q) * sn,
+                    back_k * c - swap_halves(back_k) * sn,
+                    dv[rows, :],
+                ],
+                1,
+            ).astype(BF)
+            d_all[place[0] ^ j] = piece
+            total = total + jnp.sum(piece.astype(F32), 0, keepdims=True)
+        bias_part[...] = total
+
+
+def rel_block(step, place):
+    rel = jnp.where(step < 2, 2, 0) + step % 2
+    return ((rel & 1) ^ place[1]) * 2 + ((rel >> 1) ^ place[2])
+
+
+def qkv_grad_body(place, h0, h1, d_all, bias_part, columns, wq, wk, wv, send, keep):
+    step = pl.program_id(0)
+    d_near = jnp.concatenate([d_all[place[0] ^ j] for j in range(4)], 0)
+    d_far = jnp.concatenate([d_all[place[0] ^ j] for j in range(4, 8)], 0)
+    inner = outer_sum(h0[...], d_near) + outer_sum(h1[...], d_far)
+    total = bias_part[...]
+    w = jnp.concatenate([wq[...], wk[...], wv[...]], 1).astype(F32)
+    gain = columns[:, 0:1]
+    shift = columns[:, 1:2]
+    grad = gain * inner + shift * total
+    row = lax.broadcasted_iota(jnp.int32, (256, 128), 0) % 32
+    lane = lax.broadcasted_iota(jnp.int32, (256, 128), 1)
+    extra = jnp.where(
+        lane == 0,
+        jnp.sum(w * inner, 1, keepdims=True),
+        jnp.where(lane == 1, jnp.sum(w * total, 1, keepdims=True), 0.0),
+    )
+    for m in range(6):
+        part = total[:, 128 * (m // 2) : 128 * (m // 2) + 128]
+        part = part if m % 2 else pltpu.roll(part, 64, 1)
+        extra = jnp.where((row == m) & (lane >= 64), part, extra)
+
+    @pl.when(step < 2)
+    def _():
+        send[0, :, :384] = grad.astype(BF)
+        send[0, :, 384:] = extra.astype(BF)
+
+    @pl.when(step >= 2)
+    def _():
+        keep[0, :, :384] = grad
+        keep[0, :, 384:] = extra
+
+
+def finish_body(place, came, grad_up, grad_qkv, sums, bias):
+    total = jnp.zeros((32, 128), F32)
+    for k in range(8):
+        for g in range(4):
+            lanes = slice(1024 * g + 128 * k, 1024 * g + 128 * k + 128)
+            grad_up[:, lanes] = came[k, :32, 128 * g : 128 * g + 128].astype(F32)
+            if g < 3:
+                grad_qkv[:, lanes] = came[k, 32:, 128 * g : 128 * g + 128].astype(F32)
+        extra = came[k, 32:, 384:].astype(F32)
+        total = total + extra
+        bias[6 * k : 6 * k + 6, :] = extra[:6]
+    sums[...] = total
+
+
+def last_body(place, came, w, tok, d_mid, vecs, out, acc):
+    step = pl.program_id(0)
+    for p in range(3):
+
+        @pl.when(step == p)
+        def _():
+            d_mixed = jnp.concatenate([came[k, :, 128 * p : 128 * p + 128] for k in range(8)], 1)
+            part = times_transposed(d_mixed, w[...])
+            if p == 0:
+                acc[...] = part
+            elif p == 1:
+                acc[...] += part
+            else:
+                up = acc[...] + part
+                hat, inv = standardize(tok[...].astype(F32))
+                e = up * vecs[0:1, :]
+                mean = jnp.mean(e, -1, keepdims=True)
+                inner = e - mean - hat * jnp.mean(e * hat, -1, keepdims=True)
+                out[...] = d_mid[...] + inv * inner
+
+
+def frequency_rows():
+    rows = np.zeros((8, 128), np.float32)
+    for lane in range(128):
+        pair = lane % 32
+        part, rank, count = (0, pair, 10) if pair < 10 else ((1, pair - 10, 11) if pair < 21 else (2, pair - 21, 11))
+        rows[part, lane] = 10000.0 ** (-rank / count)
+        rows[3, lane] = -1.0 if lane % 64 < 32 else 1.0
+    return rows
+
+
+def clip_starts(place, pos):
+    ids = jnp.zeros_like(pos)
+    start = jnp.zeros_like(pos)
+    end = jnp.int32(0)
+    for c in range(8):
+        length = place[8 + c]
+        end = end + length
+        past = pos >= end.astype(F32)
+        ids = jnp.where(past, ids + 1.0, ids)
+        start = jnp.where(past, end.astype(F32), start)
+    return ids, start
+
+
+def prep_body(place, freq, vecs, cos, sin, id_col, id_row, columns):
+    for j in range(8):
+        first = ((place[0] ^ j) * 128).astype(F32)
+        rows = slice(128 * j, 128 * j + 128)
+        pos = first + lax.broadcasted_iota(jnp.int32, (128, 128), 0).astype(F32)
+        ids, start = clip_starts(place, pos)
+        id_col[rows, :] = ids
+        within = pos - start
+        row14 = jnp.floor((within + 0.5) * (1.0 / 14.0))
+        t = jnp.floor((within + 0.5) * (1.0 / 196.0))
+        angle = t * freq[0:1, :] + (row14 - 14.0 * t) * freq[1:2, :] + (within - 14.0 * row14) * freq[2:3, :]
+        cos[rows, :] = jnp.cos(angle)
+        sin[rows, :] = jnp.sin(angle) * freq[3:4, :]
+        flat = first + lax.broadcasted_iota(jnp.int32, (8, 128), 1).astype(F32)
+        id_row[:, 128 * j : 128 * j + 128] = clip_starts(place, flat)[0]
+    columns[...] = vecs[0:8, :].T
+
+
+def after(value, *others):
+    return lax.optimization_barrier((value, *others))[0]
+
+
+def spread_four(a):
+    return [a, swap_over(a, "y"), swap_over(a, "zl"), swap_over(a, "zl", "y")]
+
+
+def fast_shards(
+    tokens_in, clip_lengths, attn_gain, attn_shift, qkv_weight, qkv_bias, proj_weight, proj_bias,
+    mlp_gain, mlp_shift, up_weight, up_bias, down_weight, down_bias, out_cotangent,
+):
+    x, core, zh, zl, y = (lax.axis_index(name) for name in AXES)
+    k = zh * 4 + zl * 2 + y
+    me = x * 16 + core * 8 + k
+    place = jnp.concatenate(
+        [jnp.stack([k, x, core, k, k, k, k, k]).astype(jnp.int32), clip_lengths[0]]
+    )
+    tok = tokens_in[0]
+    cot = out_cotangent[0]
+
+    far_tok = swap_over(tok, "zh")
+    near = spread_four(tok)
+    rows = [attn_gain, attn_shift, proj_bias, mlp_gain, mlp_shift, down_bias, down_bias, down_bias]
+    vecs = jnp.concatenate([v.astype(F32).reshape(-1, 1024) for v in (*rows, up_bias, qkv_bias)], 0)
+    cos_tab, sin_tab, id_col, id_row, columns = one_step(
+        prep_body,
+        [arr((1024, 128), F32), arr((1024, 128), F32), arr((1024, 128), F32), arr((8, 1024), F32),
+         arr((1024, 8), F32)],
+        [],
+        3,
+        place,
+        (jnp.asarray(frequency_rows()), vecs),
+    )
+    far_tok, cos_tab, *near = lax.optimization_barrier((far_tok, cos_tab, *near))
+    far = spread_four(far_tok)
+    cot_here, *_ = lax.optimization_barrier((cot, far_tok))
+    far_cot = swap_over(cot_here, "zh")
+    cots = spread_four(cot_here)
+
+    def table_half(part):
+        return pl.BlockSpec((512, 128), lambda i, s: (part, 0))
+
+    half = arr((512, 128), BF)
+    full = arr((1024, 128), BF)
+    common = (vecs, qkv_weight, qkv_weight, qkv_weight, cos_tab, sin_tab)
+    columns_of = [pl.BlockSpec((1024, 128), lambda i, s, p=p: (0, 8 * p + s[0])) for p in range(3)]
+
+    def qkv(body, part, blocks, more, outs):
+        specs = [whole(v.shape) for v in (*blocks, vecs)] + columns_of
+        specs += [table_half(part), table_half(part)] + [whole(v.shape) for v in more]
+        return call(
+            body, (1,), specs, [whole(o.shape) for o in outs], outs,
+            [pltpu.VMEM((512, 1024), BF)], 2, place, (*blocks, *common, *more),
+        )
+
+    hat0, q0, k0, v0 = qkv(near_body, 0, near, (), [arr((512, 1024), BF), half, half, half])
+    far = lax.optimization_barrier((q0, *far))[1:]
+    hat1, q_all, k_all, v_all = qkv(
+        far_body, 1, far, (q0, k0, v0), [arr((512, 1024), BF), full, full, full]
+    )
+    step_rows = pl.BlockSpec((256, 128), lambda i, s: (i, 0))
+    flat = whole((1024, 128))
+    att_f, att_low, probs = call(
+        attend_body,
+        (4,),
+        [
+            step_rows, flat, flat, flat, pl.BlockSpec((8, 256), lambda i, s: (0, i)),
+        ],
+        [step_rows, whole((8, 128, 128)), pl.BlockSpec((2, 1024, 256), lambda i, s: (0, 0, i))],
+        [arr((1024, 128), F32), arr((8, 128, 128), BF), arr((2, 1024, 1024), BF)],
+        [],
+        6,
+        place,
+        (q_all, k_all, v_all, id_col, id_row),
+    )
+    att_low, far_cot, *cots = lax.optimization_barrier((att_low, far_cot, *cots))
+    att_in = lax.all_to_all(att_low, ROW, 0, 0, tiled=True)
+    cots = cots + spread_four(far_cot)
+    d_act, down_bias_part = call(
+        down_back_body,
+        (4,),
+        [whole((128, 1024)), pl.BlockSpec((1024, 1024), lambda i, s: (i, 0))],
+        [pl.BlockSpec((128, 1024), lambda i, s: (0, i)), whole((1, 1024))],
+        [arr((128, 4096), F32), arr((1, 1024), F32)],
+        [],
+        4,
+        place,
+        (after(cot, att_low), down_weight),
+    )
+
+
+    middle, normed2, att_rows = one_step(
+        proj_body,
+        [arr((128, 1024), F32), arr((128, 1024), BF), arr((128, 1024), BF)],
+        [],
+        2,
+        place,
+        (after(att_in, d_act), tok, proj_weight, vecs),
+    )
+    normed2, *cots = lax.optimization_barrier((normed2, *cots))
+    far_n = swap_over(normed2, "zh")
+    near_n = spread_four(normed2)
+    wide = pl.BlockSpec((128, 1024), lambda i, s: (0, i))
+    fixed = whole((128, 1024))
+    active, d_mid, d_att, proj_send, proj_keep = call(
+        mlp_body,
+        (4,),
+        [
+            fixed, wide, wide_columns(), whole((15, 1024)), fixed, fixed, whole((1024, 1024)),
+            whole((1, 1024)), fixed,
+        ],
+        [wide, fixed, whole((8, 128, 128)), whole((16, 32, 1152)), whole((16, 32, 1152))],
+        [
+            arr((128, 4096), BF), arr((128, 1024), F32), arr((8, 128, 128), BF),
+            arr((16, 32, 1152), BF), arr((16, 32, 1152), F32),
+        ],
+        [pltpu.VMEM((128, 1024), F32), pltpu.VMEM((8, 1024), F32)],
+        8,
+        place,
+        (normed2, d_act, up_weight, vecs, middle, cot, proj_weight, down_bias_part, att_rows),
+    )
+    d_att, far_n, active, proj_send, *near_n = lax.optimization_barrier(
+        (d_att, far_n, active, proj_send, *near_n)
+    )
+    d_att_in = lax.all_to_all(d_att, ROW, 0, 0, tiled=True)
+
+    result = middle + mm(active, down_weight) + down_bias.astype(F32)
+    layer_out = result.astype(BF)[None]
+    far_n = spread_four(after(far_n, layer_out))
+
+    def core_sum(keep, send):
+        return keep + swap_over(send, "core").astype(F32)
+
+    def x_sum(keep):
+        return keep[0] + swap_over(keep[1].astype(BF), "x").astype(F32)
+
+    def half_sum(value, name):
+        count = value.shape[0] // 2
+        return value[:count] + swap_over(value[count:].astype(BF), name).astype(F32)
+
+    d_all, qkv_bias_part = call(
+        attend_back_body,
+        (4,),
+        [
+            pl.BlockSpec((2, 1024, 256), lambda i, s: (0, 0, i)), whole((8, 128, 128)), step_rows,
+            step_rows, flat, flat, flat, flat,
+        ],
+        [whole((8, 128, 384)), whole((1, 384))],
+        [arr((8, 128, 384), BF), arr((1, 384), F32)],
+        [pltpu.VMEM((1024, 128), F32)] * 3,
+        6,
+        place,
+        (probs, after(d_att_in, layer_out), att_f, q_all, k_all, v_all, cos_tab, sin_tab),
+    )
+    d_all, *far_n = lax.optimization_barrier((d_all, *far_n))
+    moved = lax.all_to_all(d_all, ROW, 0, 0, tiled=True)
+
+    def group_of(s, g):
+        return (s[1] ^ (g & 1)) * 16 + (s[2] ^ (g >> 1)) * 8 + s[0]
+
+    outs = [
+        arr((2, 128, 1024), F32), arr((2, 128, 1024), BF), arr((2, 256, 512), F32),
+        arr((2, 256, 512), BF),
+    ]
+    down_keep, down_send, up_keep, up_send = call(
+        mlp_grad_body,
+        (1,),
+        [fixed] * 16
+        + [pl.BlockSpec((1024, 128), lambda i, s, g=g: (0, group_of(s, g))) for g in range(4)]
+        + [pl.BlockSpec((128, 1024), lambda i, s, g=g: (group_of(s, g), 0)) for g in range(4)]
+        + [whole((15, 1024))],
+        [whole(o.shape) for o in outs],
+        outs,
+        [
+            pltpu.VMEM((1024, 1024), BF), pltpu.VMEM((1024, 1024), BF),
+            pltpu.VMEM((1024, 512), BF), pltpu.VMEM((512, 1024), BF), pltpu.VMEM((1024, 512), F32),
+        ],
+        8,
+        place,
+        (after(near_n[0], d_all), *near_n[1:], *far_n, *cots, *([up_weight] * 4), *([down_weight] * 4), vecs),
+    )
+
+
+    block_of = lambda i, s: (rel_block(i, s), 0)
+    lanes_of = lambda i, s: (0, rel_block(i, s))
+    send, keep = call(
+        qkv_grad_body,
+        (4,),
+        [
+            pl.BlockSpec((512, 256), lanes_of), pl.BlockSpec((512, 256), lanes_of),
+            whole((8, 128, 384)), whole((1, 384)), pl.BlockSpec((256, 8), block_of),
+        ]
+        + [pl.BlockSpec((256, 128), lambda i, s, p=p: (rel_block(i, s), 8 * p + s[0])) for p in range(3)],
+        [
+            pl.BlockSpec((1, 256, 512), lambda i, s: (jnp.minimum(i, 1), 0, 0)),
+            pl.BlockSpec((1, 256, 512), lambda i, s: (jnp.maximum(i - 2, 0), 0, 0)),
+        ],
+        [arr((2, 256, 512), BF), arr((2, 256, 512), F32)],
+        [],
+        4,
+        place,
+        (after(hat0, up_send), hat1, d_all, qkv_bias_part, columns, qkv_weight, qkv_weight, qkv_weight),
+    )
+    up_keep = core_sum(after(up_keep, moved), up_send)
+    up_sum = x_sum(up_keep)
+    keep = core_sum(after(keep, moved), send)
+    qkv_sum = x_sum(keep)
+    down_keep = core_sum(down_keep, down_send)
+    grad_down = x_sum(after(down_keep, keep))
+    proj_half = core_sum(after(proj_keep, up_send), proj_send)
+    proj_half = half_sum(proj_half, "y")
+    proj_half = half_sum(proj_half, "zl")
+    proj_half = half_sum(proj_half, "x")
+
+    def turn(value, *others):
+        return lax.all_to_all(after(value, *others), ROW, 0, 0, tiled=True)
+
+    lows = jnp.concatenate([v.astype(BF).reshape(8, 32, 512) for v in (up_sum, qkv_sum)], 1)
+    came = turn(lows, moved)
+    proj_total = half_sum(proj_half, "zh")[0]
+    grad_proj = proj_total[:, :1024]
+    own = lax.dynamic_slice(proj_total[:4, 1024:], (0, (me % 4) * 32), (4, 32))
+    grad_up_b = proj_total[4, 1024:]
+
+    grad_up, grad_qkv, sums, bias = one_step(
+        finish_body,
+        [arr((32, 4096), F32), arr((32, 3072), F32), arr((32, 128), F32), arr((48, 128), F32)],
+        [],
+        2,
+        place,
+        (came,),
+    )
+    bias = bias[:, 64:].reshape(8, 3, 128).transpose(1, 0, 2).reshape(3072)
+    grad_qkv_b = lax.dynamic_slice(bias, (me * 96,), (96,))
+
+    (tokens_grad,) = call(
+        last_body,
+        (3,),
+        [
+            whole((8, 128, 384)), pl.BlockSpec((1024, 1024), lambda i, s: (0, i)), fixed, fixed,
+            whole((15, 1024)),
+        ],
+        [fixed],
+        [arr((128, 1024), F32)],
+        [pltpu.VMEM((128, 1024), F32)],
+        5,
+        place,
+        (moved, qkv_weight, tok, d_mid, vecs),
+    )
+
+    return (
+        layer_out, tokens_grad[None], sums[:, 0], sums[:, 1], grad_qkv, grad_qkv_b, grad_proj,
+        own[2], own[0], own[1], grad_up, grad_up_b, grad_down, own[3],
+    )
+
+
+def wide_columns():
+    return pl.BlockSpec((1024, 1024), lambda i, s: (0, i))
+
+
+def fast_solution(mesh):
+    wide_mesh = Mesh(mesh.devices.reshape(2, 2, 2, 2, 2), AXES)
+    batch, blk = AXES[:2], AXES[2:]
+    spread = P(batch, blk, None)
+    return jax.shard_map(
+        fast_shards,
+        mesh=wide_mesh,
+        in_specs=(spread, P(batch, None)) + (P(),) * 12 + (spread,),
+        out_specs=(spread, spread)
+        + tuple(P(AXES, None) if i in (2, 4, 8, 10) else P(AXES) for i in range(12)),
+        check_vma=False,
+    )
+
+
 def solution(mesh):
+    if tuple(mesh.devices.shape) == (4, 8):
+        return fast_solution(mesh)
     placed = (
         P("batch", "blk", None),
         P("batch", None),

time: 1370 us -> 219 us (0.16)
  waiting for transfers between devices: 1190 us -> 35.6 us
  Pallas kernels: 0 us -> 87.6 us
  matrix products: 86.1 us -> 5.69 us
  starting transfers between devices: 0.55 us -> 59.4 us
  blocking collectives: 43.1 us -> 0 us
    reduce_scatter x6 -> x0, waiting for transfers between devices: 1090 us -> none  [the longest x1 360 us: shards(): lax.psum_scatter(grad_down_w, ('batch', 'blk'), scatter_dimension=0, tile...]
    all_gather x2 -> x0, waiting for transfers between devices: 90.9 us -> none  [the longest x1 47.2 us: shards(): lax.all_gather(key_low, 'blk', axis=0, tiled=True)]
    pallas_call x0 -> x12, Pallas kernels: none -> 87.6 us  [call(): pl.pallas_call(body, grid_spec=pltpu.PrefetchScalarGridSpec(num_scalar_pr...]
    dot_general x19 -> x1, matrix products: 86.1 us -> 5.69 us  [mm(): return jnp.dot(left, right, preferred_element_type=F32)]
    unnamed x1 -> x0, blocking collectives: 43.1 us -> none
    ppermute x0 -> x32, starting transfers between devices: none -> 41.5 us  [swap_over(): return lax.ppermute(value, AXES, [(i, i ^ mask) for i in range(32)])]
    ppermute x0 -> x32, waiting for transfers between devices: none -> 35.2 us  [swap_over(): return lax.ppermute(value, AXES, [(i, i ^ mask) for i in range(32)])]
    all_to_all x0 -> x4, starting transfers between devices: none -> 17.9 us  [the longest x1 5.3 us: fast_shards(): moved = lax.all_to_all(d_all, ROW, 0, 0, tiled=True)]
  transfers between devices with their start and end apart: 8 -> 36, of which waited for: 8 -> 10; matrix products, arithmetic and copies ran while one was open for 5% -> 13% of each run, Pallas kernels for 0% -> 39%
where the time goes in v2:
time: 219 us; the launch traced here: 218 us
  Pallas kernels  87.6 us (40%)
  starting transfers between devices  59.4 us (27%)
  waiting for transfers between devices  35.6 us (16%)
  other arithmetic  14.7 us (7%)
  local copies, waits for them, and re-layouts  13.4 us (6%)
  matrix products  5.69 us (3%)
    pallas_call x12, Pallas kernels, call(): pl.pallas_call(body, grid_spec=pltpu.PrefetchScalarGridSpec(num_scalar_pr...  87.6 us
    ppermute x32, starting transfers between devices, swap_over(): return lax.ppermute(value, AXES, [(i, i ^ mask) for i in range(32)])  41.5 us
    ppermute x32, waiting for transfers between devices, swap_over(): return lax.ppermute(value, AXES, [(i, i ^ mask) for i in range(32)])  35.2 us
    dot_general x1, matrix products, mm(): return jnp.dot(left, right, preferred_element_type=F32)  5.69 us
    add x4, other arithmetic, core_sum(): return keep + swap_over(send, 'core').astype(F32)  5.6 us
    all_to_all x1, starting transfers between devices, fast_shards(): moved = lax.all_to_all(d_all, ROW, 0, 0, tiled=True)  5.3 us
    all_to_all x1, starting transfers between devices, fast_shards(): att_in = lax.all_to_all(att_low, ROW, 0, 0, tiled=True)  4.69 us
  transfers between devices with their start and end apart: 36, of which 10 were waited for; matrix products, arithmetic and copies ran while one was open for 13% of the time, Pallas kernels for 39%

profile of v2, /device:TPU:0, one launch (start us, length us, event | category | flops | bytes accessed | tf_op | source)
XLA Modules:
  0.0 217.6 jit_solution(4926097112935069825)
XLA Ops:
  0.6 4.1 %collective-permute-start = (bf16[128,1024]{1,0:T(8,128)(2,1)}, bf16[128,1024]{1,0:T(8,128)(2,1)S(1)}, u32[]{:S(2)}, u32[]{:S(2)}) collective-permute-start(bf16[128,1024]{1,0:T(8,128)(2,1)} %bitcast.62), channel_id=1, source_target_pairs={{0,4},{1,5},{2,6},{3,7},{4,0},{5,1},{6,2},{7,3},{8,12},{9,13},{10,... | collective-permute-start | bytes 786440 | tf_op jit(solution)/shard_map/ppermute | solution.py:350
  4.7 1.5 collective-permute-start.1
  6.3 1.6 collective-permute-start.2
  8.9 0.7 reshape.121
  9.6 0.7 reshape.123
  13.7 1.3 concatenate.9.place
  15.0 1.3 concatenate.10.vecs.refs_4_.refs_24_
  16.3 5.6 %shard_map.263 = (f32[1024,128]{1,0:T(8,128)}, f32[1024,128]{1,0:T(8,128)}, f32[1024,128]{1,0:T(8,128)}, f32[8,1024]{1,0:T(8,128)}, f32[1024,8]{1,0:T(8,128)}) custom-call(s32[16]{0:T(128)} %concatenate.9.place, f32[8,128]{1,0:T(8,128)} %constant.48.clone.freq, f32[15,1024]{1,0:T(8,128)} %concatenate.10.vecs.refs_4_.refs_24_), custom_call_target="tpu_custom_call" | custom-call | bytes 3000 | tf_op jit(solution)/shard_map/pallas_call | solution.py:364
  21.9 2.1 collective-permute-done.3.refs_3_
  24.0 1.5 collective-permute-start.4
  25.7 1.8 collective-permute-start.6
  27.5 1.2 collective-permute-start.10
  28.7 2.8 %collective-permute-start.7 = (bf16[128,1024]{1,0:T(8,128)(2,1)}, bf16[128,1024]{1,0:T(8,128)(2,1)S(1)}, u32[]{:S(2)}, u32[]{:S(2)}) collective-permute-start(bf16[128,1024]{1,0:T(8,128)(2,1)} %bitcast.56), channel_id=1, source_target_pairs={{0,4},{1,5},{2,6},{3,7},{4,0},{5,1},{6,2},{7,3},{8,12},{9,13},{10,... | collective-permute-start | bytes 786440 | tf_op jit(solution)/shard_map/ppermute | solution.py:350
  32.1 1.2 collective-permute-start.8
  33.3 7.1 %collective-permute-done.5.refs_2_ = bf16[128,1024]{1,0:T(8,128)(2,1)S(1)} collective-permute-done((bf16[128,1024]{1,0:T(8,128)(2,1)S(1)}, bf16[128,1024]{1,0:T(8,128)(2,1)S(1)}, u32[]{:S(2)}, u32[]{:S(2)}) %collective-permute-start.5) | collective-permute-done | bytes 262176 | tf_op jit(solution)/shard_map/ppermute | solution.py:350
  40.4 4.4 %shard_map.264 = (bf16[512,1024]{1,0:T(8,128)(2,1)}, bf16[512,128]{1,0:T(8,128)(2,1)}, bf16[512,128]{1,0:T(8,128)(2,1)}, bf16[512,128]{1,0:T(8,128)(2,1)}) custom-call(s32[16]{0:T(128)} %concatenate.9.place, bf16[128,1024]{1,0:T(8,128)(2,1)} %bitcast.66, bf16[128,1024]{1,0:T(8,128)(2,1)} %copy-done.16, bf16[128,1024]{1,0:T(8,128)(2,1)} %copy-done.17, ...), custom_call_target="tpu_custom_call" | custom-call | bytes 2000 | tf_op jit(solution)/shard_map/pallas_call | solution.py:364
  44.8 1.2 collective-permute-done.6.refs_3_
  46.0 0.7 copy-done.28
  46.7 4.6 %shard_map.265 = (bf16[512,1024]{1,0:T(8,128)(2,1)}, bf16[1024,128]{1,0:T(8,128)(2,1)}, bf16[1024,128]{1,0:T(8,128)(2,1)}, bf16[1024,128]{1,0:T(8,128)(2,1)}) custom-call(s32[16]{0:T(128)} %concatenate.9.place, bf16[128,1024]{1,0:T(8,128)(2,1)} %copy-done.12, bf16[128,1024]{1,0:T(8,128)(2,1)} %copy-done.26, bf16[128,1024]{1,0:T(8,128)(2,1)} %copy-done.27, ...), custom_call_target="tpu_custom_call" | custom-call | bytes 2000 | tf_op jit(solution)/shard_map/pallas_call | solution.py:364
  51.3 10.5 %shard_map.266 = (f32[1024,128]{1,0:T(8,128)}, bf16[8,128,128]{2,1,0:T(8,128)(2,1)}, bf16[2,1024,1024]{2,1,0:T(8,128)(2,1)}) custom-call(s32[16]{0:T(128)} %concatenate.9.place, bf16[1024,128]{1,0:T(8,128)(2,1)} %get-tuple-element.117.q, bf16[1024,128]{1,0:T(8,128)(2,1)} %get-tuple-element.118.k_all, bf16[1024,128]{1,0:T(8,128)(2,1)} %get-tuple-element.119.v_all, ...), custom_call_target="tpu_custom_call" | custom-call | bytes 6000 | tf_op jit(solution)/shard_map/pallas_call | solution.py:364
  61.9 4.7 %all-to-all-start = ((bf16[8,128,128]{2,1,0:T(8,128)(2,1)}), bf16[8,128,128]{2,1,0:T(8,128)(2,1)S(1)}, u32[]{:S(2)}, u32[]{:S(2)}) async-start(bf16[8,128,128]{2,1,0:T(8,128)(2,1)} %get-tuple-element.124), calls=%async_computation | async-start | bytes 524288 | tf_op jit(solution)/shard_map/all_to_all | solution.py:845
  66.6 2.0 collective-permute-start.11
  68.6 1.5 collective-permute-start.12
  70.1 7.6 %shard_map.267 = (f32[128,4096]{1,0:T(8,128)}, f32[1,1024]{1,0:T(1,128)}) custom-call(s32[16]{0:T(128)} %concatenate.9.place, bf16[128,1024]{1,0:T(8,128)(2,1)} %bitcast.59, bf16[4096,1024]{1,0:T(8,128)(2,1)} %refs_23_.1), custom_call_target="tpu_custom_call" | custom-call | bytes 4000 | tf_op jit(solution)/shard_map/pallas_call | solution.py:364
  78.5 3.9 %shard_map.268 = (f32[128,1024]{1,0:T(8,128)}, bf16[128,1024]{1,0:T(8,128)(2,1)}, bf16[128,1024]{1,0:T(8,128)(2,1)}) custom-call(s32[16]{0:T(128)} %concatenate.9.place, bf16[8,128,128]{2,1,0:T(8,128)(2,1)} %copy-done.6, bf16[128,1024]{1,0:T(8,128)(2,1)} %bitcast.67, bf16[1024,1024]{1,0:T(8,128)(2,1)} %proj_w.3, f32[15,1024]{1,0:T(8,128)} %concatenate.10.vecs.refs_4_.refs_24_), custom_call_target="tpu_custom_call" | custom-call | bytes 2000 | tf_op jit(solution)/shard_map/pallas_call | solution.py:364
  82.4 3.0 %collective-permute-start.14 = (bf16[128,1024]{1,0:T(8,128)(2,1)}, bf16[128,1024]{1,0:T(8,128)(2,1)S(1)}, u32[]{:S(2)}, u32[]{:S(2)}) collective-permute-start(bf16[128,1024]{1,0:T(8,128)(2,1)} %get-tuple-element.152.normed.refs_0_), channel_id=1, source_target_pairs={{0,4},{1,5},{2,6},{3,7},{4,0},{5,1},{6,2},{7,3},{8,12},{9,13},{10,... | collective-permute-start | bytes 786440 | tf_op jit(solution)/shard_map/ppermute | solution.py:350
  85.4 1.5 collective-permute-start.15
  86.8 1.5 collective-permute-start.16
  88.9 14.7 %shard_map.269 = (bf16[128,4096]{1,0:T(8,128)(2,1)}, f32[128,1024]{1,0:T(8,128)}, bf16[8,128,128]{2,1,0:T(8,128)(2,1)}, bf16[16,32,1152]{2,1,0:T(8,128)(2,1)}, f32[16,32,1152]{2,1,0:T(8,128)}) custom-call(s32[16]{0:T(128)} %concatenate.9.place, bf16[128,1024]{1,0:T(8,128)(2,1)} %get-tuple-element.152.normed.refs_0_, f32[128,4096]{1,0:T(8,128)} %get-tuple-element.126.d_act, ...), custom_call_target="tpu_custom_call" | custom-call | bytes 8000 | tf_op jit(solution)/shard_map/pallas_call | solution.py:364
  103.8 3.7 %all-to-all-start.1 = ((bf16[8,128,128]{2,1,0:T(8,128)(2,1)}), bf16[8,128,128]{2,1,0:T(8,128)(2,1)S(1)}, u32[]{:S(2)}, u32[]{:S(2)}) async-start(bf16[8,128,128]{2,1,0:T(8,128)(2,1)} %get-tuple-element.143), calls=%async_computation.1 | async-start | bytes 524288 | tf_op jit(solution)/shard_map/all_to_all | solution.py:893
  107.4 5.7 %fusion.2 = bf16[1,128,1024]{2,1,0:T(8,128)(2,1)} fusion(f32[128,1024]{1,0:T(8,128)S(1)} %copy-done.2, bf16[128,4096]{1,0:T(8,128)(2,1)} %get-tuple-element.141, bf16[4096,1024]{1,0:T(8,128)(2,1)} %refs_23_.1, f32[1024]{0:T(1024)S(1)} %convert_element_type.71), kind=kOutput, calls=%fused_computation.6 | convolution fusion | flops 1074135040 | bytes 10227712 | tf_op jit(solution)/shard_map/dot_general | solution.py:345
  113.1 2.1 collective-permute-start.18
  115.2 1.5 collective-permute-start.19
  117.1 0.7 copy-done.5
  117.8 9.8 %shard_map.270 = (bf16[8,128,384]{2,1,0:T(8,128)(2,1)}, f32[1,384]{1,0:T(1,128)}) custom-call(s32[16]{0:T(128)} %concatenate.9.place, bf16[2,1024,1024]{2,1,0:T(8,128)(2,1)} %get-tuple-element.142.probs, bf16[8,128,128]{2,1,0:T(8,128)(2,1)} %copy-done.5, f32[1024,128]{1,0:T(8,128)} %get-tuple-element.145.att_f, bf16[1024,128]{1,0:T(8,128)(2,1)} %get-tuple-element.117.q, ...), custom_call_target="tpu_custom_call" | custom-call | bytes 6000 | tf_op jit(solution)/shard_map/pallas_call | solution.py:364
  127.6 1.2 collective-permute-done.20.refs_7_
  128.8 5.3 %all-to-all-start.2 = ((bf16[8,128,384]{2,1,0:T(8,128)(2,1)}), bf16[8,128,384]{2,1,0:T(8,128)(2,1)}, u32[]{:S(2)}, u32[]{:S(2)}) async-start(bf16[8,128,384]{2,1,0:T(8,128)(2,1)} %get-tuple-element.149.d_all), calls=%async_computation.2 | async-start | bytes 1572864 | tf_op jit(solution)/shard_map/all_to_all | solution.py:924
  134.2 10.4 %shard_map.272 = (f32[2,128,1024]{2,1,0:T(8,128)}, bf16[2,128,1024]{2,1,0:T(8,128)(2,1)}, f32[2,256,512]{2,1,0:T(8,128)}, bf16[2,256,512]{2,1,0:T(8,128)(2,1)}) custom-call(s32[16]{0:T(128)} %concatenate.9.place, bf16[128,1024]{1,0:T(8,128)(2,1)} %get-tuple-element.152.normed.refs_0_, bf16[128,1024]{1,0:T(8,128)(2,1)} %copy-done.20, ...), custom_call_target="tpu_custom_call" | custom-call | bytes 8000 | tf_op jit(solution)/shard_map/pallas_call | solution.py:364
  145.0 2.1 collective-permute-start.26
  147.3 6.5 %shard_map.273 = (bf16[2,256,512]{2,1,0:T(8,128)(2,1)}, f32[2,256,512]{2,1,0:T(8,128)}) custom-call(s32[16]{0:T(128)} %concatenate.9.place, bf16[512,1024]{1,0:T(8,128)(2,1)} %get-tuple-element.172.h0, bf16[512,1024]{1,0:T(8,128)(2,1)} %get-tuple-element.173.h1, bf16[8,128,384]{2,1,0:T(8,128)(2,1)} %get-tuple-element.149.d_all, ...), custom_call_target="tpu_custom_call" | custom-call | bytes 4000 | tf_op jit(solution)/shard_map/pallas_call | solution.py:364
  154.1 2.3 %convert_add_fusion.1 = f32[2,128,1024]{2,1,0:T(8,128)} fusion(f32[2,128,1024]{2,1,0:T(8,128)S(1)} %copy-done.7, bf16[2,128,1024]{2,1,0:T(8,128)(2,1)} %collective-permute-done.30), kind=kLoop, calls=%fused_computation.7 | loop fusion | flops 524288 | bytes 2621440 | tf_op jit(solution)/shard_map/add | solution.py:900
  156.4 5.8 %collective-permute-done.26 = bf16[8,32,1152]{2,1,0:T(8,128)(2,1)} collective-permute-done((bf16[8,32,1152]{2,1,0:T(8,128)(2,1)S(1)}, bf16[8,32,1152]{2,1,0:T(8,128)(2,1)}, u32[]{:S(2)}, u32[]{:S(2)}) %collective-permute-start.26) | collective-permute-done | bytes 589856 | tf_op jit(solution)/shard_map/ppermute | solution.py:350
  162.2 1.2 slice_add_fusion
  163.4 0.7 slice.157
  164.1 1.7 collective-permute-start.27
  165.9 1.5 convert_add_fusion.2
  167.4 0.7 fusion.9
  168.2 1.5 collective-permute-start.31
  169.7 1.5 convert_add_fusion.3
  171.9 1.6 collective-permute-start.24
  173.4 6.9 %shard_map.271 = f32[128,1024]{1,0:T(8,128)} custom-call(s32[16]{0:T(128)} %concatenate.9.place, bf16[8,128,384]{2,1,0:T(8,128)(2,1)} %all-to-all-done.2.came, bf16[1024,3072]{1,0:T(8,128)(2,1)} %wv.1, bf16[128,1024]{1,0:T(8,128)(2,1)} %bitcast.68, f32[128,1024]{1,0:T(8,128)} %get-tuple-element.150.d_mid, f32[15,1024]{1,0:T(8,128)} %concatenate.10.vecs.refs_4_.refs_24_), custom_call_target="tpu_custom_call" | custom-call | bytes 5000 | tf_op jit(solution)/shard_map/pallas_call | solution.py:364
  180.4 1.0 slice_add_fusion.1
  182.0 1.2 collective-permute-done.22
  183.3 5.5 %collective-permute-done.24 = bf16[256,512]{1,0:T(8,128)(2,1)S(1)} collective-permute-done((bf16[256,512]{1,0:T(8,128)(2,1)S(1)}, bf16[256,512]{1,0:T(8,128)(2,1)S(1)}, u32[]{:S(2)}, u32[]{:S(2)}) %collective-permute-start.24) | collective-permute-done | bytes 262176 | tf_op jit(solution)/shard_map/ppermute | solution.py:350
  188.9 0.8 pad_maximum_fusion
  189.7 4.3 %all-to-all-start.3 = ((bf16[8,64,512]{2,1,0:T(8,128)(2,1)}), bf16[8,64,512]{2,1,0:T(8,128)(2,1)S(1)}, u32[]{:S(2)}, u32[]{:S(2)}) async-start(bf16[8,64,512]{2,1,0:T(8,128)(2,1)} %pad_maximum_fusion), calls=%async_computation.3 | async-start | bytes 1048576 | tf_op jit(solution)/shard_map/all_to_all | solution.py:984
  194.0 1.0 slice_add_fusion.2
  195.0 3.0 %collective-permute-start.29 = (bf16[1,32,1152]{2,1,0:T(8,128)(2,1)S(1)}, bf16[1,32,1152]{2,1,0:T(8,128)(2,1)S(1)}, u32[]{:S(2)}, u32[]{:S(2)}) collective-permute-start(bf16[1,32,1152]{2,1,0:T(8,128)(2,1)S(1)} %slice.159), channel_id=1, source_target_pairs={{0,4},{1,5},{2,6},{3,7},{4,0},{5,1},{6,2},{7,3},{8,12},{9,13},{10,... | collective-permute-start | bytes 221192 | tf_op jit(solution)/shard_map/ppermute | solution.py:350
  198.0 0.9 bitcast_add_fusion
  198.9 10.5 %collective-permute-done.29 = bf16[1,32,1152]{2,1,0:T(8,128)(2,1)S(1)} collective-permute-done((bf16[1,32,1152]{2,1,0:T(8,128)(2,1)S(1)}, bf16[1,32,1152]{2,1,0:T(8,128)(2,1)S(1)}, u32[]{:S(2)}, u32[]{:S(2)}) %collective-permute-start.29) | collective-permute-done | bytes 73760 | tf_op jit(solution)/shard_map/ppermute | solution.py:350
  211.2 0.8 copy-done.3
  212.0 2.7 %shard_map.274 = (f32[32,4096]{1,0:T(8,128)}, f32[32,3072]{1,0:T(8,128)}, f32[32,128]{1,0:T(8,128)}, f32[48,128]{1,0:T(8,128)}) custom-call(s32[16]{0:T(128)} %concatenate.9.place, bf16[8,64,512]{2,1,0:T(8,128)(2,1)} %copy-done.3), custom_call_target="tpu_custom_call" | custom-call | bytes 2000 | tf_op jit(solution)/shard_map/pallas_call | solution.py:364
  214.6 0.8 slice.85
  215.5 1.5 slice_reduce_fusion
  (118 shorter events, 12.1 us)
Async XLA Ops:
  0.6 21.2 %collective-permute-start = (bf16[128,1024]{1,0:T(8,128)(2,1)}, bf16[128,1024]{1,0:T(8,128)(2,1)S(1)}, u32[]{:S(2)}, u32[]{:S(2)}) collective-permute-start(bf16[128,1024]{1,0:T(8,128)(2,1)} %bitcast.62), channel_id=1, source_target_pairs={{0,4},{1,5},{2,6},{3,7},{4,0},{5,1},{6,2},{7,3},{8,12},{9,13},{10,... | collective-permute-start | bytes 786440 | tf_op jit(solution)/shard_map/ppermute | solution.py:350
  4.7 17.1 %collective-permute-start.1 = (bf16[128,1024]{1,0:T(8,128)(2,1)}, bf16[128,1024]{1,0:T(8,128)(2,1)S(1)}, u32[]{:S(2)}, u32[]{:S(2)}) collective-permute-start(bf16[128,1024]{1,0:T(8,128)(2,1)} %bitcast.63), channel_id=1, source_target_pairs={{0,1},{1,0},{2,3},{3,2},{4,5},{5,4},{6,7},{7,6},{8,9},{9,8},{10,11... | collective-permute-start | bytes 786440 | tf_op jit(solution)/shard_map/ppermute | solution.py:350
  6.3 15.6 %collective-permute-start.2 = (bf16[128,1024]{1,0:T(8,128)(2,1)}, bf16[128,1024]{1,0:T(8,128)(2,1)S(1)}, u32[]{:S(2)}, u32[]{:S(2)}) collective-permute-start(bf16[128,1024]{1,0:T(8,128)(2,1)} %bitcast.64), channel_id=1, source_target_pairs={{0,2},{1,3},{2,0},{3,1},{4,6},{5,7},{6,4},{7,5},{8,10},{9,11},{10,... | collective-permute-start | bytes 786440 | tf_op jit(solution)/shard_map/ppermute | solution.py:350
  7.8 16.2 %collective-permute-start.3 = (bf16[128,1024]{1,0:T(8,128)(2,1)}, bf16[128,1024]{1,0:T(8,128)(2,1)S(1)}, u32[]{:S(2)}, u32[]{:S(2)}) collective-permute-start(bf16[128,1024]{1,0:T(8,128)(2,1)} %bitcast.65), channel_id=1, source_target_pairs={{0,3},{1,2},{2,1},{3,0},{4,7},{5,6},{6,5},{7,4},{8,11},{9,10},{10,... | collective-permute-start | bytes 786440 | tf_op jit(solution)/shard_map/ppermute | solution.py:350
  21.9 22.9 %copy-start.12 = (bf16[128,1024]{1,0:T(8,128)(2,1)}, bf16[128,1024]{1,0:T(8,128)(2,1)S(1)}, u32[]{:S(2)}) copy-start(bf16[128,1024]{1,0:T(8,128)(2,1)S(1)} %collective-permute-done.refs_0_) | copy-start | bytes 786436
  21.9 18.5 %copy-start.16 = (bf16[128,1024]{1,0:T(8,128)(2,1)}, bf16[128,1024]{1,0:T(8,128)(2,1)S(1)}, u32[]{:S(2)}) copy-start(bf16[128,1024]{1,0:T(8,128)(2,1)S(1)} %collective-permute-done.1.refs_1_) | copy-start | bytes 786436
  21.9 18.5 %copy-start.17 = (bf16[128,1024]{1,0:T(8,128)(2,1)}, bf16[128,1024]{1,0:T(8,128)(2,1)S(1)}, u32[]{:S(2)}) copy-start(bf16[128,1024]{1,0:T(8,128)(2,1)S(1)} %collective-permute-done.2.refs_2_) | copy-start | bytes 786436
  24.0 16.4 %copy-start.18 = (bf16[128,1024]{1,0:T(8,128)(2,1)}, bf16[128,1024]{1,0:T(8,128)(2,1)S(1)}, u32[]{:S(2)}) copy-start(bf16[128,1024]{1,0:T(8,128)(2,1)S(1)} %collective-permute-done.3.refs_3_) | copy-start | bytes 786436
  24.0 8.1 %collective-permute-start.4 = (bf16[128,1024]{1,0:T(8,128)(2,1)S(1)}, bf16[128,1024]{1,0:T(8,128)(2,1)S(1)}, u32[]{:S(2)}, u32[]{:S(2)}) collective-permute-start(bf16[128,1024]{1,0:T(8,128)(2,1)S(1)} %collective-permute-done.refs_0_), channel_id=1, source_target_pairs={{0,1},{1,0},{2,3},{3,2},{4,5},{5,4},{6,7},{7,6},{8,9},{9,8},{10,11... | collective-permute-start | bytes 786440 | tf_op jit(solution)/shard_map/ppermute | solution.py:350
  25.5 14.9 %collective-permute-start.5 = (bf16[128,1024]{1,0:T(8,128)(2,1)S(1)}, bf16[128,1024]{1,0:T(8,128)(2,1)S(1)}, u32[]{:S(2)}, u32[]{:S(2)}) collective-permute-start(bf16[128,1024]{1,0:T(8,128)(2,1)S(1)} %collective-permute-done.refs_0_), channel_id=1, source_target_pairs={{0,2},{1,3},{2,0},{3,1},{4,6},{5,7},{6,4},{7,5},{8,10},{9,11},{10,... | collective-permute-start | bytes 786440 | tf_op jit(solution)/shard_map/ppermute | solution.py:350
  25.7 20.2 %collective-permute-start.6 = (bf16[128,1024]{1,0:T(8,128)(2,1)S(1)}, bf16[128,1024]{1,0:T(8,128)(2,1)S(1)}, u32[]{:S(2)}, u32[]{:S(2)}) collective-permute-start(bf16[128,1024]{1,0:T(8,128)(2,1)S(1)} %collective-permute-done.refs_0_), channel_id=1, source_target_pairs={{0,3},{1,2},{2,1},{3,0},{4,7},{5,6},{6,5},{7,4},{8,11},{9,10},{10,... | collective-permute-start | bytes 786440 | tf_op jit(solution)/shard_map/ppermute | solution.py:350
  27.5 34.3 %collective-permute-start.10 = (bf16[128,1024]{1,0:T(8,128)(2,1)}, bf16[128,1024]{1,0:T(8,128)(2,1)S(1)}, u32[]{:S(2)}, u32[]{:S(2)}) collective-permute-start(bf16[128,1024]{1,0:T(8,128)(2,1)} %bitcast.55), channel_id=1, source_target_pairs={{0,3},{1,2},{2,1},{3,0},{4,7},{5,6},{6,5},{7,4},{8,11},{9,10},{10,... | collective-permute-start | bytes 786440 | tf_op jit(solution)/shard_map/ppermute | solution.py:350
  28.7 33.2 %collective-permute-start.7 = (bf16[128,1024]{1,0:T(8,128)(2,1)}, bf16[128,1024]{1,0:T(8,128)(2,1)S(1)}, u32[]{:S(2)}, u32[]{:S(2)}) collective-permute-start(bf16[128,1024]{1,0:T(8,128)(2,1)} %bitcast.56), channel_id=1, source_target_pairs={{0,4},{1,5},{2,6},{3,7},{4,0},{5,1},{6,2},{7,3},{8,12},{9,13},{10,... | collective-permute-start | bytes 786440 | tf_op jit(solution)/shard_map/ppermute | solution.py:350
  32.1 12.7 %copy-start.26 = (bf16[128,1024]{1,0:T(8,128)(2,1)}, bf16[128,1024]{1,0:T(8,128)(2,1)S(1)}, u32[]{:S(2)}) copy-start(bf16[128,1024]{1,0:T(8,128)(2,1)S(1)} %collective-permute-done.4.refs_1_) | copy-start | bytes 786436
  32.1 29.8 %collective-permute-start.8 = (bf16[128,1024]{1,0:T(8,128)(2,1)}, bf16[128,1024]{1,0:T(8,128)(2,1)S(1)}, u32[]{:S(2)}, u32[]{:S(2)}) collective-permute-start(bf16[128,1024]{1,0:T(8,128)(2,1)} %bitcast.57), channel_id=1, source_target_pairs={{0,1},{1,0},{2,3},{3,2},{4,5},{5,4},{6,7},{7,6},{8,9},{9,8},{10,11... | collective-permute-start | bytes 786440 | tf_op jit(solution)/shard_map/ppermute | solution.py:350
  40.4 4.4 %copy-start.27 = (bf16[128,1024]{1,0:T(8,128)(2,1)}, bf16[128,1024]{1,0:T(8,128)(2,1)S(1)}, u32[]{:S(2)}) copy-start(bf16[128,1024]{1,0:T(8,128)(2,1)S(1)} %collective-permute-done.5.refs_2_) | copy-start | bytes 786436
  40.4 21.6 %collective-permute-start.9 = (bf16[128,1024]{1,0:T(8,128)(2,1)}, bf16[128,1024]{1,0:T(8,128)(2,1)S(1)}, u32[]{:S(2)}, u32[]{:S(2)}) collective-permute-start(bf16[128,1024]{1,0:T(8,128)(2,1)} %bitcast.58), channel_id=1, source_target_pairs={{0,2},{1,3},{2,0},{3,1},{4,6},{5,7},{6,4},{7,5},{8,10},{9,11},{10,... | collective-permute-start | bytes 786440 | tf_op jit(solution)/shard_map/ppermute | solution.py:350
  46.0 0.7 copy-start.28
  61.9 15.9 %copy-start.8 = (bf16[128,1024]{1,0:T(8,128)(2,1)}, bf16[128,1024]{1,0:T(8,128)(2,1)S(1)}, u32[]{:S(2)}) copy-start(bf16[128,1024]{1,0:T(8,128)(2,1)S(1)} %collective-permute-done.10.refs_11_) | copy-start | bytes 786436
  61.9 15.9 %copy-start.9 = (bf16[128,1024]{1,0:T(8,128)(2,1)}, bf16[128,1024]{1,0:T(8,128)(2,1)S(1)}, u32[]{:S(2)}) copy-start(bf16[128,1024]{1,0:T(8,128)(2,1)S(1)} %collective-permute-done.7.refs_12_) | copy-start | bytes 786436
  61.9 15.8 %copy-start.10 = (bf16[128,1024]{1,0:T(8,128)(2,1)}, bf16[128,1024]{1,0:T(8,128)(2,1)S(1)}, u32[]{:S(2)}) copy-start(bf16[128,1024]{1,0:T(8,128)(2,1)S(1)} %collective-permute-done.8.refs_9_) | copy-start | bytes 786436
  61.9 15.8 %copy-start.11 = (bf16[128,1024]{1,0:T(8,128)(2,1)}, bf16[128,1024]{1,0:T(8,128)(2,1)S(1)}, u32[]{:S(2)}) copy-start(bf16[128,1024]{1,0:T(8,128)(2,1)S(1)} %collective-permute-done.9.refs_10_) | copy-start | bytes 786436
  61.9 15.8 %all-to-all-start = ((bf16[8,128,128]{2,1,0:T(8,128)(2,1)}), bf16[8,128,128]{2,1,0:T(8,128)(2,1)S(1)}, u32[]{:S(2)}, u32[]{:S(2)}) async-start(bf16[8,128,128]{2,1,0:T(8,128)(2,1)} %get-tuple-element.124), calls=%async_computation | async-start | bytes 524288 | tf_op jit(solution)/shard_map/all_to_all | solution.py:845
  66.6 15.7 %collective-permute-start.11 = (bf16[128,1024]{1,0:T(8,128)(2,1)S(1)}, bf16[128,1024]{1,0:T(8,128)(2,1)S(1)}, u32[]{:S(2)}, u32[]{:S(2)}) collective-permute-start(bf16[128,1024]{1,0:T(8,128)(2,1)S(1)} %collective-permute-done.7.refs_12_), channel_id=1, source_target_pairs={{0,1},{1,0},{2,3},{3,2},{4,5},{5,4},{6,7},{7,6},{8,9},{9,8},{10,11... | collective-permute-start | bytes 786440 | tf_op jit(solution)/shard_map/ppermute | solution.py:350
  68.6 13.7 %collective-permute-start.12 = (bf16[128,1024]{1,0:T(8,128)(2,1)S(1)}, bf16[128,1024]{1,0:T(8,128)(2,1)S(1)}, u32[]{:S(2)}, u32[]{:S(2)}) collective-permute-start(bf16[128,1024]{1,0:T(8,128)(2,1)S(1)} %collective-permute-done.7.refs_12_), channel_id=1, source_target_pairs={{0,2},{1,3},{2,0},{3,1},{4,6},{5,7},{6,4},{7,5},{8,10},{9,11},{10,... | collective-permute-start | bytes 786440 | tf_op jit(solution)/shard_map/ppermute | solution.py:350
  70.1 12.3 %collective-permute-start.13 = (bf16[128,1024]{1,0:T(8,128)(2,1)S(1)}, bf16[128,1024]{1,0:T(8,128)(2,1)S(1)}, u32[]{:S(2)}, u32[]{:S(2)}) collective-permute-start(bf16[128,1024]{1,0:T(8,128)(2,1)S(1)} %collective-permute-done.7.refs_12_), channel_id=1, source_target_pairs={{0,3},{1,2},{2,1},{3,0},{4,7},{5,6},{6,5},{7,4},{8,11},{9,10},{10,... | collective-permute-start | bytes 786440 | tf_op jit(solution)/shard_map/ppermute | solution.py:350
  77.8 0.7 copy-start.6
  82.4 21.2 %copy-start.13 = (bf16[128,1024]{1,0:T(8,128)(2,1)}, bf16[128,1024]{1,0:T(8,128)(2,1)S(1)}, u32[]{:S(2)}) copy-start(bf16[128,1024]{1,0:T(8,128)(2,1)S(1)} %collective-permute-done.11.refs_13_) | copy-start | bytes 786436
  82.4 21.2 %copy-start.14 = (bf16[128,1024]{1,0:T(8,128)(2,1)}, bf16[128,1024]{1,0:T(8,128)(2,1)S(1)}, u32[]{:S(2)}) copy-start(bf16[128,1024]{1,0:T(8,128)(2,1)S(1)} %collective-permute-done.12.refs_14_) | copy-start | bytes 786436
  82.4 6.5 %copy-start.15 = (bf16[128,1024]{1,0:T(8,128)(2,1)}, bf16[128,1024]{1,0:T(8,128)(2,1)S(1)}, u32[]{:S(2)}) copy-start(bf16[128,1024]{1,0:T(8,128)(2,1)S(1)} %collective-permute-done.13.refs_15_) | copy-start | bytes 786436
  82.4 21.2 %collective-permute-start.14 = (bf16[128,1024]{1,0:T(8,128)(2,1)}, bf16[128,1024]{1,0:T(8,128)(2,1)S(1)}, u32[]{:S(2)}, u32[]{:S(2)}) collective-permute-start(bf16[128,1024]{1,0:T(8,128)(2,1)} %get-tuple-element.152.normed.refs_0_), channel_id=1, source_target_pairs={{0,4},{1,5},{2,6},{3,7},{4,0},{5,1},{6,2},{7,3},{8,12},{9,13},{10,... | collective-permute-start | bytes 786440 | tf_op jit(solution)/shard_map/ppermute | solution.py:350
  85.4 18.3 %collective-permute-start.15 = (bf16[128,1024]{1,0:T(8,128)(2,1)}, bf16[128,1024]{1,0:T(8,128)(2,1)S(1)}, u32[]{:S(2)}, u32[]{:S(2)}) collective-permute-start(bf16[128,1024]{1,0:T(8,128)(2,1)} %get-tuple-element.152.normed.refs_0_), channel_id=1, source_target_pairs={{0,1},{1,0},{2,3},{3,2},{4,5},{5,4},{6,7},{7,6},{8,9},{9,8},{10,11... | collective-permute-start | bytes 786440 | tf_op jit(solution)/shard_map/ppermute | solution.py:350
  86.8 16.8 %collective-permute-start.16 = (bf16[128,1024]{1,0:T(8,128)(2,1)}, bf16[128,1024]{1,0:T(8,128)(2,1)S(1)}, u32[]{:S(2)}, u32[]{:S(2)}) collective-permute-start(bf16[128,1024]{1,0:T(8,128)(2,1)} %get-tuple-element.152.normed.refs_0_), channel_id=1, source_target_pairs={{0,2},{1,3},{2,0},{3,1},{4,6},{5,7},{6,4},{7,5},{8,10},{9,11},{10,... | collective-permute-start | bytes 786440 | tf_op jit(solution)/shard_map/ppermute | solution.py:350
  88.3 15.4 %collective-permute-start.17 = (bf16[128,1024]{1,0:T(8,128)(2,1)}, bf16[128,1024]{1,0:T(8,128)(2,1)S(1)}, u32[]{:S(2)}, u32[]{:S(2)}) collective-permute-start(bf16[128,1024]{1,0:T(8,128)(2,1)} %get-tuple-element.152.normed.refs_0_), channel_id=1, source_target_pairs={{0,3},{1,2},{2,1},{3,0},{4,7},{5,6},{6,5},{7,4},{8,11},{9,10},{10,... | collective-permute-start | bytes 786440 | tf_op jit(solution)/shard_map/ppermute | solution.py:350
  88.9 18.6 %copy-start.2 = (f32[128,1024]{1,0:T(8,128)S(1)}, f32[128,1024]{1,0:T(8,128)}, u32[]{:S(2)}) copy-start(f32[128,1024]{1,0:T(8,128)} %get-tuple-element.128.middle) | copy-start | bytes 1572868
  103.6 13.1 %copy-start.19 = (bf16[128,1024]{1,0:T(8,128)(2,1)}, bf16[128,1024]{1,0:T(8,128)(2,1)S(1)}, u32[]{:S(2)}) copy-start(bf16[128,1024]{1,0:T(8,128)(2,1)S(1)} %collective-permute-done.14.refs_4_) | copy-start | bytes 786436
  103.6 9.5 %copy-start.20 = (bf16[128,1024]{1,0:T(8,128)(2,1)}, bf16[128,1024]{1,0:T(8,128)(2,1)S(1)}, u32[]{:S(2)}) copy-start(bf16[128,1024]{1,0:T(8,128)(2,1)S(1)} %collective-permute-done.15.refs_1_) | copy-start | bytes 786436
  103.7 9.5 %copy-start.21 = (bf16[128,1024]{1,0:T(8,128)(2,1)}, bf16[128,1024]{1,0:T(8,128)(2,1)S(1)}, u32[]{:S(2)}) copy-start(bf16[128,1024]{1,0:T(8,128)(2,1)S(1)} %collective-permute-done.16.refs_2_) | copy-start | bytes 786436
  103.7 9.4 %copy-start.22 = (bf16[128,1024]{1,0:T(8,128)(2,1)}, bf16[128,1024]{1,0:T(8,128)(2,1)S(1)}, u32[]{:S(2)}) copy-start(bf16[128,1024]{1,0:T(8,128)(2,1)S(1)} %collective-permute-done.17.refs_3_) | copy-start | bytes 786436
  103.7 41.0 %collective-permute-start.25 = (bf16[16,32,1152]{2,1,0:T(8,128)(2,1)}, bf16[16,32,1152]{2,1,0:T(8,128)(2,1)S(1)}, u32[]{:S(2)}, u32[]{:S(2)}) collective-permute-start(bf16[16,32,1152]{2,1,0:T(8,128)(2,1)} %get-tuple-element.185), channel_id=1, source_target_pairs={{0,8},{1,9},{2,10},{3,11},{4,12},{5,13},{6,14},{7,15},{8,0},{9,1},... | collective-permute-start | bytes 3538952 | tf_op jit(solution)/shard_map/ppermute | solution.py:350
  103.8 13.3 %all-to-all-start.1 = ((bf16[8,128,128]{2,1,0:T(8,128)(2,1)}), bf16[8,128,128]{2,1,0:T(8,128)(2,1)S(1)}, u32[]{:S(2)}, u32[]{:S(2)}) async-start(bf16[8,128,128]{2,1,0:T(8,128)(2,1)} %get-tuple-element.143), calls=%async_computation.1 | async-start | bytes 524288 | tf_op jit(solution)/shard_map/all_to_all | solution.py:893
  113.1 14.5 %collective-permute-start.18 = (bf16[128,1024]{1,0:T(8,128)(2,1)S(1)}, bf16[128,1024]{1,0:T(8,128)(2,1)S(1)}, u32[]{:S(2)}, u32[]{:S(2)}) collective-permute-start(bf16[128,1024]{1,0:T(8,128)(2,1)S(1)} %collective-permute-done.14.refs_4_), channel_id=1, source_target_pairs={{0,1},{1,0},{2,3},{3,2},{4,5},{5,4},{6,7},{7,6},{8,9},{9,8},{10,11... | collective-permute-start | bytes 786440 | tf_op jit(solution)/shard_map/ppermute | solution.py:350
  115.2 12.4 %collective-permute-start.19 = (bf16[128,1024]{1,0:T(8,128)(2,1)S(1)}, bf16[128,1024]{1,0:T(8,128)(2,1)S(1)}, u32[]{:S(2)}, u32[]{:S(2)}) collective-permute-start(bf16[128,1024]{1,0:T(8,128)(2,1)S(1)} %collective-permute-done.14.refs_4_), channel_id=1, source_target_pairs={{0,2},{1,3},{2,0},{3,1},{4,6},{5,7},{6,4},{7,5},{8,10},{9,11},{10,... | collective-permute-start | bytes 786440 | tf_op jit(solution)/shard_map/ppermute | solution.py:350
  116.7 12.2 %collective-permute-start.20 = (bf16[128,1024]{1,0:T(8,128)(2,1)S(1)}, bf16[128,1024]{1,0:T(8,128)(2,1)S(1)}, u32[]{:S(2)}, u32[]{:S(2)}) collective-permute-start(bf16[128,1024]{1,0:T(8,128)(2,1)S(1)} %collective-permute-done.14.refs_4_), channel_id=1, source_target_pairs={{0,3},{1,2},{2,1},{3,0},{4,7},{5,6},{6,5},{7,4},{8,11},{9,10},{10,... | collective-permute-start | bytes 786440 | tf_op jit(solution)/shard_map/ppermute | solution.py:350
  127.6 6.5 %copy-start.23 = (bf16[128,1024]{1,0:T(8,128)(2,1)}, bf16[128,1024]{1,0:T(8,128)(2,1)S(1)}, u32[]{:S(2)}) copy-start(bf16[128,1024]{1,0:T(8,128)(2,1)S(1)} %collective-permute-done.18.refs_5_) | copy-start | bytes 786436
  127.6 6.5 %copy-start.24 = (bf16[128,1024]{1,0:T(8,128)(2,1)}, bf16[128,1024]{1,0:T(8,128)(2,1)S(1)}, u32[]{:S(2)}) copy-start(bf16[128,1024]{1,0:T(8,128)(2,1)S(1)} %collective-permute-done.19.refs_6_) | copy-start | bytes 786436
  128.8 5.3 %copy-start.25 = (bf16[128,1024]{1,0:T(8,128)(2,1)}, bf16[128,1024]{1,0:T(8,128)(2,1)S(1)}, u32[]{:S(2)}) copy-start(bf16[128,1024]{1,0:T(8,128)(2,1)S(1)} %collective-permute-done.20.refs_7_) | copy-start | bytes 786436
  128.8 37.0 %all-to-all-start.2 = ((bf16[8,128,384]{2,1,0:T(8,128)(2,1)}), bf16[8,128,384]{2,1,0:T(8,128)(2,1)}, u32[]{:S(2)}, u32[]{:S(2)}) async-start(bf16[8,128,384]{2,1,0:T(8,128)(2,1)} %get-tuple-element.149.d_all), calls=%async_computation.2 | async-start | bytes 1572864 | tf_op jit(solution)/shard_map/all_to_all | solution.py:924
  134.2 10.5 %copy-start.1 = (f32[16,32,1152]{2,1,0:T(8,128)S(1)}, f32[16,32,1152]{2,1,0:T(8,128)}, u32[]{:S(2)}) copy-start(f32[16,32,1152]{2,1,0:T(8,128)} %get-tuple-element.184) | copy-start | bytes 7077892
  144.6 9.5 %collective-permute-start.30 = (bf16[2,128,1024]{2,1,0:T(8,128)(2,1)}, bf16[2,128,1024]{2,1,0:T(8,128)(2,1)}, u32[]{:S(2)}, u32[]{:S(2)}) collective-permute-start(bf16[2,128,1024]{2,1,0:T(8,128)(2,1)} %get-tuple-element.188), channel_id=1, source_target_pairs={{0,8},{1,9},{2,10},{3,11},{4,12},{5,13},{6,14},{7,15},{8,0},{9,1},... | collective-permute-start | bytes 1572872 | tf_op jit(solution)/shard_map/ppermute | solution.py:350
  145.0 17.2 %collective-permute-start.26 = (bf16[8,32,1152]{2,1,0:T(8,128)(2,1)S(1)}, bf16[8,32,1152]{2,1,0:T(8,128)(2,1)}, u32[]{:S(2)}, u32[]{:S(2)}) collective-permute-start(bf16[8,32,1152]{2,1,0:T(8,128)(2,1)S(1)} %slice.156), channel_id=1, source_target_pairs={{0,1},{1,0},{2,3},{3,2},{4,5},{5,4},{6,7},{7,6},{8,9},{9,8},{10,11... | collective-permute-start | bytes 1769480 | tf_op jit(solution)/shard_map/ppermute | solution.py:350
  147.1 22.6 %collective-permute-start.21 = (bf16[2,256,512]{2,1,0:T(8,128)(2,1)}, bf16[2,256,512]{2,1,0:T(8,128)(2,1)}, u32[]{:S(2)}, u32[]{:S(2)}) collective-permute-start(bf16[2,256,512]{2,1,0:T(8,128)(2,1)} %get-tuple-element.170), channel_id=1, source_target_pairs={{0,8},{1,9},{2,10},{3,11},{4,12},{5,13},{6,14},{7,15},{8,0},{9,1},... | collective-permute-start | bytes 1572872 | tf_op jit(solution)/shard_map/ppermute | solution.py:350
  147.3 6.8 %copy-start.7 = (f32[2,128,1024]{2,1,0:T(8,128)S(1)}, f32[2,128,1024]{2,1,0:T(8,128)}, u32[]{:S(2)}) copy-start(f32[2,128,1024]{2,1,0:T(8,128)} %get-tuple-element.187) | copy-start | bytes 3145732
  153.7 12.1 %collective-permute-start.23 = (bf16[2,256,512]{2,1,0:T(8,128)(2,1)}, bf16[2,256,512]{2,1,0:T(8,128)(2,1)}, u32[]{:S(2)}, u32[]{:S(2)}) collective-permute-start(bf16[2,256,512]{2,1,0:T(8,128)(2,1)} %get-tuple-element.178), channel_id=1, source_target_pairs={{0,8},{1,9},{2,10},{3,11},{4,12},{5,13},{6,14},{7,15},{8,0},{9,1},... | collective-permute-start | bytes 1572872 | tf_op jit(solution)/shard_map/ppermute | solution.py:350
  163.4 4.0 %copy-start = (f32[2,128,1024]{2,1,0:T(8,128)S(1)}, f32[2,128,1024]{2,1,0:T(8,128)}, u32[]{:S(2)}) copy-start(f32[2,128,1024]{2,1,0:T(8,128)} %convert_add_fusion.1) | copy-start | bytes 3145732
  164.1 16.2 %collective-permute-start.27 = (bf16[4,32,1152]{2,1,0:T(8,128)(2,1)}, bf16[4,32,1152]{2,1,0:T(8,128)(2,1)}, u32[]{:S(2)}, u32[]{:S(2)}) collective-permute-start(bf16[4,32,1152]{2,1,0:T(8,128)(2,1)} %slice.157), channel_id=1, source_target_pairs={{0,2},{1,3},{2,0},{3,1},{4,6},{5,7},{6,4},{7,5},{8,10},{9,11},{10,... | collective-permute-start | bytes 884744 | tf_op jit(solution)/shard_map/ppermute | solution.py:350
  168.2 29.9 %collective-permute-start.31 = (bf16[128,1024]{1,0:T(8,128)(2,1)}, bf16[128,1024]{1,0:T(8,128)(2,1)S(1)}, u32[]{:S(2)}, u32[]{:S(2)}) collective-permute-start(bf16[128,1024]{1,0:T(8,128)(2,1)} %fusion.9), channel_id=1, source_target_pairs={{0,16},{1,17},{2,18},{3,19},{4,20},{5,21},{6,22},{7,23},{8,24},{9,... | collective-permute-start | bytes 786440 | tf_op jit(solution)/shard_map/ppermute | solution.py:350
  171.2 12.0 %collective-permute-start.22 = (bf16[256,512]{1,0:T(8,128)(2,1)S(1)}, bf16[256,512]{1,0:T(8,128)(2,1)S(1)}, u32[]{:S(2)}, u32[]{:S(2)}) collective-permute-start(bf16[256,512]{1,0:T(8,128)(2,1)S(1)} %fusion.7), channel_id=1, source_target_pairs={{0,16},{1,17},{2,18},{3,19},{4,20},{5,21},{6,22},{7,23},{8,24},{9,... | collective-permute-start | bytes 786440 | tf_op jit(solution)/shard_map/ppermute | solution.py:350
  171.9 16.9 %collective-permute-start.24 = (bf16[256,512]{1,0:T(8,128)(2,1)S(1)}, bf16[256,512]{1,0:T(8,128)(2,1)S(1)}, u32[]{:S(2)}, u32[]{:S(2)}) collective-permute-start(bf16[256,512]{1,0:T(8,128)(2,1)S(1)} %fusion.8), channel_id=1, source_target_pairs={{0,16},{1,17},{2,18},{3,19},{4,20},{5,21},{6,22},{7,23},{8,24},{9,... | collective-permute-start | bytes 786440 | tf_op jit(solution)/shard_map/ppermute | solution.py:350
  181.4 7.5 %copy-start.4 = (f32[4,32,1152]{2,1,0:T(8,128)}, f32[4,32,1152]{2,1,0:T(8,128)S(1)}, u32[]{:S(2)}) copy-start(f32[4,32,1152]{2,1,0:T(8,128)S(1)} %slice_add_fusion.1) | copy-start | bytes 1769476
  181.4 12.6 %collective-permute-start.28 = (bf16[2,32,1152]{2,1,0:T(8,128)(2,1)S(1)}, bf16[2,32,1152]{2,1,0:T(8,128)(2,1)S(1)}, u32[]{:S(2)}, u32[]{:S(2)}) collective-permute-start(bf16[2,32,1152]{2,1,0:T(8,128)(2,1)S(1)} %slice.158), channel_id=1, source_target_pairs={{0,16},{1,17},{2,18},{3,19},{4,20},{5,21},{6,22},{7,23},{8,24},{9,... | collective-permute-start | bytes 442376 | tf_op jit(solution)/shard_map/ppermute | solution.py:350
  189.7 21.4 %all-to-all-start.3 = ((bf16[8,64,512]{2,1,0:T(8,128)(2,1)}), bf16[8,64,512]{2,1,0:T(8,128)(2,1)S(1)}, u32[]{:S(2)}, u32[]{:S(2)}) async-start(bf16[8,64,512]{2,1,0:T(8,128)(2,1)} %pad_maximum_fusion), calls=%async_computation.3 | async-start | bytes 1048576 | tf_op jit(solution)/shard_map/all_to_all | solution.py:984
  195.0 14.3 %collective-permute-start.29 = (bf16[1,32,1152]{2,1,0:T(8,128)(2,1)S(1)}, bf16[1,32,1152]{2,1,0:T(8,128)(2,1)S(1)}, u32[]{:S(2)}, u32[]{:S(2)}) collective-permute-start(bf16[1,32,1152]{2,1,0:T(8,128)(2,1)S(1)} %slice.159), channel_id=1, source_target_pairs={{0,4},{1,5},{2,6},{3,7},{4,0},{5,1},{6,2},{7,3},{8,12},{9,13},{10,... | collective-permute-start | bytes 221192 | tf_op jit(solution)/shard_map/ppermute | solution.py:350
  211.2 0.8 copy-start.3
  (1 other events, 0.7 us)

commit v3 on v2

--- a/solution.py
+++ b/solution.py
@@ -337,8 +337,10 @@
 ROW = ("zh", "zl", "y")
 GELU_A = 0.7978845608028654
 GELU_B = 0.044715
-VMEM_MIB = 56
-COST = 1e3
+VMEM_MIB = 32
+PIN = 400000
+LOW_PIN = 200000
+NO_PIN = 1 << 30
 
 
 def mm(left, right):
@@ -359,8 +361,7 @@
     return jax.ShapeDtypeStruct(shape, dtype)
 
 
-def call(body, grid, in_specs, out_specs, out_shape, scratch, micros, scalars, args):
-    nbytes = int(micros * COST)
+def call(body, grid, in_specs, out_specs, out_shape, scratch, pin, scalars, args):
     return pl.pallas_call(
         body,
         grid_spec=pltpu.PrefetchScalarGridSpec(
@@ -370,16 +371,24 @@
             out_specs=out_specs,
             scratch_shapes=scratch,
         ),
-        out_shape=out_shape,
+        out_shape=[pltpu.HBM(o.shape, o.dtype) if big(o, pin) else o for o in out_shape],
         compiler_params=pltpu.CompilerParams(vmem_limit_bytes=VMEM_MIB << 20),
-        cost_estimate=pl.CostEstimate(flops=0, bytes_accessed=nbytes, transcendentals=0),
-    )(scalars, *args)
-
-
-def one_step(body, outs, scratch, micros, scalars, args):
+        cost_estimate=pl.CostEstimate(flops=0, bytes_accessed=1024, transcendentals=0),
+    )(scalars, *(pinned(v, pin) for v in args))
+
+
+def big(v, pin):
+    return math.prod(v.shape) * v.dtype.itemsize >= pin
+
+
+def pinned(v, pin):
+    return pltpu.with_memory_space_constraint(v, pltpu.HBM) if big(v, pin) else v
+
+
+def one_step(body, outs, scratch, pin, scalars, args):
     return call(
         body, (1,), [whole(v.shape) for v in args], [whole(o.shape) for o in outs], outs, scratch,
-        micros, scalars, args,
+        pin, scalars, args,
     )
 
 
@@ -489,9 +498,6 @@
 def proj_grad(place, att, d_b, vectors, send, keep):
     grad = outer_sum(att, d_b)
     row = lax.broadcasted_iota(jnp.int32, (32, 128), 0)
-    rel_y = place[0] & 1
-    rel_zl = (place[0] >> 1) & 1
-    rel_zh = place[0] >> 2
     for owner in range(32):
         x, core, k = owner // 16, (owner // 8) % 2, owner % 8
         rows = grad[32 * owner : 32 * owner + 32]
@@ -502,19 +508,14 @@
         group = 2 * x + core
         last = vectors[4 + group : 5 + group, 128 * k : 128 * k + 128]
         extra = jnp.where(row == 4, last, extra)
-        slot = ((rel_y ^ (k & 1)) * 8 + (rel_zl ^ ((k >> 1) & 1)) * 4) + (
-            (place[1] ^ x) * 2 + (rel_zh ^ (k >> 2))
-        )
-
-        @pl.when(core == place[2])
-        def _():
-            keep[slot, :, :1024] = rows
-            keep[slot, :, 1024:] = extra
-
-        @pl.when(core != place[2])
-        def _():
-            send[slot, :, :1024] = rows.astype(BF)
-            send[slot, :, 1024:] = extra.astype(BF)
+        rel = place[0] ^ k
+        slot = (rel & 1) * 4 + (rel & 2) + (rel >> 2)
+        for side, out in ((core == place[2], keep), (core != place[2], send)):
+
+            @pl.when(side)
+            def _():
+                out[place[1] ^ x, slot, :, :1024] = rows.astype(BF)
+                out[place[1] ^ x, slot, :, 1024:] = extra.astype(BF)
 
 
 def mlp_body(
@@ -578,7 +579,7 @@
     for g in range(4):
         rows = grad_down[128 * g : 128 * g + 128]
         if g < 2:
-            down_keep[g] = rows
+            down_keep[g] = rows.astype(BF)
         else:
             down_send[g - 2] = rows.astype(BF)
     d_hidden = (times_transposed(c, d_all[...]) * slope).astype(BF)
@@ -591,7 +592,7 @@
         first = (place[1] ^ rx) * 512
         keep = pl.multiple_of(first + place[2] * 256, 256)
         send = pl.multiple_of(first + (1 - place[2]) * 256, 256)
-        up_keep[rx] = grad[pl.ds(keep, 256), :]
+        up_keep[rx] = grad[pl.ds(keep, 256), :].astype(BF)
         up_send[rx] = grad[pl.ds(send, 256), :].astype(BF)
 
 
@@ -685,12 +686,33 @@
 
     @pl.when(step >= 2)
     def _():
-        keep[0, :, :384] = grad
-        keep[0, :, 384:] = extra
+        keep[0, :, :384] = grad.astype(BF)
+        keep[0, :, 384:] = extra.astype(BF)
+
+
+def pair_body(place, keep, came, left, send):
+    half = left.shape[0]
+    total = (keep[...].astype(F32) + came[...].astype(F32)).astype(BF)
+    left[...] = total[:half]
+    send[...] = total[half:]
+
+
+def merge_body(place, *refs):
+    keeps, cames = refs[0:6:2], refs[1:6:2]
+    proj_left, proj_came, left, send, down_left, down_send, proj_keep, proj_send = refs[6:]
+    proj_keep[...] = (proj_left[:1].astype(F32) + proj_came[:1].astype(F32)).astype(BF)
+    proj_send[...] = (proj_left[1:].astype(F32) + proj_came[1:].astype(F32)).astype(BF)
+    for side, low, down in ((0, left, down_left), (1, send, down_send)):
+        for m in range(2):
+            total = keeps[m][side].astype(F32) + cames[m][side].astype(F32)
+            for k in range(8):
+                low[k, 32 * m : 32 * m + 32, :] = total[32 * k : 32 * k + 32].astype(BF)
+        down[...] = (keeps[2][side].astype(F32) + cames[2][side].astype(F32)).astype(BF)
 
 
 def finish_body(place, came, grad_up, grad_qkv, sums, bias):
     total = jnp.zeros((32, 128), F32)
+    low = lax.broadcasted_iota(jnp.int32, (1, 128), 1) < 64
     for k in range(8):
         for g in range(4):
             lanes = slice(1024 * g + 128 * k, 1024 * g + 128 * k + 128)
@@ -699,8 +721,11 @@
                 grad_qkv[:, lanes] = came[k, 32:, 128 * g : 128 * g + 128].astype(F32)
         extra = came[k, 32:, 384:].astype(F32)
         total = total + extra
-        bias[6 * k : 6 * k + 6, :] = extra[:6]
-    sums[...] = total
+        for p in range(3):
+            left = pltpu.roll(extra[2 * p : 2 * p + 1], 64, 1)
+            both = jnp.where(low, left, extra[2 * p + 1 : 2 * p + 2])
+            bias[p : p + 1, 128 * k : 128 * k + 128] = both
+    sums[...] = total.T[:8]
 
 
 def last_body(place, came, w, tok, d_mid, vecs, out, acc):
@@ -795,15 +820,12 @@
         [arr((1024, 128), F32), arr((1024, 128), F32), arr((1024, 128), F32), arr((8, 1024), F32),
          arr((1024, 8), F32)],
         [],
-        3,
+        PIN,
         place,
         (jnp.asarray(frequency_rows()), vecs),
     )
     far_tok, cos_tab, *near = lax.optimization_barrier((far_tok, cos_tab, *near))
     far = spread_four(far_tok)
-    cot_here, *_ = lax.optimization_barrier((cot, far_tok))
-    far_cot = swap_over(cot_here, "zh")
-    cots = spread_four(cot_here)
 
     def table_half(part):
         return pl.BlockSpec((512, 128), lambda i, s: (part, 0))
@@ -818,11 +840,25 @@
         specs += [table_half(part), table_half(part)] + [whole(v.shape) for v in more]
         return call(
             body, (1,), specs, [whole(o.shape) for o in outs], outs,
-            [pltpu.VMEM((512, 1024), BF)], 2, place, (*blocks, *common, *more),
+            [pltpu.VMEM((512, 1024), BF)], PIN, place, (*blocks, *common, *more),
         )
 
     hat0, q0, k0, v0 = qkv(near_body, 0, near, (), [arr((512, 1024), BF), half, half, half])
-    far = lax.optimization_barrier((q0, *far))[1:]
+    d_act, down_bias_part = call(
+        down_back_body,
+        (4,),
+        [whole((128, 1024)), pl.BlockSpec((1024, 1024), lambda i, s: (i, 0))],
+        [pl.BlockSpec((128, 1024), lambda i, s: (0, i)), whole((1, 1024))],
+        [arr((128, 4096), F32), arr((1, 1024), F32)],
+        [],
+        PIN,
+        place,
+        (after(cot, q0), down_weight),
+    )
+    far = lax.optimization_barrier((q0, d_act, *far))[2:]
+    cot_here = after(cot, q0)
+    far_cot = swap_over(cot_here, "zh")
+    cots = spread_four(cot_here)
     hat1, q_all, k_all, v_all = qkv(
         far_body, 1, far, (q0, k0, v0), [arr((512, 1024), BF), full, full, full]
     )
@@ -837,33 +873,20 @@
         [step_rows, whole((8, 128, 128)), pl.BlockSpec((2, 1024, 256), lambda i, s: (0, 0, i))],
         [arr((1024, 128), F32), arr((8, 128, 128), BF), arr((2, 1024, 1024), BF)],
         [],
-        6,
+        PIN,
         place,
         (q_all, k_all, v_all, id_col, id_row),
     )
     att_low, far_cot, *cots = lax.optimization_barrier((att_low, far_cot, *cots))
     att_in = lax.all_to_all(att_low, ROW, 0, 0, tiled=True)
-    cots = cots + spread_four(far_cot)
-    d_act, down_bias_part = call(
-        down_back_body,
-        (4,),
-        [whole((128, 1024)), pl.BlockSpec((1024, 1024), lambda i, s: (i, 0))],
-        [pl.BlockSpec((128, 1024), lambda i, s: (0, i)), whole((1, 1024))],
-        [arr((128, 4096), F32), arr((1, 1024), F32)],
-        [],
-        4,
-        place,
-        (after(cot, att_low), down_weight),
-    )
-
-
+    cots += [far_cot, swap_over(far_cot, "y"), swap_over(far_cot, "zl")]
     middle, normed2, att_rows = one_step(
         proj_body,
         [arr((128, 1024), F32), arr((128, 1024), BF), arr((128, 1024), BF)],
         [],
-        2,
+        PIN,
         place,
-        (after(att_in, d_act), tok, proj_weight, vecs),
+        (att_in, tok, proj_weight, vecs),
     )
     normed2, *cots = lax.optimization_barrier((normed2, *cots))
     far_n = swap_over(normed2, "zh")
@@ -877,34 +900,32 @@
             fixed, wide, wide_columns(), whole((15, 1024)), fixed, fixed, whole((1024, 1024)),
             whole((1, 1024)), fixed,
         ],
-        [wide, fixed, whole((8, 128, 128)), whole((16, 32, 1152)), whole((16, 32, 1152))],
+        [wide, fixed, whole((8, 128, 128)), whole((2, 8, 32, 1152)), whole((2, 8, 32, 1152))],
         [
             arr((128, 4096), BF), arr((128, 1024), F32), arr((8, 128, 128), BF),
-            arr((16, 32, 1152), BF), arr((16, 32, 1152), F32),
+            arr((2, 8, 32, 1152), BF), arr((2, 8, 32, 1152), BF),
         ],
         [pltpu.VMEM((128, 1024), F32), pltpu.VMEM((8, 1024), F32)],
-        8,
+        LOW_PIN,
         place,
         (normed2, d_act, up_weight, vecs, middle, cot, proj_weight, down_bias_part, att_rows),
     )
-    d_att, far_n, active, proj_send, *near_n = lax.optimization_barrier(
-        (d_att, far_n, active, proj_send, *near_n)
-    )
+    d_att, far_n, far_y, active, proj_send, *near_n = lax.optimization_barrier(
+        (d_att, far_n, cots[5], active, proj_send, *near_n)
+    )
+    last_cot = swap_over(far_y, "zl")
     d_att_in = lax.all_to_all(d_att, ROW, 0, 0, tiled=True)
 
-    result = middle + mm(active, down_weight) + down_bias.astype(F32)
-    layer_out = result.astype(BF)[None]
-    far_n = spread_four(after(far_n, layer_out))
-
-    def core_sum(keep, send):
-        return keep + swap_over(send, "core").astype(F32)
-
-    def x_sum(keep):
-        return keep[0] + swap_over(keep[1].astype(BF), "x").astype(F32)
-
-    def half_sum(value, name):
-        count = value.shape[0] // 2
-        return value[:count] + swap_over(value[count:].astype(BF), name).astype(F32)
+    far_n = spread_four(far_n)
+
+    def pair(keep, came):
+        half = arr((keep.shape[0] // 2, *keep.shape[1:]), BF)
+        return one_step(pair_body, [half, half], [], NO_PIN, place, (keep, came))
+
+    flat_proj = (16, 32, 1152)
+    proj_left, proj_low = pair(
+        proj_keep.reshape(flat_proj), swap_over(proj_send.reshape(flat_proj), "core")
+    )
 
     d_all, qkv_bias_part = call(
         attend_back_body,
@@ -916,18 +937,19 @@
         [whole((8, 128, 384)), whole((1, 384))],
         [arr((8, 128, 384), BF), arr((1, 384), F32)],
         [pltpu.VMEM((1024, 128), F32)] * 3,
-        6,
+        PIN,
         place,
-        (probs, after(d_att_in, layer_out), att_f, q_all, k_all, v_all, cos_tab, sin_tab),
-    )
-    d_all, *far_n = lax.optimization_barrier((d_all, *far_n))
+        (probs, after(d_att_in, proj_low), att_f, q_all, k_all, v_all, cos_tab, sin_tab),
+    )
+    d_all, last_cot, *far_n = lax.optimization_barrier((d_all, last_cot, *far_n))
     moved = lax.all_to_all(d_all, ROW, 0, 0, tiled=True)
+    proj_left, proj_low = pair(after(proj_left, d_all), swap_over(proj_low, "x"))
 
     def group_of(s, g):
         return (s[1] ^ (g & 1)) * 16 + (s[2] ^ (g >> 1)) * 8 + s[0]
 
     outs = [
-        arr((2, 128, 1024), F32), arr((2, 128, 1024), BF), arr((2, 256, 512), F32),
+        arr((2, 128, 1024), BF), arr((2, 128, 1024), BF), arr((2, 256, 512), BF),
         arr((2, 256, 512), BF),
     ]
     down_keep, down_send, up_keep, up_send = call(
@@ -943,12 +965,13 @@
             pltpu.VMEM((1024, 1024), BF), pltpu.VMEM((1024, 1024), BF),
             pltpu.VMEM((1024, 512), BF), pltpu.VMEM((512, 1024), BF), pltpu.VMEM((1024, 512), F32),
         ],
-        8,
+        LOW_PIN,
         place,
-        (after(near_n[0], d_all), *near_n[1:], *far_n, *cots, *([up_weight] * 4), *([down_weight] * 4), vecs),
-    )
-
-
+        (after(near_n[0], d_all, proj_low), *near_n[1:], *far_n, *cots, last_cot, *([up_weight] * 4), *([down_weight] * 4), vecs),
+    )
+
+
+    proj_left, proj_low = pair(after(proj_left, up_send), swap_over(proj_low, "y"))
     block_of = lambda i, s: (rel_block(i, s), 0)
     lanes_of = lambda i, s: (0, rel_block(i, s))
     send, keep = call(
@@ -963,44 +986,28 @@
             pl.BlockSpec((1, 256, 512), lambda i, s: (jnp.minimum(i, 1), 0, 0)),
             pl.BlockSpec((1, 256, 512), lambda i, s: (jnp.maximum(i - 2, 0), 0, 0)),
         ],
-        [arr((2, 256, 512), BF), arr((2, 256, 512), F32)],
+        [arr((2, 256, 512), BF), arr((2, 256, 512), BF)],
         [],
-        4,
+        PIN,
         place,
-        (after(hat0, up_send), hat1, d_all, qkv_bias_part, columns, qkv_weight, qkv_weight, qkv_weight),
-    )
-    up_keep = core_sum(after(up_keep, moved), up_send)
-    up_sum = x_sum(up_keep)
-    keep = core_sum(after(keep, moved), send)
-    qkv_sum = x_sum(keep)
-    down_keep = core_sum(down_keep, down_send)
-    grad_down = x_sum(after(down_keep, keep))
-    proj_half = core_sum(after(proj_keep, up_send), proj_send)
-    proj_half = half_sum(proj_half, "y")
-    proj_half = half_sum(proj_half, "zl")
-    proj_half = half_sum(proj_half, "x")
-
-    def turn(value, *others):
-        return lax.all_to_all(after(value, *others), ROW, 0, 0, tiled=True)
-
-    lows = jnp.concatenate([v.astype(BF).reshape(8, 32, 512) for v in (up_sum, qkv_sum)], 1)
-    came = turn(lows, moved)
-    proj_total = half_sum(proj_half, "zh")[0]
-    grad_proj = proj_total[:, :1024]
-    own = lax.dynamic_slice(proj_total[:4, 1024:], (0, (me % 4) * 32), (4, 32))
-    grad_up_b = proj_total[4, 1024:]
-
-    grad_up, grad_qkv, sums, bias = one_step(
-        finish_body,
-        [arr((32, 4096), F32), arr((32, 3072), F32), arr((32, 128), F32), arr((48, 128), F32)],
+        (after(hat0, up_send, proj_low), hat1, d_all, qkv_bias_part, columns, qkv_weight, qkv_weight, qkv_weight),
+    )
+    def turn(value):
+        return lax.all_to_all(value, ROW, 0, 0, tiled=True)
+
+    send, proj_came = lax.optimization_barrier((send, swap_over(proj_low, "zl")))
+    left, low_send, down_left, down_low, proj_left, proj_low = one_step(
+        merge_body,
+        [arr((8, 64, 512), BF)] * 2 + [arr((128, 1024), BF)] * 2 + [arr((1, 32, 1152), BF)] * 2,
         [],
-        2,
+        PIN,
         place,
-        (came,),
-    )
-    bias = bias[:, 64:].reshape(8, 3, 128).transpose(1, 0, 2).reshape(3072)
-    grad_qkv_b = lax.dynamic_slice(bias, (me * 96,), (96,))
-
+        (
+            after(up_keep, moved), swap_over(up_send, "core"), keep, swap_over(send, "core"),
+            down_keep, swap_over(down_send, "core"), proj_left, proj_came,
+        ),
+    )
+    low_came = swap_over(low_send, "x")
     (tokens_grad,) = call(
         last_body,
         (3,),
@@ -1011,13 +1018,37 @@
         [fixed],
         [arr((128, 1024), F32)],
         [pltpu.VMEM((128, 1024), F32)],
-        5,
+        PIN,
         place,
-        (moved, qkv_weight, tok, d_mid, vecs),
-    )
+        (after(moved, left), qkv_weight, tok, d_mid, vecs),
+    )
+
+    proj_came = swap_over(proj_low, "zh")
+    left, _ = lax.optimization_barrier((left, tokens_grad))
+    lows = (left.astype(F32) + low_came.astype(F32)).astype(BF)
+    lows, proj_came = lax.optimization_barrier((lows, proj_came))
+    came = turn(lows)
+    down_low, _ = lax.optimization_barrier((down_low, lows))
+    grad_down = down_left.astype(F32) + swap_over(down_low, "x").astype(F32)
+    proj_total = proj_left[0].astype(F32) + proj_came[0].astype(F32)
+    result = middle + mm(after(active, lows), down_weight) + down_bias.astype(F32)
+    layer_out = result.astype(BF)[None]
+    grad_proj = proj_total[:, :1024]
+    own = lax.dynamic_slice(proj_total[:4, 1024:], (0, (me % 4) * 32), (4, 32))
+    grad_up_b = proj_total[4, 1024:]
+
+    grad_up, grad_qkv, sums, bias = one_step(
+        finish_body,
+        [arr((32, 4096), F32), arr((32, 3072), F32), arr((8, 32), F32), arr((3, 1024), F32)],
+        [],
+        NO_PIN,
+        place,
+        (came,),
+    )
+    grad_qkv_b = lax.dynamic_slice(bias.reshape(3072), (me * 96,), (96,))
 
     return (
-        layer_out, tokens_grad[None], sums[:, 0], sums[:, 1], grad_qkv, grad_qkv_b, grad_proj,
+        layer_out, tokens_grad[None], sums[0], sums[1], grad_qkv, grad_qkv_b, grad_proj,
         own[2], own[0], own[1], grad_up, grad_up_b, grad_down, own[3],
     )
 

time: 219 us -> 200 us (0.913)
  other arithmetic: 14.7 us -> 6.99 us
  waiting for transfers between devices: 35.6 us -> 29.7 us
  local copies, waits for them, and re-layouts: 13.4 us -> 10.5 us
    ppermute x32 -> x31, waiting for transfers between devices: 35.2 us -> 20.6 us  [swap_over(): return lax.ppermute(value, AXES, [(i, i ^ mask) for i in range(32)])]
    add x8 -> x2, other arithmetic: 9.63 us -> 0.88 us  [the longest x1 0.86 us: fast_shards(): grad_down = down_left.astype(F32) + swap_over(down_low, 'x').astype(F32)]
    all_to_all x1, waiting for transfers between devices: 0.01 us -> 4.78 us  [fast_shards(): att_in = lax.all_to_all(att_low, ROW, 0, 0, tiled=True)]
    all_to_all x1, waiting for transfers between devices: 0.01 us -> 4.37 us  [turn(): return lax.all_to_all(value, ROW, 0, 0, tiled=True)]
    slice x6 -> x0, local copies, waits for them, and re-layouts: 3.15 us -> none  [the longest x1 1.49 us: fast_shards(): sums[:, 1]]
    unnamed x58 -> x50, local copies, waits for them, and re-layouts: 3.05 us -> 5.4 us
    pallas_call x12 -> x16, Pallas kernels: 87.6 us -> 86.6 us  [call(): pl.pallas_call(body, grid_spec=pltpu.PrefetchScalarGridSpec(num_scalar_pr...]
    ppermute x32 -> x31, starting transfers between devices: 41.5 us -> 41.4 us  [swap_over(): return lax.ppermute(value, AXES, [(i, i ^ mask) for i in range(32)])]
  transfers between devices with their start and end apart: 36 -> 35, of which waited for: 10 -> 9; matrix products, arithmetic and copies ran while one was open for 13% -> 8% of each run, Pallas kernels for 39% -> 41%
where the time goes in v3:
time: 200 us; the launch traced here: 198 us
  Pallas kernels  86.6 us (43%)
  starting transfers between devices  58 us (29%)
  waiting for transfers between devices  29.7 us (15%)
  local copies, waits for them, and re-layouts  10.5 us (5%)
  other arithmetic  6.99 us (3%)
  matrix products  5.45 us (3%)
    pallas_call x16, Pallas kernels, call(): pl.pallas_call(body, grid_spec=pltpu.PrefetchScalarGridSpec(num_scalar_pr...  86.6 us
    ppermute x31, starting transfers between devices, swap_over(): return lax.ppermute(value, AXES, [(i, i ^ mask) for i in range(32)])  41.4 us
    ppermute x31, waiting for transfers between devices, swap_over(): return lax.ppermute(value, AXES, [(i, i ^ mask) for i in range(32)])  20.6 us
    dot_general x1, matrix products, mm(): return jnp.dot(left, right, preferred_element_type=F32)  5.45 us
    unnamed x50, local copies, waits for them, and re-layouts  5.4 us
    all_to_all x1, waiting for transfers between devices, fast_shards(): att_in = lax.all_to_all(att_low, ROW, 0, 0, tiled=True)  4.78 us
    all_to_all x1, starting transfers between devices, turn(): return lax.all_to_all(value, ROW, 0, 0, tiled=True)  4.76 us
    all_to_all x1, starting transfers between devices, fast_shards(): att_in = lax.all_to_all(att_low, ROW, 0, 0, tiled=True)  4.64 us
  transfers between devices with their start and end apart: 35, of which 9 were waited for; matrix products, arithmetic and copies ran while one was open for 8% of the time, Pallas kernels for 41%

profile of v3, /device:TPU:0, one launch (start us, length us, event | category | flops | bytes accessed | tf_op | source)
XLA Modules:
  0.0 198.2 jit_solution(16034092735035844933)
XLA Ops:
  0.6 4.1 %collective-permute-start = (bf16[128,1024]{1,0:T(8,128)(2,1)}, bf16[128,1024]{1,0:T(8,128)(2,1)S(1)}, u32[]{:S(2)}, u32[]{:S(2)}) collective-permute-start(bf16[128,1024]{1,0:T(8,128)(2,1)} %bitcast.42), channel_id=1, source_target_pairs={{0,4},{1,5},{2,6},{3,7},{4,0},{5,1},{6,2},{7,3},{8,12},{9,13},{10,... | collective-permute-start | bytes 786440 | tf_op jit(solution)/shard_map/ppermute | solution.py:352
  4.7 1.5 collective-permute-start.1
  6.3 1.6 collective-permute-start.2
  8.2 0.7 convert_element_type.39
  8.9 0.7 reshape.117
  9.6 0.7 reshape.119
  10.3 0.7 reshape.106
  11.0 0.7 reshape.108
  11.7 0.7 reshape.110
  12.4 0.7 reshape.112
  13.1 0.7 reshape.114
  13.7 0.7 concatenate.6.place
  15.3 4.4 %shard_map.263 = (f32[1024,128]{1,0:T(8,128)}, f32[1024,128]{1,0:T(8,128)}, f32[1024,128]{1,0:T(8,128)}, f32[8,1024]{1,0:T(8,128)S(1)}, f32[1024,8]{1,0:T(8,128)S(1)}) custom-call(s32[16]{0:T(128)S(1)} %concatenate.6.place, f32[8,128]{1,0:T(8,128)S(1)} %copy-done.8, f32[15,1024]{1,0:T(8,128)S(1)} %concatenate.7.vecs.refs_4_.refs_24_), custom_call_target="tpu_custom_call" | custom-call | bytes 1024 | tf_op jit(solution)/shard_map/pallas_call | solution.py:365
  19.7 0.8 copy-done.5
  20.5 3.5 %collective-permute-done.3.refs_3_ = bf16[128,1024]{1,0:T(8,128)(2,1)S(1)} collective-permute-done((bf16[128,1024]{1,0:T(8,128)(2,1)}, bf16[128,1024]{1,0:T(8,128)(2,1)S(1)}, u32[]{:S(2)}, u32[]{:S(2)}) %collective-permute-start.3) | collective-permute-done | bytes 262176 | tf_op jit(solution)/shard_map/ppermute | solution.py:352
  24.0 1.5 collective-permute-start.4
  25.7 1.8 collective-permute-start.6
  27.5 0.9 copy-done.1
  28.5 3.7 %shard_map.264 = (bf16[512,1024]{1,0:T(8,128)(2,1)}, bf16[512,128]{1,0:T(8,128)(2,1)S(1)}, bf16[512,128]{1,0:T(8,128)(2,1)S(1)}, bf16[512,128]{1,0:T(8,128)(2,1)S(1)}) custom-call(s32[16]{0:T(128)S(1)} %concatenate.6.place, bf16[128,1024]{1,0:T(8,128)(2,1)S(1)} %bitcast.46, bf16[128,1024]{1,0:T(8,128)(2,1)S(1)} %collective-permute-done.1.refs_1_, ...), custom_call_target="tpu_custom_call" | custom-call | bytes 1024 | tf_op jit(solution)/shard_map/pallas_call | solution.py:365
  32.1 1.2 collective-permute-start.10
  33.3 2.8 %collective-permute-start.7 = (bf16[128,1024]{1,0:T(8,128)(2,1)S(1)}, bf16[128,1024]{1,0:T(8,128)(2,1)S(1)}, u32[]{:S(2)}, u32[]{:S(2)}) collective-permute-start(bf16[128,1024]{1,0:T(8,128)(2,1)S(1)} %bitcast.38), channel_id=1, source_target_pairs={{0,4},{1,5},{2,6},{3,7},{4,0},{5,1},{6,2},{7,3},{8,12},{9,13},{10,... | collective-permute-start | bytes 786440 | tf_op jit(solution)/shard_map/ppermute | solution.py:352
  36.7 0.9 collective-permute-done.5.refs_2_
  37.6 7.5 %shard_map.265 = (f32[128,4096]{1,0:T(8,128)}, f32[1,1024]{1,0:T(1,128)S(1)}) custom-call(s32[16]{0:T(128)S(1)} %concatenate.6.place, bf16[128,1024]{1,0:T(8,128)(2,1)S(1)} %bitcast.41, bf16[4096,1024]{1,0:T(8,128)(2,1)} %refs_23_.1), custom_call_target="tpu_custom_call" | custom-call | bytes 1024 | tf_op jit(solution)/shard_map/pallas_call | solution.py:365
  45.1 1.0 collective-permute-done.6.refs_3_
  46.0 3.7 %shard_map.266 = (bf16[512,1024]{1,0:T(8,128)(2,1)}, bf16[1024,128]{1,0:T(8,128)(2,1)S(1)}, bf16[1024,128]{1,0:T(8,128)(2,1)S(1)}, bf16[1024,128]{1,0:T(8,128)(2,1)S(1)}) custom-call(s32[16]{0:T(128)S(1)} %concatenate.6.place, bf16[128,1024]{1,0:T(8,128)(2,1)S(1)} %collective-permute-done.refs_0_, bf16[128,1024]{1,0:T(8,128)(2,1)S(1)} %collective-permute-done.4.refs_1_, ...), custom_call_target="tpu_custom_call" | custom-call | bytes 1024 | tf_op jit(solution)/shard_map/pallas_call | solution.py:365
  49.7 10.2 %shard_map.267 = (f32[1024,128]{1,0:T(8,128)}, bf16[8,128,128]{2,1,0:T(8,128)(2,1)}, bf16[2,1024,1024]{2,1,0:T(8,128)(2,1)}) custom-call(s32[16]{0:T(128)S(1)} %concatenate.6.place, bf16[1024,128]{1,0:T(8,128)(2,1)S(1)} %get-tuple-element.135.q, bf16[1024,128]{1,0:T(8,128)(2,1)S(1)} %get-tuple-element.136.k_all, ...), custom_call_target="tpu_custom_call" | custom-call | bytes 1024 | tf_op jit(solution)/shard_map/pallas_call | solution.py:365
  60.0 4.6 %all-to-all-start = ((bf16[8,128,128]{2,1,0:T(8,128)(2,1)}), bf16[8,128,128]{2,1,0:T(8,128)(2,1)S(1)}, u32[]{:S(2)}, u32[]{:S(2)}) async-start(bf16[8,128,128]{2,1,0:T(8,128)(2,1)} %get-tuple-element.141), calls=%async_computation | async-start | bytes 524288 | tf_op jit(solution)/shard_map/all_to_all | solution.py:881
  64.6 2.0 %collective-permute-start.11 = (bf16[128,1024]{1,0:T(8,128)(2,1)S(1)}, bf16[128,1024]{1,0:T(8,128)(2,1)S(1)}, u32[]{:S(2)}, u32[]{:S(2)}) collective-permute-start(bf16[128,1024]{1,0:T(8,128)(2,1)S(1)} %collective-permute-done.7.refs_12_), channel_id=1, source_target_pairs={{0,1},{1,0},{2,3},{3,2},{4,5},{5,4},{6,7},{7,6},{8,9},{9,8},{10,11... | collective-permute-start | bytes 786440 | tf_op jit(solution)/shard_map/ppermute | solution.py:352
  66.6 1.5 collective-permute-start.12
  68.1 4.8 %all-to-all-done.att = bf16[8,128,128]{2,1,0:T(8,128)(2,1)S(1)} async-done(((bf16[8,128,128]{2,1,0:T(8,128)(2,1)}), bf16[8,128,128]{2,1,0:T(8,128)(2,1)S(1)}, u32[]{:S(2)}, u32[]{:S(2)}) %all-to-all-start) | async-done | bytes 262176 | tf_op jit(solution)/shard_map/all_to_all | solution.py:881
  72.9 3.4 %shard_map.268 = (f32[128,1024]{1,0:T(8,128)}, bf16[128,1024]{1,0:T(8,128)(2,1)S(1)}, bf16[128,1024]{1,0:T(8,128)(2,1)S(1)}) custom-call(s32[16]{0:T(128)S(1)} %concatenate.6.place, bf16[8,128,128]{2,1,0:T(8,128)(2,1)S(1)} %all-to-all-done.att, bf16[128,1024]{1,0:T(8,128)(2,1)S(1)} %bitcast.47, bf16[1024,1024]{1,0:T(8,128)(2,1)} %proj_w.3, ...), custom_call_target="tpu_custom_call" | custom-call | bytes 1024 | tf_op jit(solution)/shard_map/pallas_call | solution.py:365
  76.3 0.7 copy-done.7
  77.0 1.8 collective-permute-start.13
  79.3 2.1 %collective-permute-start.15 = (bf16[128,1024]{1,0:T(8,128)(2,1)S(1)}, bf16[128,1024]{1,0:T(8,128)(2,1)S(1)}, u32[]{:S(2)}, u32[]{:S(2)}) collective-permute-start(bf16[128,1024]{1,0:T(8,128)(2,1)S(1)} %get-tuple-element.172.normed.refs_0_), channel_id=1, source_target_pairs={{0,2},{1,3},{2,0},{3,1},{4,6},{5,7},{6,4},{7,5},{8,10},{9,11},{10,... | collective-permute-start | bytes 786440 | tf_op jit(solution)/shard_map/ppermute | solution.py:352
  81.4 1.5 collective-permute-start.16
  82.8 13.7 %shard_map.269 = (bf16[128,4096]{1,0:T(8,128)(2,1)}, f32[128,1024]{1,0:T(8,128)}, bf16[8,128,128]{2,1,0:T(8,128)(2,1)}, bf16[2,8,32,1152]{3,2,1,0:T(8,128)(2,1)}, bf16[2,8,32,1152]{3,2,1,0:T(8,128)(2,1)}) custom-call(s32[16]{0:T(128)S(1)} %concatenate.6.place, bf16[128,1024]{1,0:T(8,128)(2,1)} %copy-done.4, f32[128,4096]{1,0:T(8,128)} %get-tuple-element.127.d_act, ...), custom_call_target="tpu_custom_call" | custom-call | bytes 1024 | tf_op jit(solution)/shard_map/pallas_call | solution.py:365
  97.6 3.4 %all-to-all-start.1 = ((bf16[8,128,128]{2,1,0:T(8,128)(2,1)}), bf16[8,128,128]{2,1,0:T(8,128)(2,1)S(1)}, u32[]{:S(2)}, u32[]{:S(2)}) async-start(bf16[8,128,128]{2,1,0:T(8,128)(2,1)} %get-tuple-element.159), calls=%async_computation.1 | async-start | bytes 524288 | tf_op jit(solution)/shard_map/all_to_all | solution.py:917
  101.0 2.0 %collective-permute-start.18 = (bf16[128,1024]{1,0:T(8,128)(2,1)S(1)}, bf16[128,1024]{1,0:T(8,128)(2,1)}, u32[]{:S(2)}, u32[]{:S(2)}) collective-permute-start(bf16[128,1024]{1,0:T(8,128)(2,1)S(1)} %collective-permute-done.11.refs_13_), channel_id=1, source_target_pairs={{0,2},{1,3},{2,0},{3,1},{4,6},{5,7},{6,4},{7,5},{8,10},{9,11},{10,... | collective-permute-start | bytes 786440 | tf_op jit(solution)/shard_map/ppermute | solution.py:352
  103.1 1.3 collective-permute-start.19
  105.0 1.6 collective-permute-start.21
  106.6 1.3 copy-done.3
  107.8 1.6 shard_map.270
  109.4 1.5 collective-permute-start.22
  110.9 9.3 %shard_map.271 = (bf16[8,128,384]{2,1,0:T(8,128)(2,1)}, f32[1,384]{1,0:T(1,128)S(1)}) custom-call(s32[16]{0:T(128)S(1)} %concatenate.6.place, bf16[2,1024,1024]{2,1,0:T(8,128)(2,1)} %get-tuple-element.158.probs, bf16[8,128,128]{2,1,0:T(8,128)(2,1)S(1)} %all-to-all-done.1.d_att, f32[1024,128]{1,0:T(8,128)} %get-tuple-element.164.att_f, ...), custom_call_target="tpu_custom_call" | custom-call | bytes 1024 | tf_op jit(solution)/shard_map/pallas_call | solution.py:365
  120.3 6.1 %collective-permute-done.21.refs_7_ = bf16[128,1024]{1,0:T(8,128)(2,1)} collective-permute-done((bf16[128,1024]{1,0:T(8,128)(2,1)}, bf16[128,1024]{1,0:T(8,128)(2,1)}, u32[]{:S(2)}, u32[]{:S(2)}) %collective-permute-start.21) | collective-permute-done | bytes 262176 | tf_op jit(solution)/shard_map/ppermute | solution.py:352
  126.3 3.8 %all-to-all-start.2 = ((bf16[8,128,384]{2,1,0:T(8,128)(2,1)}), bf16[8,128,384]{2,1,0:T(8,128)(2,1)S(1)}, u32[]{:S(2)}, u32[]{:S(2)}) async-start(bf16[8,128,384]{2,1,0:T(8,128)(2,1)} %get-tuple-element.168.d_all), calls=%async_computation.2 | async-start | bytes 1572864 | tf_op jit(solution)/shard_map/all_to_all | solution.py:945
  130.1 0.7 shard_map.272
  130.8 2.0 collective-permute-start.24
  132.8 9.9 %shard_map.273 = (bf16[2,128,1024]{2,1,0:T(8,128)(2,1)}, bf16[2,128,1024]{2,1,0:T(8,128)(2,1)}, bf16[2,256,512]{2,1,0:T(8,128)(2,1)}, bf16[2,256,512]{2,1,0:T(8,128)(2,1)}) custom-call(s32[16]{0:T(128)S(1)} %concatenate.6.place, bf16[128,1024]{1,0:T(8,128)(2,1)} %copy-done.4, bf16[128,1024]{1,0:T(8,128)(2,1)} %copy-done.22, bf16[128,1024]{1,0:T(8,128)(2,1)} %copy-done.23, ...), custom_call_target="tpu_custom_call" | custom-call | bytes 1024 | tf_op jit(solution)/shard_map/pallas_call | solution.py:365
  142.7 4.3 %collective-permute-done.24.came = bf16[4,32,1152]{2,1,0:T(8,128)(2,1)S(1)} collective-permute-done((bf16[4,32,1152]{2,1,0:T(8,128)(2,1)S(1)}, bf16[4,32,1152]{2,1,0:T(8,128)(2,1)S(1)}, u32[]{:S(2)}, u32[]{:S(2)}) %collective-permute-start.24) | collective-permute-done | bytes 294944 | tf_op jit(solution)/shard_map/ppermute | solution.py:352
  148.6 6.0 %shard_map.275 = (bf16[2,256,512]{2,1,0:T(8,128)(2,1)}, bf16[2,256,512]{2,1,0:T(8,128)(2,1)}) custom-call(s32[16]{0:T(128)S(1)} %concatenate.6.place, bf16[512,1024]{1,0:T(8,128)(2,1)} %get-tuple-element.194.h0, bf16[512,1024]{1,0:T(8,128)(2,1)} %get-tuple-element.195.h1, bf16[8,128,384]{2,1,0:T(8,128)(2,1)} %get-tuple-element.168.d_all, ...), custom_call_target="tpu_custom_call" | custom-call | bytes 1024 | tf_op jit(solution)/shard_map/pallas_call | solution.py:365
  154.8 2.2 %collective-permute-done.26.refs_3_ = bf16[2,256,512]{2,1,0:T(8,128)(2,1)} collective-permute-done((bf16[2,256,512]{2,1,0:T(8,128)(2,1)}, bf16[2,256,512]{2,1,0:T(8,128)(2,1)}, u32[]{:S(2)}, u32[]{:S(2)}) %collective-permute-start.26) | collective-permute-done | bytes 524320 | tf_op jit(solution)/shard_map/ppermute | solution.py:352
  157.0 3.5 %shard_map.276 = (bf16[8,64,512]{2,1,0:T(8,128)(2,1)}, bf16[8,64,512]{2,1,0:T(8,128)(2,1)}, bf16[128,1024]{1,0:T(8,128)(2,1)S(1)}, bf16[128,1024]{1,0:T(8,128)(2...) custom-call(s32[16]{0:T(128)S(1)} %concatenate.6.place, ...), custom_call_target="tpu_custom_call" | custom-call | bytes 1024 | tf_op jit(solution)/shard_map/pallas_call | solution.py:365
  160.5 1.6 collective-permute-start.28
  162.0 6.7 %shard_map.277 = f32[128,1024]{1,0:T(8,128)} custom-call(s32[16]{0:T(128)S(1)} %concatenate.6.place, bf16[8,128,384]{2,1,0:T(8,128)(2,1)} %copy-done.10, bf16[1024,3072]{1,0:T(8,128)(2,1)} %w.1, bf16[128,1024]{1,0:T(8,128)(2,1)S(1)} %bitcast.48, f32[128,1024]{1,0:T(8,128)} %get-tuple-element.207.d_mid, f32[15,1024]{1,0:T(8,128)S(1)} %concatenate.7.vecs.refs_4_.refs_24_), custom_call_target="tpu_custom_call" | custom-call | bytes 1024 | tf_op jit(solution)/shard_map/pallas_call | solution.py:365
  168.7 3.5 %collective-permute-start.29 = (bf16[1,32,1152]{2,1,0:T(8,128)(2,1)S(1)}, bf16[1,32,1152]{2,1,0:T(8,128)(2,1)S(1)}, u32[]{:S(2)}, u32[]{:S(2)}) collective-permute-start(bf16[1,32,1152]{2,1,0:T(8,128)(2,1)S(1)} %get-tuple-element.210), channel_id=1, source_target_pairs={{0,4},{1,5},{2,6},{3,7},{4,0},{5,1},{6,2},{7,3},{8,12},{9,13},{10,... | collective-permute-start | bytes 221192 | tf_op jit(solution)/shard_map/ppermute | solution.py:352
  172.2 2.6 %collective-permute-done.28 = bf16[8,64,512]{2,1,0:T(8,128)(2,1)} collective-permute-done((bf16[8,64,512]{2,1,0:T(8,128)(2,1)}, bf16[8,64,512]{2,1,0:T(8,128)(2,1)}, u32[]{:S(2)}, u32[]{:S(2)}) %collective-permute-start.28) | collective-permute-done | bytes 524320 | tf_op jit(solution)/shard_map/ppermute | solution.py:352
  174.8 2.0 %add_convert_fusion = bf16[8,64,512]{2,1,0:T(8,128)(2,1)} fusion(bf16[8,64,512]{2,1,0:T(8,128)(2,1)} %collective-permute-done.28, bf16[8,64,512]{2,1,0:T(8,128)(2,1)S(1)} %copy-done.12), kind=kLoop, calls=%fused_computation.4 | loop fusion | flops 1048576 | bytes 1572864 | tf_op jit(solution)/shard_map/convert_element_type | solution.py:1028
  176.8 4.8 %all-to-all-start.3 = ((bf16[8,64,512]{2,1,0:T(8,128)(2,1)}), bf16[8,64,512]{2,1,0:T(8,128)(2,1)S(1)}, u32[]{:S(2)}, u32[]{:S(2)}) async-start(bf16[8,64,512]{2,1,0:T(8,128)(2,1)} %add_convert_fusion), calls=%async_computation.3 | async-start | bytes 1048576 | tf_op jit(solution)/shard_map/all_to_all | solution.py:996
  181.6 1.5 collective-permute-start.30
  183.1 5.4 %fusion.2 = bf16[1,128,1024]{2,1,0:T(8,128)(2,1)} fusion(f32[128,1024]{1,0:T(8,128)S(1)} %copy-done.11, bf16[128,4096]{1,0:T(8,128)(2,1)S(1)} %copy-done.9, bf16[4096,1024]{1,0:T(8,128)(2,1)} %refs_23_.1, f32[1024]{0:T(1024)S(1)} %convert_element_type.39), kind=kOutput, calls=%fused_computation.3 | convolution fusion | flops 1074135040 | bytes 10227712 | tf_op jit(solution)/shard_map/dot_general | solution.py:347
  190.4 0.9 convert_add_fusion
  191.2 4.4 %all-to-all-done.3.came = bf16[8,64,512]{2,1,0:T(8,128)(2,1)S(1)} async-done(((bf16[8,64,512]{2,1,0:T(8,128)(2,1)}), bf16[8,64,512]{2,1,0:T(8,128)(2,1)S(1)}, u32[]{:S(2)}, u32[]{:S(2)}) %all-to-all-start.3) | async-done | bytes 524320 | tf_op jit(solution)/shard_map/all_to_all | solution.py:996
  195.6 1.5 shard_map.278
  (94 shorter events, 8.5 us)
Async XLA Ops:
  0.6 19.9 %collective-permute-start = (bf16[128,1024]{1,0:T(8,128)(2,1)}, bf16[128,1024]{1,0:T(8,128)(2,1)S(1)}, u32[]{:S(2)}, u32[]{:S(2)}) collective-permute-start(bf16[128,1024]{1,0:T(8,128)(2,1)} %bitcast.42), channel_id=1, source_target_pairs={{0,4},{1,5},{2,6},{3,7},{4,0},{5,1},{6,2},{7,3},{8,12},{9,13},{10,... | collective-permute-start | bytes 786440 | tf_op jit(solution)/shard_map/ppermute | solution.py:352
  4.7 15.8 %collective-permute-start.1 = (bf16[128,1024]{1,0:T(8,128)(2,1)}, bf16[128,1024]{1,0:T(8,128)(2,1)S(1)}, u32[]{:S(2)}, u32[]{:S(2)}) collective-permute-start(bf16[128,1024]{1,0:T(8,128)(2,1)} %bitcast.43), channel_id=1, source_target_pairs={{0,1},{1,0},{2,3},{3,2},{4,5},{5,4},{6,7},{7,6},{8,9},{9,8},{10,11... | collective-permute-start | bytes 786440 | tf_op jit(solution)/shard_map/ppermute | solution.py:352
  6.3 14.3 %collective-permute-start.2 = (bf16[128,1024]{1,0:T(8,128)(2,1)}, bf16[128,1024]{1,0:T(8,128)(2,1)S(1)}, u32[]{:S(2)}, u32[]{:S(2)}) collective-permute-start(bf16[128,1024]{1,0:T(8,128)(2,1)} %bitcast.44), channel_id=1, source_target_pairs={{0,2},{1,3},{2,0},{3,1},{4,6},{5,7},{6,4},{7,5},{8,10},{9,11},{10,... | collective-permute-start | bytes 786440 | tf_op jit(solution)/shard_map/ppermute | solution.py:352
  7.8 16.2 %collective-permute-start.3 = (bf16[128,1024]{1,0:T(8,128)(2,1)}, bf16[128,1024]{1,0:T(8,128)(2,1)S(1)}, u32[]{:S(2)}, u32[]{:S(2)}) collective-permute-start(bf16[128,1024]{1,0:T(8,128)(2,1)} %bitcast.45), channel_id=1, source_target_pairs={{0,3},{1,2},{2,1},{3,0},{4,7},{5,6},{6,5},{7,4},{8,11},{9,10},{10,... | collective-permute-start | bytes 786440 | tf_op jit(solution)/shard_map/ppermute | solution.py:352
  14.6 0.7 copy-start.8
  19.7 0.8 copy-start.5
  24.0 12.1 %collective-permute-start.4 = (bf16[128,1024]{1,0:T(8,128)(2,1)S(1)}, bf16[128,1024]{1,0:T(8,128)(2,1)S(1)}, u32[]{:S(2)}, u32[]{:S(2)}) collective-permute-start(bf16[128,1024]{1,0:T(8,128)(2,1)S(1)} %collective-permute-done.refs_0_), channel_id=1, source_target_pairs={{0,1},{1,0},{2,3},{3,2},{4,5},{5,4},{6,7},{7,6},{8,9},{9,8},{10,11... | collective-permute-start | bytes 786440 | tf_op jit(solution)/shard_map/ppermute | solution.py:352
  25.5 12.1 %collective-permute-start.5 = (bf16[128,1024]{1,0:T(8,128)(2,1)S(1)}, bf16[128,1024]{1,0:T(8,128)(2,1)S(1)}, u32[]{:S(2)}, u32[]{:S(2)}) collective-permute-start(bf16[128,1024]{1,0:T(8,128)(2,1)S(1)} %collective-permute-done.refs_0_), channel_id=1, source_target_pairs={{0,2},{1,3},{2,0},{3,1},{4,6},{5,7},{6,4},{7,5},{8,10},{9,11},{10,... | collective-permute-start | bytes 786440 | tf_op jit(solution)/shard_map/ppermute | solution.py:352
  25.7 20.3 %collective-permute-start.6 = (bf16[128,1024]{1,0:T(8,128)(2,1)S(1)}, bf16[128,1024]{1,0:T(8,128)(2,1)S(1)}, u32[]{:S(2)}, u32[]{:S(2)}) collective-permute-start(bf16[128,1024]{1,0:T(8,128)(2,1)S(1)} %collective-permute-done.refs_0_), channel_id=1, source_target_pairs={{0,3},{1,2},{2,1},{3,0},{4,7},{5,6},{6,5},{7,4},{8,11},{9,10},{10,... | collective-permute-start | bytes 786440 | tf_op jit(solution)/shard_map/ppermute | solution.py:352
  27.5 0.9 copy-start.1
  28.5 3.7 %copy-start = (bf16[1,128,1024]{2,1,0:T(8,128)(2,1)S(1)}, bf16[1,128,1024]{2,1,0:T(8,128)(2,1)}, u32[]{:S(2)}) copy-start(bf16[1,128,1024]{2,1,0:T(8,128)(2,1)} %param.30) | copy-start | bytes 786436
  32.1 27.8 %collective-permute-start.10 = (bf16[128,1024]{1,0:T(8,128)(2,1)S(1)}, bf16[128,1024]{1,0:T(8,128)(2,1)S(1)}, u32[]{:S(2)}, u32[]{:S(2)}) collective-permute-start(bf16[128,1024]{1,0:T(8,128)(2,1)S(1)} %bitcast.37), channel_id=1, source_target_pairs={{0,3},{1,2},{2,1},{3,0},{4,7},{5,6},{6,5},{7,4},{8,11},{9,10},{10,... | collective-permute-start | bytes 786440 | tf_op jit(solution)/shard_map/ppermute | solution.py:352
  33.3 26.6 %collective-permute-start.7 = (bf16[128,1024]{1,0:T(8,128)(2,1)S(1)}, bf16[128,1024]{1,0:T(8,128)(2,1)S(1)}, u32[]{:S(2)}, u32[]{:S(2)}) collective-permute-start(bf16[128,1024]{1,0:T(8,128)(2,1)S(1)} %bitcast.38), channel_id=1, source_target_pairs={{0,4},{1,5},{2,6},{3,7},{4,0},{5,1},{6,2},{7,3},{8,12},{9,13},{10,... | collective-permute-start | bytes 786440 | tf_op jit(solution)/shard_map/ppermute | solution.py:352
  36.1 23.8 %collective-permute-start.8 = (bf16[128,1024]{1,0:T(8,128)(2,1)S(1)}, bf16[128,1024]{1,0:T(8,128)(2,1)S(1)}, u32[]{:S(2)}, u32[]{:S(2)}) collective-permute-start(bf16[128,1024]{1,0:T(8,128)(2,1)S(1)} %bitcast.39), channel_id=1, source_target_pairs={{0,1},{1,0},{2,3},{3,2},{4,5},{5,4},{6,7},{7,6},{8,9},{9,8},{10,11... | collective-permute-start | bytes 786440 | tf_op jit(solution)/shard_map/ppermute | solution.py:352
  37.5 22.4 %collective-permute-start.9 = (bf16[128,1024]{1,0:T(8,128)(2,1)S(1)}, bf16[128,1024]{1,0:T(8,128)(2,1)S(1)}, u32[]{:S(2)}, u32[]{:S(2)}) collective-permute-start(bf16[128,1024]{1,0:T(8,128)(2,1)S(1)} %bitcast.40), channel_id=1, source_target_pairs={{0,2},{1,3},{2,0},{3,1},{4,6},{5,7},{6,4},{7,5},{8,10},{9,11},{10,... | collective-permute-start | bytes 786440 | tf_op jit(solution)/shard_map/ppermute | solution.py:352
  46.0 26.9 %copy-start.2 = (bf16[1,128,1024]{2,1,0:T(8,128)(2,1)S(1)}, bf16[1,128,1024]{2,1,0:T(8,128)(2,1)}, u32[]{:S(2)}) copy-start(bf16[1,128,1024]{2,1,0:T(8,128)(2,1)} %param.16) | copy-start | bytes 786436
  59.9 36.7 %copy-start.15 = (bf16[128,1024]{1,0:T(8,128)(2,1)}, bf16[128,1024]{1,0:T(8,128)(2,1)S(1)}, u32[]{:S(2)}) copy-start(bf16[128,1024]{1,0:T(8,128)(2,1)S(1)} %collective-permute-done.10.refs_11_) | copy-start | bytes 786436
  59.9 36.6 %copy-start.16 = (bf16[128,1024]{1,0:T(8,128)(2,1)}, bf16[128,1024]{1,0:T(8,128)(2,1)S(1)}, u32[]{:S(2)}) copy-start(bf16[128,1024]{1,0:T(8,128)(2,1)S(1)} %collective-permute-done.7.refs_12_) | copy-start | bytes 786436
  60.0 36.6 %copy-start.17 = (bf16[128,1024]{1,0:T(8,128)(2,1)}, bf16[128,1024]{1,0:T(8,128)(2,1)S(1)}, u32[]{:S(2)}) copy-start(bf16[128,1024]{1,0:T(8,128)(2,1)S(1)} %collective-permute-done.8.refs_9_) | copy-start | bytes 786436
  60.0 36.6 %copy-start.18 = (bf16[128,1024]{1,0:T(8,128)(2,1)}, bf16[128,1024]{1,0:T(8,128)(2,1)S(1)}, u32[]{:S(2)}) copy-start(bf16[128,1024]{1,0:T(8,128)(2,1)S(1)} %collective-permute-done.9.refs_10_) | copy-start | bytes 786436
  60.0 12.9 %all-to-all-start = ((bf16[8,128,128]{2,1,0:T(8,128)(2,1)}), bf16[8,128,128]{2,1,0:T(8,128)(2,1)S(1)}, u32[]{:S(2)}, u32[]{:S(2)}) async-start(bf16[8,128,128]{2,1,0:T(8,128)(2,1)} %get-tuple-element.141), calls=%async_computation | async-start | bytes 524288 | tf_op jit(solution)/shard_map/all_to_all | solution.py:881
  64.6 12.4 %collective-permute-start.11 = (bf16[128,1024]{1,0:T(8,128)(2,1)S(1)}, bf16[128,1024]{1,0:T(8,128)(2,1)S(1)}, u32[]{:S(2)}, u32[]{:S(2)}) collective-permute-start(bf16[128,1024]{1,0:T(8,128)(2,1)S(1)} %collective-permute-done.7.refs_12_), channel_id=1, source_target_pairs={{0,1},{1,0},{2,3},{3,2},{4,5},{5,4},{6,7},{7,6},{8,9},{9,8},{10,11... | collective-permute-start | bytes 786440 | tf_op jit(solution)/shard_map/ppermute | solution.py:352
  66.6 10.4 %collective-permute-start.12 = (bf16[128,1024]{1,0:T(8,128)(2,1)S(1)}, bf16[128,1024]{1,0:T(8,128)(2,1)S(1)}, u32[]{:S(2)}, u32[]{:S(2)}) collective-permute-start(bf16[128,1024]{1,0:T(8,128)(2,1)S(1)} %collective-permute-done.7.refs_12_), channel_id=1, source_target_pairs={{0,2},{1,3},{2,0},{3,1},{4,6},{5,7},{6,4},{7,5},{8,10},{9,11},{10,... | collective-permute-start | bytes 786440 | tf_op jit(solution)/shard_map/ppermute | solution.py:352
  76.3 0.7 copy-start.7
  77.0 5.8 %copy-start.4 = (bf16[128,1024]{1,0:T(8,128)(2,1)}, bf16[128,1024]{1,0:T(8,128)(2,1)S(1)}, u32[]{:S(2)}) copy-start(bf16[128,1024]{1,0:T(8,128)(2,1)S(1)} %get-tuple-element.172.normed.refs_0_) | copy-start | bytes 786436
  77.0 24.0 %copy-start.19 = (bf16[128,1024]{1,0:T(8,128)(2,1)}, bf16[128,1024]{1,0:T(8,128)(2,1)S(1)}, u32[]{:S(2)}) copy-start(bf16[128,1024]{1,0:T(8,128)(2,1)S(1)} %collective-permute-done.11.refs_13_) | copy-start | bytes 786436
  77.0 19.6 %copy-start.20 = (bf16[128,1024]{1,0:T(8,128)(2,1)}, bf16[128,1024]{1,0:T(8,128)(2,1)S(1)}, u32[]{:S(2)}) copy-start(bf16[128,1024]{1,0:T(8,128)(2,1)S(1)} %collective-permute-done.12.refs_14_) | copy-start | bytes 786436
  77.0 19.6 %collective-permute-start.13 = (bf16[128,1024]{1,0:T(8,128)(2,1)S(1)}, bf16[128,1024]{1,0:T(8,128)(2,1)S(1)}, u32[]{:S(2)}, u32[]{:S(2)}) collective-permute-start(bf16[128,1024]{1,0:T(8,128)(2,1)S(1)} %get-tuple-element.172.normed.refs_0_), channel_id=1, source_target_pairs={{0,4},{1,5},{2,6},{3,7},{4,0},{5,1},{6,2},{7,3},{8,12},{9,13},{10,... | collective-permute-start | bytes 786440 | tf_op jit(solution)/shard_map/ppermute | solution.py:352
  78.9 17.8 %collective-permute-start.14 = (bf16[128,1024]{1,0:T(8,128)(2,1)S(1)}, bf16[128,1024]{1,0:T(8,128)(2,1)S(1)}, u32[]{:S(2)}, u32[]{:S(2)}) collective-permute-start(bf16[128,1024]{1,0:T(8,128)(2,1)S(1)} %get-tuple-element.172.normed.refs_0_), channel_id=1, source_target_pairs={{0,1},{1,0},{2,3},{3,2},{4,5},{5,4},{6,7},{7,6},{8,9},{9,8},{10,11... | collective-permute-start | bytes 786440 | tf_op jit(solution)/shard_map/ppermute | solution.py:352
  79.3 17.4 %collective-permute-start.15 = (bf16[128,1024]{1,0:T(8,128)(2,1)S(1)}, bf16[128,1024]{1,0:T(8,128)(2,1)S(1)}, u32[]{:S(2)}, u32[]{:S(2)}) collective-permute-start(bf16[128,1024]{1,0:T(8,128)(2,1)S(1)} %get-tuple-element.172.normed.refs_0_), channel_id=1, source_target_pairs={{0,2},{1,3},{2,0},{3,1},{4,6},{5,7},{6,4},{7,5},{8,10},{9,11},{10,... | collective-permute-start | bytes 786440 | tf_op jit(solution)/shard_map/ppermute | solution.py:352
  81.4 15.3 %collective-permute-start.16 = (bf16[128,1024]{1,0:T(8,128)(2,1)S(1)}, bf16[128,1024]{1,0:T(8,128)(2,1)S(1)}, u32[]{:S(2)}, u32[]{:S(2)}) collective-permute-start(bf16[128,1024]{1,0:T(8,128)(2,1)S(1)} %get-tuple-element.172.normed.refs_0_), channel_id=1, source_target_pairs={{0,3},{1,2},{2,1},{3,0},{4,7},{5,6},{6,5},{7,4},{8,11},{9,10},{10,... | collective-permute-start | bytes 786440 | tf_op jit(solution)/shard_map/ppermute | solution.py:352
  96.6 0.7 copy-start.21
  96.6 0.8 copy-start.22
  96.7 0.9 copy-start.23
  96.7 0.9 copy-start.24
  97.6 9.0 %collective-permute-start.17 = (bf16[16,32,1152]{2,1,0:T(8,128)(2,1)}, bf16[16,32,1152]{2,1,0:T(8,128)(2,1)S(1)}, u32[]{:S(2)}, u32[]{:S(2)}) collective-permute-start(bf16[16,32,1152]{2,1,0:T(8,128)(2,1)} %bitcast.60), channel_id=1, source_target_pairs={{0,8},{1,9},{2,10},{3,11},{4,12},{5,13},{6,14},{7,15},{8,0},{9,1},... | collective-permute-start | bytes 3538952 | tf_op jit(solution)/shard_map/ppermute | solution.py:352
  97.6 13.3 %all-to-all-start.1 = ((bf16[8,128,128]{2,1,0:T(8,128)(2,1)}), bf16[8,128,128]{2,1,0:T(8,128)(2,1)S(1)}, u32[]{:S(2)}, u32[]{:S(2)}) async-start(bf16[8,128,128]{2,1,0:T(8,128)(2,1)} %get-tuple-element.159), calls=%async_computation.1 | async-start | bytes 524288 | tf_op jit(solution)/shard_map/all_to_all | solution.py:917
  101.0 19.2 %collective-permute-start.18 = (bf16[128,1024]{1,0:T(8,128)(2,1)S(1)}, bf16[128,1024]{1,0:T(8,128)(2,1)}, u32[]{:S(2)}, u32[]{:S(2)}) collective-permute-start(bf16[128,1024]{1,0:T(8,128)(2,1)S(1)} %collective-permute-done.11.refs_13_), channel_id=1, source_target_pairs={{0,2},{1,3},{2,0},{3,1},{4,6},{5,7},{6,4},{7,5},{8,10},{9,11},{10,... | collective-permute-start | bytes 786440 | tf_op jit(solution)/shard_map/ppermute | solution.py:352
  103.1 17.2 %collective-permute-start.19 = (bf16[128,1024]{1,0:T(8,128)(2,1)}, bf16[128,1024]{1,0:T(8,128)(2,1)}, u32[]{:S(2)}, u32[]{:S(2)}) collective-permute-start(bf16[128,1024]{1,0:T(8,128)(2,1)} %copy-done.21), channel_id=1, source_target_pairs={{0,1},{1,0},{2,3},{3,2},{4,5},{5,4},{6,7},{7,6},{8,9},{9,8},{10,11... | collective-permute-start | bytes 786440 | tf_op jit(solution)/shard_map/ppermute | solution.py:352
  104.4 15.8 %collective-permute-start.20 = (bf16[128,1024]{1,0:T(8,128)(2,1)}, bf16[128,1024]{1,0:T(8,128)(2,1)}, u32[]{:S(2)}, u32[]{:S(2)}) collective-permute-start(bf16[128,1024]{1,0:T(8,128)(2,1)} %copy-done.21), channel_id=1, source_target_pairs={{0,2},{1,3},{2,0},{3,1},{4,6},{5,7},{6,4},{7,5},{8,10},{9,11},{10,... | collective-permute-start | bytes 786440 | tf_op jit(solution)/shard_map/ppermute | solution.py:352
  105.0 21.3 %collective-permute-start.21 = (bf16[128,1024]{1,0:T(8,128)(2,1)}, bf16[128,1024]{1,0:T(8,128)(2,1)}, u32[]{:S(2)}, u32[]{:S(2)}) collective-permute-start(bf16[128,1024]{1,0:T(8,128)(2,1)} %copy-done.21), channel_id=1, source_target_pairs={{0,3},{1,2},{2,1},{3,0},{4,7},{5,6},{6,5},{7,4},{8,11},{9,10},{10,... | collective-permute-start | bytes 786440 | tf_op jit(solution)/shard_map/ppermute | solution.py:352
  106.6 1.3 copy-start.3
  109.4 20.7 %collective-permute-start.22 = (bf16[8,32,1152]{2,1,0:T(8,128)(2,1)}, bf16[8,32,1152]{2,1,0:T(8,128)(2,1)S(1)}, u32[]{:S(2)}, u32[]{:S(2)}) collective-permute-start(bf16[8,32,1152]{2,1,0:T(8,128)(2,1)} %get-tuple-element.162), channel_id=1, source_target_pairs={{0,16},{1,17},{2,18},{3,19},{4,20},{5,21},{6,22},{7,23},{8,24},{9,... | collective-permute-start | bytes 1769480 | tf_op jit(solution)/shard_map/ppermute | solution.py:352
  126.3 28.4 %all-to-all-start.2 = ((bf16[8,128,384]{2,1,0:T(8,128)(2,1)}), bf16[8,128,384]{2,1,0:T(8,128)(2,1)S(1)}, u32[]{:S(2)}, u32[]{:S(2)}) async-start(bf16[8,128,384]{2,1,0:T(8,128)(2,1)} %get-tuple-element.168.d_all), calls=%async_computation.2 | async-start | bytes 1572864 | tf_op jit(solution)/shard_map/all_to_all | solution.py:945
  130.8 17.8 %copy-start.6 = (f32[1024,8]{1,0:T(8,128)S(1)}, f32[1024,8]{1,0:T(8,128)}, u32[]{:S(2)}) copy-start(f32[1024,8]{1,0:T(8,128)} %copy-done.5) | copy-start | bytes 98308
  130.8 16.2 %collective-permute-start.24 = (bf16[4,32,1152]{2,1,0:T(8,128)(2,1)S(1)}, bf16[4,32,1152]{2,1,0:T(8,128)(2,1)S(1)}, u32[]{:S(2)}, u32[]{:S(2)}) collective-permute-start(bf16[4,32,1152]{2,1,0:T(8,128)(2,1)S(1)} %get-tuple-element.171), channel_id=1, source_target_pairs={{0,1},{1,0},{2,3},{3,2},{4,5},{5,4},{6,7},{7,6},{8,9},{9,8},{10,11... | collective-permute-start | bytes 884744 | tf_op jit(solution)/shard_map/ppermute | solution.py:352
  147.6 7.0 %collective-permute-start.25 = (bf16[2,32,1152]{2,1,0:T(8,128)(2,1)S(1)}, bf16[2,32,1152]{2,1,0:T(8,128)(2,1)S(1)}, u32[]{:S(2)}, u32[]{:S(2)}) collective-permute-start(bf16[2,32,1152]{2,1,0:T(8,128)(2,1)S(1)} %get-tuple-element.193), channel_id=1, source_target_pairs={{0,2},{1,3},{2,0},{3,1},{4,6},{5,7},{6,4},{7,5},{8,10},{9,11},{10,... | collective-permute-start | bytes 442376 | tf_op jit(solution)/shard_map/ppermute | solution.py:352
  148.1 6.6 %collective-permute-start.23 = (bf16[2,256,512]{2,1,0:T(8,128)(2,1)}, bf16[2,256,512]{2,1,0:T(8,128)(2,1)S(1)}, u32[]{:S(2)}, u32[]{:S(2)}) collective-permute-start(bf16[2,256,512]{2,1,0:T(8,128)(2,1)} %get-tuple-element.189), channel_id=1, source_target_pairs={{0,8},{1,9},{2,10},{3,11},{4,12},{5,13},{6,14},{7,15},{8,0},{9,1},... | collective-permute-start | bytes 1572872 | tf_op jit(solution)/shard_map/ppermute | solution.py:352
  148.1 6.7 %collective-permute-start.27 = (bf16[2,128,1024]{2,1,0:T(8,128)(2,1)}, bf16[2,128,1024]{2,1,0:T(8,128)(2,1)S(1)}, u32[]{:S(2)}, u32[]{:S(2)}) collective-permute-start(bf16[2,128,1024]{2,1,0:T(8,128)(2,1)} %get-tuple-element.202), channel_id=1, source_target_pairs={{0,8},{1,9},{2,10},{3,11},{4,12},{5,13},{6,14},{7,15},{8,0},{9,1},... | collective-permute-start | bytes 1572872 | tf_op jit(solution)/shard_map/ppermute | solution.py:352
  154.6 2.3 %collective-permute-start.26 = (bf16[2,256,512]{2,1,0:T(8,128)(2,1)}, bf16[2,256,512]{2,1,0:T(8,128)(2,1)}, u32[]{:S(2)}, u32[]{:S(2)}) collective-permute-start(bf16[2,256,512]{2,1,0:T(8,128)(2,1)} %get-tuple-element.200), channel_id=1, source_target_pairs={{0,8},{1,9},{2,10},{3,11},{4,12},{5,13},{6,14},{7,15},{8,0},{9,1},... | collective-permute-start | bytes 1572872 | tf_op jit(solution)/shard_map/ppermute | solution.py:352
  154.7 2.2 %copy-start.10 = (bf16[8,128,384]{2,1,0:T(8,128)(2,1)}, bf16[8,128,384]{2,1,0:T(8,128)(2,1)S(1)}, u32[]{:S(2)}) copy-start(bf16[8,128,384]{2,1,0:T(8,128)(2,1)S(1)} %all-to-all-done.2.came) | copy-start | bytes 2359300
  154.8 2.2 %copy-start.13 = (bf16[2,256,512]{2,1,0:T(8,128)(2,1)}, bf16[2,256,512]{2,1,0:T(8,128)(2,1)S(1)}, u32[]{:S(2)}) copy-start(bf16[2,256,512]{2,1,0:T(8,128)(2,1)S(1)} %collective-permute-done.23.refs_1_) | copy-start | bytes 1572868
  154.8 2.2 %copy-start.14 = (bf16[2,128,1024]{2,1,0:T(8,128)(2,1)}, bf16[2,128,1024]{2,1,0:T(8,128)(2,1)S(1)}, u32[]{:S(2)}) copy-start(bf16[2,128,1024]{2,1,0:T(8,128)(2,1)S(1)} %collective-permute-done.27.refs_5_) | copy-start | bytes 1572868
  160.5 14.4 %copy-start.12 = (bf16[8,64,512]{2,1,0:T(8,128)(2,1)S(1)}, bf16[8,64,512]{2,1,0:T(8,128)(2,1)}, u32[]{:S(2)}) copy-start(bf16[8,64,512]{2,1,0:T(8,128)(2,1)} %get-tuple-element.208) | copy-start | bytes 1572868
  160.5 22.6 %copy-start.9 = (bf16[128,4096]{1,0:T(8,128)(2,1)S(1)}, bf16[128,4096]{1,0:T(8,128)(2,1)}, u32[]{:S(2)}) copy-start(bf16[128,4096]{1,0:T(8,128)(2,1)} %get-tuple-element.212) | copy-start | bytes 3145732
  160.5 22.6 %copy-start.11 = (f32[128,1024]{1,0:T(8,128)S(1)}, f32[128,1024]{1,0:T(8,128)}, u32[]{:S(2)}) copy-start(f32[128,1024]{1,0:T(8,128)} %get-tuple-element.142.middle) | copy-start | bytes 1572868
  160.5 14.3 %collective-permute-start.28 = (bf16[8,64,512]{2,1,0:T(8,128)(2,1)}, bf16[8,64,512]{2,1,0:T(8,128)(2,1)}, u32[]{:S(2)}, u32[]{:S(2)}) collective-permute-start(bf16[8,64,512]{2,1,0:T(8,128)(2,1)} %get-tuple-element.209), channel_id=1, source_target_pairs={{0,16},{1,17},{2,18},{3,19},{4,20},{5,21},{6,22},{7,23},{8,24},{9,... | collective-permute-start | bytes 1572872 | tf_op jit(solution)/shard_map/ppermute | solution.py:352
  168.7 8.1 %collective-permute-start.29 = (bf16[1,32,1152]{2,1,0:T(8,128)(2,1)S(1)}, bf16[1,32,1152]{2,1,0:T(8,128)(2,1)S(1)}, u32[]{:S(2)}, u32[]{:S(2)}) collective-permute-start(bf16[1,32,1152]{2,1,0:T(8,128)(2,1)S(1)} %get-tuple-element.210), channel_id=1, source_target_pairs={{0,4},{1,5},{2,6},{3,7},{4,0},{5,1},{6,2},{7,3},{8,12},{9,13},{10,... | collective-permute-start | bytes 221192 | tf_op jit(solution)/shard_map/ppermute | solution.py:352
  176.8 18.7 %all-to-all-start.3 = ((bf16[8,64,512]{2,1,0:T(8,128)(2,1)}), bf16[8,64,512]{2,1,0:T(8,128)(2,1)S(1)}, u32[]{:S(2)}, u32[]{:S(2)}) async-start(bf16[8,64,512]{2,1,0:T(8,128)(2,1)} %add_convert_fusion), calls=%async_computation.3 | async-start | bytes 1048576 | tf_op jit(solution)/shard_map/all_to_all | solution.py:996
  181.6 8.8 %collective-permute-start.30 = (bf16[128,1024]{1,0:T(8,128)(2,1)S(1)}, bf16[128,1024]{1,0:T(8,128)(2,1)S(1)}, u32[]{:S(2)}, u32[]{:S(2)}) collective-permute-start(bf16[128,1024]{1,0:T(8,128)(2,1)S(1)} %get-tuple-element.221), channel_id=1, source_target_pairs={{0,16},{1,17},{2,18},{3,19},{4,20},{5,21},{6,22},{7,23},{8,24},{9,... | collective-permute-start | bytes 786440 | tf_op jit(solution)/shard_map/ppermute | solution.py:352

commit v4 on v3

--- a/solution.py
+++ b/solution.py
@@ -361,7 +361,9 @@
     return jax.ShapeDtypeStruct(shape, dtype)
 
 
-def call(body, grid, in_specs, out_specs, out_shape, scratch, pin, scalars, args):
+def call(
+    body, grid, in_specs, out_specs, out_shape, scratch, pin, scalars, args, out_pin=None
+):
     return pl.pallas_call(
         body,
         grid_spec=pltpu.PrefetchScalarGridSpec(
@@ -371,7 +373,7 @@
             out_specs=out_specs,
             scratch_shapes=scratch,
         ),
-        out_shape=[pltpu.HBM(o.shape, o.dtype) if big(o, pin) else o for o in out_shape],
+        out_shape=[pltpu.HBM(o.shape, o.dtype) if big(o, out_pin or pin) else o for o in out_shape],
         compiler_params=pltpu.CompilerParams(vmem_limit_bytes=VMEM_MIB << 20),
         cost_estimate=pl.CostEstimate(flops=0, bytes_accessed=1024, transcendentals=0),
     )(scalars, *(pinned(v, pin) for v in args))
@@ -385,10 +387,10 @@
     return pltpu.with_memory_space_constraint(v, pltpu.HBM) if big(v, pin) else v
 
 
-def one_step(body, outs, scratch, pin, scalars, args):
+def one_step(body, outs, scratch, pin, scalars, args, out_pin=None):
     return call(
         body, (1,), [whole(v.shape) for v in args], [whole(o.shape) for o in outs], outs, scratch,
-        pin, scalars, args,
+        pin, scalars, args, out_pin,
     )
 
 
@@ -464,22 +466,25 @@
     return lax.broadcasted_iota(jnp.int32, shape, 1) // 64 == head
 
 
-def attend_body(place, q, k_all, v_all, id_col, id_row, att_f, att_low, probs):
+def attend_body(place, q, k_all, v_all, id_col, id_row, att_f, att_low, probs, row_scale):
     keys = k_all[...]
     values = v_all[...]
     queries = q[...]
     own = id_col[...]
     allowed = jnp.concatenate([own, own], 1) == id_row[0:1, :]
-    halves = []
+    halves, scales = [], []
     for head in range(2):
         mine = jnp.where(head_mask(queries.shape, head), queries, jnp.zeros_like(queries))
         scores = jnp.where(allowed, times_transposed(keys, mine), NEG_FILL)
         weights = jnp.exp(scores - jnp.max(scores, 0, keepdims=True))
-        low = (weights * (1.0 / jnp.sum(weights, 0, keepdims=True))).astype(BF)
+        low = weights.astype(BF)
         probs[head] = low
-        halves.append(outer_sum(values, low)[64 * head : 64 * head + 64])
+        scale = 1.0 / jnp.sum(weights, 0, keepdims=True)
+        scales.append(scale)
+        halves.append(outer_sum(values, low)[64 * head : 64 * head + 64] * scale)
     out = jnp.concatenate(halves, 0).T
     att_f[...] = out
+    row_scale[...] = jnp.concatenate([jnp.broadcast_to(v, (64, 256)) for v in scales], 0).T
     step = pl.program_id(0)
     att_low[place[0] ^ (2 * step)] = out[:128].astype(BF)
     att_low[place[0] ^ (2 * step + 1)] = out[128:].astype(BF)
@@ -509,7 +514,7 @@
         last = vectors[4 + group : 5 + group, 128 * k : 128 * k + 128]
         extra = jnp.where(row == 4, last, extra)
         rel = place[0] ^ k
-        slot = (rel & 1) * 4 + (rel & 2) + (rel >> 2)
+        slot = (rel & 1) * 4 + (rel >> 2) * 2 + ((rel >> 1) & 1)
         for side, out in ((core == place[2], keep), (core != place[2], send)):
 
             @pl.when(side)
@@ -597,13 +602,15 @@
 
 
 def attend_back_body(
-    place, probs, d_att, att_f, q, k_all, v_all, cos, sin, d_all, bias_part, dq, dk, dv
+    place, probs, d_att, att_f, row_scale, q, k_all, v_all, cos, sin, d_all, bias_part, dq, dk, dv
 ):
     step = pl.program_id(0)
     keys = k_all[...]
     values = v_all[...]
     queries = q[...]
     d_out = jnp.concatenate([d_att[place[0] ^ (2 * step)], d_att[place[0] ^ (2 * step + 1)]], 0)
+    scaled = d_out.astype(F32) * row_scale[...]
+    d_out = scaled.astype(BF)
     products = (d_out.astype(F32) * att_f[...]).T
     key_parts, value_parts, query_parts = [], [], []
     for head in range(2):
@@ -657,13 +664,14 @@
     return ((rel & 1) ^ place[1]) * 2 + ((rel >> 1) ^ place[2])
 
 
-def qkv_grad_body(place, h0, h1, d_all, bias_part, columns, wq, wk, wv, send, keep):
+def qkv_grad_body(place, h0, h1, d_all, bias_part, vecs, wq, wk, wv, send, keep):
     step = pl.program_id(0)
     d_near = jnp.concatenate([d_all[place[0] ^ j] for j in range(4)], 0)
     d_far = jnp.concatenate([d_all[place[0] ^ j] for j in range(4, 8)], 0)
     inner = outer_sum(h0[...], d_near) + outer_sum(h1[...], d_far)
     total = bias_part[...]
     w = jnp.concatenate([wq[...], wk[...], wv[...]], 1).astype(F32)
+    columns = vecs[...].T
     gain = columns[:, 0:1]
     shift = columns[:, 1:2]
     grad = gain * inner + shift * total
@@ -697,11 +705,15 @@
     send[...] = total[half:]
 
 
+def add_body(place, left, came, out):
+    out[...] = (left[...].astype(F32) + came[...].astype(F32)).astype(BF)
+
+
 def merge_body(place, *refs):
     keeps, cames = refs[0:6:2], refs[1:6:2]
     proj_left, proj_came, left, send, down_left, down_send, proj_keep, proj_send = refs[6:]
-    proj_keep[...] = (proj_left[:1].astype(F32) + proj_came[:1].astype(F32)).astype(BF)
-    proj_send[...] = (proj_left[1:].astype(F32) + proj_came[1:].astype(F32)).astype(BF)
+    proj_keep[...] = (proj_left[:2].astype(F32) + proj_came[:2].astype(F32)).astype(BF)
+    proj_send[...] = (proj_left[2:].astype(F32) + proj_came[2:].astype(F32)).astype(BF)
     for side, low, down in ((0, left, down_left), (1, send, down_send)):
         for m in range(2):
             total = keeps[m][side].astype(F32) + cames[m][side].astype(F32)
@@ -728,6 +740,23 @@
     sums[...] = total.T[:8]
 
 
+def out_body(place, active, down, middle, vecs, out, acc):
+    step = pl.program_id(0)
+    part = mm(active[...], down[...])
+
+    @pl.when(step == 0)
+    def _():
+        acc[...] = part + middle[...] + vecs[5:6, :]
+
+    @pl.when(step > 0)
+    def _():
+        acc[...] += part
+
+    @pl.when(step == pl.num_programs(0) - 1)
+    def _():
+        out[...] = acc[...].astype(BF)
+
+
 def last_body(place, came, w, tok, d_mid, vecs, out, acc):
     step = pl.program_id(0)
     for p in range(3):
@@ -772,7 +801,7 @@
     return ids, start
 
 
-def prep_body(place, freq, vecs, cos, sin, id_col, id_row, columns):
+def prep_body(place, freq, cos, sin, id_col, id_row):
     for j in range(8):
         first = ((place[0] ^ j) * 128).astype(F32)
         rows = slice(128 * j, 128 * j + 128)
@@ -787,7 +816,6 @@
         sin[rows, :] = jnp.sin(angle) * freq[3:4, :]
         flat = first + lax.broadcasted_iota(jnp.int32, (8, 128), 1).astype(F32)
         id_row[:, 128 * j : 128 * j + 128] = clip_starts(place, flat)[0]
-    columns[...] = vecs[0:8, :].T
 
 
 def after(value, *others):
@@ -815,16 +843,15 @@
     near = spread_four(tok)
     rows = [attn_gain, attn_shift, proj_bias, mlp_gain, mlp_shift, down_bias, down_bias, down_bias]
     vecs = jnp.concatenate([v.astype(F32).reshape(-1, 1024) for v in (*rows, up_bias, qkv_bias)], 0)
-    cos_tab, sin_tab, id_col, id_row, columns = one_step(
+    cos_tab, sin_tab, id_col, id_row = one_step(
         prep_body,
-        [arr((1024, 128), F32), arr((1024, 128), F32), arr((1024, 128), F32), arr((8, 1024), F32),
-         arr((1024, 8), F32)],
+        [arr((1024, 128), F32), arr((1024, 128), F32), arr((1024, 128), F32), arr((8, 1024), F32)],
         [],
         PIN,
         place,
-        (jnp.asarray(frequency_rows()), vecs),
-    )
-    far_tok, cos_tab, *near = lax.optimization_barrier((far_tok, cos_tab, *near))
+        (jnp.asarray(frequency_rows()),),
+    )
+    far_tok, cos_tab, vecs, *near = lax.optimization_barrier((far_tok, cos_tab, vecs, *near))
     far = spread_four(far_tok)
 
     def table_half(part):
@@ -864,14 +891,16 @@
     )
     step_rows = pl.BlockSpec((256, 128), lambda i, s: (i, 0))
     flat = whole((1024, 128))
-    att_f, att_low, probs = call(
+    att_f, att_low, probs, row_scale = call(
         attend_body,
         (4,),
         [
             step_rows, flat, flat, flat, pl.BlockSpec((8, 256), lambda i, s: (0, i)),
         ],
-        [step_rows, whole((8, 128, 128)), pl.BlockSpec((2, 1024, 256), lambda i, s: (0, 0, i))],
-        [arr((1024, 128), F32), arr((8, 128, 128), BF), arr((2, 1024, 1024), BF)],
+        [step_rows, whole((8, 128, 128)), pl.BlockSpec((2, 1024, 256), lambda i, s: (0, 0, i)),
+         step_rows],
+        [arr((1024, 128), F32), arr((8, 128, 128), BF), arr((2, 1024, 1024), BF),
+         arr((1024, 128), F32)],
         [],
         PIN,
         place,
@@ -887,6 +916,7 @@
         PIN,
         place,
         (att_in, tok, proj_weight, vecs),
+        LOW_PIN,
     )
     normed2, *cots = lax.optimization_barrier((normed2, *cots))
     far_n = swap_over(normed2, "zh")
@@ -932,16 +962,38 @@
         (4,),
         [
             pl.BlockSpec((2, 1024, 256), lambda i, s: (0, 0, i)), whole((8, 128, 128)), step_rows,
-            step_rows, flat, flat, flat, flat,
+            step_rows, step_rows, flat, flat, flat, flat,
         ],
         [whole((8, 128, 384)), whole((1, 384))],
         [arr((8, 128, 384), BF), arr((1, 384), F32)],
         [pltpu.VMEM((1024, 128), F32)] * 3,
         PIN,
         place,
-        (probs, after(d_att_in, proj_low), att_f, q_all, k_all, v_all, cos_tab, sin_tab),
-    )
-    d_all, last_cot, *far_n = lax.optimization_barrier((d_all, last_cot, *far_n))
+        (probs, after(d_att_in, proj_low), att_f, row_scale, q_all, k_all, v_all, cos_tab, sin_tab),
+    )
+    block_of = lambda i, s: (rel_block(i, s), 0)
+    lanes_of = lambda i, s: (0, rel_block(i, s))
+    send, keep = call(
+        qkv_grad_body,
+        (4,),
+        [
+            pl.BlockSpec((512, 256), lanes_of), pl.BlockSpec((512, 256), lanes_of),
+            whole((8, 128, 384)), whole((1, 384)), pl.BlockSpec((8, 256), lanes_of),
+        ]
+        + [pl.BlockSpec((256, 128), lambda i, s, p=p: (rel_block(i, s), 8 * p + s[0])) for p in range(3)],
+        [
+            pl.BlockSpec((1, 256, 512), lambda i, s: (jnp.minimum(i, 1), 0, 0)),
+            pl.BlockSpec((1, 256, 512), lambda i, s: (jnp.maximum(i - 2, 0), 0, 0)),
+        ],
+        [arr((2, 256, 512), BF), arr((2, 256, 512), BF)],
+        [],
+        PIN,
+        place,
+        (hat0, hat1, d_all, qkv_bias_part, vecs, qkv_weight, qkv_weight, qkv_weight),
+    )
+    def turn(value):
+        return lax.all_to_all(value, ROW, 0, 0, tiled=True)
+    d_all, send, last_cot, *far_n = lax.optimization_barrier((d_all, send, last_cot, *far_n))
     moved = lax.all_to_all(d_all, ROW, 0, 0, tiled=True)
     proj_left, proj_low = pair(after(proj_left, d_all), swap_over(proj_low, "x"))
 
@@ -971,34 +1023,12 @@
     )
 
 
-    proj_left, proj_low = pair(after(proj_left, up_send), swap_over(proj_low, "y"))
-    block_of = lambda i, s: (rel_block(i, s), 0)
-    lanes_of = lambda i, s: (0, rel_block(i, s))
-    send, keep = call(
-        qkv_grad_body,
-        (4,),
-        [
-            pl.BlockSpec((512, 256), lanes_of), pl.BlockSpec((512, 256), lanes_of),
-            whole((8, 128, 384)), whole((1, 384)), pl.BlockSpec((256, 8), block_of),
-        ]
-        + [pl.BlockSpec((256, 128), lambda i, s, p=p: (rel_block(i, s), 8 * p + s[0])) for p in range(3)],
-        [
-            pl.BlockSpec((1, 256, 512), lambda i, s: (jnp.minimum(i, 1), 0, 0)),
-            pl.BlockSpec((1, 256, 512), lambda i, s: (jnp.maximum(i - 2, 0), 0, 0)),
-        ],
-        [arr((2, 256, 512), BF), arr((2, 256, 512), BF)],
-        [],
-        PIN,
-        place,
-        (after(hat0, up_send, proj_low), hat1, d_all, qkv_bias_part, columns, qkv_weight, qkv_weight, qkv_weight),
-    )
-    def turn(value):
-        return lax.all_to_all(value, ROW, 0, 0, tiled=True)
-
-    send, proj_came = lax.optimization_barrier((send, swap_over(proj_low, "zl")))
+    up_send, down_send, proj_came = lax.optimization_barrier(
+        (up_send, down_send, swap_over(proj_low, "y"))
+    )
     left, low_send, down_left, down_low, proj_left, proj_low = one_step(
         merge_body,
-        [arr((8, 64, 512), BF)] * 2 + [arr((128, 1024), BF)] * 2 + [arr((1, 32, 1152), BF)] * 2,
+        [arr((8, 64, 512), BF)] * 2 + [arr((128, 1024), BF)] * 2 + [arr((2, 32, 1152), BF)] * 2,
         [],
         PIN,
         place,
@@ -1006,6 +1036,7 @@
             after(up_keep, moved), swap_over(up_send, "core"), keep, swap_over(send, "core"),
             down_keep, swap_over(down_send, "core"), proj_left, proj_came,
         ),
+        NO_PIN,
     )
     low_came = swap_over(low_send, "x")
     (tokens_grad,) = call(
@@ -1023,16 +1054,27 @@
         (after(moved, left), qkv_weight, tok, d_mid, vecs),
     )
 
-    proj_came = swap_over(proj_low, "zh")
-    left, _ = lax.optimization_barrier((left, tokens_grad))
-    lows = (left.astype(F32) + low_came.astype(F32)).astype(BF)
-    lows, proj_came = lax.optimization_barrier((lows, proj_came))
+    proj_left, proj_low = pair(after(proj_left, tokens_grad), swap_over(proj_low, "zh"))
+    left, proj_low, low_came = lax.optimization_barrier((left, proj_low, low_came))
+    (lows,) = one_step(add_body, [arr((8, 64, 512), BF)], [], NO_PIN, place, (left, low_came))
+    lows, proj_low = lax.optimization_barrier((lows, proj_low))
     came = turn(lows)
+    proj_came = swap_over(proj_low, "zl")
     down_low, _ = lax.optimization_barrier((down_low, lows))
     grad_down = down_left.astype(F32) + swap_over(down_low, "x").astype(F32)
     proj_total = proj_left[0].astype(F32) + proj_came[0].astype(F32)
-    result = middle + mm(after(active, lows), down_weight) + down_bias.astype(F32)
-    layer_out = result.astype(BF)[None]
+    (layer_out,) = call(
+        out_body,
+        (4,),
+        [wide, pl.BlockSpec((1024, 1024), lambda i, s: (i, 0)), fixed, whole((15, 1024))],
+        [fixed],
+        [arr((128, 1024), BF)],
+        [pltpu.VMEM((128, 1024), F32)],
+        PIN,
+        place,
+        (after(active, lows), down_weight, middle, vecs),
+    )
+    layer_out = layer_out[None]
     grad_proj = proj_total[:, :1024]
     own = lax.dynamic_slice(proj_total[:4, 1024:], (0, (me % 4) * 32), (4, 32))
     grad_up_b = proj_total[4, 1024:]

time: 200 us -> 192 us (0.960)
  Pallas kernels: 86.6 us -> 93.6 us
  other arithmetic: 6.99 us -> 0.88 us
  matrix products: 5.45 us -> 0 us
  local copies, waits for them, and re-layouts: 10.5 us -> 14.5 us
  waiting for transfers between devices: 29.7 us -> 25.8 us
  starting transfers between devices: 58 us -> 54.7 us
    pallas_call x16 -> x18, Pallas kernels: 86.6 us -> 93.6 us  [call(): pl.pallas_call(body, grid_spec=pltpu.PrefetchScalarGridSpec(num_scalar_pr...]
    dot_general x1 -> x0, matrix products: 5.45 us -> none  [mm(): return jnp.dot(left, right, preferred_element_type=F32)]
    ppermute x31, waiting for transfers between devices: 20.6 us -> 15.5 us  [swap_over(): return lax.ppermute(value, AXES, [(i, i ^ mask) for i in range(32)])]
    reshape x2 -> x8, local copies, waits for them, and re-layouts: 1.41 us -> 5.52 us  [fast_shards(): v.astype(F32).reshape(-1, 1024)]
    ppermute x31, starting transfers between devices: 41.4 us -> 37.5 us  [swap_over(): return lax.ppermute(value, AXES, [(i, i ^ mask) for i in range(32)])]
    reshape x5 -> x0, other arithmetic: 3.42 us -> none  [fast_shards(): v.astype(F32).reshape(-1, 1024)]
    convert_element_type x2 -> x0, other arithmetic: 2.7 us -> none  [the longest x1 2.01 us: fast_shards(): lows = (left.astype(F32) + low_came.astype(F32)).astype(BF)]
    all_to_all x1, waiting for transfers between devices: 0.01 us -> 2.63 us  [fast_shards(): moved = lax.all_to_all(d_all, ROW, 0, 0, tiled=True)]
  transfers between devices with their start and end apart: 35 -> 35, of which waited for: 9 -> 11; matrix products, arithmetic and copies ran while one was open for 8% -> 5% of each run, Pallas kernels for 41% -> 46%
where the time goes in v4:
time: 192 us; the launch traced here: 190 us
  Pallas kernels  93.6 us (49%)
  starting transfers between devices  54.7 us (28%)
  waiting for transfers between devices  25.8 us (13%)
  local copies, waits for them, and re-layouts  14.5 us (8%)
    pallas_call x18, Pallas kernels, call(): pl.pallas_call(body, grid_spec=pltpu.PrefetchScalarGridSpec(num_scalar_pr...  93.6 us
    ppermute x31, starting transfers between devices, swap_over(): return lax.ppermute(value, AXES, [(i, i ^ mask) for i in range(32)])  37.5 us
    ppermute x31, waiting for transfers between devices, swap_over(): return lax.ppermute(value, AXES, [(i, i ^ mask) for i in range(32)])  15.5 us
    reshape x8, local copies, waits for them, and re-layouts, fast_shards(): v.astype(F32).reshape(-1, 1024)  5.52 us
    unnamed x32, local copies, waits for them, and re-layouts  5.26 us
    all_to_all x1, waiting for transfers between devices, fast_shards(): att_in = lax.all_to_all(att_low, ROW, 0, 0, tiled=True)  4.78 us
    all_to_all x1, starting transfers between devices, turn(): return lax.all_to_all(value, ROW, 0, 0, tiled=True)  4.69 us
    all_to_all x1, starting transfers between devices, fast_shards(): att_in = lax.all_to_all(att_low, ROW, 0, 0, tiled=True)  4.63 us
  transfers between devices with their start and end apart: 35, of which 11 were waited for; matrix products, arithmetic and copies ran while one was open for 5% of the time, Pallas kernels for 46%

profile of v4, /device:TPU:0, one launch (start us, length us, event | category | flops | bytes accessed | tf_op | source)
XLA Modules:
  0.0 190.3 jit_solution(14487114258850130036)
XLA Ops:
  0.6 4.1 %collective-permute-start = (bf16[128,1024]{1,0:T(8,128)(2,1)}, bf16[128,1024]{1,0:T(8,128)(2,1)S(1)}, u32[]{:S(2)}, u32[]{:S(2)}) collective-permute-start(bf16[128,1024]{1,0:T(8,128)(2,1)} %bitcast.33), channel_id=1, source_target_pairs={{0,4},{1,5},{2,6},{3,7},{4,0},{5,1},{6,2},{7,3},{8,12},{9,13},{10,... | collective-permute-start | bytes 786440 | tf_op jit(solution)/shard_map/ppermute | solution.py:352
  4.7 1.5 collective-permute-start.1
  6.3 1.6 collective-permute-start.2
  8.2 0.7 reshape.80
  8.9 0.7 reshape.81
  9.6 0.7 reshape.74
  10.3 0.7 reshape.75
  11.0 0.7 reshape.76
  11.7 0.7 reshape.77
  12.4 0.7 reshape.78
  13.9 0.7 concatenate.9.place
  14.6 0.7 copy-done.4
  15.3 4.3 %shard_map.263 = (f32[1024,128]{1,0:T(8,128)}, f32[1024,128]{1,0:T(8,128)}, f32[1024,128]{1,0:T(8,128)}, f32[8,1024]{1,0:T(8,128)S(1)}) custom-call(s32[16]{0:T(128)S(1)} %concatenate.9.place, f32[8,128]{1,0:T(8,128)S(1)} %copy-done.4), custom_call_target="tpu_custom_call" | custom-call | bytes 1024 | tf_op jit(solution)/shard_map/pallas_call | solution.py:367
  20.2 3.8 %collective-permute-done.3.refs_3_ = bf16[128,1024]{1,0:T(8,128)(2,1)S(1)} collective-permute-done((bf16[128,1024]{1,0:T(8,128)(2,1)}, bf16[128,1024]{1,0:T(8,128)(2,1)S(1)}, u32[]{:S(2)}, u32[]{:S(2)}) %collective-permute-start.3) | collective-permute-done | bytes 262176 | tf_op jit(solution)/shard_map/ppermute | solution.py:352
  24.0 1.5 collective-permute-start.4
  25.7 1.8 collective-permute-start.6
  27.5 0.9 copy-done.1
  28.5 3.7 %shard_map.264 = (bf16[512,1024]{1,0:T(8,128)(2,1)}, bf16[512,128]{1,0:T(8,128)(2,1)S(1)}, bf16[512,128]{1,0:T(8,128)(2,1)S(1)}, bf16[512,128]{1,0:T(8,128)(2,1)S(1)}) custom-call(s32[16]{0:T(128)S(1)} %concatenate.9.place, bf16[128,1024]{1,0:T(8,128)(2,1)S(1)} %bitcast.37, bf16[128,1024]{1,0:T(8,128)(2,1)S(1)} %collective-permute-done.1.refs_1_, ...), custom_call_target="tpu_custom_call" | custom-call | bytes 1024 | tf_op jit(solution)/shard_map/pallas_call | solution.py:367
  32.1 1.2 collective-permute-start.10
  33.3 2.8 %collective-permute-start.7 = (bf16[128,1024]{1,0:T(8,128)(2,1)S(1)}, bf16[128,1024]{1,0:T(8,128)(2,1)S(1)}, u32[]{:S(2)}, u32[]{:S(2)}) collective-permute-start(bf16[128,1024]{1,0:T(8,128)(2,1)S(1)} %bitcast.29), channel_id=1, source_target_pairs={{0,4},{1,5},{2,6},{3,7},{4,0},{5,1},{6,2},{7,3},{8,12},{9,13},{10,... | collective-permute-start | bytes 786440 | tf_op jit(solution)/shard_map/ppermute | solution.py:352
  36.7 0.9 collective-permute-done.5.refs_2_
  37.6 7.4 %shard_map.265 = (f32[128,4096]{1,0:T(8,128)}, f32[1,1024]{1,0:T(1,128)S(1)}) custom-call(s32[16]{0:T(128)S(1)} %concatenate.9.place, bf16[128,1024]{1,0:T(8,128)(2,1)S(1)} %bitcast.32, bf16[4096,1024]{1,0:T(8,128)(2,1)} %down.3), custom_call_target="tpu_custom_call" | custom-call | bytes 1024 | tf_op jit(solution)/shard_map/pallas_call | solution.py:367
  45.0 1.0 collective-permute-done.6.refs_3_
  46.0 3.7 %shard_map.266 = (bf16[512,1024]{1,0:T(8,128)(2,1)}, bf16[1024,128]{1,0:T(8,128)(2,1)S(1)}, bf16[1024,128]{1,0:T(8,128)(2,1)S(1)}, bf16[1024,128]{1,0:T(8,128)(2,1)S(1)}) custom-call(s32[16]{0:T(128)S(1)} %concatenate.9.place, bf16[128,1024]{1,0:T(8,128)(2,1)S(1)} %collective-permute-done.refs_0_, bf16[128,1024]{1,0:T(8,128)(2,1)S(1)} %collective-permute-done.4.refs_1_, ...), custom_call_target="tpu_custom_call" | custom-call | bytes 1024 | tf_op jit(solution)/shard_map/pallas_call | solution.py:367
  49.7 9.4 %shard_map.267 = (f32[1024,128]{1,0:T(8,128)}, bf16[8,128,128]{2,1,0:T(8,128)(2,1)}, bf16[2,1024,1024]{2,1,0:T(8,128)(2,1)}, f32[1024,128]{1,0:T(8,128)}) custom-call(s32[16]{0:T(128)S(1)} %concatenate.9.place, bf16[1024,128]{1,0:T(8,128)(2,1)S(1)} %get-tuple-element.140.q, bf16[1024,128]{1,0:T(8,128)(2,1)S(1)} %get-tuple-element.141.k_all, ...), custom_call_target="tpu_custom_call" | custom-call | bytes 1024 | tf_op jit(solution)/shard_map/pallas_call | solution.py:367
  59.2 0.7 copy-done.9
  60.0 4.6 %all-to-all-start = ((bf16[8,128,128]{2,1,0:T(8,128)(2,1)}), bf16[8,128,128]{2,1,0:T(8,128)(2,1)S(1)}, u32[]{:S(2)}, u32[]{:S(2)}) async-start(bf16[8,128,128]{2,1,0:T(8,128)(2,1)} %get-tuple-element.146), calls=%async_computation | async-start | bytes 524288 | tf_op jit(solution)/shard_map/all_to_all | solution.py:910
  64.6 2.0 %collective-permute-start.11 = (bf16[128,1024]{1,0:T(8,128)(2,1)S(1)}, bf16[128,1024]{1,0:T(8,128)(2,1)}, u32[]{:S(2)}, u32[]{:S(2)}) collective-permute-start(bf16[128,1024]{1,0:T(8,128)(2,1)S(1)} %collective-permute-done.7.refs_12_), channel_id=1, source_target_pairs={{0,1},{1,0},{2,3},{3,2},{4,5},{5,4},{6,7},{7,6},{8,9},{9,8},{10,11... | collective-permute-start | bytes 786440 | tf_op jit(solution)/shard_map/ppermute | solution.py:352
  66.6 1.5 collective-permute-start.12
  68.1 4.8 %all-to-all-done.att = bf16[8,128,128]{2,1,0:T(8,128)(2,1)S(1)} async-done(((bf16[8,128,128]{2,1,0:T(8,128)(2,1)}), bf16[8,128,128]{2,1,0:T(8,128)(2,1)S(1)}, u32[]{:S(2)}, u32[]{:S(2)}) %all-to-all-start) | async-done | bytes 262176 | tf_op jit(solution)/shard_map/all_to_all | solution.py:910
  72.9 3.7 %shard_map.268 = (f32[128,1024]{1,0:T(8,128)}, bf16[128,1024]{1,0:T(8,128)(2,1)}, bf16[128,1024]{1,0:T(8,128)(2,1)}) custom-call(s32[16]{0:T(128)S(1)} %concatenate.9.place, bf16[8,128,128]{2,1,0:T(8,128)(2,1)S(1)} %all-to-all-done.att, bf16[128,1024]{1,0:T(8,128)(2,1)S(1)} %bitcast.38, bf16[1024,1024]{1,0:T(8,128)(2,1)} %proj_w.3, ...), custom_call_target="tpu_custom_call" | custom-call | bytes 1024 | tf_op jit(solution)/shard_map/pallas_call | solution.py:367
  76.5 1.2 collective-permute-done.12.refs_14_
  77.7 1.5 collective-permute-start.13
  79.5 2.2 %collective-permute-start.15 = (bf16[128,1024]{1,0:T(8,128)(2,1)}, bf16[128,1024]{1,0:T(8,128)(2,1)S(1)}, u32[]{:S(2)}, u32[]{:S(2)}) collective-permute-start(bf16[128,1024]{1,0:T(8,128)(2,1)} %get-tuple-element.182.normed.refs_0_), channel_id=1, source_target_pairs={{0,2},{1,3},{2,0},{3,1},{4,6},{5,7},{6,4},{7,5},{8,10},{9,11},{10,... | collective-permute-start | bytes 786440 | tf_op jit(solution)/shard_map/ppermute | solution.py:352
  81.7 1.4 collective-permute-start.16
  83.1 13.8 %shard_map.269 = (bf16[128,4096]{1,0:T(8,128)(2,1)}, f32[128,1024]{1,0:T(8,128)}, bf16[8,128,128]{2,1,0:T(8,128)(2,1)}, bf16[2,8,32,1152]{3,2,1,0:T(8,128)(2,1)}, bf16[2,8,32,1152]{3,2,1,0:T(8,128)(2,1)}) custom-call(s32[16]{0:T(128)S(1)} %concatenate.9.place, bf16[128,1024]{1,0:T(8,128)(2,1)} %get-tuple-element.182.normed.refs_0_, ...), custom_call_target="tpu_custom_call" | custom-call | bytes 1024 | tf_op jit(solution)/shard_map/pallas_call | solution.py:367
  97.1 0.8 copy-done.14
  97.8 3.4 %all-to-all-start.1 = ((bf16[8,128,128]{2,1,0:T(8,128)(2,1)}), bf16[8,128,128]{2,1,0:T(8,128)(2,1)S(1)}, u32[]{:S(2)}, u32[]{:S(2)}) async-start(bf16[8,128,128]{2,1,0:T(8,128)(2,1)} %get-tuple-element.164), calls=%async_computation.1 | async-start | bytes 524288 | tf_op jit(solution)/shard_map/all_to_all | solution.py:947
  101.3 2.0 %collective-permute-start.18 = (bf16[128,1024]{1,0:T(8,128)(2,1)}, bf16[128,1024]{1,0:T(8,128)(2,1)S(1)}, u32[]{:S(2)}, u32[]{:S(2)}) collective-permute-start(bf16[128,1024]{1,0:T(8,128)(2,1)} %collective-permute-done.11.refs_13_), channel_id=1, source_target_pairs={{0,2},{1,3},{2,0},{3,1},{4,6},{5,7},{6,4},{7,5},{8,10},{9,11},{10,... | collective-permute-start | bytes 786440 | tf_op jit(solution)/shard_map/ppermute | solution.py:352
  103.3 1.4 collective-permute-start.19
  105.2 1.6 collective-permute-start.21
  106.8 1.3 copy-done.3
  108.1 1.6 shard_map.270
  109.6 1.5 collective-permute-start.22
  111.1 9.4 %shard_map.271 = (bf16[8,128,384]{2,1,0:T(8,128)(2,1)}, f32[1,384]{1,0:T(1,128)S(1)}) custom-call(s32[16]{0:T(128)S(1)} %concatenate.9.place, bf16[2,1024,1024]{2,1,0:T(8,128)(2,1)} %get-tuple-element.163.probs, bf16[8,128,128]{2,1,0:T(8,128)(2,1)S(1)} %all-to-all-done.1.d_att, f32[1024,128]{1,0:T(8,128)} %get-tuple-element.169.att_f, ...), custom_call_target="tpu_custom_call" | custom-call | bytes 1024 | tf_op jit(solution)/shard_map/pallas_call | solution.py:367
  120.5 6.2 %shard_map.272 = (bf16[2,256,512]{2,1,0:T(8,128)(2,1)}, bf16[2,256,512]{2,1,0:T(8,128)(2,1)}) custom-call(s32[16]{0:T(128)S(1)} %concatenate.9.place, bf16[512,1024]{1,0:T(8,128)(2,1)} %get-tuple-element.172.h0, bf16[512,1024]{1,0:T(8,128)(2,1)} %get-tuple-element.173.h1, bf16[8,128,384]{2,1,0:T(8,128)(2,1)} %get-tuple-element.178.d_all, ...), custom_call_target="tpu_custom_call" | custom-call | bytes 1024 | tf_op jit(solution)/shard_map/pallas_call | solution.py:367
  126.7 4.5 %all-to-all-start.2 = ((bf16[8,128,384]{2,1,0:T(8,128)(2,1)}), bf16[8,128,384]{2,1,0:T(8,128)(2,1)S(1)}, u32[]{:S(2)}, u32[]{:S(2)}) async-start(bf16[8,128,384]{2,1,0:T(8,128)(2,1)} %get-tuple-element.178.d_all), calls=%async_computation.2 | async-start | bytes 1572864 | tf_op jit(solution)/shard_map/all_to_all | solution.py:997
  131.9 2.1 %collective-permute-start.23 = (bf16[4,32,1152]{2,1,0:T(8,128)(2,1)S(1)}, bf16[4,32,1152]{2,1,0:T(8,128)(2,1)S(1)}, u32[]{:S(2)}, u32[]{:S(2)}) collective-permute-start(bf16[4,32,1152]{2,1,0:T(8,128)(2,1)S(1)} %get-tuple-element.181), channel_id=1, source_target_pairs={{0,1},{1,0},{2,3},{3,2},{4,5},{5,4},{6,7},{7,6},{8,9},{9,8},{10,11... | collective-permute-start | bytes 884744 | tf_op jit(solution)/shard_map/ppermute | solution.py:352
  134.0 9.9 %shard_map.274 = (bf16[2,128,1024]{2,1,0:T(8,128)(2,1)}, bf16[2,128,1024]{2,1,0:T(8,128)(2,1)}, bf16[2,256,512]{2,1,0:T(8,128)(2,1)}, bf16[2,256,512]{2,1,0:T(8,128)(2,1)}) custom-call(s32[16]{0:T(128)S(1)} %concatenate.9.place, bf16[128,1024]{1,0:T(8,128)(2,1)} %get-tuple-element.182.normed.refs_0_, bf16[128,1024]{1,0:T(8,128)(2,1)} %copy-done.12, ...), custom_call_target="tpu_custom_call" | custom-call | bytes 1024 | tf_op jit(solution)/shard_map/pallas_call | solution.py:367
  143.9 3.7 %collective-permute-done.23.refs_7_ = bf16[4,32,1152]{2,1,0:T(8,128)(2,1)S(1)} collective-permute-done((bf16[4,32,1152]{2,1,0:T(8,128)(2,1)S(1)}, bf16[4,32,1152]{2,1,0:T(8,128)(2,1)S(1)}, u32[]{:S(2)}, u32[]{:S(2)}) %collective-permute-start.23) | collective-permute-done | bytes 294944 | tf_op jit(solution)/shard_map/ppermute | solution.py:352
  148.1 2.6 %all-to-all-done.2.came = bf16[8,128,384]{2,1,0:T(8,128)(2,1)S(1)} async-done(((bf16[8,128,384]{2,1,0:T(8,128)(2,1)}), bf16[8,128,384]{2,1,0:T(8,128)(2,1)S(1)}, u32[]{:S(2)}, u32[]{:S(2)}) %all-to-all-start.2) | async-done | bytes 786464 | tf_op jit(solution)/shard_map/all_to_all | solution.py:997
  150.7 0.8 copy-done.6
  151.6 2.8 %shard_map.275 = (bf16[8,64,512]{2,1,0:T(8,128)(2,1)S(1)}, bf16[8,64,512]{2,1,0:T(8,128)(2,1)S(1)}, bf16[128,1024]{1,0:T(8,128)(2,1)S(1)}, bf16[128,1024]{1,0:T(...) custom-call(s32[16]{0:T(128)S(1)} %concatenate.9.place, ...), custom_call_target="tpu_custom_call" | custom-call | bytes 1024 | tf_op jit(solution)/shard_map/pallas_call | solution.py:367
  154.4 1.5 collective-permute-start.28
  155.8 6.7 %shard_map.276 = f32[128,1024]{1,0:T(8,128)} custom-call(s32[16]{0:T(128)S(1)} %concatenate.9.place, bf16[8,128,384]{2,1,0:T(8,128)(2,1)} %copy-done.5, bf16[1024,3072]{1,0:T(8,128)(2,1)} %w.1, bf16[128,1024]{1,0:T(8,128)(2,1)S(1)} %bitcast.39, f32[128,1024]{1,0:T(8,128)} %get-tuple-element.211.d_mid, f32[15,1024]{1,0:T(8,128)S(1)} %concatenate.11.refs_4_.vecs.refs_24_), custom_call_target="tpu_custom_call" | custom-call | bytes 1024 | tf_op jit(solution)/shard_map/pallas_call | solution.py:367
  162.5 2.1 %collective-permute-done.27.came = bf16[2,32,1152]{2,1,0:T(8,128)(2,1)S(1)} collective-permute-done((bf16[2,32,1152]{2,1,0:T(8,128)(2,1)S(1)}, bf16[2,32,1152]{2,1,0:T(8,128)(2,1)S(1)}, u32[]{:S(2)}, u32[]{:S(2)}) %collective-permute-start.27) | collective-permute-done | bytes 147488 | tf_op jit(solution)/shard_map/ppermute | solution.py:352
  165.2 2.2 %collective-permute-done.28.came = bf16[8,64,512]{2,1,0:T(8,128)(2,1)S(1)} collective-permute-done((bf16[8,64,512]{2,1,0:T(8,128)(2,1)S(1)}, bf16[8,64,512]{2,1,0:T(8,128)(2,1)S(1)}, u32[]{:S(2)}, u32[]{:S(2)}) %collective-permute-start.28) | collective-permute-done | bytes 524320 | tf_op jit(solution)/shard_map/ppermute | solution.py:352
  167.4 1.5 shard_map.278
  169.3 4.7 %all-to-all-start.3 = ((bf16[8,64,512]{2,1,0:T(8,128)(2,1)}), bf16[8,64,512]{2,1,0:T(8,128)(2,1)S(1)}, u32[]{:S(2)}, u32[]{:S(2)}) async-start(bf16[8,64,512]{2,1,0:T(8,128)(2,1)} %shard_map.278), calls=%async_computation.3 | async-start | bytes 1048576 | tf_op jit(solution)/shard_map/all_to_all | solution.py:995
  174.0 1.5 collective-permute-start.30
  175.5 6.7 %shard_map.279 = bf16[128,1024]{1,0:T(8,128)(2,1)} custom-call(s32[16]{0:T(128)S(1)} %concatenate.9.place, bf16[128,4096]{1,0:T(8,128)(2,1)} %get-tuple-element.220.active, bf16[4096,1024]{1,0:T(8,128)(2,1)} %down.3, f32[128,1024]{1,0:T(8,128)} %get-tuple-element.154.middle, f32[15,1024]{1,0:T(8,128)S(1)} %concatenate.11.refs_4_.vecs.refs_24_), custom_call_target="tpu_custom_call" | custom-call | bytes 1024 | tf_op jit(solution)/shard_map/pallas_call | solution.py:367
  184.0 0.9 convert_add_fusion
  184.8 2.9 %all-to-all-done.3.came = bf16[8,64,512]{2,1,0:T(8,128)(2,1)S(1)} async-done(((bf16[8,64,512]{2,1,0:T(8,128)(2,1)}), bf16[8,64,512]{2,1,0:T(8,128)(2,1)S(1)}, u32[]{:S(2)}, u32[]{:S(2)}) %all-to-all-start.3) | async-done | bytes 524320 | tf_op jit(solution)/shard_map/all_to_all | solution.py:995
  187.7 1.5 shard_map.280
  (77 shorter events, 8.6 us)
Async XLA Ops:
  0.6 19.0 %collective-permute-start = (bf16[128,1024]{1,0:T(8,128)(2,1)}, bf16[128,1024]{1,0:T(8,128)(2,1)S(1)}, u32[]{:S(2)}, u32[]{:S(2)}) collective-permute-start(bf16[128,1024]{1,0:T(8,128)(2,1)} %bitcast.33), channel_id=1, source_target_pairs={{0,4},{1,5},{2,6},{3,7},{4,0},{5,1},{6,2},{7,3},{8,12},{9,13},{10,... | collective-permute-start | bytes 786440 | tf_op jit(solution)/shard_map/ppermute | solution.py:352
  4.7 14.9 %collective-permute-start.1 = (bf16[128,1024]{1,0:T(8,128)(2,1)}, bf16[128,1024]{1,0:T(8,128)(2,1)S(1)}, u32[]{:S(2)}, u32[]{:S(2)}) collective-permute-start(bf16[128,1024]{1,0:T(8,128)(2,1)} %bitcast.34), channel_id=1, source_target_pairs={{0,1},{1,0},{2,3},{3,2},{4,5},{5,4},{6,7},{7,6},{8,9},{9,8},{10,11... | collective-permute-start | bytes 786440 | tf_op jit(solution)/shard_map/ppermute | solution.py:352
  6.3 13.9 %collective-permute-start.2 = (bf16[128,1024]{1,0:T(8,128)(2,1)}, bf16[128,1024]{1,0:T(8,128)(2,1)S(1)}, u32[]{:S(2)}, u32[]{:S(2)}) collective-permute-start(bf16[128,1024]{1,0:T(8,128)(2,1)} %bitcast.35), channel_id=1, source_target_pairs={{0,2},{1,3},{2,0},{3,1},{4,6},{5,7},{6,4},{7,5},{8,10},{9,11},{10,... | collective-permute-start | bytes 786440 | tf_op jit(solution)/shard_map/ppermute | solution.py:352
  7.8 16.2 %collective-permute-start.3 = (bf16[128,1024]{1,0:T(8,128)(2,1)}, bf16[128,1024]{1,0:T(8,128)(2,1)S(1)}, u32[]{:S(2)}, u32[]{:S(2)}) collective-permute-start(bf16[128,1024]{1,0:T(8,128)(2,1)} %bitcast.36), channel_id=1, source_target_pairs={{0,3},{1,2},{2,1},{3,0},{4,7},{5,6},{6,5},{7,4},{8,11},{9,10},{10,... | collective-permute-start | bytes 786440 | tf_op jit(solution)/shard_map/ppermute | solution.py:352
  14.6 0.7 copy-start.4
  24.0 12.1 %collective-permute-start.4 = (bf16[128,1024]{1,0:T(8,128)(2,1)S(1)}, bf16[128,1024]{1,0:T(8,128)(2,1)S(1)}, u32[]{:S(2)}, u32[]{:S(2)}) collective-permute-start(bf16[128,1024]{1,0:T(8,128)(2,1)S(1)} %collective-permute-done.refs_0_), channel_id=1, source_target_pairs={{0,1},{1,0},{2,3},{3,2},{4,5},{5,4},{6,7},{7,6},{8,9},{9,8},{10,11... | collective-permute-start | bytes 786440 | tf_op jit(solution)/shard_map/ppermute | solution.py:352
  25.5 12.1 %collective-permute-start.5 = (bf16[128,1024]{1,0:T(8,128)(2,1)S(1)}, bf16[128,1024]{1,0:T(8,128)(2,1)S(1)}, u32[]{:S(2)}, u32[]{:S(2)}) collective-permute-start(bf16[128,1024]{1,0:T(8,128)(2,1)S(1)} %collective-permute-done.refs_0_), channel_id=1, source_target_pairs={{0,2},{1,3},{2,0},{3,1},{4,6},{5,7},{6,4},{7,5},{8,10},{9,11},{10,... | collective-permute-start | bytes 786440 | tf_op jit(solution)/shard_map/ppermute | solution.py:352
  25.7 20.3 %collective-permute-start.6 = (bf16[128,1024]{1,0:T(8,128)(2,1)S(1)}, bf16[128,1024]{1,0:T(8,128)(2,1)S(1)}, u32[]{:S(2)}, u32[]{:S(2)}) collective-permute-start(bf16[128,1024]{1,0:T(8,128)(2,1)S(1)} %collective-permute-done.refs_0_), channel_id=1, source_target_pairs={{0,3},{1,2},{2,1},{3,0},{4,7},{5,6},{6,5},{7,4},{8,11},{9,10},{10,... | collective-permute-start | bytes 786440 | tf_op jit(solution)/shard_map/ppermute | solution.py:352
  27.5 0.9 copy-start.1
  28.5 3.7 %copy-start = (bf16[1,128,1024]{2,1,0:T(8,128)(2,1)S(1)}, bf16[1,128,1024]{2,1,0:T(8,128)(2,1)}, u32[]{:S(2)}) copy-start(bf16[1,128,1024]{2,1,0:T(8,128)(2,1)} %param.30) | copy-start | bytes 786436
  32.1 27.0 %collective-permute-start.10 = (bf16[128,1024]{1,0:T(8,128)(2,1)S(1)}, bf16[128,1024]{1,0:T(8,128)(2,1)S(1)}, u32[]{:S(2)}, u32[]{:S(2)}) collective-permute-start(bf16[128,1024]{1,0:T(8,128)(2,1)S(1)} %bitcast.28), channel_id=1, source_target_pairs={{0,3},{1,2},{2,1},{3,0},{4,7},{5,6},{6,5},{7,4},{8,11},{9,10},{10,... | collective-permute-start | bytes 786440 | tf_op jit(solution)/shard_map/ppermute | solution.py:352
  33.3 25.9 %collective-permute-start.7 = (bf16[128,1024]{1,0:T(8,128)(2,1)S(1)}, bf16[128,1024]{1,0:T(8,128)(2,1)S(1)}, u32[]{:S(2)}, u32[]{:S(2)}) collective-permute-start(bf16[128,1024]{1,0:T(8,128)(2,1)S(1)} %bitcast.29), channel_id=1, source_target_pairs={{0,4},{1,5},{2,6},{3,7},{4,0},{5,1},{6,2},{7,3},{8,12},{9,13},{10,... | collective-permute-start | bytes 786440 | tf_op jit(solution)/shard_map/ppermute | solution.py:352
  36.1 23.1 %collective-permute-start.8 = (bf16[128,1024]{1,0:T(8,128)(2,1)S(1)}, bf16[128,1024]{1,0:T(8,128)(2,1)S(1)}, u32[]{:S(2)}, u32[]{:S(2)}) collective-permute-start(bf16[128,1024]{1,0:T(8,128)(2,1)S(1)} %bitcast.30), channel_id=1, source_target_pairs={{0,1},{1,0},{2,3},{3,2},{4,5},{5,4},{6,7},{7,6},{8,9},{9,8},{10,11... | collective-permute-start | bytes 786440 | tf_op jit(solution)/shard_map/ppermute | solution.py:352
  37.5 21.7 %collective-permute-start.9 = (bf16[128,1024]{1,0:T(8,128)(2,1)S(1)}, bf16[128,1024]{1,0:T(8,128)(2,1)S(1)}, u32[]{:S(2)}, u32[]{:S(2)}) collective-permute-start(bf16[128,1024]{1,0:T(8,128)(2,1)S(1)} %bitcast.31), channel_id=1, source_target_pairs={{0,2},{1,3},{2,0},{3,1},{4,6},{5,7},{6,4},{7,5},{8,10},{9,11},{10,... | collective-permute-start | bytes 786440 | tf_op jit(solution)/shard_map/ppermute | solution.py:352
  46.0 26.8 %copy-start.2 = (bf16[1,128,1024]{2,1,0:T(8,128)(2,1)S(1)}, bf16[1,128,1024]{2,1,0:T(8,128)(2,1)}, u32[]{:S(2)}) copy-start(bf16[1,128,1024]{2,1,0:T(8,128)(2,1)} %param.16) | copy-start | bytes 786436
  59.2 37.8 %copy-start.7 = (bf16[128,1024]{1,0:T(8,128)(2,1)}, bf16[128,1024]{1,0:T(8,128)(2,1)S(1)}, u32[]{:S(2)}) copy-start(bf16[128,1024]{1,0:T(8,128)(2,1)S(1)} %collective-permute-done.10.refs_11_) | copy-start | bytes 786436
  59.2 37.8 %copy-start.8 = (bf16[128,1024]{1,0:T(8,128)(2,1)}, bf16[128,1024]{1,0:T(8,128)(2,1)S(1)}, u32[]{:S(2)}) copy-start(bf16[128,1024]{1,0:T(8,128)(2,1)S(1)} %collective-permute-done.7.refs_12_) | copy-start | bytes 786436
  59.2 0.7 copy-start.9
  59.9 37.0 %copy-start.10 = (bf16[128,1024]{1,0:T(8,128)(2,1)}, bf16[128,1024]{1,0:T(8,128)(2,1)S(1)}, u32[]{:S(2)}) copy-start(bf16[128,1024]{1,0:T(8,128)(2,1)S(1)} %collective-permute-done.9.refs_10_) | copy-start | bytes 786436
  60.0 12.9 %all-to-all-start = ((bf16[8,128,128]{2,1,0:T(8,128)(2,1)}), bf16[8,128,128]{2,1,0:T(8,128)(2,1)S(1)}, u32[]{:S(2)}, u32[]{:S(2)}) async-start(bf16[8,128,128]{2,1,0:T(8,128)(2,1)} %get-tuple-element.146), calls=%async_computation | async-start | bytes 524288 | tf_op jit(solution)/shard_map/all_to_all | solution.py:910
  64.6 11.9 %collective-permute-start.11 = (bf16[128,1024]{1,0:T(8,128)(2,1)S(1)}, bf16[128,1024]{1,0:T(8,128)(2,1)}, u32[]{:S(2)}, u32[]{:S(2)}) collective-permute-start(bf16[128,1024]{1,0:T(8,128)(2,1)S(1)} %collective-permute-done.7.refs_12_), channel_id=1, source_target_pairs={{0,1},{1,0},{2,3},{3,2},{4,5},{5,4},{6,7},{7,6},{8,9},{9,8},{10,11... | collective-permute-start | bytes 786440 | tf_op jit(solution)/shard_map/ppermute | solution.py:352
  66.6 11.1 %collective-permute-start.12 = (bf16[128,1024]{1,0:T(8,128)(2,1)S(1)}, bf16[128,1024]{1,0:T(8,128)(2,1)S(1)}, u32[]{:S(2)}, u32[]{:S(2)}) collective-permute-start(bf16[128,1024]{1,0:T(8,128)(2,1)S(1)} %collective-permute-done.7.refs_12_), channel_id=1, source_target_pairs={{0,2},{1,3},{2,0},{3,1},{4,6},{5,7},{6,4},{7,5},{8,10},{9,11},{10,... | collective-permute-start | bytes 786440 | tf_op jit(solution)/shard_map/ppermute | solution.py:352
  77.7 19.3 %copy-start.11 = (bf16[128,1024]{1,0:T(8,128)(2,1)}, bf16[128,1024]{1,0:T(8,128)(2,1)S(1)}, u32[]{:S(2)}) copy-start(bf16[128,1024]{1,0:T(8,128)(2,1)S(1)} %collective-permute-done.12.refs_14_) | copy-start | bytes 786436
  77.7 19.3 %collective-permute-start.13 = (bf16[128,1024]{1,0:T(8,128)(2,1)}, bf16[128,1024]{1,0:T(8,128)(2,1)}, u32[]{:S(2)}, u32[]{:S(2)}) collective-permute-start(bf16[128,1024]{1,0:T(8,128)(2,1)} %get-tuple-element.182.normed.refs_0_), channel_id=1, source_target_pairs={{0,4},{1,5},{2,6},{3,7},{4,0},{5,1},{6,2},{7,3},{8,12},{9,13},{10,... | collective-permute-start | bytes 786440 | tf_op jit(solution)/shard_map/ppermute | solution.py:352
  79.2 17.8 %collective-permute-start.14 = (bf16[128,1024]{1,0:T(8,128)(2,1)}, bf16[128,1024]{1,0:T(8,128)(2,1)S(1)}, u32[]{:S(2)}, u32[]{:S(2)}) collective-permute-start(bf16[128,1024]{1,0:T(8,128)(2,1)} %get-tuple-element.182.normed.refs_0_), channel_id=1, source_target_pairs={{0,1},{1,0},{2,3},{3,2},{4,5},{5,4},{6,7},{7,6},{8,9},{9,8},{10,11... | collective-permute-start | bytes 786440 | tf_op jit(solution)/shard_map/ppermute | solution.py:352
  79.5 17.5 %collective-permute-start.15 = (bf16[128,1024]{1,0:T(8,128)(2,1)}, bf16[128,1024]{1,0:T(8,128)(2,1)S(1)}, u32[]{:S(2)}, u32[]{:S(2)}) collective-permute-start(bf16[128,1024]{1,0:T(8,128)(2,1)} %get-tuple-element.182.normed.refs_0_), channel_id=1, source_target_pairs={{0,2},{1,3},{2,0},{3,1},{4,6},{5,7},{6,4},{7,5},{8,10},{9,11},{10,... | collective-permute-start | bytes 786440 | tf_op jit(solution)/shard_map/ppermute | solution.py:352
  81.7 15.3 %collective-permute-start.16 = (bf16[128,1024]{1,0:T(8,128)(2,1)}, bf16[128,1024]{1,0:T(8,128)(2,1)S(1)}, u32[]{:S(2)}, u32[]{:S(2)}) collective-permute-start(bf16[128,1024]{1,0:T(8,128)(2,1)} %get-tuple-element.182.normed.refs_0_), channel_id=1, source_target_pairs={{0,3},{1,2},{2,1},{3,0},{4,7},{5,6},{6,5},{7,4},{8,11},{9,10},{10,... | collective-permute-start | bytes 786440 | tf_op jit(solution)/shard_map/ppermute | solution.py:352
  97.0 0.8 copy-start.12
  97.0 9.8 %copy-start.13 = (bf16[128,1024]{1,0:T(8,128)(2,1)}, bf16[128,1024]{1,0:T(8,128)(2,1)S(1)}, u32[]{:S(2)}) copy-start(bf16[128,1024]{1,0:T(8,128)(2,1)S(1)} %collective-permute-done.15.refs_2_) | copy-start | bytes 786436
  97.0 0.8 copy-start.14
  97.8 9.0 %collective-permute-start.17 = (bf16[16,32,1152]{2,1,0:T(8,128)(2,1)}, bf16[16,32,1152]{2,1,0:T(8,128)(2,1)S(1)}, u32[]{:S(2)}, u32[]{:S(2)}) collective-permute-start(bf16[16,32,1152]{2,1,0:T(8,128)(2,1)} %bitcast.44), channel_id=1, source_target_pairs={{0,8},{1,9},{2,10},{3,11},{4,12},{5,13},{6,14},{7,15},{8,0},{9,1},... | collective-permute-start | bytes 3538952 | tf_op jit(solution)/shard_map/ppermute | solution.py:352
  97.8 13.3 %all-to-all-start.1 = ((bf16[8,128,128]{2,1,0:T(8,128)(2,1)}), bf16[8,128,128]{2,1,0:T(8,128)(2,1)S(1)}, u32[]{:S(2)}, u32[]{:S(2)}) async-start(bf16[8,128,128]{2,1,0:T(8,128)(2,1)} %get-tuple-element.164), calls=%async_computation.1 | async-start | bytes 524288 | tf_op jit(solution)/shard_map/all_to_all | solution.py:947
  101.3 25.4 %collective-permute-start.18 = (bf16[128,1024]{1,0:T(8,128)(2,1)}, bf16[128,1024]{1,0:T(8,128)(2,1)S(1)}, u32[]{:S(2)}, u32[]{:S(2)}) collective-permute-start(bf16[128,1024]{1,0:T(8,128)(2,1)} %collective-permute-done.11.refs_13_), channel_id=1, source_target_pairs={{0,2},{1,3},{2,0},{3,1},{4,6},{5,7},{6,4},{7,5},{8,10},{9,11},{10,... | collective-permute-start | bytes 786440 | tf_op jit(solution)/shard_map/ppermute | solution.py:352
  103.3 23.4 %collective-permute-start.19 = (bf16[128,1024]{1,0:T(8,128)(2,1)}, bf16[128,1024]{1,0:T(8,128)(2,1)}, u32[]{:S(2)}, u32[]{:S(2)}) collective-permute-start(bf16[128,1024]{1,0:T(8,128)(2,1)} %collective-permute-done.13.refs_4_), channel_id=1, source_target_pairs={{0,1},{1,0},{2,3},{3,2},{4,5},{5,4},{6,7},{7,6},{8,9},{9,8},{10,11... | collective-permute-start | bytes 786440 | tf_op jit(solution)/shard_map/ppermute | solution.py:352
  104.6 22.1 %collective-permute-start.20 = (bf16[128,1024]{1,0:T(8,128)(2,1)}, bf16[128,1024]{1,0:T(8,128)(2,1)}, u32[]{:S(2)}, u32[]{:S(2)}) collective-permute-start(bf16[128,1024]{1,0:T(8,128)(2,1)} %collective-permute-done.13.refs_4_), channel_id=1, source_target_pairs={{0,2},{1,3},{2,0},{3,1},{4,6},{5,7},{6,4},{7,5},{8,10},{9,11},{10,... | collective-permute-start | bytes 786440 | tf_op jit(solution)/shard_map/ppermute | solution.py:352
  105.2 21.5 %collective-permute-start.21 = (bf16[128,1024]{1,0:T(8,128)(2,1)}, bf16[128,1024]{1,0:T(8,128)(2,1)}, u32[]{:S(2)}, u32[]{:S(2)}) collective-permute-start(bf16[128,1024]{1,0:T(8,128)(2,1)} %collective-permute-done.13.refs_4_), channel_id=1, source_target_pairs={{0,3},{1,2},{2,1},{3,0},{4,7},{5,6},{6,5},{7,4},{8,11},{9,10},{10,... | collective-permute-start | bytes 786440 | tf_op jit(solution)/shard_map/ppermute | solution.py:352
  106.8 1.3 copy-start.3
  109.6 21.6 %collective-permute-start.22 = (bf16[8,32,1152]{2,1,0:T(8,128)(2,1)}, bf16[8,32,1152]{2,1,0:T(8,128)(2,1)S(1)}, u32[]{:S(2)}, u32[]{:S(2)}) collective-permute-start(bf16[8,32,1152]{2,1,0:T(8,128)(2,1)} %get-tuple-element.167), channel_id=1, source_target_pairs={{0,16},{1,17},{2,18},{3,19},{4,20},{5,21},{6,22},{7,23},{8,24},{9,... | collective-permute-start | bytes 1769480 | tf_op jit(solution)/shard_map/ppermute | solution.py:352
  126.7 7.3 %copy-start.15 = (bf16[128,1024]{1,0:T(8,128)(2,1)}, bf16[128,1024]{1,0:T(8,128)(2,1)S(1)}, u32[]{:S(2)}) copy-start(bf16[128,1024]{1,0:T(8,128)(2,1)S(1)} %collective-permute-done.18.refs_15_) | copy-start | bytes 786436
  126.7 24.0 %all-to-all-start.2 = ((bf16[8,128,384]{2,1,0:T(8,128)(2,1)}), bf16[8,128,384]{2,1,0:T(8,128)(2,1)S(1)}, u32[]{:S(2)}, u32[]{:S(2)}) async-start(bf16[8,128,384]{2,1,0:T(8,128)(2,1)} %get-tuple-element.178.d_all), calls=%async_computation.2 | async-start | bytes 1572864 | tf_op jit(solution)/shard_map/all_to_all | solution.py:997
  131.9 15.7 %collective-permute-start.23 = (bf16[4,32,1152]{2,1,0:T(8,128)(2,1)S(1)}, bf16[4,32,1152]{2,1,0:T(8,128)(2,1)S(1)}, u32[]{:S(2)}, u32[]{:S(2)}) collective-permute-start(bf16[4,32,1152]{2,1,0:T(8,128)(2,1)S(1)} %get-tuple-element.181), channel_id=1, source_target_pairs={{0,1},{1,0},{2,3},{3,2},{4,5},{5,4},{6,7},{7,6},{8,9},{9,8},{10,11... | collective-permute-start | bytes 884744 | tf_op jit(solution)/shard_map/ppermute | solution.py:352
  134.0 16.8 %collective-permute-start.25 = (bf16[2,256,512]{2,1,0:T(8,128)(2,1)}, bf16[2,256,512]{2,1,0:T(8,128)(2,1)S(1)}, u32[]{:S(2)}, u32[]{:S(2)}) collective-permute-start(bf16[2,256,512]{2,1,0:T(8,128)(2,1)} %get-tuple-element.203), channel_id=1, source_target_pairs={{0,8},{1,9},{2,10},{3,11},{4,12},{5,13},{6,14},{7,15},{8,0},{9,1},... | collective-permute-start | bytes 1572872 | tf_op jit(solution)/shard_map/ppermute | solution.py:352
  147.6 3.2 %collective-permute-start.24 = (bf16[2,256,512]{2,1,0:T(8,128)(2,1)}, bf16[2,256,512]{2,1,0:T(8,128)(2,1)}, u32[]{:S(2)}, u32[]{:S(2)}) collective-permute-start(bf16[2,256,512]{2,1,0:T(8,128)(2,1)} %get-tuple-element.201), channel_id=1, source_target_pairs={{0,8},{1,9},{2,10},{3,11},{4,12},{5,13},{6,14},{7,15},{8,0},{9,1},... | collective-permute-start | bytes 1572872 | tf_op jit(solution)/shard_map/ppermute | solution.py:352
  147.6 3.2 %collective-permute-start.26 = (bf16[2,128,1024]{2,1,0:T(8,128)(2,1)}, bf16[2,128,1024]{2,1,0:T(8,128)(2,1)}, u32[]{:S(2)}, u32[]{:S(2)}) collective-permute-start(bf16[2,128,1024]{2,1,0:T(8,128)(2,1)} %get-tuple-element.205), channel_id=1, source_target_pairs={{0,8},{1,9},{2,10},{3,11},{4,12},{5,13},{6,14},{7,15},{8,0},{9,1},... | collective-permute-start | bytes 1572872 | tf_op jit(solution)/shard_map/ppermute | solution.py:352
  150.7 5.1 %copy-start.5 = (bf16[8,128,384]{2,1,0:T(8,128)(2,1)}, bf16[8,128,384]{2,1,0:T(8,128)(2,1)S(1)}, u32[]{:S(2)}) copy-start(bf16[8,128,384]{2,1,0:T(8,128)(2,1)S(1)} %all-to-all-done.2.came) | copy-start | bytes 2359300
  150.7 0.8 copy-start.6
  154.4 13.1 %collective-permute-start.28 = (bf16[8,64,512]{2,1,0:T(8,128)(2,1)S(1)}, bf16[8,64,512]{2,1,0:T(8,128)(2,1)S(1)}, u32[]{:S(2)}, u32[]{:S(2)}) collective-permute-start(bf16[8,64,512]{2,1,0:T(8,128)(2,1)S(1)} %get-tuple-element.215), channel_id=1, source_target_pairs={{0,16},{1,17},{2,18},{3,19},{4,20},{5,21},{6,22},{7,23},{8,24},{9,... | collective-permute-start | bytes 1572872 | tf_op jit(solution)/shard_map/ppermute | solution.py:352
  155.8 8.8 %collective-permute-start.27 = (bf16[2,32,1152]{2,1,0:T(8,128)(2,1)S(1)}, bf16[2,32,1152]{2,1,0:T(8,128)(2,1)S(1)}, u32[]{:S(2)}, u32[]{:S(2)}) collective-permute-start(bf16[2,32,1152]{2,1,0:T(8,128)(2,1)S(1)} %get-tuple-element.213), channel_id=1, source_target_pairs={{0,4},{1,5},{2,6},{3,7},{4,0},{5,1},{6,2},{7,3},{8,12},{9,13},{10,... | collective-permute-start | bytes 442376 | tf_op jit(solution)/shard_map/ppermute | solution.py:352
  168.9 13.3 %collective-permute-start.29 = (bf16[1,32,1152]{2,1,0:T(8,128)(2,1)S(1)}, bf16[1,32,1152]{2,1,0:T(8,128)(2,1)S(1)}, u32[]{:S(2)}, u32[]{:S(2)}) collective-permute-start(bf16[1,32,1152]{2,1,0:T(8,128)(2,1)S(1)} %get-tuple-element.225), channel_id=1, source_target_pairs={{0,2},{1,3},{2,0},{3,1},{4,6},{5,7},{6,4},{7,5},{8,10},{9,11},{10,... | collective-permute-start | bytes 221192 | tf_op jit(solution)/shard_map/ppermute | solution.py:352
  169.3 18.4 %all-to-all-start.3 = ((bf16[8,64,512]{2,1,0:T(8,128)(2,1)}), bf16[8,64,512]{2,1,0:T(8,128)(2,1)S(1)}, u32[]{:S(2)}, u32[]{:S(2)}) async-start(bf16[8,64,512]{2,1,0:T(8,128)(2,1)} %shard_map.278), calls=%async_computation.3 | async-start | bytes 1048576 | tf_op jit(solution)/shard_map/all_to_all | solution.py:995
  174.0 10.0 %collective-permute-start.30 = (bf16[128,1024]{1,0:T(8,128)(2,1)S(1)}, bf16[128,1024]{1,0:T(8,128)(2,1)S(1)}, u32[]{:S(2)}, u32[]{:S(2)}) collective-permute-start(bf16[128,1024]{1,0:T(8,128)(2,1)S(1)} %get-tuple-element.229), channel_id=1, source_target_pairs={{0,16},{1,17},{2,18},{3,19},{4,20},{5,21},{6,22},{7,23},{8,24},{9,... | collective-permute-start | bytes 786440 | tf_op jit(solution)/shard_map/ppermute | solution.py:352

commit v5 on v4

--- a/solution.py
+++ b/solution.py
@@ -705,21 +705,21 @@
     send[...] = total[half:]
 
 
-def add_body(place, left, came, out):
-    out[...] = (left[...].astype(F32) + came[...].astype(F32)).astype(BF)
+def low_body(place, up_left, up_came, qkv_left, qkv_came, out):
+    out[:, :32] = (up_left[...].astype(F32) + up_came[...].astype(F32)).astype(BF)
+    out[:, 32:] = (qkv_left[...].astype(F32) + qkv_came[...].astype(F32)).astype(BF)
 
 
 def merge_body(place, *refs):
-    keeps, cames = refs[0:6:2], refs[1:6:2]
-    proj_left, proj_came, left, send, down_left, down_send, proj_keep, proj_send = refs[6:]
+    up, up_came, down, down_came, proj_left, proj_came = refs[:6]
+    left, send, down_left, down_send, proj_keep, proj_send = refs[6:]
     proj_keep[...] = (proj_left[:2].astype(F32) + proj_came[:2].astype(F32)).astype(BF)
     proj_send[...] = (proj_left[2:].astype(F32) + proj_came[2:].astype(F32)).astype(BF)
-    for side, low, down in ((0, left, down_left), (1, send, down_send)):
-        for m in range(2):
-            total = keeps[m][side].astype(F32) + cames[m][side].astype(F32)
-            for k in range(8):
-                low[k, 32 * m : 32 * m + 32, :] = total[32 * k : 32 * k + 32].astype(BF)
-        down[...] = (keeps[2][side].astype(F32) + cames[2][side].astype(F32)).astype(BF)
+    for side, low, low_down in ((0, left, down_left), (1, send, down_send)):
+        total = (up[side].astype(F32) + up_came[side].astype(F32)).astype(BF)
+        for k in range(8):
+            low[k] = total[32 * k : 32 * k + 32]
+        low_down[...] = (down[side].astype(F32) + down_came[side].astype(F32)).astype(BF)
 
 
 def finish_body(place, came, grad_up, grad_qkv, sums, bias):
@@ -997,6 +997,12 @@
     moved = lax.all_to_all(d_all, ROW, 0, 0, tiled=True)
     proj_left, proj_low = pair(after(proj_left, d_all), swap_over(proj_low, "x"))
 
+    flat_qkv = (16, 32, 512)
+    qkv_left, qkv_low = pair(
+        keep.reshape(flat_qkv), swap_over(send.reshape(flat_qkv), "core")
+    )
+    qkv_came = swap_over(qkv_low, "x")
+
     def group_of(s, g):
         return (s[1] ^ (g & 1)) * 16 + (s[2] ^ (g >> 1)) * 8 + s[0]
 
@@ -1019,21 +1025,21 @@
         ],
         LOW_PIN,
         place,
-        (after(near_n[0], d_all, proj_low), *near_n[1:], *far_n, *cots, last_cot, *([up_weight] * 4), *([down_weight] * 4), vecs),
-    )
-
-
-    up_send, down_send, proj_came = lax.optimization_barrier(
-        (up_send, down_send, swap_over(proj_low, "y"))
+        (after(near_n[0], d_all, proj_low, qkv_low), *near_n[1:], *far_n, *cots, last_cot, *([up_weight] * 4), *([down_weight] * 4), vecs),
+    )
+
+
+    up_send, down_send, proj_came, qkv_came = lax.optimization_barrier(
+        (up_send, down_send, swap_over(proj_low, "y"), qkv_came)
     )
     left, low_send, down_left, down_low, proj_left, proj_low = one_step(
         merge_body,
-        [arr((8, 64, 512), BF)] * 2 + [arr((128, 1024), BF)] * 2 + [arr((2, 32, 1152), BF)] * 2,
+        [arr((8, 32, 512), BF)] * 2 + [arr((128, 1024), BF)] * 2 + [arr((2, 32, 1152), BF)] * 2,
         [],
         PIN,
         place,
         (
-            after(up_keep, moved), swap_over(up_send, "core"), keep, swap_over(send, "core"),
+            after(up_keep, moved), swap_over(up_send, "core"),
             down_keep, swap_over(down_send, "core"), proj_left, proj_came,
         ),
         NO_PIN,
@@ -1054,11 +1060,12 @@
         (after(moved, left), qkv_weight, tok, d_mid, vecs),
     )
 
-    proj_left, proj_low = pair(after(proj_left, tokens_grad), swap_over(proj_low, "zh"))
-    left, proj_low, low_came = lax.optimization_barrier((left, proj_low, low_came))
-    (lows,) = one_step(add_body, [arr((8, 64, 512), BF)], [], NO_PIN, place, (left, low_came))
-    lows, proj_low = lax.optimization_barrier((lows, proj_low))
+    left, low_came, _ = lax.optimization_barrier((left, low_came, tokens_grad))
+    (lows,) = one_step(
+        low_body, [arr((8, 64, 512), BF)], [], NO_PIN, place, (left, low_came, qkv_left, qkv_came)
+    )
     came = turn(lows)
+    proj_left, proj_low = pair(after(proj_left, lows), swap_over(proj_low, "zh"))
     proj_came = swap_over(proj_low, "zl")
     down_low, _ = lax.optimization_barrier((down_low, lows))
     grad_down = down_left.astype(F32) + swap_over(down_low, "x").astype(F32)

time: 192 us -> 190 us (0.990)
  waiting for transfers between devices: 25.8 us -> 23 us
    ppermute x31 -> x32, waiting for transfers between devices: 15.5 us -> 12.5 us  [swap_over(): return lax.ppermute(value, AXES, [(i, i ^ mask) for i in range(32)])]
    ppermute x31 -> x32, starting transfers between devices: 37.5 us -> 39.8 us  [swap_over(): return lax.ppermute(value, AXES, [(i, i ^ mask) for i in range(32)])]
    pallas_call x18 -> x19, Pallas kernels: 93.6 us -> 93.7 us  [call(): pl.pallas_call(body, grid_spec=pltpu.PrefetchScalarGridSpec(num_scalar_pr...]
  transfers between devices with their start and end apart: 35 -> 36, of which waited for: 11 -> 12; matrix products, arithmetic and copies ran while one was open for 5% -> 5% of each run, Pallas kernels for 46% -> 47%
where the time goes in v5:
time: 190 us; the launch traced here: 189 us
  Pallas kernels  93.7 us (49%)
  starting transfers between devices  55.9 us (29%)
  waiting for transfers between devices  23 us (12%)
  local copies, waits for them, and re-layouts  14.3 us (8%)
    pallas_call x19, Pallas kernels, call(): pl.pallas_call(body, grid_spec=pltpu.PrefetchScalarGridSpec(num_scalar_pr...  93.7 us
    ppermute x32, starting transfers between devices, swap_over(): return lax.ppermute(value, AXES, [(i, i ^ mask) for i in range(32)])  39.8 us
    ppermute x32, waiting for transfers between devices, swap_over(): return lax.ppermute(value, AXES, [(i, i ^ mask) for i in range(32)])  12.5 us
    reshape x8, local copies, waits for them, and re-layouts, fast_shards(): v.astype(F32).reshape(-1, 1024)  5.52 us
    unnamed x32, local copies, waits for them, and re-layouts  5.08 us
    all_to_all x1, waiting for transfers between devices, fast_shards(): att_in = lax.all_to_all(att_low, ROW, 0, 0, tiled=True)  4.78 us
    all_to_all x1, starting transfers between devices, fast_shards(): att_in = lax.all_to_all(att_low, ROW, 0, 0, tiled=True)  4.63 us
    all_to_all x1, starting transfers between devices, fast_shards(): moved = lax.all_to_all(d_all, ROW, 0, 0, tiled=True)  4.6 us
  transfers between devices with their start and end apart: 36, of which 12 were waited for; matrix products, arithmetic and copies ran while one was open for 5% of the time, Pallas kernels for 47%

profile of v5, /device:TPU:0, one launch (start us, length us, event | category | flops | bytes accessed | tf_op | source)
XLA Modules:
  0.0 188.7 jit_solution(11697589600122649818)
XLA Ops:
  0.6 4.1 %collective-permute-start = (bf16[128,1024]{1,0:T(8,128)(2,1)}, bf16[128,1024]{1,0:T(8,128)(2,1)S(1)}, u32[]{:S(2)}, u32[]{:S(2)}) collective-permute-start(bf16[128,1024]{1,0:T(8,128)(2,1)} %bitcast.35), channel_id=1, source_target_pairs={{0,4},{1,5},{2,6},{3,7},{4,0},{5,1},{6,2},{7,3},{8,12},{9,13},{10,... | collective-permute-start | bytes 786440 | tf_op jit(solution)/shard_map/ppermute | solution.py:352
  4.7 1.5 collective-permute-start.1
  6.3 1.6 collective-permute-start.2
  8.2 0.7 reshape.86
  8.9 0.7 reshape.87
  9.6 0.7 reshape.80
  10.3 0.7 reshape.81
  11.0 0.7 reshape.82
  11.7 0.7 reshape.83
  12.4 0.7 reshape.84
  13.1 0.7 reshape.85
  13.9 0.7 concatenate.9.place
  14.6 0.7 copy-done.5
  15.3 4.3 %shard_map.263 = (f32[1024,128]{1,0:T(8,128)}, f32[1024,128]{1,0:T(8,128)}, f32[1024,128]{1,0:T(8,128)}, f32[8,1024]{1,0:T(8,128)S(1)}) custom-call(s32[16]{0:T(128)S(1)} %concatenate.9.place, f32[8,128]{1,0:T(8,128)S(1)} %copy-done.5), custom_call_target="tpu_custom_call" | custom-call | bytes 1024 | tf_op jit(solution)/shard_map/pallas_call | solution.py:367
  20.2 3.8 %collective-permute-done.3.refs_3_ = bf16[128,1024]{1,0:T(8,128)(2,1)S(1)} collective-permute-done((bf16[128,1024]{1,0:T(8,128)(2,1)}, bf16[128,1024]{1,0:T(8,128)(2,1)S(1)}, u32[]{:S(2)}, u32[]{:S(2)}) %collective-permute-start.3) | collective-permute-done | bytes 262176 | tf_op jit(solution)/shard_map/ppermute | solution.py:352
  24.0 1.5 collective-permute-start.4
  25.7 1.8 collective-permute-start.6
  27.5 0.9 copy-done.1
  28.5 3.7 %shard_map.264 = (bf16[512,1024]{1,0:T(8,128)(2,1)}, bf16[512,128]{1,0:T(8,128)(2,1)S(1)}, bf16[512,128]{1,0:T(8,128)(2,1)S(1)}, bf16[512,128]{1,0:T(8,128)(2,1)S(1)}) custom-call(s32[16]{0:T(128)S(1)} %concatenate.9.place, bf16[128,1024]{1,0:T(8,128)(2,1)S(1)} %bitcast.39, bf16[128,1024]{1,0:T(8,128)(2,1)S(1)} %collective-permute-done.1.refs_1_, ...), custom_call_target="tpu_custom_call" | custom-call | bytes 1024 | tf_op jit(solution)/shard_map/pallas_call | solution.py:367
  32.2 1.2 collective-permute-start.10
  33.3 2.8 %collective-permute-start.7 = (bf16[128,1024]{1,0:T(8,128)(2,1)S(1)}, bf16[128,1024]{1,0:T(8,128)(2,1)S(1)}, u32[]{:S(2)}, u32[]{:S(2)}) collective-permute-start(bf16[128,1024]{1,0:T(8,128)(2,1)S(1)} %bitcast.31), channel_id=1, source_target_pairs={{0,4},{1,5},{2,6},{3,7},{4,0},{5,1},{6,2},{7,3},{8,12},{9,13},{10,... | collective-permute-start | bytes 786440 | tf_op jit(solution)/shard_map/ppermute | solution.py:352
  36.8 7.4 %shard_map.265 = (f32[128,4096]{1,0:T(8,128)}, f32[1,1024]{1,0:T(1,128)S(1)}) custom-call(s32[16]{0:T(128)S(1)} %concatenate.9.place, bf16[128,1024]{1,0:T(8,128)(2,1)S(1)} %bitcast.34, bf16[4096,1024]{1,0:T(8,128)(2,1)} %down.3), custom_call_target="tpu_custom_call" | custom-call | bytes 1024 | tf_op jit(solution)/shard_map/pallas_call | solution.py:367
  44.2 1.8 collective-permute-done.6.refs_3_
  46.0 3.7 %shard_map.266 = (bf16[512,1024]{1,0:T(8,128)(2,1)}, bf16[1024,128]{1,0:T(8,128)(2,1)S(1)}, bf16[1024,128]{1,0:T(8,128)(2,1)S(1)}, bf16[1024,128]{1,0:T(8,128)(2,1)S(1)}) custom-call(s32[16]{0:T(128)S(1)} %concatenate.9.place, bf16[128,1024]{1,0:T(8,128)(2,1)S(1)} %collective-permute-done.refs_0_, bf16[128,1024]{1,0:T(8,128)(2,1)S(1)} %collective-permute-done.4.refs_1_, ...), custom_call_target="tpu_custom_call" | custom-call | bytes 1024 | tf_op jit(solution)/shard_map/pallas_call | solution.py:367
  49.7 9.4 %shard_map.267 = (f32[1024,128]{1,0:T(8,128)}, bf16[8,128,128]{2,1,0:T(8,128)(2,1)}, bf16[2,1024,1024]{2,1,0:T(8,128)(2,1)}, f32[1024,128]{1,0:T(8,128)}) custom-call(s32[16]{0:T(128)S(1)} %concatenate.9.place, bf16[1024,128]{1,0:T(8,128)(2,1)S(1)} %get-tuple-element.140.q, bf16[1024,128]{1,0:T(8,128)(2,1)S(1)} %get-tuple-element.141.k_all, ...), custom_call_target="tpu_custom_call" | custom-call | bytes 1024 | tf_op jit(solution)/shard_map/pallas_call | solution.py:367
  59.2 0.7 copy-done.9
  59.9 4.6 %all-to-all-start = ((bf16[8,128,128]{2,1,0:T(8,128)(2,1)}), bf16[8,128,128]{2,1,0:T(8,128)(2,1)S(1)}, u32[]{:S(2)}, u32[]{:S(2)}) async-start(bf16[8,128,128]{2,1,0:T(8,128)(2,1)} %get-tuple-element.146), calls=%async_computation | async-start | bytes 524288 | tf_op jit(solution)/shard_map/all_to_all | solution.py:910
  64.6 2.0 %collective-permute-start.11 = (bf16[128,1024]{1,0:T(8,128)(2,1)S(1)}, bf16[128,1024]{1,0:T(8,128)(2,1)}, u32[]{:S(2)}, u32[]{:S(2)}) collective-permute-start(bf16[128,1024]{1,0:T(8,128)(2,1)S(1)} %collective-permute-done.7.refs_12_), channel_id=1, source_target_pairs={{0,1},{1,0},{2,3},{3,2},{4,5},{5,4},{6,7},{7,6},{8,9},{9,8},{10,11... | collective-permute-start | bytes 786440 | tf_op jit(solution)/shard_map/ppermute | solution.py:352
  66.6 1.5 collective-permute-start.12
  68.1 4.8 %all-to-all-done.att = bf16[8,128,128]{2,1,0:T(8,128)(2,1)S(1)} async-done(((bf16[8,128,128]{2,1,0:T(8,128)(2,1)}), bf16[8,128,128]{2,1,0:T(8,128)(2,1)S(1)}, u32[]{:S(2)}, u32[]{:S(2)}) %all-to-all-start) | async-done | bytes 262176 | tf_op jit(solution)/shard_map/all_to_all | solution.py:910
  72.8 3.7 %shard_map.268 = (f32[128,1024]{1,0:T(8,128)}, bf16[128,1024]{1,0:T(8,128)(2,1)}, bf16[128,1024]{1,0:T(8,128)(2,1)}) custom-call(s32[16]{0:T(128)S(1)} %concatenate.9.place, bf16[8,128,128]{2,1,0:T(8,128)(2,1)S(1)} %all-to-all-done.att, bf16[128,1024]{1,0:T(8,128)(2,1)S(1)} %bitcast.40, bf16[1024,1024]{1,0:T(8,128)(2,1)} %proj_w.3, ...), custom_call_target="tpu_custom_call" | custom-call | bytes 1024 | tf_op jit(solution)/shard_map/pallas_call | solution.py:367
  76.5 1.2 collective-permute-done.12.refs_14_
  77.7 1.5 collective-permute-start.13
  79.5 2.2 %collective-permute-start.15 = (bf16[128,1024]{1,0:T(8,128)(2,1)}, bf16[128,1024]{1,0:T(8,128)(2,1)S(1)}, u32[]{:S(2)}, u32[]{:S(2)}) collective-permute-start(bf16[128,1024]{1,0:T(8,128)(2,1)} %get-tuple-element.185.normed.refs_0_), channel_id=1, source_target_pairs={{0,2},{1,3},{2,0},{3,1},{4,6},{5,7},{6,4},{7,5},{8,10},{9,11},{10,... | collective-permute-start | bytes 786440 | tf_op jit(solution)/shard_map/ppermute | solution.py:352
  81.7 1.4 collective-permute-start.16
  83.1 13.7 %shard_map.269 = (bf16[128,4096]{1,0:T(8,128)(2,1)}, f32[128,1024]{1,0:T(8,128)}, bf16[8,128,128]{2,1,0:T(8,128)(2,1)}, bf16[2,8,32,1152]{3,2,1,0:T(8,128)(2,1)}, bf16[2,8,32,1152]{3,2,1,0:T(8,128)(2,1)}) custom-call(s32[16]{0:T(128)S(1)} %concatenate.9.place, bf16[128,1024]{1,0:T(8,128)(2,1)} %get-tuple-element.185.normed.refs_0_, ...), custom_call_target="tpu_custom_call" | custom-call | bytes 1024 | tf_op jit(solution)/shard_map/pallas_call | solution.py:367
  97.0 0.8 copy-done.14
  97.7 3.4 %all-to-all-start.1 = ((bf16[8,128,128]{2,1,0:T(8,128)(2,1)}), bf16[8,128,128]{2,1,0:T(8,128)(2,1)S(1)}, u32[]{:S(2)}, u32[]{:S(2)}) async-start(bf16[8,128,128]{2,1,0:T(8,128)(2,1)} %get-tuple-element.164), calls=%async_computation.1 | async-start | bytes 524288 | tf_op jit(solution)/shard_map/all_to_all | solution.py:947
  101.2 2.0 %collective-permute-start.18 = (bf16[128,1024]{1,0:T(8,128)(2,1)}, bf16[128,1024]{1,0:T(8,128)(2,1)S(1)}, u32[]{:S(2)}, u32[]{:S(2)}) collective-permute-start(bf16[128,1024]{1,0:T(8,128)(2,1)} %collective-permute-done.11.refs_13_), channel_id=1, source_target_pairs={{0,2},{1,3},{2,0},{3,1},{4,6},{5,7},{6,4},{7,5},{8,10},{9,11},{10,... | collective-permute-start | bytes 786440 | tf_op jit(solution)/shard_map/ppermute | solution.py:352
  103.2 1.4 collective-permute-start.19
  105.1 1.6 collective-permute-start.21
  106.7 1.3 copy-done.3
  108.0 1.6 shard_map.270
  109.5 1.5 collective-permute-start.22
  111.0 9.4 %shard_map.271 = (bf16[8,128,384]{2,1,0:T(8,128)(2,1)}, f32[1,384]{1,0:T(1,128)S(1)}) custom-call(s32[16]{0:T(128)S(1)} %concatenate.9.place, bf16[2,1024,1024]{2,1,0:T(8,128)(2,1)} %get-tuple-element.163.probs, bf16[8,128,128]{2,1,0:T(8,128)(2,1)S(1)} %all-to-all-done.1.d_att, f32[1024,128]{1,0:T(8,128)} %get-tuple-element.169.att_f, ...), custom_call_target="tpu_custom_call" | custom-call | bytes 1024 | tf_op jit(solution)/shard_map/pallas_call | solution.py:367
  120.4 6.2 %shard_map.272 = (bf16[2,256,512]{2,1,0:T(8,128)(2,1)}, bf16[2,256,512]{2,1,0:T(8,128)(2,1)}) custom-call(s32[16]{0:T(128)S(1)} %concatenate.9.place, bf16[512,1024]{1,0:T(8,128)(2,1)} %get-tuple-element.172.h0, bf16[512,1024]{1,0:T(8,128)(2,1)} %get-tuple-element.173.h1, bf16[8,128,384]{2,1,0:T(8,128)(2,1)} %get-tuple-element.178.d_all, ...), custom_call_target="tpu_custom_call" | custom-call | bytes 1024 | tf_op jit(solution)/shard_map/pallas_call | solution.py:367
  126.6 4.6 %all-to-all-start.2 = ((bf16[8,128,384]{2,1,0:T(8,128)(2,1)}), bf16[8,128,384]{2,1,0:T(8,128)(2,1)}, u32[]{:S(2)}, u32[]{:S(2)}) async-start(bf16[8,128,384]{2,1,0:T(8,128)(2,1)} %get-tuple-element.178.d_all), calls=%async_computation.2 | async-start | bytes 1572864 | tf_op jit(solution)/shard_map/all_to_all | solution.py:997
  132.0 2.0 %collective-permute-start.24 = (bf16[4,32,1152]{2,1,0:T(8,128)(2,1)S(1)}, bf16[4,32,1152]{2,1,0:T(8,128)(2,1)S(1)}, u32[]{:S(2)}, u32[]{:S(2)}) collective-permute-start(bf16[4,32,1152]{2,1,0:T(8,128)(2,1)S(1)} %get-tuple-element.181), channel_id=1, source_target_pairs={{0,1},{1,0},{2,3},{3,2},{4,5},{5,4},{6,7},{7,6},{8,9},{9,8},{10,11... | collective-permute-start | bytes 884744 | tf_op jit(solution)/shard_map/ppermute | solution.py:352
  134.7 1.2 collective-permute-start.25
  135.9 9.9 %shard_map.275 = (bf16[2,128,1024]{2,1,0:T(8,128)(2,1)}, bf16[2,128,1024]{2,1,0:T(8,128)(2,1)}, bf16[2,256,512]{2,1,0:T(8,128)(2,1)}, bf16[2,256,512]{2,1,0:T(8,128)(2,1)}) custom-call(s32[16]{0:T(128)S(1)} %concatenate.9.place, bf16[128,1024]{1,0:T(8,128)(2,1)} %get-tuple-element.185.normed.refs_0_, bf16[128,1024]{1,0:T(8,128)(2,1)} %copy-done.12, ...), custom_call_target="tpu_custom_call" | custom-call | bytes 1024 | tf_op jit(solution)/shard_map/pallas_call | solution.py:367
  145.8 2.9 %collective-permute-done.24.refs_5_ = bf16[4,32,1152]{2,1,0:T(8,128)(2,1)S(1)} collective-permute-done((bf16[4,32,1152]{2,1,0:T(8,128)(2,1)S(1)}, bf16[4,32,1152]{2,1,0:T(8,128)(2,1)S(1)}, u32[]{:S(2)}, u32[]{:S(2)}) %collective-permute-start.24) | collective-permute-done | bytes 294944 | tf_op jit(solution)/shard_map/ppermute | solution.py:352
  149.2 1.8 all-to-all-done.2.came
  152.3 2.4 %shard_map.276 = (bf16[8,32,512]{2,1,0:T(8,128)(2,1)S(1)}, bf16[8,32,512]{2,1,0:T(8,128)(2,1)S(1)}, bf16[128,1024]{1,0:T(8,128)(2,1)S(1)}, bf16[128,1024]{1,0:T(...) custom-call(s32[16]{0:T(128)S(1)} %concatenate.9.place, ...), custom_call_target="tpu_custom_call" | custom-call | bytes 1024 | tf_op jit(solution)/shard_map/pallas_call | solution.py:367
  154.7 1.2 collective-permute-start.28
  155.8 6.7 %shard_map.277 = f32[128,1024]{1,0:T(8,128)} custom-call(s32[16]{0:T(128)S(1)} %concatenate.9.place, bf16[8,128,384]{2,1,0:T(8,128)(2,1)} %all-to-all-done.2.came, bf16[1024,3072]{1,0:T(8,128)(2,1)} %w.1, bf16[128,1024]{1,0:T(8,128)(2,1)S(1)} %bitcast.41, f32[128,1024]{1,0:T(8,128)} %get-tuple-element.212.d_mid, f32[15,1024]{1,0:T(8,128)S(1)} %concatenate.11.refs_4_.vecs.refs_24_), custom_call_target="tpu_custom_call" | custom-call | bytes 1024 | tf_op jit(solution)/shard_map/pallas_call | solution.py:367
  163.1 1.5 shard_map.278
  164.6 1.0 collective-permute-done.29.came
  166.1 2.3 %collective-permute-start.30 = (bf16[1,32,1152]{2,1,0:T(8,128)(2,1)S(1)}, bf16[1,32,1152]{2,1,0:T(8,128)(2,1)S(1)}, u32[]{:S(2)}, u32[]{:S(2)}) collective-permute-start(bf16[1,32,1152]{2,1,0:T(8,128)(2,1)S(1)} %get-tuple-element.225), channel_id=1, source_target_pairs={{0,2},{1,3},{2,0},{3,1},{4,6},{5,7},{6,4},{7,5},{8,10},{9,11},{10,... | collective-permute-start | bytes 221192 | tf_op jit(solution)/shard_map/ppermute | solution.py:352
  168.4 3.5 %all-to-all-start.3 = ((bf16[8,64,512]{2,1,0:T(8,128)(2,1)}), bf16[8,64,512]{2,1,0:T(8,128)(2,1)S(1)}, u32[]{:S(2)}, u32[]{:S(2)}) async-start(bf16[8,64,512]{2,1,0:T(8,128)(2,1)} %shard_map.278), calls=%async_computation.3 | async-start | bytes 1048576 | tf_op jit(solution)/shard_map/all_to_all | solution.py:995
  171.9 1.0 collective-permute-start.31
  172.8 6.7 %shard_map.279 = bf16[128,1024]{1,0:T(8,128)(2,1)} custom-call(s32[16]{0:T(128)S(1)} %concatenate.9.place, bf16[128,4096]{1,0:T(8,128)(2,1)} %get-tuple-element.217.active, bf16[4096,1024]{1,0:T(8,128)(2,1)} %down.3, f32[128,1024]{1,0:T(8,128)} %get-tuple-element.154.middle, f32[15,1024]{1,0:T(8,128)S(1)} %concatenate.11.refs_4_.vecs.refs_24_), custom_call_target="tpu_custom_call" | custom-call | bytes 1024 | tf_op jit(solution)/shard_map/pallas_call | solution.py:367
  181.4 0.9 convert_add_fusion
  182.2 3.8 %all-to-all-done.3.came = bf16[8,64,512]{2,1,0:T(8,128)(2,1)S(1)} async-done(((bf16[8,64,512]{2,1,0:T(8,128)(2,1)}), bf16[8,64,512]{2,1,0:T(8,128)(2,1)S(1)}, u32[]{:S(2)}, u32[]{:S(2)}) %all-to-all-start.3) | async-done | bytes 524320 | tf_op jit(solution)/shard_map/all_to_all | solution.py:995
  186.1 1.5 shard_map.280
  (80 shorter events, 10.2 us)
Async XLA Ops:
  0.6 19.0 %collective-permute-start = (bf16[128,1024]{1,0:T(8,128)(2,1)}, bf16[128,1024]{1,0:T(8,128)(2,1)S(1)}, u32[]{:S(2)}, u32[]{:S(2)}) collective-permute-start(bf16[128,1024]{1,0:T(8,128)(2,1)} %bitcast.35), channel_id=1, source_target_pairs={{0,4},{1,5},{2,6},{3,7},{4,0},{5,1},{6,2},{7,3},{8,12},{9,13},{10,... | collective-permute-start | bytes 786440 | tf_op jit(solution)/shard_map/ppermute | solution.py:352
  4.7 14.9 %collective-permute-start.1 = (bf16[128,1024]{1,0:T(8,128)(2,1)}, bf16[128,1024]{1,0:T(8,128)(2,1)S(1)}, u32[]{:S(2)}, u32[]{:S(2)}) collective-permute-start(bf16[128,1024]{1,0:T(8,128)(2,1)} %bitcast.36), channel_id=1, source_target_pairs={{0,1},{1,0},{2,3},{3,2},{4,5},{5,4},{6,7},{7,6},{8,9},{9,8},{10,11... | collective-permute-start | bytes 786440 | tf_op jit(solution)/shard_map/ppermute | solution.py:352
  6.3 13.9 %collective-permute-start.2 = (bf16[128,1024]{1,0:T(8,128)(2,1)}, bf16[128,1024]{1,0:T(8,128)(2,1)S(1)}, u32[]{:S(2)}, u32[]{:S(2)}) collective-permute-start(bf16[128,1024]{1,0:T(8,128)(2,1)} %bitcast.37), channel_id=1, source_target_pairs={{0,2},{1,3},{2,0},{3,1},{4,6},{5,7},{6,4},{7,5},{8,10},{9,11},{10,... | collective-permute-start | bytes 786440 | tf_op jit(solution)/shard_map/ppermute | solution.py:352
  7.8 16.2 %collective-permute-start.3 = (bf16[128,1024]{1,0:T(8,128)(2,1)}, bf16[128,1024]{1,0:T(8,128)(2,1)S(1)}, u32[]{:S(2)}, u32[]{:S(2)}) collective-permute-start(bf16[128,1024]{1,0:T(8,128)(2,1)} %bitcast.38), channel_id=1, source_target_pairs={{0,3},{1,2},{2,1},{3,0},{4,7},{5,6},{6,5},{7,4},{8,11},{9,10},{10,... | collective-permute-start | bytes 786440 | tf_op jit(solution)/shard_map/ppermute | solution.py:352
  14.6 0.7 copy-start.5
  24.0 12.1 %collective-permute-start.4 = (bf16[128,1024]{1,0:T(8,128)(2,1)S(1)}, bf16[128,1024]{1,0:T(8,128)(2,1)S(1)}, u32[]{:S(2)}, u32[]{:S(2)}) collective-permute-start(bf16[128,1024]{1,0:T(8,128)(2,1)S(1)} %collective-permute-done.refs_0_), channel_id=1, source_target_pairs={{0,1},{1,0},{2,3},{3,2},{4,5},{5,4},{6,7},{7,6},{8,9},{9,8},{10,11... | collective-permute-start | bytes 786440 | tf_op jit(solution)/shard_map/ppermute | solution.py:352
  25.5 11.2 %collective-permute-start.5 = (bf16[128,1024]{1,0:T(8,128)(2,1)S(1)}, bf16[128,1024]{1,0:T(8,128)(2,1)S(1)}, u32[]{:S(2)}, u32[]{:S(2)}) collective-permute-start(bf16[128,1024]{1,0:T(8,128)(2,1)S(1)} %collective-permute-done.refs_0_), channel_id=1, source_target_pairs={{0,2},{1,3},{2,0},{3,1},{4,6},{5,7},{6,4},{7,5},{8,10},{9,11},{10,... | collective-permute-start | bytes 786440 | tf_op jit(solution)/shard_map/ppermute | solution.py:352
  25.7 20.3 %collective-permute-start.6 = (bf16[128,1024]{1,0:T(8,128)(2,1)S(1)}, bf16[128,1024]{1,0:T(8,128)(2,1)S(1)}, u32[]{:S(2)}, u32[]{:S(2)}) collective-permute-start(bf16[128,1024]{1,0:T(8,128)(2,1)S(1)} %collective-permute-done.refs_0_), channel_id=1, source_target_pairs={{0,3},{1,2},{2,1},{3,0},{4,7},{5,6},{6,5},{7,4},{8,11},{9,10},{10,... | collective-permute-start | bytes 786440 | tf_op jit(solution)/shard_map/ppermute | solution.py:352
  27.5 0.9 copy-start.1
  28.5 3.7 %copy-start = (bf16[1,128,1024]{2,1,0:T(8,128)(2,1)S(1)}, bf16[1,128,1024]{2,1,0:T(8,128)(2,1)}, u32[]{:S(2)}) copy-start(bf16[1,128,1024]{2,1,0:T(8,128)(2,1)} %param.30) | copy-start | bytes 786436
  32.2 27.0 %collective-permute-start.10 = (bf16[128,1024]{1,0:T(8,128)(2,1)S(1)}, bf16[128,1024]{1,0:T(8,128)(2,1)S(1)}, u32[]{:S(2)}, u32[]{:S(2)}) collective-permute-start(bf16[128,1024]{1,0:T(8,128)(2,1)S(1)} %bitcast.30), channel_id=1, source_target_pairs={{0,3},{1,2},{2,1},{3,0},{4,7},{5,6},{6,5},{7,4},{8,11},{9,10},{10,... | collective-permute-start | bytes 786440 | tf_op jit(solution)/shard_map/ppermute | solution.py:352
  33.3 25.9 %collective-permute-start.7 = (bf16[128,1024]{1,0:T(8,128)(2,1)S(1)}, bf16[128,1024]{1,0:T(8,128)(2,1)S(1)}, u32[]{:S(2)}, u32[]{:S(2)}) collective-permute-start(bf16[128,1024]{1,0:T(8,128)(2,1)S(1)} %bitcast.31), channel_id=1, source_target_pairs={{0,4},{1,5},{2,6},{3,7},{4,0},{5,1},{6,2},{7,3},{8,12},{9,13},{10,... | collective-permute-start | bytes 786440 | tf_op jit(solution)/shard_map/ppermute | solution.py:352
  36.1 23.1 %collective-permute-start.8 = (bf16[128,1024]{1,0:T(8,128)(2,1)S(1)}, bf16[128,1024]{1,0:T(8,128)(2,1)S(1)}, u32[]{:S(2)}, u32[]{:S(2)}) collective-permute-start(bf16[128,1024]{1,0:T(8,128)(2,1)S(1)} %bitcast.32), channel_id=1, source_target_pairs={{0,1},{1,0},{2,3},{3,2},{4,5},{5,4},{6,7},{7,6},{8,9},{9,8},{10,11... | collective-permute-start | bytes 786440 | tf_op jit(solution)/shard_map/ppermute | solution.py:352
  36.7 22.5 %collective-permute-start.9 = (bf16[128,1024]{1,0:T(8,128)(2,1)S(1)}, bf16[128,1024]{1,0:T(8,128)(2,1)S(1)}, u32[]{:S(2)}, u32[]{:S(2)}) collective-permute-start(bf16[128,1024]{1,0:T(8,128)(2,1)S(1)} %bitcast.33), channel_id=1, source_target_pairs={{0,2},{1,3},{2,0},{3,1},{4,6},{5,7},{6,4},{7,5},{8,10},{9,11},{10,... | collective-permute-start | bytes 786440 | tf_op jit(solution)/shard_map/ppermute | solution.py:352
  46.0 26.8 %copy-start.2 = (bf16[1,128,1024]{2,1,0:T(8,128)(2,1)S(1)}, bf16[1,128,1024]{2,1,0:T(8,128)(2,1)}, u32[]{:S(2)}) copy-start(bf16[1,128,1024]{2,1,0:T(8,128)(2,1)} %param.16) | copy-start | bytes 786436
  59.2 37.7 %copy-start.7 = (bf16[128,1024]{1,0:T(8,128)(2,1)}, bf16[128,1024]{1,0:T(8,128)(2,1)S(1)}, u32[]{:S(2)}) copy-start(bf16[128,1024]{1,0:T(8,128)(2,1)S(1)} %collective-permute-done.10.refs_11_) | copy-start | bytes 786436
  59.2 37.7 %copy-start.8 = (bf16[128,1024]{1,0:T(8,128)(2,1)}, bf16[128,1024]{1,0:T(8,128)(2,1)S(1)}, u32[]{:S(2)}) copy-start(bf16[128,1024]{1,0:T(8,128)(2,1)S(1)} %collective-permute-done.7.refs_12_) | copy-start | bytes 786436
  59.2 0.7 copy-start.9
  59.9 36.9 %copy-start.10 = (bf16[128,1024]{1,0:T(8,128)(2,1)}, bf16[128,1024]{1,0:T(8,128)(2,1)S(1)}, u32[]{:S(2)}) copy-start(bf16[128,1024]{1,0:T(8,128)(2,1)S(1)} %collective-permute-done.9.refs_10_) | copy-start | bytes 786436
  59.9 12.9 %all-to-all-start = ((bf16[8,128,128]{2,1,0:T(8,128)(2,1)}), bf16[8,128,128]{2,1,0:T(8,128)(2,1)S(1)}, u32[]{:S(2)}, u32[]{:S(2)}) async-start(bf16[8,128,128]{2,1,0:T(8,128)(2,1)} %get-tuple-element.146), calls=%async_computation | async-start | bytes 524288 | tf_op jit(solution)/shard_map/all_to_all | solution.py:910
  64.6 11.9 %collective-permute-start.11 = (bf16[128,1024]{1,0:T(8,128)(2,1)S(1)}, bf16[128,1024]{1,0:T(8,128)(2,1)}, u32[]{:S(2)}, u32[]{:S(2)}) collective-permute-start(bf16[128,1024]{1,0:T(8,128)(2,1)S(1)} %collective-permute-done.7.refs_12_), channel_id=1, source_target_pairs={{0,1},{1,0},{2,3},{3,2},{4,5},{5,4},{6,7},{7,6},{8,9},{9,8},{10,11... | collective-permute-start | bytes 786440 | tf_op jit(solution)/shard_map/ppermute | solution.py:352
  66.6 11.1 %collective-permute-start.12 = (bf16[128,1024]{1,0:T(8,128)(2,1)S(1)}, bf16[128,1024]{1,0:T(8,128)(2,1)S(1)}, u32[]{:S(2)}, u32[]{:S(2)}) collective-permute-start(bf16[128,1024]{1,0:T(8,128)(2,1)S(1)} %collective-permute-done.7.refs_12_), channel_id=1, source_target_pairs={{0,2},{1,3},{2,0},{3,1},{4,6},{5,7},{6,4},{7,5},{8,10},{9,11},{10,... | collective-permute-start | bytes 786440 | tf_op jit(solution)/shard_map/ppermute | solution.py:352
  77.7 19.2 %copy-start.11 = (bf16[128,1024]{1,0:T(8,128)(2,1)}, bf16[128,1024]{1,0:T(8,128)(2,1)S(1)}, u32[]{:S(2)}) copy-start(bf16[128,1024]{1,0:T(8,128)(2,1)S(1)} %collective-permute-done.12.refs_14_) | copy-start | bytes 786436
  77.7 19.2 %collective-permute-start.13 = (bf16[128,1024]{1,0:T(8,128)(2,1)}, bf16[128,1024]{1,0:T(8,128)(2,1)}, u32[]{:S(2)}, u32[]{:S(2)}) collective-permute-start(bf16[128,1024]{1,0:T(8,128)(2,1)} %get-tuple-element.185.normed.refs_0_), channel_id=1, source_target_pairs={{0,4},{1,5},{2,6},{3,7},{4,0},{5,1},{6,2},{7,3},{8,12},{9,13},{10,... | collective-permute-start | bytes 786440 | tf_op jit(solution)/shard_map/ppermute | solution.py:352
  79.2 17.7 %collective-permute-start.14 = (bf16[128,1024]{1,0:T(8,128)(2,1)}, bf16[128,1024]{1,0:T(8,128)(2,1)S(1)}, u32[]{:S(2)}, u32[]{:S(2)}) collective-permute-start(bf16[128,1024]{1,0:T(8,128)(2,1)} %get-tuple-element.185.normed.refs_0_), channel_id=1, source_target_pairs={{0,1},{1,0},{2,3},{3,2},{4,5},{5,4},{6,7},{7,6},{8,9},{9,8},{10,11... | collective-permute-start | bytes 786440 | tf_op jit(solution)/shard_map/ppermute | solution.py:352
  79.5 17.4 %collective-permute-start.15 = (bf16[128,1024]{1,0:T(8,128)(2,1)}, bf16[128,1024]{1,0:T(8,128)(2,1)S(1)}, u32[]{:S(2)}, u32[]{:S(2)}) collective-permute-start(bf16[128,1024]{1,0:T(8,128)(2,1)} %get-tuple-element.185.normed.refs_0_), channel_id=1, source_target_pairs={{0,2},{1,3},{2,0},{3,1},{4,6},{5,7},{6,4},{7,5},{8,10},{9,11},{10,... | collective-permute-start | bytes 786440 | tf_op jit(solution)/shard_map/ppermute | solution.py:352
  81.7 15.2 %collective-permute-start.16 = (bf16[128,1024]{1,0:T(8,128)(2,1)}, bf16[128,1024]{1,0:T(8,128)(2,1)S(1)}, u32[]{:S(2)}, u32[]{:S(2)}) collective-permute-start(bf16[128,1024]{1,0:T(8,128)(2,1)} %get-tuple-element.185.normed.refs_0_), channel_id=1, source_target_pairs={{0,3},{1,2},{2,1},{3,0},{4,7},{5,6},{6,5},{7,4},{8,11},{9,10},{10,... | collective-permute-start | bytes 786440 | tf_op jit(solution)/shard_map/ppermute | solution.py:352
  96.9 0.8 copy-start.12
  96.9 9.8 %copy-start.13 = (bf16[128,1024]{1,0:T(8,128)(2,1)}, bf16[128,1024]{1,0:T(8,128)(2,1)S(1)}, u32[]{:S(2)}) copy-start(bf16[128,1024]{1,0:T(8,128)(2,1)S(1)} %collective-permute-done.15.refs_2_) | copy-start | bytes 786436
  97.0 0.8 copy-start.14
  97.7 9.0 %collective-permute-start.17 = (bf16[16,32,1152]{2,1,0:T(8,128)(2,1)}, bf16[16,32,1152]{2,1,0:T(8,128)(2,1)S(1)}, u32[]{:S(2)}, u32[]{:S(2)}) collective-permute-start(bf16[16,32,1152]{2,1,0:T(8,128)(2,1)} %bitcast.47), channel_id=1, source_target_pairs={{0,8},{1,9},{2,10},{3,11},{4,12},{5,13},{6,14},{7,15},{8,0},{9,1},... | collective-permute-start | bytes 3538952 | tf_op jit(solution)/shard_map/ppermute | solution.py:352
  97.7 13.3 %all-to-all-start.1 = ((bf16[8,128,128]{2,1,0:T(8,128)(2,1)}), bf16[8,128,128]{2,1,0:T(8,128)(2,1)S(1)}, u32[]{:S(2)}, u32[]{:S(2)}) async-start(bf16[8,128,128]{2,1,0:T(8,128)(2,1)} %get-tuple-element.164), calls=%async_computation.1 | async-start | bytes 524288 | tf_op jit(solution)/shard_map/all_to_all | solution.py:947
  101.2 25.4 %collective-permute-start.18 = (bf16[128,1024]{1,0:T(8,128)(2,1)}, bf16[128,1024]{1,0:T(8,128)(2,1)S(1)}, u32[]{:S(2)}, u32[]{:S(2)}) collective-permute-start(bf16[128,1024]{1,0:T(8,128)(2,1)} %collective-permute-done.11.refs_13_), channel_id=1, source_target_pairs={{0,2},{1,3},{2,0},{3,1},{4,6},{5,7},{6,4},{7,5},{8,10},{9,11},{10,... | collective-permute-start | bytes 786440 | tf_op jit(solution)/shard_map/ppermute | solution.py:352
  103.2 23.4 %collective-permute-start.19 = (bf16[128,1024]{1,0:T(8,128)(2,1)}, bf16[128,1024]{1,0:T(8,128)(2,1)}, u32[]{:S(2)}, u32[]{:S(2)}) collective-permute-start(bf16[128,1024]{1,0:T(8,128)(2,1)} %collective-permute-done.13.refs_4_), channel_id=1, source_target_pairs={{0,1},{1,0},{2,3},{3,2},{4,5},{5,4},{6,7},{7,6},{8,9},{9,8},{10,11... | collective-permute-start | bytes 786440 | tf_op jit(solution)/shard_map/ppermute | solution.py:352
  104.6 22.1 %collective-permute-start.20 = (bf16[128,1024]{1,0:T(8,128)(2,1)}, bf16[128,1024]{1,0:T(8,128)(2,1)}, u32[]{:S(2)}, u32[]{:S(2)}) collective-permute-start(bf16[128,1024]{1,0:T(8,128)(2,1)} %collective-permute-done.13.refs_4_), channel_id=1, source_target_pairs={{0,2},{1,3},{2,0},{3,1},{4,6},{5,7},{6,4},{7,5},{8,10},{9,11},{10,... | collective-permute-start | bytes 786440 | tf_op jit(solution)/shard_map/ppermute | solution.py:352
  105.1 21.5 %collective-permute-start.21 = (bf16[128,1024]{1,0:T(8,128)(2,1)}, bf16[128,1024]{1,0:T(8,128)(2,1)}, u32[]{:S(2)}, u32[]{:S(2)}) collective-permute-start(bf16[128,1024]{1,0:T(8,128)(2,1)} %collective-permute-done.13.refs_4_), channel_id=1, source_target_pairs={{0,3},{1,2},{2,1},{3,0},{4,7},{5,6},{6,5},{7,4},{8,11},{9,10},{10,... | collective-permute-start | bytes 786440 | tf_op jit(solution)/shard_map/ppermute | solution.py:352
  106.7 1.3 copy-start.3
  109.5 21.8 %collective-permute-start.22 = (bf16[8,32,1152]{2,1,0:T(8,128)(2,1)}, bf16[8,32,1152]{2,1,0:T(8,128)(2,1)S(1)}, u32[]{:S(2)}, u32[]{:S(2)}) collective-permute-start(bf16[8,32,1152]{2,1,0:T(8,128)(2,1)} %get-tuple-element.167), channel_id=1, source_target_pairs={{0,16},{1,17},{2,18},{3,19},{4,20},{5,21},{6,22},{7,23},{8,24},{9,... | collective-permute-start | bytes 1769480 | tf_op jit(solution)/shard_map/ppermute | solution.py:352
  126.6 7.4 %copy-start.4 = (bf16[2,256,512]{2,1,0:T(8,128)(2,1)S(1)}, bf16[2,256,512]{2,1,0:T(8,128)(2,1)}, u32[]{:S(2)}) copy-start(bf16[2,256,512]{2,1,0:T(8,128)(2,1)} %get-tuple-element.182) | copy-start | bytes 1572868
  126.6 9.3 %copy-start.15 = (bf16[128,1024]{1,0:T(8,128)(2,1)}, bf16[128,1024]{1,0:T(8,128)(2,1)S(1)}, u32[]{:S(2)}) copy-start(bf16[128,1024]{1,0:T(8,128)(2,1)S(1)} %collective-permute-done.18.refs_15_) | copy-start | bytes 786436
  126.6 24.4 %all-to-all-start.2 = ((bf16[8,128,384]{2,1,0:T(8,128)(2,1)}), bf16[8,128,384]{2,1,0:T(8,128)(2,1)}, u32[]{:S(2)}, u32[]{:S(2)}) async-start(bf16[8,128,384]{2,1,0:T(8,128)(2,1)} %get-tuple-element.178.d_all), calls=%async_computation.2 | async-start | bytes 1572864 | tf_op jit(solution)/shard_map/all_to_all | solution.py:997
  131.2 2.8 %collective-permute-start.23 = (bf16[16,32,512]{2,1,0:T(8,128)(2,1)}, bf16[16,32,512]{2,1,0:T(8,128)(2,1)S(1)}, u32[]{:S(2)}, u32[]{:S(2)}) collective-permute-start(bf16[16,32,512]{2,1,0:T(8,128)(2,1)} %bitcast.48), channel_id=1, source_target_pairs={{0,8},{1,9},{2,10},{3,11},{4,12},{5,13},{6,14},{7,15},{8,0},{9,1},... | collective-permute-start | bytes 1572872 | tf_op jit(solution)/shard_map/ppermute | solution.py:352
  132.0 16.7 %collective-permute-start.24 = (bf16[4,32,1152]{2,1,0:T(8,128)(2,1)S(1)}, bf16[4,32,1152]{2,1,0:T(8,128)(2,1)S(1)}, u32[]{:S(2)}, u32[]{:S(2)}) collective-permute-start(bf16[4,32,1152]{2,1,0:T(8,128)(2,1)S(1)} %get-tuple-element.181), channel_id=1, source_target_pairs={{0,1},{1,0},{2,3},{3,2},{4,5},{5,4},{6,7},{7,6},{8,9},{9,8},{10,11... | collective-permute-start | bytes 884744 | tf_op jit(solution)/shard_map/ppermute | solution.py:352
  134.7 11.1 %collective-permute-start.25 = (bf16[8,32,512]{2,1,0:T(8,128)(2,1)S(1)}, bf16[8,32,512]{2,1,0:T(8,128)(2,1)S(1)}, u32[]{:S(2)}, u32[]{:S(2)}) collective-permute-start(bf16[8,32,512]{2,1,0:T(8,128)(2,1)S(1)} %get-tuple-element.184), channel_id=1, source_target_pairs={{0,16},{1,17},{2,18},{3,19},{4,20},{5,21},{6,22},{7,23},{8,24},{9,... | collective-permute-start | bytes 786440 | tf_op jit(solution)/shard_map/ppermute | solution.py:352
  148.7 2.8 %collective-permute-start.26 = (bf16[2,256,512]{2,1,0:T(8,128)(2,1)}, bf16[2,256,512]{2,1,0:T(8,128)(2,1)S(1)}, u32[]{:S(2)}, u32[]{:S(2)}) collective-permute-start(bf16[2,256,512]{2,1,0:T(8,128)(2,1)} %get-tuple-element.204), channel_id=1, source_target_pairs={{0,8},{1,9},{2,10},{3,11},{4,12},{5,13},{6,14},{7,15},{8,0},{9,1},... | collective-permute-start | bytes 1572872 | tf_op jit(solution)/shard_map/ppermute | solution.py:352
  148.7 3.0 %collective-permute-start.27 = (bf16[2,128,1024]{2,1,0:T(8,128)(2,1)}, bf16[2,128,1024]{2,1,0:T(8,128)(2,1)}, u32[]{:S(2)}, u32[]{:S(2)}) collective-permute-start(bf16[2,128,1024]{2,1,0:T(8,128)(2,1)} %get-tuple-element.206), channel_id=1, source_target_pairs={{0,8},{1,9},{2,10},{3,11},{4,12},{5,13},{6,14},{7,15},{8,0},{9,1},... | collective-permute-start | bytes 1572872 | tf_op jit(solution)/shard_map/ppermute | solution.py:352
  151.5 0.8 copy-start.6
  154.7 8.4 %collective-permute-start.28 = (bf16[8,32,512]{2,1,0:T(8,128)(2,1)S(1)}, bf16[8,32,512]{2,1,0:T(8,128)(2,1)S(1)}, u32[]{:S(2)}, u32[]{:S(2)}) collective-permute-start(bf16[8,32,512]{2,1,0:T(8,128)(2,1)S(1)} %get-tuple-element.210), channel_id=1, source_target_pairs={{0,16},{1,17},{2,18},{3,19},{4,20},{5,21},{6,22},{7,23},{8,24},{9,... | collective-permute-start | bytes 786440 | tf_op jit(solution)/shard_map/ppermute | solution.py:352
  155.8 9.7 %collective-permute-start.29 = (bf16[2,32,1152]{2,1,0:T(8,128)(2,1)S(1)}, bf16[2,32,1152]{2,1,0:T(8,128)(2,1)S(1)}, u32[]{:S(2)}, u32[]{:S(2)}) collective-permute-start(bf16[2,32,1152]{2,1,0:T(8,128)(2,1)S(1)} %get-tuple-element.223), channel_id=1, source_target_pairs={{0,4},{1,5},{2,6},{3,7},{4,0},{5,1},{6,2},{7,3},{8,12},{9,13},{10,... | collective-permute-start | bytes 442376 | tf_op jit(solution)/shard_map/ppermute | solution.py:352
  166.1 13.4 %collective-permute-start.30 = (bf16[1,32,1152]{2,1,0:T(8,128)(2,1)S(1)}, bf16[1,32,1152]{2,1,0:T(8,128)(2,1)S(1)}, u32[]{:S(2)}, u32[]{:S(2)}) collective-permute-start(bf16[1,32,1152]{2,1,0:T(8,128)(2,1)S(1)} %get-tuple-element.225), channel_id=1, source_target_pairs={{0,2},{1,3},{2,0},{3,1},{4,6},{5,7},{6,4},{7,5},{8,10},{9,11},{10,... | collective-permute-start | bytes 221192 | tf_op jit(solution)/shard_map/ppermute | solution.py:352
  168.4 17.7 %all-to-all-start.3 = ((bf16[8,64,512]{2,1,0:T(8,128)(2,1)}), bf16[8,64,512]{2,1,0:T(8,128)(2,1)S(1)}, u32[]{:S(2)}, u32[]{:S(2)}) async-start(bf16[8,64,512]{2,1,0:T(8,128)(2,1)} %shard_map.278), calls=%async_computation.3 | async-start | bytes 1048576 | tf_op jit(solution)/shard_map/all_to_all | solution.py:995
  171.9 9.5 %collective-permute-start.31 = (bf16[128,1024]{1,0:T(8,128)(2,1)S(1)}, bf16[128,1024]{1,0:T(8,128)(2,1)S(1)}, u32[]{:S(2)}, u32[]{:S(2)}) collective-permute-start(bf16[128,1024]{1,0:T(8,128)(2,1)S(1)} %get-tuple-element.229), channel_id=1, source_target_pairs={{0,16},{1,17},{2,18},{3,19},{4,20},{5,21},{6,22},{7,23},{8,24},{9,... | collective-permute-start | bytes 786440 | tf_op jit(solution)/shard_map/ppermute | solution.py:352

commit v6 on v5

--- a/solution.py
+++ b/solution.py
@@ -722,9 +722,10 @@
         low_down[...] = (down[side].astype(F32) + down_came[side].astype(F32)).astype(BF)
 
 
-def finish_body(place, came, grad_up, grad_qkv, sums, bias):
+def finish_body(place, came, grad_up, grad_qkv, gain, shift, bias):
     total = jnp.zeros((32, 128), F32)
     low = lax.broadcasted_iota(jnp.int32, (1, 128), 1) < 64
+    parts = ([], [], [])
     for k in range(8):
         for g in range(4):
             lanes = slice(1024 * g + 128 * k, 1024 * g + 128 * k + 128)
@@ -736,8 +737,13 @@
         for p in range(3):
             left = pltpu.roll(extra[2 * p : 2 * p + 1], 64, 1)
             both = jnp.where(low, left, extra[2 * p + 1 : 2 * p + 2])
-            bias[p : p + 1, 128 * k : 128 * k + 128] = both
-    sums[...] = total.T[:8]
+            parts[p].append(both)
+    turned = total.T
+    gain[...] = turned[0:1]
+    shift[...] = turned[1:2]
+    row = jnp.broadcast_to(jnp.concatenate(parts[0] + parts[1] + parts[2], 1), (8, 3072))
+    me = place[1] * 16 + place[2] * 8 + place[0]
+    bias[...] = pltpu.roll(row, lax.rem(3072 - me * 96, 3072), 1)[0:1, :96]
 
 
 def out_body(place, active, down, middle, vecs, out, acc):
@@ -1086,18 +1092,17 @@
     own = lax.dynamic_slice(proj_total[:4, 1024:], (0, (me % 4) * 32), (4, 32))
     grad_up_b = proj_total[4, 1024:]
 
-    grad_up, grad_qkv, sums, bias = one_step(
+    grad_up, grad_qkv, gain_sum, shift_sum, grad_qkv_b = one_step(
         finish_body,
-        [arr((32, 4096), F32), arr((32, 3072), F32), arr((8, 32), F32), arr((3, 1024), F32)],
+        [arr((32, 4096), F32), arr((32, 3072), F32), arr((1, 32), F32), arr((1, 32), F32), arr((1, 96), F32)],
         [],
         NO_PIN,
         place,
         (came,),
     )
-    grad_qkv_b = lax.dynamic_slice(bias.reshape(3072), (me * 96,), (96,))
 
     return (
-        layer_out, tokens_grad[None], sums[0], sums[1], grad_qkv, grad_qkv_b, grad_proj,
+        layer_out, tokens_grad[None], gain_sum[0], shift_sum[0], grad_qkv, grad_qkv_b[0], grad_proj,
         own[2], own[0], own[1], grad_up, grad_up_b, grad_down, own[3],
     )
 

time: 190 us -> 189 us (level)
  transfers between devices with their start and end apart: 36 -> 36, of which waited for: 12 -> 13; matrix products, arithmetic and copies ran while one was open for 5% -> 5% of each run, Pallas kernels for 47% -> 48%
where the time goes in v6:
time: 189 us; the launch traced here: 188 us
  Pallas kernels  93.8 us (50%)
  starting transfers between devices  55.9 us (30%)
  waiting for transfers between devices  22.9 us (12%)
  local copies, waits for them, and re-layouts  13.2 us (7%)
    pallas_call x19, Pallas kernels, call(): pl.pallas_call(body, grid_spec=pltpu.PrefetchScalarGridSpec(num_scalar_pr...  93.8 us
    ppermute x32, starting transfers between devices, swap_over(): return lax.ppermute(value, AXES, [(i, i ^ mask) for i in range(32)])  39.7 us
    ppermute x32, waiting for transfers between devices, swap_over(): return lax.ppermute(value, AXES, [(i, i ^ mask) for i in range(32)])  12.5 us
    reshape x8, local copies, waits for them, and re-layouts, fast_shards(): v.astype(F32).reshape(-1, 1024)  5.52 us
    unnamed x32, local copies, waits for them, and re-layouts  5.09 us
    all_to_all x1, waiting for transfers between devices, fast_shards(): att_in = lax.all_to_all(att_low, ROW, 0, 0, tiled=True)  4.78 us
    all_to_all x1, starting transfers between devices, fast_shards(): att_in = lax.all_to_all(att_low, ROW, 0, 0, tiled=True)  4.63 us
    all_to_all x1, starting transfers between devices, fast_shards(): moved = lax.all_to_all(d_all, ROW, 0, 0, tiled=True)  4.61 us
  transfers between devices with their start and end apart: 36, of which 13 were waited for; matrix products, arithmetic and copies ran while one was open for 5% of the time, Pallas kernels for 48%

profile of v6, /device:TPU:0, one launch (start us, length us, event | category | flops | bytes accessed | tf_op | source)
XLA Modules:
  0.0 187.6 jit_solution(10219034370669438774)
XLA Ops:
  0.6 4.1 %collective-permute-start = (bf16[128,1024]{1,0:T(8,128)(2,1)}, bf16[128,1024]{1,0:T(8,128)(2,1)S(1)}, u32[]{:S(2)}, u32[]{:S(2)}) collective-permute-start(bf16[128,1024]{1,0:T(8,128)(2,1)} %bitcast.34), channel_id=1, source_target_pairs={{0,4},{1,5},{2,6},{3,7},{4,0},{5,1},{6,2},{7,3},{8,12},{9,13},{10,... | collective-permute-start | bytes 786440 | tf_op jit(solution)/shard_map/ppermute | solution.py:352
  4.7 1.5 collective-permute-start.1
  6.3 1.6 collective-permute-start.2
  8.2 0.7 reshape.83
  8.9 0.7 reshape.84
  9.6 0.7 reshape.77
  10.3 0.7 reshape.78
  11.0 0.7 reshape.79
  11.7 0.7 reshape.80
  12.4 0.7 reshape.81
  13.9 0.7 concatenate.9.place
  14.6 0.7 copy-done.5
  15.3 4.3 %shard_map.263 = (f32[1024,128]{1,0:T(8,128)}, f32[1024,128]{1,0:T(8,128)}, f32[1024,128]{1,0:T(8,128)}, f32[8,1024]{1,0:T(8,128)S(1)}) custom-call(s32[16]{0:T(128)S(1)} %concatenate.9.place, f32[8,128]{1,0:T(8,128)S(1)} %copy-done.5), custom_call_target="tpu_custom_call" | custom-call | bytes 1024 | tf_op jit(solution)/shard_map/pallas_call | solution.py:367
  20.2 3.8 %collective-permute-done.3.refs_3_ = bf16[128,1024]{1,0:T(8,128)(2,1)S(1)} collective-permute-done((bf16[128,1024]{1,0:T(8,128)(2,1)}, bf16[128,1024]{1,0:T(8,128)(2,1)S(1)}, u32[]{:S(2)}, u32[]{:S(2)}) %collective-permute-start.3) | collective-permute-done | bytes 262176 | tf_op jit(solution)/shard_map/ppermute | solution.py:352
  24.0 1.5 collective-permute-start.4
  25.7 1.8 collective-permute-start.6
  27.5 0.9 copy-done.1
  28.5 3.7 %shard_map.264 = (bf16[512,1024]{1,0:T(8,128)(2,1)}, bf16[512,128]{1,0:T(8,128)(2,1)S(1)}, bf16[512,128]{1,0:T(8,128)(2,1)S(1)}, bf16[512,128]{1,0:T(8,128)(2,1)S(1)}) custom-call(s32[16]{0:T(128)S(1)} %concatenate.9.place, bf16[128,1024]{1,0:T(8,128)(2,1)S(1)} %bitcast.38, bf16[128,1024]{1,0:T(8,128)(2,1)S(1)} %collective-permute-done.1.refs_1_, ...), custom_call_target="tpu_custom_call" | custom-call | bytes 1024 | tf_op jit(solution)/shard_map/pallas_call | solution.py:367
  32.1 1.2 collective-permute-start.10
  33.3 2.8 %collective-permute-start.7 = (bf16[128,1024]{1,0:T(8,128)(2,1)S(1)}, bf16[128,1024]{1,0:T(8,128)(2,1)S(1)}, u32[]{:S(2)}, u32[]{:S(2)}) collective-permute-start(bf16[128,1024]{1,0:T(8,128)(2,1)S(1)} %bitcast.30), channel_id=1, source_target_pairs={{0,4},{1,5},{2,6},{3,7},{4,0},{5,1},{6,2},{7,3},{8,12},{9,13},{10,... | collective-permute-start | bytes 786440 | tf_op jit(solution)/shard_map/ppermute | solution.py:352
  36.7 0.9 collective-permute-done.5.refs_2_
  37.6 7.5 %shard_map.265 = (f32[128,4096]{1,0:T(8,128)}, f32[1,1024]{1,0:T(1,128)S(1)}) custom-call(s32[16]{0:T(128)S(1)} %concatenate.9.place, bf16[128,1024]{1,0:T(8,128)(2,1)S(1)} %bitcast.33, bf16[4096,1024]{1,0:T(8,128)(2,1)} %down.3), custom_call_target="tpu_custom_call" | custom-call | bytes 1024 | tf_op jit(solution)/shard_map/pallas_call | solution.py:367
  45.0 1.0 collective-permute-done.6.refs_3_
  46.0 3.7 %shard_map.266 = (bf16[512,1024]{1,0:T(8,128)(2,1)}, bf16[1024,128]{1,0:T(8,128)(2,1)S(1)}, bf16[1024,128]{1,0:T(8,128)(2,1)S(1)}, bf16[1024,128]{1,0:T(8,128)(2,1)S(1)}) custom-call(s32[16]{0:T(128)S(1)} %concatenate.9.place, bf16[128,1024]{1,0:T(8,128)(2,1)S(1)} %collective-permute-done.refs_0_, bf16[128,1024]{1,0:T(8,128)(2,1)S(1)} %collective-permute-done.4.refs_1_, ...), custom_call_target="tpu_custom_call" | custom-call | bytes 1024 | tf_op jit(solution)/shard_map/pallas_call | solution.py:367
  49.7 9.4 %shard_map.267 = (f32[1024,128]{1,0:T(8,128)}, bf16[8,128,128]{2,1,0:T(8,128)(2,1)}, bf16[2,1024,1024]{2,1,0:T(8,128)(2,1)}, f32[1024,128]{1,0:T(8,128)}) custom-call(s32[16]{0:T(128)S(1)} %concatenate.9.place, bf16[1024,128]{1,0:T(8,128)(2,1)S(1)} %get-tuple-element.141.q, bf16[1024,128]{1,0:T(8,128)(2,1)S(1)} %get-tuple-element.142.k_all, ...), custom_call_target="tpu_custom_call" | custom-call | bytes 1024 | tf_op jit(solution)/shard_map/pallas_call | solution.py:367
  59.2 0.7 copy-done.9
  59.9 4.6 %all-to-all-start = ((bf16[8,128,128]{2,1,0:T(8,128)(2,1)}), bf16[8,128,128]{2,1,0:T(8,128)(2,1)S(1)}, u32[]{:S(2)}, u32[]{:S(2)}) async-start(bf16[8,128,128]{2,1,0:T(8,128)(2,1)} %get-tuple-element.147), calls=%async_computation | async-start | bytes 524288 | tf_op jit(solution)/shard_map/all_to_all | solution.py:916
  64.6 2.0 %collective-permute-start.11 = (bf16[128,1024]{1,0:T(8,128)(2,1)S(1)}, bf16[128,1024]{1,0:T(8,128)(2,1)}, u32[]{:S(2)}, u32[]{:S(2)}) collective-permute-start(bf16[128,1024]{1,0:T(8,128)(2,1)S(1)} %collective-permute-done.7.refs_12_), channel_id=1, source_target_pairs={{0,1},{1,0},{2,3},{3,2},{4,5},{5,4},{6,7},{7,6},{8,9},{9,8},{10,11... | collective-permute-start | bytes 786440 | tf_op jit(solution)/shard_map/ppermute | solution.py:352
  66.6 1.5 collective-permute-start.12
  68.1 4.8 %all-to-all-done.att = bf16[8,128,128]{2,1,0:T(8,128)(2,1)S(1)} async-done(((bf16[8,128,128]{2,1,0:T(8,128)(2,1)}), bf16[8,128,128]{2,1,0:T(8,128)(2,1)S(1)}, u32[]{:S(2)}, u32[]{:S(2)}) %all-to-all-start) | async-done | bytes 262176 | tf_op jit(solution)/shard_map/all_to_all | solution.py:916
  72.8 3.7 %shard_map.268 = (f32[128,1024]{1,0:T(8,128)}, bf16[128,1024]{1,0:T(8,128)(2,1)}, bf16[128,1024]{1,0:T(8,128)(2,1)}) custom-call(s32[16]{0:T(128)S(1)} %concatenate.9.place, bf16[8,128,128]{2,1,0:T(8,128)(2,1)S(1)} %all-to-all-done.att, bf16[128,1024]{1,0:T(8,128)(2,1)S(1)} %bitcast.39, bf16[1024,1024]{1,0:T(8,128)(2,1)} %proj_w.3, ...), custom_call_target="tpu_custom_call" | custom-call | bytes 1024 | tf_op jit(solution)/shard_map/pallas_call | solution.py:367
  76.5 1.1 collective-permute-done.12.refs_14_
  77.6 1.5 collective-permute-start.13
  79.5 2.2 %collective-permute-start.15 = (bf16[128,1024]{1,0:T(8,128)(2,1)}, bf16[128,1024]{1,0:T(8,128)(2,1)S(1)}, u32[]{:S(2)}, u32[]{:S(2)}) collective-permute-start(bf16[128,1024]{1,0:T(8,128)(2,1)} %get-tuple-element.186.normed.refs_0_), channel_id=1, source_target_pairs={{0,2},{1,3},{2,0},{3,1},{4,6},{5,7},{6,4},{7,5},{8,10},{9,11},{10,... | collective-permute-start | bytes 786440 | tf_op jit(solution)/shard_map/ppermute | solution.py:352
  81.7 1.4 collective-permute-start.16
  83.1 13.8 %shard_map.269 = (bf16[128,4096]{1,0:T(8,128)(2,1)}, f32[128,1024]{1,0:T(8,128)}, bf16[8,128,128]{2,1,0:T(8,128)(2,1)}, bf16[2,8,32,1152]{3,2,1,0:T(8,128)(2,1)}, bf16[2,8,32,1152]{3,2,1,0:T(8,128)(2,1)}) custom-call(s32[16]{0:T(128)S(1)} %concatenate.9.place, bf16[128,1024]{1,0:T(8,128)(2,1)} %get-tuple-element.186.normed.refs_0_, ...), custom_call_target="tpu_custom_call" | custom-call | bytes 1024 | tf_op jit(solution)/shard_map/pallas_call | solution.py:367
  96.9 0.8 copy-done.14
  97.7 3.4 %all-to-all-start.1 = ((bf16[8,128,128]{2,1,0:T(8,128)(2,1)}), bf16[8,128,128]{2,1,0:T(8,128)(2,1)S(1)}, u32[]{:S(2)}, u32[]{:S(2)}) async-start(bf16[8,128,128]{2,1,0:T(8,128)(2,1)} %get-tuple-element.165), calls=%async_computation.1 | async-start | bytes 524288 | tf_op jit(solution)/shard_map/all_to_all | solution.py:953
  101.1 2.0 %collective-permute-start.18 = (bf16[128,1024]{1,0:T(8,128)(2,1)}, bf16[128,1024]{1,0:T(8,128)(2,1)S(1)}, u32[]{:S(2)}, u32[]{:S(2)}) collective-permute-start(bf16[128,1024]{1,0:T(8,128)(2,1)} %collective-permute-done.11.refs_13_), channel_id=1, source_target_pairs={{0,2},{1,3},{2,0},{3,1},{4,6},{5,7},{6,4},{7,5},{8,10},{9,11},{10,... | collective-permute-start | bytes 786440 | tf_op jit(solution)/shard_map/ppermute | solution.py:352
  103.1 1.4 collective-permute-start.19
  105.1 1.6 collective-permute-start.21
  106.6 1.3 copy-done.3
  107.9 1.6 shard_map.270
  109.5 1.5 collective-permute-start.22
  111.0 9.4 %shard_map.271 = (bf16[8,128,384]{2,1,0:T(8,128)(2,1)}, f32[1,384]{1,0:T(1,128)S(1)}) custom-call(s32[16]{0:T(128)S(1)} %concatenate.9.place, bf16[2,1024,1024]{2,1,0:T(8,128)(2,1)} %get-tuple-element.164.probs, bf16[8,128,128]{2,1,0:T(8,128)(2,1)S(1)} %all-to-all-done.1.d_att, f32[1024,128]{1,0:T(8,128)} %get-tuple-element.170.att_f, ...), custom_call_target="tpu_custom_call" | custom-call | bytes 1024 | tf_op jit(solution)/shard_map/pallas_call | solution.py:367
  120.4 6.2 %shard_map.272 = (bf16[2,256,512]{2,1,0:T(8,128)(2,1)}, bf16[2,256,512]{2,1,0:T(8,128)(2,1)}) custom-call(s32[16]{0:T(128)S(1)} %concatenate.9.place, bf16[512,1024]{1,0:T(8,128)(2,1)} %get-tuple-element.173.h0, bf16[512,1024]{1,0:T(8,128)(2,1)} %get-tuple-element.174.h1, bf16[8,128,384]{2,1,0:T(8,128)(2,1)} %get-tuple-element.179.d_all, ...), custom_call_target="tpu_custom_call" | custom-call | bytes 1024 | tf_op jit(solution)/shard_map/pallas_call | solution.py:367
  126.6 4.6 %all-to-all-start.2 = ((bf16[8,128,384]{2,1,0:T(8,128)(2,1)}), bf16[8,128,384]{2,1,0:T(8,128)(2,1)}, u32[]{:S(2)}, u32[]{:S(2)}) async-start(bf16[8,128,384]{2,1,0:T(8,128)(2,1)} %get-tuple-element.179.d_all), calls=%async_computation.2 | async-start | bytes 1572864 | tf_op jit(solution)/shard_map/all_to_all | solution.py:1003
  132.0 2.0 %collective-permute-start.24 = (bf16[4,32,1152]{2,1,0:T(8,128)(2,1)S(1)}, bf16[4,32,1152]{2,1,0:T(8,128)(2,1)S(1)}, u32[]{:S(2)}, u32[]{:S(2)}) collective-permute-start(bf16[4,32,1152]{2,1,0:T(8,128)(2,1)S(1)} %get-tuple-element.182), channel_id=1, source_target_pairs={{0,1},{1,0},{2,3},{3,2},{4,5},{5,4},{6,7},{7,6},{8,9},{9,8},{10,11... | collective-permute-start | bytes 884744 | tf_op jit(solution)/shard_map/ppermute | solution.py:352
  134.7 1.2 collective-permute-start.25
  135.8 9.9 %shard_map.275 = (bf16[2,128,1024]{2,1,0:T(8,128)(2,1)}, bf16[2,128,1024]{2,1,0:T(8,128)(2,1)}, bf16[2,256,512]{2,1,0:T(8,128)(2,1)}, bf16[2,256,512]{2,1,0:T(8,128)(2,1)}) custom-call(s32[16]{0:T(128)S(1)} %concatenate.9.place, bf16[128,1024]{1,0:T(8,128)(2,1)} %get-tuple-element.186.normed.refs_0_, bf16[128,1024]{1,0:T(8,128)(2,1)} %copy-done.12, ...), custom_call_target="tpu_custom_call" | custom-call | bytes 1024 | tf_op jit(solution)/shard_map/pallas_call | solution.py:367
  145.7 2.9 %collective-permute-done.24.refs_5_ = bf16[4,32,1152]{2,1,0:T(8,128)(2,1)S(1)} collective-permute-done((bf16[4,32,1152]{2,1,0:T(8,128)(2,1)S(1)}, bf16[4,32,1152]{2,1,0:T(8,128)(2,1)S(1)}, u32[]{:S(2)}, u32[]{:S(2)}) %collective-permute-start.24) | collective-permute-done | bytes 294944 | tf_op jit(solution)/shard_map/ppermute | solution.py:352
  149.2 1.8 all-to-all-done.2.came
  152.3 2.4 %shard_map.276 = (bf16[8,32,512]{2,1,0:T(8,128)(2,1)S(1)}, bf16[8,32,512]{2,1,0:T(8,128)(2,1)S(1)}, bf16[128,1024]{1,0:T(8,128)(2,1)S(1)}, bf16[128,1024]{1,0:T(...) custom-call(s32[16]{0:T(128)S(1)} %concatenate.9.place, ...), custom_call_target="tpu_custom_call" | custom-call | bytes 1024 | tf_op jit(solution)/shard_map/pallas_call | solution.py:367
  154.6 1.2 collective-permute-start.28
  155.8 6.7 %shard_map.277 = f32[128,1024]{1,0:T(8,128)} custom-call(s32[16]{0:T(128)S(1)} %concatenate.9.place, bf16[8,128,384]{2,1,0:T(8,128)(2,1)} %all-to-all-done.2.came, bf16[1024,3072]{1,0:T(8,128)(2,1)} %w.1, bf16[128,1024]{1,0:T(8,128)(2,1)S(1)} %bitcast.40, f32[128,1024]{1,0:T(8,128)} %get-tuple-element.213.d_mid, f32[15,1024]{1,0:T(8,128)S(1)} %concatenate.11.refs_4_.vecs.refs_24_), custom_call_target="tpu_custom_call" | custom-call | bytes 1024 | tf_op jit(solution)/shard_map/pallas_call | solution.py:367
  163.1 1.5 shard_map.278
  164.5 1.0 collective-permute-done.29.came
  166.1 2.3 %collective-permute-start.30 = (bf16[1,32,1152]{2,1,0:T(8,128)(2,1)S(1)}, bf16[1,32,1152]{2,1,0:T(8,128)(2,1)S(1)}, u32[]{:S(2)}, u32[]{:S(2)}) collective-permute-start(bf16[1,32,1152]{2,1,0:T(8,128)(2,1)S(1)} %get-tuple-element.227), channel_id=1, source_target_pairs={{0,2},{1,3},{2,0},{3,1},{4,6},{5,7},{6,4},{7,5},{8,10},{9,11},{10,... | collective-permute-start | bytes 221192 | tf_op jit(solution)/shard_map/ppermute | solution.py:352
  168.3 3.5 %all-to-all-start.3 = ((bf16[8,64,512]{2,1,0:T(8,128)(2,1)}), bf16[8,64,512]{2,1,0:T(8,128)(2,1)S(1)}, u32[]{:S(2)}, u32[]{:S(2)}) async-start(bf16[8,64,512]{2,1,0:T(8,128)(2,1)} %shard_map.278), calls=%async_computation.3 | async-start | bytes 1048576 | tf_op jit(solution)/shard_map/all_to_all | solution.py:1001
  171.8 1.0 collective-permute-start.31
  172.8 6.7 %shard_map.279 = bf16[128,1024]{1,0:T(8,128)(2,1)} custom-call(s32[16]{0:T(128)S(1)} %concatenate.9.place, bf16[128,4096]{1,0:T(8,128)(2,1)} %get-tuple-element.218.active, bf16[4096,1024]{1,0:T(8,128)(2,1)} %down.3, f32[128,1024]{1,0:T(8,128)} %get-tuple-element.155.middle, f32[15,1024]{1,0:T(8,128)S(1)} %concatenate.11.refs_4_.vecs.refs_24_), custom_call_target="tpu_custom_call" | custom-call | bytes 1024 | tf_op jit(solution)/shard_map/pallas_call | solution.py:367
  181.3 0.9 convert_add_fusion
  182.2 3.8 %all-to-all-done.3.came = bf16[8,64,512]{2,1,0:T(8,128)(2,1)S(1)} async-done(((bf16[8,64,512]{2,1,0:T(8,128)(2,1)}), bf16[8,64,512]{2,1,0:T(8,128)(2,1)S(1)}, u32[]{:S(2)}, u32[]{:S(2)}) %all-to-all-start.3) | async-done | bytes 524320 | tf_op jit(solution)/shard_map/all_to_all | solution.py:1001
  186.0 1.6 shard_map.280
  (77 shorter events, 9.7 us)
Async XLA Ops:
  0.6 19.0 %collective-permute-start = (bf16[128,1024]{1,0:T(8,128)(2,1)}, bf16[128,1024]{1,0:T(8,128)(2,1)S(1)}, u32[]{:S(2)}, u32[]{:S(2)}) collective-permute-start(bf16[128,1024]{1,0:T(8,128)(2,1)} %bitcast.34), channel_id=1, source_target_pairs={{0,4},{1,5},{2,6},{3,7},{4,0},{5,1},{6,2},{7,3},{8,12},{9,13},{10,... | collective-permute-start | bytes 786440 | tf_op jit(solution)/shard_map/ppermute | solution.py:352
  4.7 14.9 %collective-permute-start.1 = (bf16[128,1024]{1,0:T(8,128)(2,1)}, bf16[128,1024]{1,0:T(8,128)(2,1)S(1)}, u32[]{:S(2)}, u32[]{:S(2)}) collective-permute-start(bf16[128,1024]{1,0:T(8,128)(2,1)} %bitcast.35), channel_id=1, source_target_pairs={{0,1},{1,0},{2,3},{3,2},{4,5},{5,4},{6,7},{7,6},{8,9},{9,8},{10,11... | collective-permute-start | bytes 786440 | tf_op jit(solution)/shard_map/ppermute | solution.py:352
  6.3 13.9 %collective-permute-start.2 = (bf16[128,1024]{1,0:T(8,128)(2,1)}, bf16[128,1024]{1,0:T(8,128)(2,1)S(1)}, u32[]{:S(2)}, u32[]{:S(2)}) collective-permute-start(bf16[128,1024]{1,0:T(8,128)(2,1)} %bitcast.36), channel_id=1, source_target_pairs={{0,2},{1,3},{2,0},{3,1},{4,6},{5,7},{6,4},{7,5},{8,10},{9,11},{10,... | collective-permute-start | bytes 786440 | tf_op jit(solution)/shard_map/ppermute | solution.py:352
  7.8 16.2 %collective-permute-start.3 = (bf16[128,1024]{1,0:T(8,128)(2,1)}, bf16[128,1024]{1,0:T(8,128)(2,1)S(1)}, u32[]{:S(2)}, u32[]{:S(2)}) collective-permute-start(bf16[128,1024]{1,0:T(8,128)(2,1)} %bitcast.37), channel_id=1, source_target_pairs={{0,3},{1,2},{2,1},{3,0},{4,7},{5,6},{6,5},{7,4},{8,11},{9,10},{10,... | collective-permute-start | bytes 786440 | tf_op jit(solution)/shard_map/ppermute | solution.py:352
  14.6 0.7 copy-start.5
  24.0 12.1 %collective-permute-start.4 = (bf16[128,1024]{1,0:T(8,128)(2,1)S(1)}, bf16[128,1024]{1,0:T(8,128)(2,1)S(1)}, u32[]{:S(2)}, u32[]{:S(2)}) collective-permute-start(bf16[128,1024]{1,0:T(8,128)(2,1)S(1)} %collective-permute-done.refs_0_), channel_id=1, source_target_pairs={{0,1},{1,0},{2,3},{3,2},{4,5},{5,4},{6,7},{7,6},{8,9},{9,8},{10,11... | collective-permute-start | bytes 786440 | tf_op jit(solution)/shard_map/ppermute | solution.py:352
  25.5 12.1 %collective-permute-start.5 = (bf16[128,1024]{1,0:T(8,128)(2,1)S(1)}, bf16[128,1024]{1,0:T(8,128)(2,1)S(1)}, u32[]{:S(2)}, u32[]{:S(2)}) collective-permute-start(bf16[128,1024]{1,0:T(8,128)(2,1)S(1)} %collective-permute-done.refs_0_), channel_id=1, source_target_pairs={{0,2},{1,3},{2,0},{3,1},{4,6},{5,7},{6,4},{7,5},{8,10},{9,11},{10,... | collective-permute-start | bytes 786440 | tf_op jit(solution)/shard_map/ppermute | solution.py:352
  25.7 20.3 %collective-permute-start.6 = (bf16[128,1024]{1,0:T(8,128)(2,1)S(1)}, bf16[128,1024]{1,0:T(8,128)(2,1)S(1)}, u32[]{:S(2)}, u32[]{:S(2)}) collective-permute-start(bf16[128,1024]{1,0:T(8,128)(2,1)S(1)} %collective-permute-done.refs_0_), channel_id=1, source_target_pairs={{0,3},{1,2},{2,1},{3,0},{4,7},{5,6},{6,5},{7,4},{8,11},{9,10},{10,... | collective-permute-start | bytes 786440 | tf_op jit(solution)/shard_map/ppermute | solution.py:352
  27.5 0.9 copy-start.1
  28.5 3.7 %copy-start = (bf16[1,128,1024]{2,1,0:T(8,128)(2,1)S(1)}, bf16[1,128,1024]{2,1,0:T(8,128)(2,1)}, u32[]{:S(2)}) copy-start(bf16[1,128,1024]{2,1,0:T(8,128)(2,1)} %param.30) | copy-start | bytes 786436
  32.1 27.0 %collective-permute-start.10 = (bf16[128,1024]{1,0:T(8,128)(2,1)S(1)}, bf16[128,1024]{1,0:T(8,128)(2,1)S(1)}, u32[]{:S(2)}, u32[]{:S(2)}) collective-permute-start(bf16[128,1024]{1,0:T(8,128)(2,1)S(1)} %bitcast.29), channel_id=1, source_target_pairs={{0,3},{1,2},{2,1},{3,0},{4,7},{5,6},{6,5},{7,4},{8,11},{9,10},{10,... | collective-permute-start | bytes 786440 | tf_op jit(solution)/shard_map/ppermute | solution.py:352
  33.3 25.9 %collective-permute-start.7 = (bf16[128,1024]{1,0:T(8,128)(2,1)S(1)}, bf16[128,1024]{1,0:T(8,128)(2,1)S(1)}, u32[]{:S(2)}, u32[]{:S(2)}) collective-permute-start(bf16[128,1024]{1,0:T(8,128)(2,1)S(1)} %bitcast.30), channel_id=1, source_target_pairs={{0,4},{1,5},{2,6},{3,7},{4,0},{5,1},{6,2},{7,3},{8,12},{9,13},{10,... | collective-permute-start | bytes 786440 | tf_op jit(solution)/shard_map/ppermute | solution.py:352
  36.1 23.1 %collective-permute-start.8 = (bf16[128,1024]{1,0:T(8,128)(2,1)S(1)}, bf16[128,1024]{1,0:T(8,128)(2,1)S(1)}, u32[]{:S(2)}, u32[]{:S(2)}) collective-permute-start(bf16[128,1024]{1,0:T(8,128)(2,1)S(1)} %bitcast.31), channel_id=1, source_target_pairs={{0,1},{1,0},{2,3},{3,2},{4,5},{5,4},{6,7},{7,6},{8,9},{9,8},{10,11... | collective-permute-start | bytes 786440 | tf_op jit(solution)/shard_map/ppermute | solution.py:352
  37.5 21.7 %collective-permute-start.9 = (bf16[128,1024]{1,0:T(8,128)(2,1)S(1)}, bf16[128,1024]{1,0:T(8,128)(2,1)S(1)}, u32[]{:S(2)}, u32[]{:S(2)}) collective-permute-start(bf16[128,1024]{1,0:T(8,128)(2,1)S(1)} %bitcast.32), channel_id=1, source_target_pairs={{0,2},{1,3},{2,0},{3,1},{4,6},{5,7},{6,4},{7,5},{8,10},{9,11},{10,... | collective-permute-start | bytes 786440 | tf_op jit(solution)/shard_map/ppermute | solution.py:352
  46.0 26.8 %copy-start.2 = (bf16[1,128,1024]{2,1,0:T(8,128)(2,1)S(1)}, bf16[1,128,1024]{2,1,0:T(8,128)(2,1)}, u32[]{:S(2)}) copy-start(bf16[1,128,1024]{2,1,0:T(8,128)(2,1)} %param.16) | copy-start | bytes 786436
  59.2 37.6 %copy-start.7 = (bf16[128,1024]{1,0:T(8,128)(2,1)}, bf16[128,1024]{1,0:T(8,128)(2,1)S(1)}, u32[]{:S(2)}) copy-start(bf16[128,1024]{1,0:T(8,128)(2,1)S(1)} %collective-permute-done.10.refs_11_) | copy-start | bytes 786436
  59.2 37.6 %copy-start.8 = (bf16[128,1024]{1,0:T(8,128)(2,1)}, bf16[128,1024]{1,0:T(8,128)(2,1)S(1)}, u32[]{:S(2)}) copy-start(bf16[128,1024]{1,0:T(8,128)(2,1)S(1)} %collective-permute-done.7.refs_12_) | copy-start | bytes 786436
  59.2 0.7 copy-start.9
  59.9 36.9 %copy-start.10 = (bf16[128,1024]{1,0:T(8,128)(2,1)}, bf16[128,1024]{1,0:T(8,128)(2,1)S(1)}, u32[]{:S(2)}) copy-start(bf16[128,1024]{1,0:T(8,128)(2,1)S(1)} %collective-permute-done.9.refs_10_) | copy-start | bytes 786436
  59.9 12.9 %all-to-all-start = ((bf16[8,128,128]{2,1,0:T(8,128)(2,1)}), bf16[8,128,128]{2,1,0:T(8,128)(2,1)S(1)}, u32[]{:S(2)}, u32[]{:S(2)}) async-start(bf16[8,128,128]{2,1,0:T(8,128)(2,1)} %get-tuple-element.147), calls=%async_computation | async-start | bytes 524288 | tf_op jit(solution)/shard_map/all_to_all | solution.py:916
  64.6 11.9 %collective-permute-start.11 = (bf16[128,1024]{1,0:T(8,128)(2,1)S(1)}, bf16[128,1024]{1,0:T(8,128)(2,1)}, u32[]{:S(2)}, u32[]{:S(2)}) collective-permute-start(bf16[128,1024]{1,0:T(8,128)(2,1)S(1)} %collective-permute-done.7.refs_12_), channel_id=1, source_target_pairs={{0,1},{1,0},{2,3},{3,2},{4,5},{5,4},{6,7},{7,6},{8,9},{9,8},{10,11... | collective-permute-start | bytes 786440 | tf_op jit(solution)/shard_map/ppermute | solution.py:352
  66.6 11.0 %collective-permute-start.12 = (bf16[128,1024]{1,0:T(8,128)(2,1)S(1)}, bf16[128,1024]{1,0:T(8,128)(2,1)S(1)}, u32[]{:S(2)}, u32[]{:S(2)}) collective-permute-start(bf16[128,1024]{1,0:T(8,128)(2,1)S(1)} %collective-permute-done.7.refs_12_), channel_id=1, source_target_pairs={{0,2},{1,3},{2,0},{3,1},{4,6},{5,7},{6,4},{7,5},{8,10},{9,11},{10,... | collective-permute-start | bytes 786440 | tf_op jit(solution)/shard_map/ppermute | solution.py:352
  77.6 19.3 %copy-start.11 = (bf16[128,1024]{1,0:T(8,128)(2,1)}, bf16[128,1024]{1,0:T(8,128)(2,1)S(1)}, u32[]{:S(2)}) copy-start(bf16[128,1024]{1,0:T(8,128)(2,1)S(1)} %collective-permute-done.12.refs_14_) | copy-start | bytes 786436
  77.6 19.3 %collective-permute-start.13 = (bf16[128,1024]{1,0:T(8,128)(2,1)}, bf16[128,1024]{1,0:T(8,128)(2,1)}, u32[]{:S(2)}, u32[]{:S(2)}) collective-permute-start(bf16[128,1024]{1,0:T(8,128)(2,1)} %get-tuple-element.186.normed.refs_0_), channel_id=1, source_target_pairs={{0,4},{1,5},{2,6},{3,7},{4,0},{5,1},{6,2},{7,3},{8,12},{9,13},{10,... | collective-permute-start | bytes 786440 | tf_op jit(solution)/shard_map/ppermute | solution.py:352
  79.1 17.7 %collective-permute-start.14 = (bf16[128,1024]{1,0:T(8,128)(2,1)}, bf16[128,1024]{1,0:T(8,128)(2,1)S(1)}, u32[]{:S(2)}, u32[]{:S(2)}) collective-permute-start(bf16[128,1024]{1,0:T(8,128)(2,1)} %get-tuple-element.186.normed.refs_0_), channel_id=1, source_target_pairs={{0,1},{1,0},{2,3},{3,2},{4,5},{5,4},{6,7},{7,6},{8,9},{9,8},{10,11... | collective-permute-start | bytes 786440 | tf_op jit(solution)/shard_map/ppermute | solution.py:352
  79.5 17.4 %collective-permute-start.15 = (bf16[128,1024]{1,0:T(8,128)(2,1)}, bf16[128,1024]{1,0:T(8,128)(2,1)S(1)}, u32[]{:S(2)}, u32[]{:S(2)}) collective-permute-start(bf16[128,1024]{1,0:T(8,128)(2,1)} %get-tuple-element.186.normed.refs_0_), channel_id=1, source_target_pairs={{0,2},{1,3},{2,0},{3,1},{4,6},{5,7},{6,4},{7,5},{8,10},{9,11},{10,... | collective-permute-start | bytes 786440 | tf_op jit(solution)/shard_map/ppermute | solution.py:352
  81.7 15.2 %collective-permute-start.16 = (bf16[128,1024]{1,0:T(8,128)(2,1)}, bf16[128,1024]{1,0:T(8,128)(2,1)S(1)}, u32[]{:S(2)}, u32[]{:S(2)}) collective-permute-start(bf16[128,1024]{1,0:T(8,128)(2,1)} %get-tuple-element.186.normed.refs_0_), channel_id=1, source_target_pairs={{0,3},{1,2},{2,1},{3,0},{4,7},{5,6},{6,5},{7,4},{8,11},{9,10},{10,... | collective-permute-start | bytes 786440 | tf_op jit(solution)/shard_map/ppermute | solution.py:352
  96.9 0.8 copy-start.12
  96.9 9.8 %copy-start.13 = (bf16[128,1024]{1,0:T(8,128)(2,1)}, bf16[128,1024]{1,0:T(8,128)(2,1)S(1)}, u32[]{:S(2)}) copy-start(bf16[128,1024]{1,0:T(8,128)(2,1)S(1)} %collective-permute-done.15.refs_2_) | copy-start | bytes 786436
  96.9 0.8 copy-start.14
  97.7 9.0 %collective-permute-start.17 = (bf16[16,32,1152]{2,1,0:T(8,128)(2,1)}, bf16[16,32,1152]{2,1,0:T(8,128)(2,1)S(1)}, u32[]{:S(2)}, u32[]{:S(2)}) collective-permute-start(bf16[16,32,1152]{2,1,0:T(8,128)(2,1)} %bitcast.46), channel_id=1, source_target_pairs={{0,8},{1,9},{2,10},{3,11},{4,12},{5,13},{6,14},{7,15},{8,0},{9,1},... | collective-permute-start | bytes 3538952 | tf_op jit(solution)/shard_map/ppermute | solution.py:352
  97.7 13.3 %all-to-all-start.1 = ((bf16[8,128,128]{2,1,0:T(8,128)(2,1)}), bf16[8,128,128]{2,1,0:T(8,128)(2,1)S(1)}, u32[]{:S(2)}, u32[]{:S(2)}) async-start(bf16[8,128,128]{2,1,0:T(8,128)(2,1)} %get-tuple-element.165), calls=%async_computation.1 | async-start | bytes 524288 | tf_op jit(solution)/shard_map/all_to_all | solution.py:953
  101.1 25.4 %collective-permute-start.18 = (bf16[128,1024]{1,0:T(8,128)(2,1)}, bf16[128,1024]{1,0:T(8,128)(2,1)S(1)}, u32[]{:S(2)}, u32[]{:S(2)}) collective-permute-start(bf16[128,1024]{1,0:T(8,128)(2,1)} %collective-permute-done.11.refs_13_), channel_id=1, source_target_pairs={{0,2},{1,3},{2,0},{3,1},{4,6},{5,7},{6,4},{7,5},{8,10},{9,11},{10,... | collective-permute-start | bytes 786440 | tf_op jit(solution)/shard_map/ppermute | solution.py:352
  103.1 23.4 %collective-permute-start.19 = (bf16[128,1024]{1,0:T(8,128)(2,1)}, bf16[128,1024]{1,0:T(8,128)(2,1)}, u32[]{:S(2)}, u32[]{:S(2)}) collective-permute-start(bf16[128,1024]{1,0:T(8,128)(2,1)} %collective-permute-done.13.refs_4_), channel_id=1, source_target_pairs={{0,1},{1,0},{2,3},{3,2},{4,5},{5,4},{6,7},{7,6},{8,9},{9,8},{10,11... | collective-permute-start | bytes 786440 | tf_op jit(solution)/shard_map/ppermute | solution.py:352
  104.5 22.1 %collective-permute-start.20 = (bf16[128,1024]{1,0:T(8,128)(2,1)}, bf16[128,1024]{1,0:T(8,128)(2,1)}, u32[]{:S(2)}, u32[]{:S(2)}) collective-permute-start(bf16[128,1024]{1,0:T(8,128)(2,1)} %collective-permute-done.13.refs_4_), channel_id=1, source_target_pairs={{0,2},{1,3},{2,0},{3,1},{4,6},{5,7},{6,4},{7,5},{8,10},{9,11},{10,... | collective-permute-start | bytes 786440 | tf_op jit(solution)/shard_map/ppermute | solution.py:352
  105.1 21.5 %collective-permute-start.21 = (bf16[128,1024]{1,0:T(8,128)(2,1)}, bf16[128,1024]{1,0:T(8,128)(2,1)}, u32[]{:S(2)}, u32[]{:S(2)}) collective-permute-start(bf16[128,1024]{1,0:T(8,128)(2,1)} %collective-permute-done.13.refs_4_), channel_id=1, source_target_pairs={{0,3},{1,2},{2,1},{3,0},{4,7},{5,6},{6,5},{7,4},{8,11},{9,10},{10,... | collective-permute-start | bytes 786440 | tf_op jit(solution)/shard_map/ppermute | solution.py:352
  106.6 1.3 copy-start.3
  109.5 21.8 %collective-permute-start.22 = (bf16[8,32,1152]{2,1,0:T(8,128)(2,1)}, bf16[8,32,1152]{2,1,0:T(8,128)(2,1)S(1)}, u32[]{:S(2)}, u32[]{:S(2)}) collective-permute-start(bf16[8,32,1152]{2,1,0:T(8,128)(2,1)} %get-tuple-element.168), channel_id=1, source_target_pairs={{0,16},{1,17},{2,18},{3,19},{4,20},{5,21},{6,22},{7,23},{8,24},{9,... | collective-permute-start | bytes 1769480 | tf_op jit(solution)/shard_map/ppermute | solution.py:352
  126.5 7.5 %copy-start.4 = (bf16[2,256,512]{2,1,0:T(8,128)(2,1)S(1)}, bf16[2,256,512]{2,1,0:T(8,128)(2,1)}, u32[]{:S(2)}) copy-start(bf16[2,256,512]{2,1,0:T(8,128)(2,1)} %get-tuple-element.183) | copy-start | bytes 1572868
  126.5 9.3 %copy-start.15 = (bf16[128,1024]{1,0:T(8,128)(2,1)}, bf16[128,1024]{1,0:T(8,128)(2,1)S(1)}, u32[]{:S(2)}) copy-start(bf16[128,1024]{1,0:T(8,128)(2,1)S(1)} %collective-permute-done.18.refs_15_) | copy-start | bytes 786436
  126.6 24.4 %all-to-all-start.2 = ((bf16[8,128,384]{2,1,0:T(8,128)(2,1)}), bf16[8,128,384]{2,1,0:T(8,128)(2,1)}, u32[]{:S(2)}, u32[]{:S(2)}) async-start(bf16[8,128,384]{2,1,0:T(8,128)(2,1)} %get-tuple-element.179.d_all), calls=%async_computation.2 | async-start | bytes 1572864 | tf_op jit(solution)/shard_map/all_to_all | solution.py:1003
  131.2 2.8 %collective-permute-start.23 = (bf16[16,32,512]{2,1,0:T(8,128)(2,1)}, bf16[16,32,512]{2,1,0:T(8,128)(2,1)S(1)}, u32[]{:S(2)}, u32[]{:S(2)}) collective-permute-start(bf16[16,32,512]{2,1,0:T(8,128)(2,1)} %bitcast.47), channel_id=1, source_target_pairs={{0,8},{1,9},{2,10},{3,11},{4,12},{5,13},{6,14},{7,15},{8,0},{9,1},... | collective-permute-start | bytes 1572872 | tf_op jit(solution)/shard_map/ppermute | solution.py:352
  132.0 16.7 %collective-permute-start.24 = (bf16[4,32,1152]{2,1,0:T(8,128)(2,1)S(1)}, bf16[4,32,1152]{2,1,0:T(8,128)(2,1)S(1)}, u32[]{:S(2)}, u32[]{:S(2)}) collective-permute-start(bf16[4,32,1152]{2,1,0:T(8,128)(2,1)S(1)} %get-tuple-element.182), channel_id=1, source_target_pairs={{0,1},{1,0},{2,3},{3,2},{4,5},{5,4},{6,7},{7,6},{8,9},{9,8},{10,11... | collective-permute-start | bytes 884744 | tf_op jit(solution)/shard_map/ppermute | solution.py:352
  134.7 11.1 %collective-permute-start.25 = (bf16[8,32,512]{2,1,0:T(8,128)(2,1)S(1)}, bf16[8,32,512]{2,1,0:T(8,128)(2,1)S(1)}, u32[]{:S(2)}, u32[]{:S(2)}) collective-permute-start(bf16[8,32,512]{2,1,0:T(8,128)(2,1)S(1)} %get-tuple-element.185), channel_id=1, source_target_pairs={{0,16},{1,17},{2,18},{3,19},{4,20},{5,21},{6,22},{7,23},{8,24},{9,... | collective-permute-start | bytes 786440 | tf_op jit(solution)/shard_map/ppermute | solution.py:352
  148.6 2.8 %collective-permute-start.26 = (bf16[2,256,512]{2,1,0:T(8,128)(2,1)}, bf16[2,256,512]{2,1,0:T(8,128)(2,1)S(1)}, u32[]{:S(2)}, u32[]{:S(2)}) collective-permute-start(bf16[2,256,512]{2,1,0:T(8,128)(2,1)} %get-tuple-element.205), channel_id=1, source_target_pairs={{0,8},{1,9},{2,10},{3,11},{4,12},{5,13},{6,14},{7,15},{8,0},{9,1},... | collective-permute-start | bytes 1572872 | tf_op jit(solution)/shard_map/ppermute | solution.py:352
  148.6 3.0 %collective-permute-start.27 = (bf16[2,128,1024]{2,1,0:T(8,128)(2,1)}, bf16[2,128,1024]{2,1,0:T(8,128)(2,1)}, u32[]{:S(2)}, u32[]{:S(2)}) collective-permute-start(bf16[2,128,1024]{2,1,0:T(8,128)(2,1)} %get-tuple-element.207), channel_id=1, source_target_pairs={{0,8},{1,9},{2,10},{3,11},{4,12},{5,13},{6,14},{7,15},{8,0},{9,1},... | collective-permute-start | bytes 1572872 | tf_op jit(solution)/shard_map/ppermute | solution.py:352
  151.5 0.8 copy-start.6
  154.6 8.4 %collective-permute-start.28 = (bf16[8,32,512]{2,1,0:T(8,128)(2,1)S(1)}, bf16[8,32,512]{2,1,0:T(8,128)(2,1)S(1)}, u32[]{:S(2)}, u32[]{:S(2)}) collective-permute-start(bf16[8,32,512]{2,1,0:T(8,128)(2,1)S(1)} %get-tuple-element.211), channel_id=1, source_target_pairs={{0,16},{1,17},{2,18},{3,19},{4,20},{5,21},{6,22},{7,23},{8,24},{9,... | collective-permute-start | bytes 786440 | tf_op jit(solution)/shard_map/ppermute | solution.py:352
  155.8 9.7 %collective-permute-start.29 = (bf16[2,32,1152]{2,1,0:T(8,128)(2,1)S(1)}, bf16[2,32,1152]{2,1,0:T(8,128)(2,1)S(1)}, u32[]{:S(2)}, u32[]{:S(2)}) collective-permute-start(bf16[2,32,1152]{2,1,0:T(8,128)(2,1)S(1)} %get-tuple-element.225), channel_id=1, source_target_pairs={{0,4},{1,5},{2,6},{3,7},{4,0},{5,1},{6,2},{7,3},{8,12},{9,13},{10,... | collective-permute-start | bytes 442376 | tf_op jit(solution)/shard_map/ppermute | solution.py:352
  166.1 13.4 %collective-permute-start.30 = (bf16[1,32,1152]{2,1,0:T(8,128)(2,1)S(1)}, bf16[1,32,1152]{2,1,0:T(8,128)(2,1)S(1)}, u32[]{:S(2)}, u32[]{:S(2)}) collective-permute-start(bf16[1,32,1152]{2,1,0:T(8,128)(2,1)S(1)} %get-tuple-element.227), channel_id=1, source_target_pairs={{0,2},{1,3},{2,0},{3,1},{4,6},{5,7},{6,4},{7,5},{8,10},{9,11},{10,... | collective-permute-start | bytes 221192 | tf_op jit(solution)/shard_map/ppermute | solution.py:352
  168.3 17.7 %all-to-all-start.3 = ((bf16[8,64,512]{2,1,0:T(8,128)(2,1)}), bf16[8,64,512]{2,1,0:T(8,128)(2,1)S(1)}, u32[]{:S(2)}, u32[]{:S(2)}) async-start(bf16[8,64,512]{2,1,0:T(8,128)(2,1)} %shard_map.278), calls=%async_computation.3 | async-start | bytes 1048576 | tf_op jit(solution)/shard_map/all_to_all | solution.py:1001
  171.8 9.5 %collective-permute-start.31 = (bf16[128,1024]{1,0:T(8,128)(2,1)S(1)}, bf16[128,1024]{1,0:T(8,128)(2,1)S(1)}, u32[]{:S(2)}, u32[]{:S(2)}) collective-permute-start(bf16[128,1024]{1,0:T(8,128)(2,1)S(1)} %get-tuple-element.231), channel_id=1, source_target_pairs={{0,16},{1,17},{2,18},{3,19},{4,20},{5,21},{6,22},{7,23},{8,24},{9,... | collective-permute-start | bytes 786440 | tf_op jit(solution)/shard_map/ppermute | solution.py:352

commit v7 on v6

--- a/solution.py
+++ b/solution.py
@@ -471,7 +471,7 @@
     values = v_all[...]
     queries = q[...]
     own = id_col[...]
-    allowed = jnp.concatenate([own, own], 1) == id_row[0:1, :]
+    allowed = jnp.concatenate([own] * 4, 1) == id_row[0:1, :]
     halves, scales = [], []
     for head in range(2):
         mine = jnp.where(head_mask(queries.shape, head), queries, jnp.zeros_like(queries))
@@ -484,10 +484,10 @@
         halves.append(outer_sum(values, low)[64 * head : 64 * head + 64] * scale)
     out = jnp.concatenate(halves, 0).T
     att_f[...] = out
-    row_scale[...] = jnp.concatenate([jnp.broadcast_to(v, (64, 256)) for v in scales], 0).T
+    row_scale[...] = jnp.concatenate([jnp.broadcast_to(v, (64, 512)) for v in scales], 0).T
     step = pl.program_id(0)
-    att_low[place[0] ^ (2 * step)] = out[:128].astype(BF)
-    att_low[place[0] ^ (2 * step + 1)] = out[128:].astype(BF)
+    for m in range(4):
+        att_low[place[0] ^ (4 * step + m)] = out[128 * m : 128 * m + 128].astype(BF)
 
 
 def proj_body(place, att, tok, proj_w, vecs, middle, normed, att_rows):
@@ -608,7 +608,7 @@
     keys = k_all[...]
     values = v_all[...]
     queries = q[...]
-    d_out = jnp.concatenate([d_att[place[0] ^ (2 * step)], d_att[place[0] ^ (2 * step + 1)]], 0)
+    d_out = jnp.concatenate([d_att[place[0] ^ (4 * step + m)] for m in range(4)], 0)
     scaled = d_out.astype(F32) * row_scale[...]
     d_out = scaled.astype(BF)
     products = (d_out.astype(F32) * att_f[...]).T
@@ -625,7 +625,7 @@
     first = head_mask((1024, 128), 0)
     dk_new = jnp.where(first, key_parts[0], key_parts[1])
     dv_new = jnp.where(first, value_parts[0], value_parts[1])
-    dq[pl.ds(pl.multiple_of(step * 256, 256), 256), :] = jnp.concatenate(query_parts, 0).T
+    dq[pl.ds(pl.multiple_of(step * 512, 512), 512), :] = jnp.concatenate(query_parts, 0).T
 
     @pl.when(step == 0)
     def _():
@@ -897,14 +897,15 @@
     )
     step_rows = pl.BlockSpec((256, 128), lambda i, s: (i, 0))
     flat = whole((1024, 128))
+    two_rows = pl.BlockSpec((512, 128), lambda i, s: (i, 0))
     att_f, att_low, probs, row_scale = call(
         attend_body,
-        (4,),
+        (2,),
         [
-            step_rows, flat, flat, flat, pl.BlockSpec((8, 256), lambda i, s: (0, i)),
+            two_rows, flat, flat, flat, pl.BlockSpec((8, 512), lambda i, s: (0, i)),
         ],
-        [step_rows, whole((8, 128, 128)), pl.BlockSpec((2, 1024, 256), lambda i, s: (0, 0, i)),
-         step_rows],
+        [two_rows, whole((8, 128, 128)), pl.BlockSpec((2, 1024, 512), lambda i, s: (0, 0, i)),
+         two_rows],
         [arr((1024, 128), F32), arr((8, 128, 128), BF), arr((2, 1024, 1024), BF),
          arr((1024, 128), F32)],
         [],
@@ -965,10 +966,10 @@
 
     d_all, qkv_bias_part = call(
         attend_back_body,
-        (4,),
+        (2,),
         [
-            pl.BlockSpec((2, 1024, 256), lambda i, s: (0, 0, i)), whole((8, 128, 128)), step_rows,
-            step_rows, step_rows, flat, flat, flat, flat,
+            pl.BlockSpec((2, 1024, 512), lambda i, s: (0, 0, i)), whole((8, 128, 128)), two_rows,
+            two_rows, two_rows, flat, flat, flat, flat,
         ],
         [whole((8, 128, 384)), whole((1, 384))],
         [arr((8, 128, 384), BF), arr((1, 384), F32)],

time: 189 us -> 187 us (0.989)
  Pallas kernels: 93.8 us -> 91.4 us
    pallas_call x19, Pallas kernels: 93.8 us -> 91.4 us  [call(): pl.pallas_call(body, grid_spec=pltpu.PrefetchScalarGridSpec(num_scalar_pr...]
  transfers between devices with their start and end apart: 36 -> 36, of which waited for: 13 -> 11; matrix products, arithmetic and copies ran while one was open for 5% -> 5% of each run, Pallas kernels for 48% -> 47%
where the time goes in v7:
time: 187 us; the launch traced here: 186 us
  Pallas kernels  91.4 us (49%)
  starting transfers between devices  55.9 us (30%)
  waiting for transfers between devices  23.1 us (12%)
  local copies, waits for them, and re-layouts  13.3 us (7%)
    pallas_call x19, Pallas kernels, call(): pl.pallas_call(body, grid_spec=pltpu.PrefetchScalarGridSpec(num_scalar_pr...  91.4 us
    ppermute x32, starting transfers between devices, swap_over(): return lax.ppermute(value, AXES, [(i, i ^ mask) for i in range(32)])  39.9 us
    ppermute x32, waiting for transfers between devices, swap_over(): return lax.ppermute(value, AXES, [(i, i ^ mask) for i in range(32)])  11.7 us
    reshape x8, local copies, waits for them, and re-layouts, fast_shards(): v.astype(F32).reshape(-1, 1024)  5.52 us
    unnamed x32, local copies, waits for them, and re-layouts  5.21 us
    all_to_all x1, waiting for transfers between devices, fast_shards(): att_in = lax.all_to_all(att_low, ROW, 0, 0, tiled=True)  4.78 us
    all_to_all x1, starting transfers between devices, fast_shards(): att_in = lax.all_to_all(att_low, ROW, 0, 0, tiled=True)  4.63 us
    all_to_all x1, starting transfers between devices, fast_shards(): moved = lax.all_to_all(d_all, ROW, 0, 0, tiled=True)  4.43 us
  transfers between devices with their start and end apart: 36, of which 11 were waited for; matrix products, arithmetic and copies ran while one was open for 5% of the time, Pallas kernels for 47%

profile of v7, /device:TPU:0, one launch (start us, length us, event | category | flops | bytes accessed | tf_op | source)
XLA Modules:
  0.0 185.5 jit_solution(13295925399538134822)
XLA Ops:
  0.6 4.1 %collective-permute-start = (bf16[128,1024]{1,0:T(8,128)(2,1)}, bf16[128,1024]{1,0:T(8,128)(2,1)S(1)}, u32[]{:S(2)}, u32[]{:S(2)}) collective-permute-start(bf16[128,1024]{1,0:T(8,128)(2,1)} %bitcast.34), channel_id=1, source_target_pairs={{0,4},{1,5},{2,6},{3,7},{4,0},{5,1},{6,2},{7,3},{8,12},{9,13},{10,... | collective-permute-start | bytes 786440 | tf_op jit(solution)/shard_map/ppermute | solution.py:352
  4.7 1.5 collective-permute-start.1
  6.3 1.6 collective-permute-start.2
  8.2 0.7 reshape.83
  8.9 0.7 reshape.84
  9.6 0.7 reshape.77
  10.3 0.7 reshape.78
  11.0 0.7 reshape.79
  11.7 0.7 reshape.80
  12.4 0.7 reshape.81
  13.9 0.7 concatenate.9.place
  14.6 0.7 copy-done.5
  15.3 4.3 %shard_map.263 = (f32[1024,128]{1,0:T(8,128)}, f32[1024,128]{1,0:T(8,128)}, f32[1024,128]{1,0:T(8,128)}, f32[8,1024]{1,0:T(8,128)S(1)}) custom-call(s32[16]{0:T(128)S(1)} %concatenate.9.place, f32[8,128]{1,0:T(8,128)S(1)} %copy-done.5), custom_call_target="tpu_custom_call" | custom-call | bytes 1024 | tf_op jit(solution)/shard_map/pallas_call | solution.py:367
  20.2 3.8 %collective-permute-done.3.refs_3_ = bf16[128,1024]{1,0:T(8,128)(2,1)S(1)} collective-permute-done((bf16[128,1024]{1,0:T(8,128)(2,1)}, bf16[128,1024]{1,0:T(8,128)(2,1)S(1)}, u32[]{:S(2)}, u32[]{:S(2)}) %collective-permute-start.3) | collective-permute-done | bytes 262176 | tf_op jit(solution)/shard_map/ppermute | solution.py:352
  24.0 1.5 collective-permute-start.4
  25.7 1.8 collective-permute-start.6
  27.5 0.9 copy-done.1
  28.5 3.7 %shard_map.264 = (bf16[512,1024]{1,0:T(8,128)(2,1)}, bf16[512,128]{1,0:T(8,128)(2,1)S(1)}, bf16[512,128]{1,0:T(8,128)(2,1)S(1)}, bf16[512,128]{1,0:T(8,128)(2,1)S(1)}) custom-call(s32[16]{0:T(128)S(1)} %concatenate.9.place, bf16[128,1024]{1,0:T(8,128)(2,1)S(1)} %bitcast.38, bf16[128,1024]{1,0:T(8,128)(2,1)S(1)} %collective-permute-done.1.refs_1_, ...), custom_call_target="tpu_custom_call" | custom-call | bytes 1024 | tf_op jit(solution)/shard_map/pallas_call | solution.py:367
  32.1 1.2 collective-permute-start.10
  33.3 2.8 %collective-permute-start.7 = (bf16[128,1024]{1,0:T(8,128)(2,1)S(1)}, bf16[128,1024]{1,0:T(8,128)(2,1)S(1)}, u32[]{:S(2)}, u32[]{:S(2)}) collective-permute-start(bf16[128,1024]{1,0:T(8,128)(2,1)S(1)} %bitcast.30), channel_id=1, source_target_pairs={{0,4},{1,5},{2,6},{3,7},{4,0},{5,1},{6,2},{7,3},{8,12},{9,13},{10,... | collective-permute-start | bytes 786440 | tf_op jit(solution)/shard_map/ppermute | solution.py:352
  36.7 0.9 collective-permute-done.5.refs_2_
  37.6 7.5 %shard_map.265 = (f32[128,4096]{1,0:T(8,128)}, f32[1,1024]{1,0:T(1,128)S(1)}) custom-call(s32[16]{0:T(128)S(1)} %concatenate.9.place, bf16[128,1024]{1,0:T(8,128)(2,1)S(1)} %bitcast.33, bf16[4096,1024]{1,0:T(8,128)(2,1)} %down.3), custom_call_target="tpu_custom_call" | custom-call | bytes 1024 | tf_op jit(solution)/shard_map/pallas_call | solution.py:367
  45.0 1.0 collective-permute-done.6.refs_3_
  46.0 3.7 %shard_map.266 = (bf16[512,1024]{1,0:T(8,128)(2,1)}, bf16[1024,128]{1,0:T(8,128)(2,1)S(1)}, bf16[1024,128]{1,0:T(8,128)(2,1)S(1)}, bf16[1024,128]{1,0:T(8,128)(2,1)S(1)}) custom-call(s32[16]{0:T(128)S(1)} %concatenate.9.place, bf16[128,1024]{1,0:T(8,128)(2,1)S(1)} %collective-permute-done.refs_0_, bf16[128,1024]{1,0:T(8,128)(2,1)S(1)} %collective-permute-done.4.refs_1_, ...), custom_call_target="tpu_custom_call" | custom-call | bytes 1024 | tf_op jit(solution)/shard_map/pallas_call | solution.py:367
  49.7 7.6 %shard_map.267 = (f32[1024,128]{1,0:T(8,128)}, bf16[8,128,128]{2,1,0:T(8,128)(2,1)}, bf16[2,1024,1024]{2,1,0:T(8,128)(2,1)}, f32[1024,128]{1,0:T(8,128)}) custom-call(s32[16]{0:T(128)S(1)} %concatenate.9.place, bf16[1024,128]{1,0:T(8,128)(2,1)S(1)} %get-tuple-element.141.q, bf16[1024,128]{1,0:T(8,128)(2,1)S(1)} %get-tuple-element.142.k_all, ...), custom_call_target="tpu_custom_call" | custom-call | bytes 1024 | tf_op jit(solution)/shard_map/pallas_call | solution.py:367
  57.4 0.7 copy-done.9
  58.2 4.6 %all-to-all-start = ((bf16[8,128,128]{2,1,0:T(8,128)(2,1)}), bf16[8,128,128]{2,1,0:T(8,128)(2,1)S(1)}, u32[]{:S(2)}, u32[]{:S(2)}) async-start(bf16[8,128,128]{2,1,0:T(8,128)(2,1)} %get-tuple-element.147), calls=%async_computation | async-start | bytes 524288 | tf_op jit(solution)/shard_map/all_to_all | solution.py:917
  62.8 2.0 %collective-permute-start.11 = (bf16[128,1024]{1,0:T(8,128)(2,1)S(1)}, bf16[128,1024]{1,0:T(8,128)(2,1)}, u32[]{:S(2)}, u32[]{:S(2)}) collective-permute-start(bf16[128,1024]{1,0:T(8,128)(2,1)S(1)} %collective-permute-done.7.refs_12_), channel_id=1, source_target_pairs={{0,1},{1,0},{2,3},{3,2},{4,5},{5,4},{6,7},{7,6},{8,9},{9,8},{10,11... | collective-permute-start | bytes 786440 | tf_op jit(solution)/shard_map/ppermute | solution.py:352
  64.8 1.5 collective-permute-start.12
  66.3 4.8 %all-to-all-done.att = bf16[8,128,128]{2,1,0:T(8,128)(2,1)S(1)} async-done(((bf16[8,128,128]{2,1,0:T(8,128)(2,1)}), bf16[8,128,128]{2,1,0:T(8,128)(2,1)S(1)}, u32[]{:S(2)}, u32[]{:S(2)}) %all-to-all-start) | async-done | bytes 262176 | tf_op jit(solution)/shard_map/all_to_all | solution.py:917
  71.1 3.7 %shard_map.268 = (f32[128,1024]{1,0:T(8,128)}, bf16[128,1024]{1,0:T(8,128)(2,1)}, bf16[128,1024]{1,0:T(8,128)(2,1)}) custom-call(s32[16]{0:T(128)S(1)} %concatenate.9.place, bf16[8,128,128]{2,1,0:T(8,128)(2,1)S(1)} %all-to-all-done.att, bf16[128,1024]{1,0:T(8,128)(2,1)S(1)} %bitcast.39, bf16[1024,1024]{1,0:T(8,128)(2,1)} %proj_w.3, ...), custom_call_target="tpu_custom_call" | custom-call | bytes 1024 | tf_op jit(solution)/shard_map/pallas_call | solution.py:367
  74.7 1.1 collective-permute-done.12.refs_14_
  75.8 1.5 collective-permute-start.13
  77.7 2.2 %collective-permute-start.15 = (bf16[128,1024]{1,0:T(8,128)(2,1)}, bf16[128,1024]{1,0:T(8,128)(2,1)S(1)}, u32[]{:S(2)}, u32[]{:S(2)}) collective-permute-start(bf16[128,1024]{1,0:T(8,128)(2,1)} %get-tuple-element.186.normed.refs_0_), channel_id=1, source_target_pairs={{0,2},{1,3},{2,0},{3,1},{4,6},{5,7},{6,4},{7,5},{8,10},{9,11},{10,... | collective-permute-start | bytes 786440 | tf_op jit(solution)/shard_map/ppermute | solution.py:352
  79.9 1.4 collective-permute-start.16
  81.3 13.7 %shard_map.269 = (bf16[128,4096]{1,0:T(8,128)(2,1)}, f32[128,1024]{1,0:T(8,128)}, bf16[8,128,128]{2,1,0:T(8,128)(2,1)}, bf16[2,8,32,1152]{3,2,1,0:T(8,128)(2,1)}, bf16[2,8,32,1152]{3,2,1,0:T(8,128)(2,1)}) custom-call(s32[16]{0:T(128)S(1)} %concatenate.9.place, bf16[128,1024]{1,0:T(8,128)(2,1)} %get-tuple-element.186.normed.refs_0_, ...), custom_call_target="tpu_custom_call" | custom-call | bytes 1024 | tf_op jit(solution)/shard_map/pallas_call | solution.py:367
  95.1 0.8 copy-done.14
  95.9 3.4 %all-to-all-start.1 = ((bf16[8,128,128]{2,1,0:T(8,128)(2,1)}), bf16[8,128,128]{2,1,0:T(8,128)(2,1)S(1)}, u32[]{:S(2)}, u32[]{:S(2)}) async-start(bf16[8,128,128]{2,1,0:T(8,128)(2,1)} %get-tuple-element.165), calls=%async_computation.1 | async-start | bytes 524288 | tf_op jit(solution)/shard_map/all_to_all | solution.py:954
  99.3 2.0 %collective-permute-start.18 = (bf16[128,1024]{1,0:T(8,128)(2,1)}, bf16[128,1024]{1,0:T(8,128)(2,1)S(1)}, u32[]{:S(2)}, u32[]{:S(2)}) collective-permute-start(bf16[128,1024]{1,0:T(8,128)(2,1)} %collective-permute-done.11.refs_13_), channel_id=1, source_target_pairs={{0,2},{1,3},{2,0},{3,1},{4,6},{5,7},{6,4},{7,5},{8,10},{9,11},{10,... | collective-permute-start | bytes 786440 | tf_op jit(solution)/shard_map/ppermute | solution.py:352
  101.4 1.4 collective-permute-start.19
  103.3 1.6 collective-permute-start.21
  104.9 1.3 copy-done.3
  106.1 1.6 shard_map.270
  107.7 1.5 collective-permute-start.22
  109.2 8.7 %shard_map.271 = (bf16[8,128,384]{2,1,0:T(8,128)(2,1)}, f32[1,384]{1,0:T(1,128)S(1)}) custom-call(s32[16]{0:T(128)S(1)} %concatenate.9.place, bf16[2,1024,1024]{2,1,0:T(8,128)(2,1)} %get-tuple-element.164.probs, bf16[8,128,128]{2,1,0:T(8,128)(2,1)S(1)} %all-to-all-done.1.d_att, f32[1024,128]{1,0:T(8,128)} %get-tuple-element.170.att_f, ...), custom_call_target="tpu_custom_call" | custom-call | bytes 1024 | tf_op jit(solution)/shard_map/pallas_call | solution.py:367
  117.9 6.2 %shard_map.272 = (bf16[2,256,512]{2,1,0:T(8,128)(2,1)}, bf16[2,256,512]{2,1,0:T(8,128)(2,1)}) custom-call(s32[16]{0:T(128)S(1)} %concatenate.9.place, bf16[512,1024]{1,0:T(8,128)(2,1)} %get-tuple-element.173.h0, bf16[512,1024]{1,0:T(8,128)(2,1)} %get-tuple-element.174.h1, bf16[8,128,384]{2,1,0:T(8,128)(2,1)} %get-tuple-element.179.d_all, ...), custom_call_target="tpu_custom_call" | custom-call | bytes 1024 | tf_op jit(solution)/shard_map/pallas_call | solution.py:367
  124.6 4.4 %all-to-all-start.2 = ((bf16[8,128,384]{2,1,0:T(8,128)(2,1)}), bf16[8,128,384]{2,1,0:T(8,128)(2,1)}, u32[]{:S(2)}, u32[]{:S(2)}) async-start(bf16[8,128,384]{2,1,0:T(8,128)(2,1)} %get-tuple-element.179.d_all), calls=%async_computation.2 | async-start | bytes 1572864 | tf_op jit(solution)/shard_map/all_to_all | solution.py:1004
  129.8 1.7 collective-permute-start.24
  132.2 1.5 collective-permute-start.25
  133.7 9.9 %shard_map.275 = (bf16[2,128,1024]{2,1,0:T(8,128)(2,1)}, bf16[2,128,1024]{2,1,0:T(8,128)(2,1)}, bf16[2,256,512]{2,1,0:T(8,128)(2,1)}, bf16[2,256,512]{2,1,0:T(8,128)(2,1)}) custom-call(s32[16]{0:T(128)S(1)} %concatenate.9.place, bf16[128,1024]{1,0:T(8,128)(2,1)} %get-tuple-element.186.normed.refs_0_, bf16[128,1024]{1,0:T(8,128)(2,1)} %copy-done.12, ...), custom_call_target="tpu_custom_call" | custom-call | bytes 1024 | tf_op jit(solution)/shard_map/pallas_call | solution.py:367
  143.7 2.5 %collective-permute-done.24.refs_5_ = bf16[4,32,1152]{2,1,0:T(8,128)(2,1)S(1)} collective-permute-done((bf16[4,32,1152]{2,1,0:T(8,128)(2,1)S(1)}, bf16[4,32,1152]{2,1,0:T(8,128)(2,1)S(1)}, u32[]{:S(2)}, u32[]{:S(2)}) %collective-permute-start.24) | collective-permute-done | bytes 294944 | tf_op jit(solution)/shard_map/ppermute | solution.py:352
  146.7 2.4 %all-to-all-done.2.came = bf16[8,128,384]{2,1,0:T(8,128)(2,1)} async-done(((bf16[8,128,384]{2,1,0:T(8,128)(2,1)}), bf16[8,128,384]{2,1,0:T(8,128)(2,1)}, u32[]{:S(2)}, u32[]{:S(2)}) %all-to-all-start.2) | async-done | bytes 786464 | tf_op jit(solution)/shard_map/all_to_all | solution.py:1004
  149.2 0.8 copy-done.6
  150.0 2.4 %shard_map.276 = (bf16[8,32,512]{2,1,0:T(8,128)(2,1)S(1)}, bf16[8,32,512]{2,1,0:T(8,128)(2,1)S(1)}, bf16[128,1024]{1,0:T(8,128)(2,1)S(1)}, bf16[128,1024]{1,0:T(...) custom-call(s32[16]{0:T(128)S(1)} %concatenate.9.place, ...), custom_call_target="tpu_custom_call" | custom-call | bytes 1024 | tf_op jit(solution)/shard_map/pallas_call | solution.py:367
  152.3 1.6 collective-permute-start.28
  154.0 6.7 %shard_map.277 = f32[128,1024]{1,0:T(8,128)} custom-call(s32[16]{0:T(128)S(1)} %concatenate.9.place, bf16[8,128,384]{2,1,0:T(8,128)(2,1)} %all-to-all-done.2.came, bf16[1024,3072]{1,0:T(8,128)(2,1)} %w.1, bf16[128,1024]{1,0:T(8,128)(2,1)S(1)} %bitcast.40, f32[128,1024]{1,0:T(8,128)} %get-tuple-element.213.d_mid, f32[15,1024]{1,0:T(8,128)S(1)} %concatenate.11.refs_4_.vecs.refs_24_), custom_call_target="tpu_custom_call" | custom-call | bytes 1024 | tf_op jit(solution)/shard_map/pallas_call | solution.py:367
  160.7 1.5 shard_map.278
  162.2 1.2 collective-permute-done.29.came
  164.0 2.3 %collective-permute-start.30 = (bf16[1,32,1152]{2,1,0:T(8,128)(2,1)S(1)}, bf16[1,32,1152]{2,1,0:T(8,128)(2,1)S(1)}, u32[]{:S(2)}, u32[]{:S(2)}) collective-permute-start(bf16[1,32,1152]{2,1,0:T(8,128)(2,1)S(1)} %get-tuple-element.227), channel_id=1, source_target_pairs={{0,2},{1,3},{2,0},{3,1},{4,6},{5,7},{6,4},{7,5},{8,10},{9,11},{10,... | collective-permute-start | bytes 221192 | tf_op jit(solution)/shard_map/ppermute | solution.py:352
  166.2 3.5 %all-to-all-start.3 = ((bf16[8,64,512]{2,1,0:T(8,128)(2,1)}), bf16[8,64,512]{2,1,0:T(8,128)(2,1)S(1)}, u32[]{:S(2)}, u32[]{:S(2)}) async-start(bf16[8,64,512]{2,1,0:T(8,128)(2,1)} %shard_map.278), calls=%async_computation.3 | async-start | bytes 1048576 | tf_op jit(solution)/shard_map/all_to_all | solution.py:1002
  170.3 6.7 %shard_map.279 = bf16[128,1024]{1,0:T(8,128)(2,1)} custom-call(s32[16]{0:T(128)S(1)} %concatenate.9.place, bf16[128,4096]{1,0:T(8,128)(2,1)} %get-tuple-element.218.active, bf16[4096,1024]{1,0:T(8,128)(2,1)} %down.3, f32[128,1024]{1,0:T(8,128)} %get-tuple-element.155.middle, f32[15,1024]{1,0:T(8,128)S(1)} %concatenate.11.refs_4_.vecs.refs_24_), custom_call_target="tpu_custom_call" | custom-call | bytes 1024 | tf_op jit(solution)/shard_map/pallas_call | solution.py:367
  178.9 0.9 convert_add_fusion
  179.7 4.2 %all-to-all-done.3.came = bf16[8,64,512]{2,1,0:T(8,128)(2,1)S(1)} async-done(((bf16[8,64,512]{2,1,0:T(8,128)(2,1)}), bf16[8,64,512]{2,1,0:T(8,128)(2,1)S(1)}, u32[]{:S(2)}, u32[]{:S(2)}) %all-to-all-start.3) | async-done | bytes 524320 | tf_op jit(solution)/shard_map/all_to_all | solution.py:1002
  183.9 1.6 shard_map.280
  (77 shorter events, 9.1 us)
Async XLA Ops:
  0.6 19.0 %collective-permute-start = (bf16[128,1024]{1,0:T(8,128)(2,1)}, bf16[128,1024]{1,0:T(8,128)(2,1)S(1)}, u32[]{:S(2)}, u32[]{:S(2)}) collective-permute-start(bf16[128,1024]{1,0:T(8,128)(2,1)} %bitcast.34), channel_id=1, source_target_pairs={{0,4},{1,5},{2,6},{3,7},{4,0},{5,1},{6,2},{7,3},{8,12},{9,13},{10,... | collective-permute-start | bytes 786440 | tf_op jit(solution)/shard_map/ppermute | solution.py:352
  4.7 14.9 %collective-permute-start.1 = (bf16[128,1024]{1,0:T(8,128)(2,1)}, bf16[128,1024]{1,0:T(8,128)(2,1)S(1)}, u32[]{:S(2)}, u32[]{:S(2)}) collective-permute-start(bf16[128,1024]{1,0:T(8,128)(2,1)} %bitcast.35), channel_id=1, source_target_pairs={{0,1},{1,0},{2,3},{3,2},{4,5},{5,4},{6,7},{7,6},{8,9},{9,8},{10,11... | collective-permute-start | bytes 786440 | tf_op jit(solution)/shard_map/ppermute | solution.py:352
  6.3 13.9 %collective-permute-start.2 = (bf16[128,1024]{1,0:T(8,128)(2,1)}, bf16[128,1024]{1,0:T(8,128)(2,1)S(1)}, u32[]{:S(2)}, u32[]{:S(2)}) collective-permute-start(bf16[128,1024]{1,0:T(8,128)(2,1)} %bitcast.36), channel_id=1, source_target_pairs={{0,2},{1,3},{2,0},{3,1},{4,6},{5,7},{6,4},{7,5},{8,10},{9,11},{10,... | collective-permute-start | bytes 786440 | tf_op jit(solution)/shard_map/ppermute | solution.py:352
  7.8 16.2 %collective-permute-start.3 = (bf16[128,1024]{1,0:T(8,128)(2,1)}, bf16[128,1024]{1,0:T(8,128)(2,1)S(1)}, u32[]{:S(2)}, u32[]{:S(2)}) collective-permute-start(bf16[128,1024]{1,0:T(8,128)(2,1)} %bitcast.37), channel_id=1, source_target_pairs={{0,3},{1,2},{2,1},{3,0},{4,7},{5,6},{6,5},{7,4},{8,11},{9,10},{10,... | collective-permute-start | bytes 786440 | tf_op jit(solution)/shard_map/ppermute | solution.py:352
  14.6 0.7 copy-start.5
  24.0 12.1 %collective-permute-start.4 = (bf16[128,1024]{1,0:T(8,128)(2,1)S(1)}, bf16[128,1024]{1,0:T(8,128)(2,1)S(1)}, u32[]{:S(2)}, u32[]{:S(2)}) collective-permute-start(bf16[128,1024]{1,0:T(8,128)(2,1)S(1)} %collective-permute-done.refs_0_), channel_id=1, source_target_pairs={{0,1},{1,0},{2,3},{3,2},{4,5},{5,4},{6,7},{7,6},{8,9},{9,8},{10,11... | collective-permute-start | bytes 786440 | tf_op jit(solution)/shard_map/ppermute | solution.py:352
  25.5 12.1 %collective-permute-start.5 = (bf16[128,1024]{1,0:T(8,128)(2,1)S(1)}, bf16[128,1024]{1,0:T(8,128)(2,1)S(1)}, u32[]{:S(2)}, u32[]{:S(2)}) collective-permute-start(bf16[128,1024]{1,0:T(8,128)(2,1)S(1)} %collective-permute-done.refs_0_), channel_id=1, source_target_pairs={{0,2},{1,3},{2,0},{3,1},{4,6},{5,7},{6,4},{7,5},{8,10},{9,11},{10,... | collective-permute-start | bytes 786440 | tf_op jit(solution)/shard_map/ppermute | solution.py:352
  25.7 20.3 %collective-permute-start.6 = (bf16[128,1024]{1,0:T(8,128)(2,1)S(1)}, bf16[128,1024]{1,0:T(8,128)(2,1)S(1)}, u32[]{:S(2)}, u32[]{:S(2)}) collective-permute-start(bf16[128,1024]{1,0:T(8,128)(2,1)S(1)} %collective-permute-done.refs_0_), channel_id=1, source_target_pairs={{0,3},{1,2},{2,1},{3,0},{4,7},{5,6},{6,5},{7,4},{8,11},{9,10},{10,... | collective-permute-start | bytes 786440 | tf_op jit(solution)/shard_map/ppermute | solution.py:352
  27.5 0.9 copy-start.1
  28.5 3.7 %copy-start = (bf16[1,128,1024]{2,1,0:T(8,128)(2,1)S(1)}, bf16[1,128,1024]{2,1,0:T(8,128)(2,1)}, u32[]{:S(2)}) copy-start(bf16[1,128,1024]{2,1,0:T(8,128)(2,1)} %param.30) | copy-start | bytes 786436
  32.1 25.2 %collective-permute-start.10 = (bf16[128,1024]{1,0:T(8,128)(2,1)S(1)}, bf16[128,1024]{1,0:T(8,128)(2,1)S(1)}, u32[]{:S(2)}, u32[]{:S(2)}) collective-permute-start(bf16[128,1024]{1,0:T(8,128)(2,1)S(1)} %bitcast.29), channel_id=1, source_target_pairs={{0,3},{1,2},{2,1},{3,0},{4,7},{5,6},{6,5},{7,4},{8,11},{9,10},{10,... | collective-permute-start | bytes 786440 | tf_op jit(solution)/shard_map/ppermute | solution.py:352
  33.3 24.1 %collective-permute-start.7 = (bf16[128,1024]{1,0:T(8,128)(2,1)S(1)}, bf16[128,1024]{1,0:T(8,128)(2,1)S(1)}, u32[]{:S(2)}, u32[]{:S(2)}) collective-permute-start(bf16[128,1024]{1,0:T(8,128)(2,1)S(1)} %bitcast.30), channel_id=1, source_target_pairs={{0,4},{1,5},{2,6},{3,7},{4,0},{5,1},{6,2},{7,3},{8,12},{9,13},{10,... | collective-permute-start | bytes 786440 | tf_op jit(solution)/shard_map/ppermute | solution.py:352
  36.1 21.3 %collective-permute-start.8 = (bf16[128,1024]{1,0:T(8,128)(2,1)S(1)}, bf16[128,1024]{1,0:T(8,128)(2,1)S(1)}, u32[]{:S(2)}, u32[]{:S(2)}) collective-permute-start(bf16[128,1024]{1,0:T(8,128)(2,1)S(1)} %bitcast.31), channel_id=1, source_target_pairs={{0,1},{1,0},{2,3},{3,2},{4,5},{5,4},{6,7},{7,6},{8,9},{9,8},{10,11... | collective-permute-start | bytes 786440 | tf_op jit(solution)/shard_map/ppermute | solution.py:352
  37.5 19.9 %collective-permute-start.9 = (bf16[128,1024]{1,0:T(8,128)(2,1)S(1)}, bf16[128,1024]{1,0:T(8,128)(2,1)S(1)}, u32[]{:S(2)}, u32[]{:S(2)}) collective-permute-start(bf16[128,1024]{1,0:T(8,128)(2,1)S(1)} %bitcast.32), channel_id=1, source_target_pairs={{0,2},{1,3},{2,0},{3,1},{4,6},{5,7},{6,4},{7,5},{8,10},{9,11},{10,... | collective-permute-start | bytes 786440 | tf_op jit(solution)/shard_map/ppermute | solution.py:352
  46.0 25.0 %copy-start.2 = (bf16[1,128,1024]{2,1,0:T(8,128)(2,1)S(1)}, bf16[1,128,1024]{2,1,0:T(8,128)(2,1)}, u32[]{:S(2)}) copy-start(bf16[1,128,1024]{2,1,0:T(8,128)(2,1)} %param.16) | copy-start | bytes 786436
  57.4 37.6 %copy-start.7 = (bf16[128,1024]{1,0:T(8,128)(2,1)}, bf16[128,1024]{1,0:T(8,128)(2,1)S(1)}, u32[]{:S(2)}) copy-start(bf16[128,1024]{1,0:T(8,128)(2,1)S(1)} %collective-permute-done.10.refs_11_) | copy-start | bytes 786436
  57.4 37.6 %copy-start.8 = (bf16[128,1024]{1,0:T(8,128)(2,1)}, bf16[128,1024]{1,0:T(8,128)(2,1)S(1)}, u32[]{:S(2)}) copy-start(bf16[128,1024]{1,0:T(8,128)(2,1)S(1)} %collective-permute-done.7.refs_12_) | copy-start | bytes 786436
  57.4 0.7 copy-start.9
  58.1 36.9 %copy-start.10 = (bf16[128,1024]{1,0:T(8,128)(2,1)}, bf16[128,1024]{1,0:T(8,128)(2,1)S(1)}, u32[]{:S(2)}) copy-start(bf16[128,1024]{1,0:T(8,128)(2,1)S(1)} %collective-permute-done.9.refs_10_) | copy-start | bytes 786436
  58.2 12.9 %all-to-all-start = ((bf16[8,128,128]{2,1,0:T(8,128)(2,1)}), bf16[8,128,128]{2,1,0:T(8,128)(2,1)S(1)}, u32[]{:S(2)}, u32[]{:S(2)}) async-start(bf16[8,128,128]{2,1,0:T(8,128)(2,1)} %get-tuple-element.147), calls=%async_computation | async-start | bytes 524288 | tf_op jit(solution)/shard_map/all_to_all | solution.py:917
  62.8 11.9 %collective-permute-start.11 = (bf16[128,1024]{1,0:T(8,128)(2,1)S(1)}, bf16[128,1024]{1,0:T(8,128)(2,1)}, u32[]{:S(2)}, u32[]{:S(2)}) collective-permute-start(bf16[128,1024]{1,0:T(8,128)(2,1)S(1)} %collective-permute-done.7.refs_12_), channel_id=1, source_target_pairs={{0,1},{1,0},{2,3},{3,2},{4,5},{5,4},{6,7},{7,6},{8,9},{9,8},{10,11... | collective-permute-start | bytes 786440 | tf_op jit(solution)/shard_map/ppermute | solution.py:352
  64.8 11.0 %collective-permute-start.12 = (bf16[128,1024]{1,0:T(8,128)(2,1)S(1)}, bf16[128,1024]{1,0:T(8,128)(2,1)S(1)}, u32[]{:S(2)}, u32[]{:S(2)}) collective-permute-start(bf16[128,1024]{1,0:T(8,128)(2,1)S(1)} %collective-permute-done.7.refs_12_), channel_id=1, source_target_pairs={{0,2},{1,3},{2,0},{3,1},{4,6},{5,7},{6,4},{7,5},{8,10},{9,11},{10,... | collective-permute-start | bytes 786440 | tf_op jit(solution)/shard_map/ppermute | solution.py:352
  75.8 19.3 %copy-start.11 = (bf16[128,1024]{1,0:T(8,128)(2,1)}, bf16[128,1024]{1,0:T(8,128)(2,1)S(1)}, u32[]{:S(2)}) copy-start(bf16[128,1024]{1,0:T(8,128)(2,1)S(1)} %collective-permute-done.12.refs_14_) | copy-start | bytes 786436
  75.8 19.3 %collective-permute-start.13 = (bf16[128,1024]{1,0:T(8,128)(2,1)}, bf16[128,1024]{1,0:T(8,128)(2,1)}, u32[]{:S(2)}, u32[]{:S(2)}) collective-permute-start(bf16[128,1024]{1,0:T(8,128)(2,1)} %get-tuple-element.186.normed.refs_0_), channel_id=1, source_target_pairs={{0,4},{1,5},{2,6},{3,7},{4,0},{5,1},{6,2},{7,3},{8,12},{9,13},{10,... | collective-permute-start | bytes 786440 | tf_op jit(solution)/shard_map/ppermute | solution.py:352
  77.3 17.7 %collective-permute-start.14 = (bf16[128,1024]{1,0:T(8,128)(2,1)}, bf16[128,1024]{1,0:T(8,128)(2,1)S(1)}, u32[]{:S(2)}, u32[]{:S(2)}) collective-permute-start(bf16[128,1024]{1,0:T(8,128)(2,1)} %get-tuple-element.186.normed.refs_0_), channel_id=1, source_target_pairs={{0,1},{1,0},{2,3},{3,2},{4,5},{5,4},{6,7},{7,6},{8,9},{9,8},{10,11... | collective-permute-start | bytes 786440 | tf_op jit(solution)/shard_map/ppermute | solution.py:352
  77.7 17.4 %collective-permute-start.15 = (bf16[128,1024]{1,0:T(8,128)(2,1)}, bf16[128,1024]{1,0:T(8,128)(2,1)S(1)}, u32[]{:S(2)}, u32[]{:S(2)}) collective-permute-start(bf16[128,1024]{1,0:T(8,128)(2,1)} %get-tuple-element.186.normed.refs_0_), channel_id=1, source_target_pairs={{0,2},{1,3},{2,0},{3,1},{4,6},{5,7},{6,4},{7,5},{8,10},{9,11},{10,... | collective-permute-start | bytes 786440 | tf_op jit(solution)/shard_map/ppermute | solution.py:352
  79.9 15.2 %collective-permute-start.16 = (bf16[128,1024]{1,0:T(8,128)(2,1)}, bf16[128,1024]{1,0:T(8,128)(2,1)S(1)}, u32[]{:S(2)}, u32[]{:S(2)}) collective-permute-start(bf16[128,1024]{1,0:T(8,128)(2,1)} %get-tuple-element.186.normed.refs_0_), channel_id=1, source_target_pairs={{0,3},{1,2},{2,1},{3,0},{4,7},{5,6},{6,5},{7,4},{8,11},{9,10},{10,... | collective-permute-start | bytes 786440 | tf_op jit(solution)/shard_map/ppermute | solution.py:352
  95.1 0.8 copy-start.12
  95.1 9.8 %copy-start.13 = (bf16[128,1024]{1,0:T(8,128)(2,1)}, bf16[128,1024]{1,0:T(8,128)(2,1)S(1)}, u32[]{:S(2)}) copy-start(bf16[128,1024]{1,0:T(8,128)(2,1)S(1)} %collective-permute-done.15.refs_2_) | copy-start | bytes 786436
  95.1 0.8 copy-start.14
  95.9 9.0 %collective-permute-start.17 = (bf16[16,32,1152]{2,1,0:T(8,128)(2,1)}, bf16[16,32,1152]{2,1,0:T(8,128)(2,1)S(1)}, u32[]{:S(2)}, u32[]{:S(2)}) collective-permute-start(bf16[16,32,1152]{2,1,0:T(8,128)(2,1)} %bitcast.46), channel_id=1, source_target_pairs={{0,8},{1,9},{2,10},{3,11},{4,12},{5,13},{6,14},{7,15},{8,0},{9,1},... | collective-permute-start | bytes 3538952 | tf_op jit(solution)/shard_map/ppermute | solution.py:352
  95.9 13.3 %all-to-all-start.1 = ((bf16[8,128,128]{2,1,0:T(8,128)(2,1)}), bf16[8,128,128]{2,1,0:T(8,128)(2,1)S(1)}, u32[]{:S(2)}, u32[]{:S(2)}) async-start(bf16[8,128,128]{2,1,0:T(8,128)(2,1)} %get-tuple-element.165), calls=%async_computation.1 | async-start | bytes 524288 | tf_op jit(solution)/shard_map/all_to_all | solution.py:954
  99.3 24.8 %collective-permute-start.18 = (bf16[128,1024]{1,0:T(8,128)(2,1)}, bf16[128,1024]{1,0:T(8,128)(2,1)S(1)}, u32[]{:S(2)}, u32[]{:S(2)}) collective-permute-start(bf16[128,1024]{1,0:T(8,128)(2,1)} %collective-permute-done.11.refs_13_), channel_id=1, source_target_pairs={{0,2},{1,3},{2,0},{3,1},{4,6},{5,7},{6,4},{7,5},{8,10},{9,11},{10,... | collective-permute-start | bytes 786440 | tf_op jit(solution)/shard_map/ppermute | solution.py:352
  101.4 22.7 %collective-permute-start.19 = (bf16[128,1024]{1,0:T(8,128)(2,1)}, bf16[128,1024]{1,0:T(8,128)(2,1)}, u32[]{:S(2)}, u32[]{:S(2)}) collective-permute-start(bf16[128,1024]{1,0:T(8,128)(2,1)} %collective-permute-done.13.refs_4_), channel_id=1, source_target_pairs={{0,1},{1,0},{2,3},{3,2},{4,5},{5,4},{6,7},{7,6},{8,9},{9,8},{10,11... | collective-permute-start | bytes 786440 | tf_op jit(solution)/shard_map/ppermute | solution.py:352
  102.7 21.4 %collective-permute-start.20 = (bf16[128,1024]{1,0:T(8,128)(2,1)}, bf16[128,1024]{1,0:T(8,128)(2,1)}, u32[]{:S(2)}, u32[]{:S(2)}) collective-permute-start(bf16[128,1024]{1,0:T(8,128)(2,1)} %collective-permute-done.13.refs_4_), channel_id=1, source_target_pairs={{0,2},{1,3},{2,0},{3,1},{4,6},{5,7},{6,4},{7,5},{8,10},{9,11},{10,... | collective-permute-start | bytes 786440 | tf_op jit(solution)/shard_map/ppermute | solution.py:352
  103.3 21.3 %collective-permute-start.21 = (bf16[128,1024]{1,0:T(8,128)(2,1)}, bf16[128,1024]{1,0:T(8,128)(2,1)}, u32[]{:S(2)}, u32[]{:S(2)}) collective-permute-start(bf16[128,1024]{1,0:T(8,128)(2,1)} %collective-permute-done.13.refs_4_), channel_id=1, source_target_pairs={{0,3},{1,2},{2,1},{3,0},{4,7},{5,6},{6,5},{7,4},{8,11},{9,10},{10,... | collective-permute-start | bytes 786440 | tf_op jit(solution)/shard_map/ppermute | solution.py:352
  104.9 1.3 copy-start.3
  107.7 21.4 %collective-permute-start.22 = (bf16[8,32,1152]{2,1,0:T(8,128)(2,1)}, bf16[8,32,1152]{2,1,0:T(8,128)(2,1)S(1)}, u32[]{:S(2)}, u32[]{:S(2)}) collective-permute-start(bf16[8,32,1152]{2,1,0:T(8,128)(2,1)} %get-tuple-element.168), channel_id=1, source_target_pairs={{0,16},{1,17},{2,18},{3,19},{4,20},{5,21},{6,22},{7,23},{8,24},{9,... | collective-permute-start | bytes 1769480 | tf_op jit(solution)/shard_map/ppermute | solution.py:352
  124.1 7.5 %copy-start.4 = (bf16[2,256,512]{2,1,0:T(8,128)(2,1)S(1)}, bf16[2,256,512]{2,1,0:T(8,128)(2,1)}, u32[]{:S(2)}) copy-start(bf16[2,256,512]{2,1,0:T(8,128)(2,1)} %get-tuple-element.183) | copy-start | bytes 1572868
  124.1 9.6 %copy-start.15 = (bf16[128,1024]{1,0:T(8,128)(2,1)}, bf16[128,1024]{1,0:T(8,128)(2,1)S(1)}, u32[]{:S(2)}) copy-start(bf16[128,1024]{1,0:T(8,128)(2,1)S(1)} %collective-permute-done.18.refs_15_) | copy-start | bytes 786436
  124.6 24.5 %all-to-all-start.2 = ((bf16[8,128,384]{2,1,0:T(8,128)(2,1)}), bf16[8,128,384]{2,1,0:T(8,128)(2,1)}, u32[]{:S(2)}, u32[]{:S(2)}) async-start(bf16[8,128,384]{2,1,0:T(8,128)(2,1)} %get-tuple-element.179.d_all), calls=%async_computation.2 | async-start | bytes 1572864 | tf_op jit(solution)/shard_map/all_to_all | solution.py:1004
  129.1 2.5 %collective-permute-start.23 = (bf16[16,32,512]{2,1,0:T(8,128)(2,1)}, bf16[16,32,512]{2,1,0:T(8,128)(2,1)S(1)}, u32[]{:S(2)}, u32[]{:S(2)}) collective-permute-start(bf16[16,32,512]{2,1,0:T(8,128)(2,1)} %bitcast.47), channel_id=1, source_target_pairs={{0,8},{1,9},{2,10},{3,11},{4,12},{5,13},{6,14},{7,15},{8,0},{9,1},... | collective-permute-start | bytes 1572872 | tf_op jit(solution)/shard_map/ppermute | solution.py:352
  129.8 16.4 %collective-permute-start.24 = (bf16[4,32,1152]{2,1,0:T(8,128)(2,1)S(1)}, bf16[4,32,1152]{2,1,0:T(8,128)(2,1)S(1)}, u32[]{:S(2)}, u32[]{:S(2)}) collective-permute-start(bf16[4,32,1152]{2,1,0:T(8,128)(2,1)S(1)} %get-tuple-element.182), channel_id=1, source_target_pairs={{0,1},{1,0},{2,3},{3,2},{4,5},{5,4},{6,7},{7,6},{8,9},{9,8},{10,11... | collective-permute-start | bytes 884744 | tf_op jit(solution)/shard_map/ppermute | solution.py:352
  132.2 11.5 %collective-permute-start.25 = (bf16[8,32,512]{2,1,0:T(8,128)(2,1)S(1)}, bf16[8,32,512]{2,1,0:T(8,128)(2,1)S(1)}, u32[]{:S(2)}, u32[]{:S(2)}) collective-permute-start(bf16[8,32,512]{2,1,0:T(8,128)(2,1)S(1)} %get-tuple-element.185), channel_id=1, source_target_pairs={{0,16},{1,17},{2,18},{3,19},{4,20},{5,21},{6,22},{7,23},{8,24},{9,... | collective-permute-start | bytes 786440 | tf_op jit(solution)/shard_map/ppermute | solution.py:352
  146.2 3.0 %collective-permute-start.26 = (bf16[2,256,512]{2,1,0:T(8,128)(2,1)}, bf16[2,256,512]{2,1,0:T(8,128)(2,1)S(1)}, u32[]{:S(2)}, u32[]{:S(2)}) collective-permute-start(bf16[2,256,512]{2,1,0:T(8,128)(2,1)} %get-tuple-element.205), channel_id=1, source_target_pairs={{0,8},{1,9},{2,10},{3,11},{4,12},{5,13},{6,14},{7,15},{8,0},{9,1},... | collective-permute-start | bytes 1572872 | tf_op jit(solution)/shard_map/ppermute | solution.py:352
  146.2 3.0 %collective-permute-start.27 = (bf16[2,128,1024]{2,1,0:T(8,128)(2,1)}, bf16[2,128,1024]{2,1,0:T(8,128)(2,1)}, u32[]{:S(2)}, u32[]{:S(2)}) collective-permute-start(bf16[2,128,1024]{2,1,0:T(8,128)(2,1)} %get-tuple-element.207), channel_id=1, source_target_pairs={{0,8},{1,9},{2,10},{3,11},{4,12},{5,13},{6,14},{7,15},{8,0},{9,1},... | collective-permute-start | bytes 1572872 | tf_op jit(solution)/shard_map/ppermute | solution.py:352
  149.2 0.8 copy-start.6
  152.3 8.4 %collective-permute-start.28 = (bf16[8,32,512]{2,1,0:T(8,128)(2,1)S(1)}, bf16[8,32,512]{2,1,0:T(8,128)(2,1)S(1)}, u32[]{:S(2)}, u32[]{:S(2)}) collective-permute-start(bf16[8,32,512]{2,1,0:T(8,128)(2,1)S(1)} %get-tuple-element.211), channel_id=1, source_target_pairs={{0,16},{1,17},{2,18},{3,19},{4,20},{5,21},{6,22},{7,23},{8,24},{9,... | collective-permute-start | bytes 786440 | tf_op jit(solution)/shard_map/ppermute | solution.py:352
  153.9 9.5 %collective-permute-start.29 = (bf16[2,32,1152]{2,1,0:T(8,128)(2,1)S(1)}, bf16[2,32,1152]{2,1,0:T(8,128)(2,1)S(1)}, u32[]{:S(2)}, u32[]{:S(2)}) collective-permute-start(bf16[2,32,1152]{2,1,0:T(8,128)(2,1)S(1)} %get-tuple-element.225), channel_id=1, source_target_pairs={{0,4},{1,5},{2,6},{3,7},{4,0},{5,1},{6,2},{7,3},{8,12},{9,13},{10,... | collective-permute-start | bytes 442376 | tf_op jit(solution)/shard_map/ppermute | solution.py:352
  164.0 13.1 %collective-permute-start.30 = (bf16[1,32,1152]{2,1,0:T(8,128)(2,1)S(1)}, bf16[1,32,1152]{2,1,0:T(8,128)(2,1)S(1)}, u32[]{:S(2)}, u32[]{:S(2)}) collective-permute-start(bf16[1,32,1152]{2,1,0:T(8,128)(2,1)S(1)} %get-tuple-element.227), channel_id=1, source_target_pairs={{0,2},{1,3},{2,0},{3,1},{4,6},{5,7},{6,4},{7,5},{8,10},{9,11},{10,... | collective-permute-start | bytes 221192 | tf_op jit(solution)/shard_map/ppermute | solution.py:352
  166.2 17.7 %all-to-all-start.3 = ((bf16[8,64,512]{2,1,0:T(8,128)(2,1)}), bf16[8,64,512]{2,1,0:T(8,128)(2,1)S(1)}, u32[]{:S(2)}, u32[]{:S(2)}) async-start(bf16[8,64,512]{2,1,0:T(8,128)(2,1)} %shard_map.278), calls=%async_computation.3 | async-start | bytes 1048576 | tf_op jit(solution)/shard_map/all_to_all | solution.py:1002
  169.8 9.1 %collective-permute-start.31 = (bf16[128,1024]{1,0:T(8,128)(2,1)S(1)}, bf16[128,1024]{1,0:T(8,128)(2,1)S(1)}, u32[]{:S(2)}, u32[]{:S(2)}) collective-permute-start(bf16[128,1024]{1,0:T(8,128)(2,1)S(1)} %get-tuple-element.231), channel_id=1, source_target_pairs={{0,16},{1,17},{2,18},{3,19},{4,20},{5,21},{6,22},{7,23},{8,24},{9,... | collective-permute-start | bytes 786440 | tf_op jit(solution)/shard_map/ppermute | solution.py:352
